TPU v7x, 128 devices: a whole 4x4x4 slice. The times are simulated.
128 devices in a mesh: grid: 8 (over x, core), cell: 16 (over z, y).
Axes of the slice: x: 4, y: 4, z: 4, core: 2. Of those that a mesh axis runs over, the one named last changes fastest.
Arguments:
- probes: float32 [16, 8, 524288], P(None, 'grid', 'cell'), may hold values from -180 to 180
- centre: float32 [8, 524288], P('grid', 'cell'), may hold values from 2.5 to 3.5
- lower_coef: float32 [8, 524288], P('grid', 'cell'), may hold values from 0.1 to 1
- upper_coef: float32 [8, 524288], P('grid', 'cell'), may hold values from 0.1 to 1
- donor_cells: int32 [8, 4, 98304], P('grid', None, 'cell'), may hold values from 0 to 32767
- receptor_cells: int32 [8, 98304], P('grid', 'cell'), may hold values from 0 to 32767
- weights: float32 [8, 4, 98304], P('grid', None, 'cell'), may hold values from 0.05 to 0.6
Outputs:
- basis: float32 [16, 8, 524288], P(None, 'grid', 'cell')
- factor: float32 [16, 16], replicated
Inputs may be any that keep to these rules, and one draw needn't show every extreme that they name: `donor_cells`: indices within the donor block. `receptor_cells`: indices within the receptor block.
All inputs are finite; a program needn't handle non-finite values.
Results may differ from a plain program's by a relative error of at most 0.00005.
Values sent between devices are 32-bit elements; how exact they have to be, the bound alone decides.
No kernel may reach another device: no remote copies, remote signals or barrier semaphores. Data moves between devices by JAX's collectives and lax.ppermute only.
A program may use at most 320 MiB of HBM per device.

v0:
```python
import jax
import jax.numpy as jnp
from jax import lax
from jax.sharding import PartitionSpec as P


def shifted(block, axis, distance):
    devices = range(lax.axis_size(axis))
    route = [((i - distance) % len(devices), i) for i in devices]
    return lax.ppermute(block, axis, route)


def padded_2(block, sides, width):
    for axis, dim in sides:
        count = lax.axis_size(axis)
        forward = [(i, i + 1) for i in range(count - 1)]
        backward = [(target, source) for source, target in forward]
        low = lax.ppermute(
            lax.slice_in_dim(block, block.shape[dim] - width, None, axis=dim), axis, forward
        )
        high = lax.ppermute(lax.slice_in_dim(block, 0, width, axis=dim), axis, backward)
        block = jnp.concatenate([low, block, high], axis=dim)
    return block


def to_receptors(pieces, place):
    columns = [lax.index_in_dim(pieces, column, place + 1, keepdims=False) for column in range(3)]
    for offset in (-1, 1):
        columns[offset + 1] = shifted(columns[offset + 1], "cell", offset)
    joined = jnp.stack(columns, axis=place + 1)
    layers = [lax.index_in_dim(joined, layer, place, keepdims=False) for layer in range(2)]
    for offset in (1, 2):
        layers[offset - 1] = shifted(layers[offset - 1], "grid", offset)
    return jnp.stack(layers, axis=place)


def to_donors(pieces, place):
    columns = [lax.index_in_dim(pieces, column, place + 1, keepdims=False) for column in range(3)]
    for offset in (-1, 1):
        columns[offset + 1] = shifted(columns[offset + 1], "cell", -offset)
    joined = jnp.stack(columns, axis=place + 1)
    layers = [lax.index_in_dim(joined, layer, place, keepdims=False) for layer in range(2)]
    for offset in (1, 2):
        layers[offset - 1] = shifted(layers[offset - 1], "grid", -offset)
    return jnp.stack(layers, axis=place)


def body(probes, centre, lower_coef, upper_coef, donor_cells, receptor_cells, weights):
    state = probes[:, 0, :]
    width = state.shape[1]
    fringe_len = donor_cells.shape[2] // 6
    padded = padded_2(probes, (("cell", 2),), 1)
    tangent = centre * state - lower_coef * padded[:, 0, :width] - upper_coef * padded[:, 0, 2:]
    donor_index = donor_cells[0].reshape(4, 2, 3, fringe_len)
    recv_index = receptor_cells[0].reshape(2, 3, fringe_len)
    recv_weight = weights[0].reshape(4, 2, 3, fringe_len)
    donor_vals = state[:, donor_index]
    arrived = to_receptors(donor_vals, 2)
    coupled = jnp.sum(recv_weight[None] * arrived, axis=1)
    tangent = tangent.at[:, recv_index].add(coupled)
    stacked = jnp.stack([upper_coef * tangent, lower_coef * tangent])[:, :, None, :]
    rims = padded_2(stacked, (("cell", 3),), 1)
    adjoint = centre * tangent - rims[0, :, 0, :width] - rims[1, :, 0, 2:]
    at_receptor = tangent[:, recv_index]
    outgoing = recv_weight[None] * at_receptor[:, None]
    terms = to_donors(outgoing, 2)
    adjoint = adjoint.at[:, donor_index].add(terms)
    local_gram = jnp.dot(adjoint, adjoint.T, precision=lax.Precision.HIGHEST)
    total_cells = lax.axis_size("grid") * lax.axis_size("cell") * width
    gram_matrix = lax.psum(local_gram, ("grid", "cell")) / jnp.float32(total_cells)
    factor = jnp.linalg.cholesky(gram_matrix)
    basis = jax.scipy.linalg.solve_triangular(factor, adjoint, lower=True)
    return (basis[:, None, :], factor)


def solution(mesh):
    in_specs = (
        P(None, "grid", "cell"),
        P("grid", "cell"),
        P("grid", "cell"),
        P("grid", "cell"),
        P("grid", None, "cell"),
        P("grid", "cell"),
        P("grid", None, "cell"),
    )
    out_specs = (P(None, "grid", "cell"), P())
    return jax.shard_map(body, mesh=mesh, in_specs=in_specs, out_specs=out_specs, check_vma=False)
```

profile of v0, /device:TPU:0, one launch (start us, length us, event | category | flops | bytes accessed | tf_op | source)
XLA Modules:
  0.0 582.7 jit_solution(1943283486254255386)
XLA Ops:
  0.6 11.2 %copy.230 = f32[16,1,32768]{0,2,1:T(8,128)} copy(f32[16,1,32768]{2,1,0:T(1,128)} %param.7) | data formatting | bytes 4194304 | tf_op args[0]
  12.1 87.1 %gather_fusion = f32[24576,16]{1,0:T(8,128)} fusion(f32[16,32768]{0,1:T(8,128)} %bitcast.102, s32[24576]{0:T(1024)S(1)} %broadcast_clamp_fusion), kind=kCustom, calls=%fused_computation | custom fusion | bytes 3244032 | tf_op jit(solution)/shard_map/gather | solution.py:57
  99.3 7.5 %copy.237 = f32[4,2,3,1024,16]{3,4,1,0,2:T(8,128)S(1)} copy(f32[4,2,3,1024,16]{4,3,2,1,0:T(8,128)} %bitcast.104) | data formatting | bytes 3145728 | tf_op jit(solution)/shard_map/gather | solution.py:57
  106.8 0.9 slice_bitcast_fusion.7
  107.7 1.7 collective-permute-start.3
  109.4 4.9 collective-permute-start.2
  114.3 0.7 fusion.15
  115.0 1.3 collective-permute-start.1
  116.3 4.5 collective-permute-start
  120.8 0.5 broadcast.114
  121.3 0.7 reduce.9
  122.2 0.6 broadcast_clamp_fusion.1
  122.8 3.6 collective-permute-done.3
  126.4 0.2 pad_maximum_fusion.5
  126.6 0.2 slice_bitcast_fusion.3
  126.8 1.6 collective-permute-start.5
  128.5 23.2 %fusion.8 = f32[16,32768]{0,1:T(8,128)} fusion(f32[16,1,1]{0,2,1:T(1,128)S(1)} %collective-permute-done.1, f32[16,1,32768]{0,2,1:T(8,128)} %copy.230, f32[16,1,1]{0,2,1:T(1,128)S(1)} %collective-permute-done, f32[32768]{0:T(1024)S(1)} %bitcast.116, f32[32768]{0:T(1024)S(1)} %bitcast.118, f32[32768]{0:T(1024)S(1)} %bitcast.119), kind=kLoop, calls=%fused_computation.17 | loop fusion | flops 3670016 | bytes 4587648 | tf_op jit(solution)/shard_map/sub | solution.py:53
  151.7 3.5 collective-permute-done.4
  155.3 0.2 fusion.12
  155.5 1.0 copy.258
  156.5 41.5 %scatter_fusion = f32[16,32768]{0,1:T(8,128)} fusion(f32[16,32768]{0,1:T(8,128)} %fusion.8, s32[6144]{0:T(1024)} %copy-done.7, f32[6144,16]{1,0:T(8,128)S(1)} %bitcast.106), kind=kCustom, calls=%fused_computation.2 | custom fusion | flops 98304 | bytes 1204224 | tf_op jit(solution)/shard_map/scatter-add | solution.py:60
  198.0 18.3 %multiply_bitcast_fusion.1 = (f32[1,16,32768]{1,2,0:T(8,128)}, f32[1,16,32768]{1,2,0:T(8,128)}) fusion(f32[16,32768]{0,1:T(8,128)} %scatter_fusion, f32[32768]{0:T(1024)} %bitcast.115, f32[32768]{0:T(1024)} %bitcast.117), kind=kLoop, calls=%fused_computation.23 | loop fusion | flops 1048576 | bytes 6553600 | tf_op jit(solution)/shard_map/stack | solution.py:61
  216.3 21.8 %gather_fusion.1 = f32[6144,16]{1,0:T(8,128)S(1)} fusion(f32[16,32768]{0,1:T(8,128)} %scatter_fusion, s32[6144]{0:T(1024)S(1)} %copy-done.8), kind=kCustom, calls=%fused_computation.1 | custom fusion | bytes 811008 | tf_op jit(solution)/shard_map/gather | solution.py:64
  238.1 1.1 copy.245
  239.2 1.1 broadcast_multiply_fusion
  240.3 0.2 slice_bitcast_fusion.5
  240.6 4.6 collective-permute-start.9
  245.2 0.1 collective-permute-start.8
  245.3 32.7 %fusion = (f32[2,16,1,32768]{1,3,2,0:T(8,128)}, f32[2,16,1,32768]{1,3,0,2:T(8,128)}) fusion(f32[1,16,32768]{1,2,0:T(8,128)} %get-tuple-element.23, f32[1,16,32768]{1,2,0:T(8,128)} %get-tuple-element.22), kind=kLoop, calls=%fused_computation.6 | loop fusion | flops 1048576 | bytes 12582912 | tf_op jit(solution)/shard_map/broadcast_in_dim | solution.py:61
  278.0 0.7 slice.100
  278.7 1.3 collective-permute-start.7
  280.0 0.7 slice.99
  280.7 4.5 collective-permute-start.6
  285.4 0.2 pad_maximum_fusion.6
  285.5 0.1 slice_bitcast_fusion.1
  285.7 1.8 collective-permute-start.11
  287.5 30.8 %fusion.3 = f32[16,32768]{0,1:T(8,128)} fusion(f32[2,16,1,1]{1,3,0,2:T(1,128)S(1)} %collective-permute-done.7, f32[2,16,1,32768]{1,3,0,2:T(8,128)} %get-tuple-element.21, f32[2,16,1,32768]{1,3,2,0:T(8,128)} %get-tuple-element.20, f32[2,16,1,1]{1,3,2,0:T(1,128)S(1)} %collective-permute-done.6, f32[16,32768]{0,1:T(8,128)} %scatter_fusion, f32[32768]{0:T(1024)S(1)} %bitcast.120), kind=kLoop, calls=%fused_computation.10 | loop fusion | flops 2621440 | bytes 12714240 | tf_op jit(solution)/shard_map/sub | solution.py:63
  318.3 0.1 maximum_bitcast_fusion
  318.4 6.6 %copy.259 = f32[4,2,3,1024,16]{4,3,2,1,0:T(8,128)} copy(f32[4,2,3,1024,16]{3,4,2,1,0:T(8,128)S(1)} %maximum_bitcast_fusion) | data formatting | bytes 3145728 | tf_op jit(solution)/shard_map/stack | solution.py:45
  325.0 129.2 %scatter_fusion.1 = f32[16,32768]{0,1:T(8,128)} fusion(f32[16,32768]{0,1:T(8,128)} %fusion.3, s32[24576]{0:T(1024)S(1)} %copy-done.2, f32[24576,16]{1,0:T(8,128)} %bitcast.103), kind=kCustom, calls=%fused_computation.3 | custom fusion | flops 393216 | bytes 4816896 | tf_op jit(solution)/shard_map/scatter-add | solution.py:67
  454.2 37.1 %fusion.16 = f32[16,16]{0,1:T(8,128)S(1)} fusion(f32[16,32768]{0,1:T(8,128)} %scatter_fusion.1), kind=kOutput, calls=%fused_computation.55 | convolution fusion | flops 100663296 | bytes 2098176 | tf_op jit(solution)/shard_map/dot_general | solution.py:68
  491.4 66.1 %psum.7 = f32[16,16]{0,1:T(8,128)S(1)} all-reduce(f32[16,16]{0,1:T(8,128)S(1)} %fusion.16), channel_id=1, replica_groups=mesh['grid'=8,'cell'=16] {'grid','cell'}, use_global_device_ids=true, to_apply=%region_3.0 | all-reduce | flops 256 | bytes 2048 | tf_op jit(solution)/shard_map/psum | solution.py:70
  557.5 1.5 cholesky.16
  559.0 0.6 compare_reduce_fusion
  559.6 1.2 select_bitcast_fusion
  560.9 1.2 custom-call.7
  562.1 17.1 %convolution_bitcast_fusion = f32[16,1,32768]{2,0,1:T(8,128)S(1)} fusion(f32[16,32768]{0,1:T(8,128)} %scatter_fusion.1, f32[1,16,16]{1,2,0:T(8,128)S(1)} %custom-call.7), kind=kOutput, calls=%fused_computation.4 | convolution fusion | flops 100663296 | bytes 4195328 | tf_op jit(solution)/shard_map/jit(_solve_triangular)/triangular_solve | solution.py:72
  579.2 3.5 copy.256
  (54 shorter events, 0.8 us)
Async XLA Ops:
  0.6 11.3 %copy-start.10 = (s32[1,4,6144]{2,1,0:T(4,128)S(1)}, s32[1,4,6144]{2,1,0:T(4,128)}, u32[]{:S(2)}) copy-start(s32[1,4,6144]{2,1,0:T(4,128)} %param.11) | copy-start | bytes 294916
  12.1 87.2 %copy-start.1 = (s32[24576]{0:T(1024)}, s32[24576]{0:T(1024)S(1)}, u32[]{:S(2)}) copy-start(s32[24576]{0:T(1024)S(1)} %reshape.74) | copy-start | bytes 294916
  12.1 109.2 %copy-start.11 = (s32[1,6144]{1,0:T(1,128)S(1)}, s32[1,6144]{1,0:T(1,128)}, u32[]{:S(2)}) copy-start(s32[1,6144]{1,0:T(1,128)} %param.12) | copy-start | bytes 73732
  12.1 110.0 %copy-start.9 = (f32[1,4,6144]{2,1,0:T(4,128)S(1)}, f32[1,4,6144]{2,1,0:T(4,128)}, u32[]{:S(2)}) copy-start(f32[1,4,6144]{2,1,0:T(4,128)} %param.13) | copy-start | bytes 294916
  99.2 29.3 %copy-start.3 = (f32[1,32768]{1,0:T(1,128)S(1)}, f32[1,32768]{1,0:T(1,128)}, u32[]{:S(2)}) copy-start(f32[1,32768]{1,0:T(1,128)} %param.10) | copy-start | bytes 393220
  99.2 29.3 %copy-start.4 = (f32[1,32768]{1,0:T(1,128)S(1)}, f32[1,32768]{1,0:T(1,128)}, u32[]{:S(2)}) copy-start(f32[1,32768]{1,0:T(1,128)} %param.9) | copy-start | bytes 393220
  99.2 29.3 %copy-start.5 = (f32[1,32768]{1,0:T(1,128)S(1)}, f32[1,32768]{1,0:T(1,128)}, u32[]{:S(2)}) copy-start(f32[1,32768]{1,0:T(1,128)} %param.8) | copy-start | bytes 393220
  107.7 18.7 %collective-permute-start.3 = (f32[16,4,2,1024]{3,0,2,1:T(8,128)}, f32[16,4,2,1024]{3,0,2,1:T(8,128)S(1)}, u32[]{:S(2)}, u32[]{:S(2)}) collective-permute-start(f32[16,4,2,1024]{3,0,2,1:T(8,128)} %get-tuple-element.35), channel_id=1, source_target_pairs={{15,0},{0,1},{1,2},{2,3},{3,4},{4,5},{5,6},{6,7},{7,8},{8,9},{9,10... | collective-permute-start | bytes 1572872 | tf_op jit(solution)/shard_map/ppermute | solution.py:10
  109.4 17.0 %collective-permute-start.2 = (f32[16,4,2,1024]{3,0,2,1:T(8,128)S(1)}, f32[16,4,2,1024]{3,0,2,1:T(8,128)S(1)}, u32[]{:S(2)}, u32[]{:S(2)}) collective-permute-start(f32[16,4,2,1024]{3,0,2,1:T(8,128)S(1)} %get-tuple-element.33), channel_id=1, source_target_pairs={{1,0},{2,1},{3,2},{4,3},{5,4},{6,5},{7,6},{8,7},{9,8},{10,9},{11,1... | collective-permute-start | bytes 1572872 | tf_op jit(solution)/shard_map/ppermute | solution.py:10
  115.0 13.5 %collective-permute-start.1 = (f32[16,1,1]{0,2,1:T(1,128)S(1)}, f32[16,1,1]{0,2,1:T(1,128)S(1)}, u32[]{:S(2)}, u32[]{:S(2)}) collective-permute-start(f32[16,1,1]{0,2,1:T(1,128)S(1)} %get-tuple-element.25), channel_id=1, source_target_pairs={{1,0},{2,1},{3,2},{4,3},{5,4},{6,5},{7,6},{8,7},{9,8},{10,9},{11,1... | collective-permute-start | bytes 200 | tf_op jit(solution)/shard_map/ppermute | solution.py:21
  116.3 12.2 %collective-permute-start = (f32[16,1,1]{0,2,1:T(1,128)S(1)}, f32[16,1,1]{0,2,1:T(1,128)S(1)}, u32[]{:S(2)}, u32[]{:S(2)}) collective-permute-start(f32[16,1,1]{0,2,1:T(1,128)S(1)} %get-tuple-element.24), channel_id=1, source_target_pairs={{0,1},{1,2},{2,3},{3,4},{4,5},{5,6},{6,7},{7,8},{8,9},{9,10},{10,1... | collective-permute-start | bytes 200 | tf_op jit(solution)/shard_map/ppermute | solution.py:18
  122.1 4.7 copy-start.7
  122.2 33.1 %copy-start = (f32[4,2,3,1024]{3,2,0,1:T(4,128)}, f32[4,2,3,1024]{3,2,0,1:T(4,128)S(1)}, u32[]{:S(2)}) copy-start(f32[4,2,3,1024]{3,2,0,1:T(4,128)S(1)} %copy.235) | copy-start | bytes 294916
  126.8 24.9 %collective-permute-start.5 = (f32[16,4,3,1024]{3,0,2,1:T(8,128)S(1)}, f32[16,4,3,1024]{3,0,2,1:T(8,128)S(1)}, u32[]{:S(2)}, u32[]{:S(2)}) collective-permute-start(f32[16,4,3,1024]{3,0,2,1:T(8,128)S(1)} %copy.239), channel_id=1, source_target_pairs={{96,0},{112,16},{0,32},{16,48},{32,64},{48,80},{64,96},{80,112},{9... | collective-permute-start | bytes 2359304 | tf_op jit(solution)/shard_map/ppermute | solution.py:10
  128.5 26.8 %collective-permute-start.4 = (f32[16,4,3,1024]{3,0,2,1:T(8,128)S(1)}, f32[16,4,3,1024]{3,0,2,1:T(8,128)S(1)}, u32[]{:S(2)}, u32[]{:S(2)}) collective-permute-start(f32[16,4,3,1024]{3,0,2,1:T(8,128)S(1)} %copy.238), channel_id=1, source_target_pairs={{112,0},{0,16},{16,32},{32,48},{48,64},{64,80},{80,96},{96,112},{1... | collective-permute-start | bytes 2359304 | tf_op jit(solution)/shard_map/ppermute | solution.py:10
  198.0 18.3 %copy-start.8 = (s32[6144]{0:T(1024)S(1)}, s32[6144]{0:T(1024)}, u32[]{:S(2)}) copy-start(s32[6144]{0:T(1024)} %broadcast_clamp_fusion.1) | copy-start | bytes 73732
  240.6 44.7 %collective-permute-start.9 = (f32[16,4,2,1024]{3,0,2,1:T(8,128)S(1)}, f32[16,4,2,1024]{3,0,2,1:T(8,128)S(1)}, u32[]{:S(2)}, u32[]{:S(2)}) collective-permute-start(f32[16,4,2,1024]{3,0,2,1:T(8,128)S(1)} %copy.248), channel_id=1, source_target_pairs={{1,0},{2,1},{3,2},{4,3},{5,4},{6,5},{7,6},{8,7},{9,8},{10,9},{11,1... | collective-permute-start | bytes 1572872 | tf_op jit(solution)/shard_map/ppermute | solution.py:10
  245.2 40.1 %collective-permute-start.8 = (f32[16,4,2,1024]{3,0,2,1:T(8,128)S(1)}, f32[16,4,2,1024]{3,0,2,1:T(8,128)S(1)}, u32[]{:S(2)}, u32[]{:S(2)}) collective-permute-start(f32[16,4,2,1024]{3,0,2,1:T(8,128)S(1)} %copy.246), channel_id=1, source_target_pairs={{15,0},{0,1},{1,2},{2,3},{3,4},{4,5},{5,6},{6,7},{7,8},{8,9},{9,10... | collective-permute-start | bytes 1572872 | tf_op jit(solution)/shard_map/ppermute | solution.py:10
  245.3 42.2 %copy-start.6 = (f32[1,32768]{1,0:T(1,128)S(1)}, f32[1,32768]{1,0:T(1,128)}, u32[]{:S(2)}) copy-start(f32[1,32768]{1,0:T(1,128)} %param.8) | copy-start | bytes 393220
  278.7 8.7 %collective-permute-start.7 = (f32[2,16,1,1]{1,3,0,2:T(1,128)S(1)}, f32[2,16,1,1]{1,3,0,2:T(1,128)S(1)}, u32[]{:S(2)}, u32[]{:S(2)}) collective-permute-start(f32[2,16,1,1]{1,3,0,2:T(1,128)S(1)} %slice.100), channel_id=1, source_target_pairs={{1,0},{2,1},{3,2},{4,3},{5,4},{6,5},{7,6},{8,7},{9,8},{10,9},{11,1... | collective-permute-start | bytes 392 | tf_op jit(solution)/shard_map/ppermute | solution.py:21
  280.7 6.8 %collective-permute-start.6 = (f32[2,16,1,1]{1,3,2,0:T(1,128)S(1)}, f32[2,16,1,1]{1,3,2,0:T(1,128)S(1)}, u32[]{:S(2)}, u32[]{:S(2)}) collective-permute-start(f32[2,16,1,1]{1,3,2,0:T(1,128)S(1)} %slice.99), channel_id=1, source_target_pairs={{0,1},{1,2},{2,3},{3,4},{4,5},{5,6},{6,7},{7,8},{8,9},{9,10},{10,1... | collective-permute-start | bytes 392 | tf_op jit(solution)/shard_map/ppermute | solution.py:18
  285.7 32.6 %collective-permute-start.11 = (f32[16,4,3,1024]{3,0,2,1:T(8,128)S(1)}, f32[16,4,3,1024]{3,0,2,1:T(8,128)S(1)}, u32[]{:S(2)}, u32[]{:S(2)}) collective-permute-start(f32[16,4,3,1024]{3,0,2,1:T(8,128)S(1)} %get-tuple-element.27), channel_id=1, source_target_pairs={{32,0},{48,16},{64,32},{80,48},{96,64},{112,80},{0,96},{16,112},{3... | collective-permute-start | bytes 2359304 | tf_op jit(solution)/shard_map/ppermute | solution.py:10
  287.5 30.8 %collective-permute-start.10 = (f32[16,4,3,1024]{3,0,2,1:T(8,128)S(1)}, f32[16,4,3,1024]{3,0,2,1:T(8,128)S(1)}, u32[]{:S(2)}, u32[]{:S(2)}) collective-permute-start(f32[16,4,3,1024]{3,0,2,1:T(8,128)S(1)} %get-tuple-element.26), channel_id=1, source_target_pairs={{16,0},{32,16},{48,32},{64,48},{80,64},{96,80},{112,96},{0,112},{1... | collective-permute-start | bytes 2359304 | tf_op jit(solution)/shard_map/ppermute | solution.py:10
  318.3 6.7 %copy-start.2 = (s32[24576]{0:T(1024)S(1)}, s32[24576]{0:T(1024)}, u32[]{:S(2)}) copy-start(s32[24576]{0:T(1024)} %copy-done.1) | copy-start | bytes 294916
where the time goes:
time: 584 us; the launch traced here: 583 us
  other arithmetic  283 us (48%)
  local copies, waits for them, and re-layouts  145 us (25%)
  blocking collectives  66.1 us (11%)
  matrix products  54.2 us (9%)
  starting transfers between devices  26.3 us (5%)
  waiting for transfers between devices  7.12 us (1%)
    scatter-add x1, other arithmetic, body(): adjoint = adjoint.at[:, donor_index].add(terms)  129 us
    gather x2, local copies, waits for them, and re-layouts, body(): donor_vals = state[:, donor_index]  94.6 us
    psum x1, blocking collectives, body(): lax.psum(local_gram, ('grid', 'cell')) / jnp.float32(total_cells)  66.1 us
    scatter-add x1, other arithmetic, body(): tangent = tangent.at[:, recv_index].add(coupled)  41.5 us
    dot_general x1, matrix products, body(): local_gram = jnp.dot(adjoint, adjoint.T, precision=lax.Precision.HIGHEST)  37.1 us
    broadcast_in_dim x1, other arithmetic, body(): jnp.stack([upper_coef * tangent, lower_coef * tangent])[:, :, None, :]  32.7 us
    sub x1, other arithmetic, body(): adjoint = centre * tangent - rims[0, :, 0, :width] - rims[1, :, 0, 2:]  30.8 us
    sub x1, other arithmetic, body(): centre * state - lower_coef * padded[:, 0, :width]  23.2 us
  transfers between devices with their start and end apart: 12, of which 2 were waited for; matrix products, arithmetic and copies ran while one was open for 16% of the time, Pallas kernels for 0%

commit v1 on v0

v1 whole, which is shorter than its diff:
```python
import functools

import jax
import jax.numpy as jnp
from jax import lax
from jax.experimental import pallas as pl
from jax.experimental.pallas import tpu as pltpu
from jax.sharding import PartitionSpec as P

f32 = jnp.float32
i32 = jnp.int32
bf16 = jnp.bfloat16

PROBES = 16
GROUPS = 8
ROWS = 4096
LANES = 128
PARTNERS = 6
FRINGE = 1024
SLOTS = PARTNERS * FRINGE
TILES = ROWS // LANES
WAYS = 8
UNROLL = 8

AXES = ("grid", "cell")
PARTNER_OFFSETS = [(d, e) for d in (1, 2) for e in (-1, 0, 1)]

VMEM = pl.BlockSpec(memory_space=pltpu.VMEM)
HBM = pl.BlockSpec(memory_space=pl.ANY)
PARAMS = pltpu.CompilerParams(vmem_limit_bytes=56 << 20)


def aligned(start, size):
    return pl.ds(pl.multiple_of(start, size), size)


def rows_of(start, size):
    return pl.ds(pl.multiple_of(start, 8), size)


def split(x):
    high = x.astype(bf16)
    return high, (x - high.astype(f32)).astype(bf16)


def start_index_copies(rows_hbm, parts, sem):
    count = parts[0].shape[0]
    copies = [
        pltpu.make_async_copy(rows_hbm.at[pl.ds(w * count, count)], parts[w], sem.at[w])
        for w in range(WAYS)
    ]
    for copy in copies:
        copy.start()
    return copies


def gather_rows(table, parts, staged):
    count = parts[0].shape[0]

    def step(j, carry):
        for u in range(UNROLL):
            q = j * UNROLL + u
            for w in range(WAYS):
                row = parts[w][q]
                staged[pl.ds(w * count + q, 1), :] = table[pl.ds(row, 1), :]
        return carry

    lax.fori_loop(0, count // UNROLL, step, 0)


def clear(sums):
    def step(j, carry):
        for total in sums:
            for u in range(4):
                total[rows_of(j * 32 + u * 8, 8), :] = jnp.zeros((8, LANES), f32)
        return carry

    lax.fori_loop(0, ROWS // 32, step, 0)


def add_rows(sums, parts, staged):
    count = parts[0].shape[0]

    def step(j, carry):
        for u in range(UNROLL):
            q = j * UNROLL + u
            for w in range(WAYS):
                row = parts[w][q]
                term = staged[pl.ds(w * count + q, 1), :]
                sums[w][pl.ds(row, 1), :] = sums[w][pl.ds(row, 1), :] + term
        return carry

    lax.fori_loop(0, count // UNROLL, step, 0)


def groups_of(cells, m, offset):
    return jnp.broadcast_to(cells[m : m + 1, aligned(offset, LANES)], (8, LANES)) >> 12


def select_fields(staged, cells, weights, out):
    many = cells.shape[0]
    for k in range(PARTNERS):

        def step(b, carry):
            local = aligned(b * LANES, LANES)
            offset = k * FRINGE + b * LANES
            total = [jnp.zeros((8, LANES), f32)] * 2
            for m in range(many):
                field = staged[aligned(m * SLOTS + offset, LANES), :].T
                group = groups_of(cells, m, offset)
                scale = 1.0 if weights is None else jnp.broadcast_to(weights[k][m : m + 1, local], (8, LANES))
                for g in range(GROUPS):
                    factor = jnp.where(group == g, scale, 0.0)
                    for h in range(2):
                        at = g * PROBES + h * 8
                        total[h] = total[h] + field[at : at + 8, :] * factor
            for h in range(2):
                out[k][h * 8 : h * 8 + 8, local] = total[h]
            return carry

        lax.fori_loop(0, FRINGE // LANES, step, 0)


def spread_fields(messages, cells, weights, staged):
    many = cells.shape[0]
    for k in range(PARTNERS):

        def step(b, carry):
            local = aligned(b * LANES, LANES)
            offset = k * FRINGE + b * LANES
            field = [messages[k][h * 8 : h * 8 + 8, local] for h in range(2)]
            for m in range(many):
                group = groups_of(cells, m, offset)
                scaled = field
                if weights is not None:
                    scale = jnp.broadcast_to(weights[k][m : m + 1, local], (8, LANES))
                    scaled = [part * scale for part in field]
                terms = [jnp.where(group == g, scaled[h], 0.0) for g in range(GROUPS) for h in range(2)]
                staged[aligned(m * SLOTS + offset, LANES), :] = jnp.concatenate(terms, axis=0).T
            return carry

        lax.fori_loop(0, FRINGE // LANES, step, 0)


def fill_ends(padded, low, high):
    lane = lax.broadcasted_iota(i32, (1, LANES), 1)
    before = pltpu.roll(padded[ROWS : ROWS + 8, :], PROBES, 1)[7:8, :]
    after = pltpu.roll(padded[8:16, :], LANES - PROBES, 1)[0:1, :]
    padded[7:8, :] = jnp.where(lane < PROBES, low, before)
    padded[ROWS + 8 : ROWS + 9, :] = jnp.where(lane >= LANES - PROBES, high, after)


def pack_kernel(probes, centre, lower, upper, low, high, table, tangent, c_out, l_out, u_out, padded):
    def packed(ref, height, tile):
        parts = []
        for g in range(GROUPS):
            part = ref[:, aligned(g * ROWS + tile * LANES, LANES)]
            parts.append(part if height == PROBES else jnp.broadcast_to(part, (PROBES, LANES)))
        return jnp.concatenate(parts, axis=0).T

    def step(tile, carry):
        at = aligned(tile * LANES, LANES)
        block = packed(probes, PROBES, tile)
        table[at, :] = block
        padded[rows_of(tile * LANES + 8, LANES), :] = block
        c_out[at, :] = packed(centre, 1, tile)
        l_out[at, :] = packed(lower, 1, tile)
        u_out[at, :] = packed(upper, 1, tile)
        return carry

    lax.fori_loop(0, TILES, step, 0)
    ends = [jnp.broadcast_to(low[...], (PROBES, LANES)), jnp.zeros((96, LANES), f32)]
    ends.append(jnp.broadcast_to(high[...], (PROBES, LANES)))
    ends = jnp.concatenate(ends, axis=0).T[0:1, :]
    fill_ends(padded, ends, ends)

    def stencil(j, carry):
        for u in range(4):
            start = j * 32 + u * 8
            at = rows_of(start, 8)
            tangent[at, :] = (
                c_out[at, :] * padded[rows_of(start + 8, 8), :]
                - l_out[at, :] * padded[pl.ds(start + 7, 8), :]
                - u_out[at, :] * padded[pl.ds(start + 9, 8), :]
            )
        return carry

    lax.fori_loop(0, ROWS // 32, stencil, 0)


def field(height=ROWS):
    return jax.ShapeDtypeStruct((height, LANES), f32)


def pack(probes, centre, lower, upper, low, high):
    return pl.pallas_call(
        pack_kernel,
        out_shape=[field()] * 5,
        in_specs=[VMEM] * 6,
        out_specs=[VMEM] * 5,
        scratch_shapes=[pltpu.VMEM((ROWS + 16, LANES), f32)],
        compiler_params=PARAMS,
        name="pack",
    )(probes, centre, lower, upper, low, high)


def index_scratch(count):
    return [pltpu.SemaphoreType.DMA((WAYS,))] + [pltpu.SMEM((count // WAYS,), i32)] * WAYS


def send_kernel(*refs):
    table, cells, rows_hbm = refs[:3]
    weights = refs[3:9]
    out = refs[9:15]
    staged, sem = refs[15:17]
    parts = refs[17:]
    copies = start_index_copies(rows_hbm, parts, sem)
    for copy in copies:
        copy.wait()
    gather_rows(table, parts, staged)
    select_fields(staged, cells, weights, out)


MESSAGE = jax.ShapeDtypeStruct((PROBES, FRINGE), f32)


def send(table, cells, rows, weights):
    count = 4 * SLOTS
    return pl.pallas_call(
        send_kernel,
        out_shape=[MESSAGE] * PARTNERS,
        in_specs=[VMEM, VMEM, HBM] + [VMEM] * PARTNERS,
        out_specs=[VMEM] * PARTNERS,
        scratch_shapes=[pltpu.VMEM((count, LANES), f32)] + index_scratch(count),
        compiler_params=PARAMS,
        name="send",
    )(table, cells, rows, *weights)


def couple_kernel(*refs):
    base, lower, upper, cells, rows_hbm = refs[:5]
    messages = refs[5:11]
    tangent = refs[11]
    out = refs[12:18]
    first, last = refs[18:20]
    staged, sem = refs[20:22]
    parts = refs[22 : 22 + WAYS]
    sums = refs[22 + WAYS :]
    copies = start_index_copies(rows_hbm, parts, sem)
    clear(sums)
    spread_fields(messages, cells, None, staged)
    for copy in copies:
        copy.wait()
    add_rows(sums, parts, staged)

    def total(j, carry):
        for u in range(4):
            at = rows_of(j * 32 + u * 8, 8)
            value = base[at, :]
            for part in sums:
                value = value + part[at, :]
            tangent[at, :] = value
        return carry

    lax.fori_loop(0, ROWS // 32, total, 0)
    first[...] = lower[0:8, :] * tangent[0:8, :]
    last[...] = upper[ROWS - 8 : ROWS, :] * tangent[ROWS - 8 : ROWS, :]
    gather_rows(tangent, parts, staged)
    select_fields(staged, cells, None, out)


def couple(base, lower, upper, cells, rows, messages):
    return pl.pallas_call(
        couple_kernel,
        out_shape=[field()] + [MESSAGE] * PARTNERS + [field(8)] * 2,
        in_specs=[VMEM] * 4 + [HBM] + [VMEM] * PARTNERS,
        out_specs=[VMEM] * (PARTNERS + 3),
        scratch_shapes=[pltpu.VMEM((SLOTS, LANES), f32)]
        + index_scratch(SLOTS)
        + [pltpu.VMEM((ROWS, LANES), f32)] * WAYS,
        compiler_params=PARAMS,
        name="couple",
    )(base, lower, upper, cells, rows, *messages)


def adjoint_kernel(*refs):
    tangent, centre, lower, upper, low, high, cells, rows_hbm = refs[:8]
    weights = refs[8:14]
    messages = refs[14:20]
    adjoint, gram = refs[20:22]
    staged, sem = refs[22:24]
    parts = refs[24 : 24 + WAYS]
    sums = refs[24 + WAYS : 24 + 2 * WAYS]
    raised, lowered = refs[24 + 2 * WAYS :]
    copies = start_index_copies(rows_hbm, parts, sem)
    clear(sums)
    spread_fields(messages, cells, weights, staged)

    def products(j, carry):
        for u in range(4):
            start = j * 32 + u * 8
            at = rows_of(start, 8)
            value = tangent[at, :]
            raised[rows_of(start + 8, 8), :] = upper[at, :] * value
            lowered[rows_of(start + 8, 8), :] = lower[at, :] * value
        return carry

    lax.fori_loop(0, ROWS // 32, products, 0)
    low_row = pltpu.roll(low[...], PROBES, 1)[7:8, :]
    high_row = pltpu.roll(high[...], LANES - PROBES, 1)[0:1, :]
    fill_ends(raised, low_row, jnp.zeros((1, LANES), f32))
    fill_ends(lowered, jnp.zeros((1, LANES), f32), high_row)
    for copy in copies:
        copy.wait()
    add_rows(sums, parts, staged)
    gram[...] = jnp.zeros((LANES, LANES), f32)

    def total(tile, carry):
        for u in range(LANES // 8):
            start = tile * LANES + u * 8
            at = rows_of(start, 8)
            value = centre[at, :] * tangent[at, :] - raised[pl.ds(start + 7, 8), :] - lowered[pl.ds(start + 9, 8), :]
            for part in sums:
                value = value + part[at, :]
            adjoint[at, :] = value
        block = adjoint[aligned(tile * LANES, LANES), :]
        gram[...] += jnp.dot(block.T, block, precision=lax.Precision.HIGHEST, preferred_element_type=f32)
        return carry

    lax.fori_loop(0, TILES, total, 0)


def adjoint_of(tangent, centre, lower, upper, low, high, cells, rows, weights, messages):
    count = 4 * SLOTS
    return pl.pallas_call(
        adjoint_kernel,
        out_shape=[field(), field(LANES)],
        in_specs=[VMEM] * 7 + [HBM] + [VMEM] * (2 * PARTNERS),
        out_specs=[VMEM] * 2,
        scratch_shapes=[pltpu.VMEM((count, LANES), f32)]
        + index_scratch(count)
        + [pltpu.VMEM((ROWS, LANES), f32)] * WAYS
        + [pltpu.VMEM((ROWS + 16, LANES), f32)] * 2,
        compiler_params=PARAMS,
        name="adjoint",
    )(tangent, centre, lower, upper, low, high, cells, rows, *weights, *messages)


def basis_kernel(gram, adjoint, basis, factor):
    row = lax.broadcasted_iota(i32, (PROBES, 1), 0)
    lane = lax.broadcasted_iota(i32, (PROBES, LANES), 1)
    left = gram[...]
    right = jnp.where(lax.broadcasted_iota(i32, (PROBES, LANES), 0) == lane % PROBES, 1.0, 0.0)
    for j in range(PROBES):
        pivot = left[j : j + 1, j : j + 1]
        ratio = jnp.where(row > j, left[:, j : j + 1] / pivot, 0.0)
        root = jnp.sqrt(pivot)
        left_row, right_row = left[j : j + 1, :], right[j : j + 1, :]
        left = jnp.where(row == j, left_row / root, left - ratio * left_row)
        right = jnp.where(row == j, right_row / root, right - ratio * right_row)
    across = lax.broadcasted_iota(i32, (PROBES, PROBES), 1)
    down = lax.broadcasted_iota(i32, (PROBES, PROBES), 0)
    factor[...] = jnp.where(across >= down, left, 0.0).T
    inverse = jnp.concatenate([right] * GROUPS, axis=0)
    same = lax.broadcasted_iota(i32, (LANES, LANES), 0) // PROBES
    same = same == lax.broadcasted_iota(i32, (LANES, LANES), 1) // PROBES
    high, low = split(jnp.where(same, inverse, 0.0))
    left_side = jnp.concatenate([high, high, low], axis=1)

    def step(tile, carry):
        high, low = split(adjoint[aligned(tile * LANES, LANES), :])
        right_side = jnp.concatenate([high, low, high], axis=1)
        block = lax.dot_general(left_side, right_side, (((1,), (1,)), ((), ())), preferred_element_type=f32)
        for g in range(GROUPS):
            basis[:, aligned(g * ROWS + tile * LANES, LANES)] = block[g * PROBES : (g + 1) * PROBES, :]
        return carry

    lax.fori_loop(0, TILES, step, 0)


def basis_of(gram, adjoint):
    return pl.pallas_call(
        basis_kernel,
        out_shape=[
            jax.ShapeDtypeStruct((PROBES, GROUPS * ROWS), f32),
            jax.ShapeDtypeStruct((PROBES, PROBES), f32),
        ],
        in_specs=[VMEM] * 2,
        out_specs=[VMEM] * 2,
        compiler_params=PARAMS,
        name="basis",
    )(gram, adjoint)


def moved(value, place):
    grids, columns = (lax.axis_size(axis) for axis in AXES)
    route = []
    for g in range(grids):
        for c in range(columns):
            to_g, to_c = place(g, c)
            if 0 <= to_c < columns:
                route.append((g * columns + c, (to_g % grids) * columns + to_c))
    return lax.ppermute(value, AXES, route)


def to_receptors(messages):
    columns = lax.axis_size("cell")
    return [
        moved(message, lambda g, c, d=d, e=e: (g + d, (c + e) % columns))
        for message, (d, e) in zip(messages, PARTNER_OFFSETS)
    ]


def to_donors(messages):
    columns = lax.axis_size("cell")
    return [
        moved(message, lambda g, c, d=d, e=e: (g - d, (c - e) % columns))
        for message, (d, e) in zip(messages, PARTNER_OFFSETS)
    ]


def to_next(value):
    return moved(value, lambda g, c: (g, c + 1))


def to_previous(value):
    return moved(value, lambda g, c: (g, c - 1))


def summed(value):
    value = value + moved(value, lambda g, c: (g ^ 1, c))
    value = value + moved(value, lambda g, c: (g ^ 2, c))
    value = value + moved(value, lambda g, c: ((6 - (g & 6)) | (g & 1), c))
    value = value + moved(value, lambda g, c: (g, c ^ 1))
    value = value + moved(value, lambda g, c: (g, (c & 12) | (3 - (c & 3))))
    value = value + moved(value, lambda g, c: (g, c ^ 4))
    value = value + moved(value, lambda g, c: (g, (12 - (c & 12)) | (c & 3)))
    return value


def body(probes, centre, lower_coef, upper_coef, donor_cells, receptor_cells, weights):
    state = probes[:, 0, :]
    width = state.shape[1]
    donors = donor_cells[0]
    donor_rows = (donors & (ROWS - 1)).reshape(-1)
    receptor_rows = (receptor_cells & (ROWS - 1)).reshape(-1)
    donor_weights = to_donors([weights[0, :, k * FRINGE : (k + 1) * FRINGE] for k in range(PARTNERS)])
    low = to_next(state[:, width - 1 :])
    high = to_previous(state[:, :1])
    table, base, c, l, u = pack(state, centre, lower_coef, upper_coef, low, high)
    messages = to_receptors(send(table, donors, donor_rows, donor_weights))
    outs = couple(base, l, u, receptor_cells, receptor_rows, messages)
    tangent = outs[0]
    messages = to_donors(outs[1:7])
    high = to_previous(outs[7])
    low = to_next(outs[8])
    adjoint, gram = adjoint_of(tangent, c, l, u, low, high, donors, donor_rows, donor_weights, messages)
    gram = sum(gram[g * PROBES : (g + 1) * PROBES, g * PROBES : (g + 1) * PROBES] for g in range(GROUPS))
    cells = lax.axis_size("grid") * lax.axis_size("cell") * width
    gram = summed(gram) / f32(cells)
    basis, factor = basis_of(gram, adjoint)
    return (basis[:, None, :], factor)


def solution(mesh):
    in_specs = (
        P(None, "grid", "cell"),
        P("grid", "cell"),
        P("grid", "cell"),
        P("grid", "cell"),
        P("grid", None, "cell"),
        P("grid", "cell"),
        P("grid", None, "cell"),
    )
    out_specs = (P(None, "grid", "cell"), P())
    return jax.shard_map(body, mesh=mesh, in_specs=in_specs, out_specs=out_specs, check_vma=False)
```

time: 584 us -> 220 us (0.38)
  other arithmetic: 283 us -> 3.04 us
  local copies, waits for them, and re-layouts: 145 us -> 11.2 us
  Pallas kernels: 0 us -> 116 us
  blocking collectives: 66.1 us -> 0 us
  matrix products: 54.2 us -> 0 us
  starting transfers between devices: 26.3 us -> 57.1 us
  waiting for transfers between devices: 7.12 us -> 30.4 us
    scatter-add x2 -> x0, other arithmetic: 171 us -> none  [the longest x1 129 us: body(): adjoint = adjoint.at[:, donor_index].add(terms)]
    gather x4 -> x0, local copies, waits for them, and re-layouts: 118 us -> none  [the longest x2 94.6 us: body(): donor_vals = state[:, donor_index]]
    pallas_call x0 -> x5, Pallas kernels: none -> 116 us  [the longest x1 41 us: adjoint_of(): pl.pallas_call(adjoint_kernel, out_shape=[field(), field(LANES)], in_spec...]
    psum x1 -> x0, blocking collectives: 66.1 us -> none  [body(): lax.psum(local_gram, ('grid', 'cell')) / jnp.float32(total_cells)]
    sub x2 -> x0, other arithmetic: 54 us -> none  [the longest x1 30.8 us: body(): adjoint = centre * tangent - rims[0, :, 0, :width] - rims[1, :, 0, 2:]]
    dot_general x1 -> x0, matrix products: 37.1 us -> none  [body(): local_gram = jnp.dot(adjoint, adjoint.T, precision=lax.Precision.HIGHEST)]
    broadcast_in_dim x1 -> x0, other arithmetic: 32.7 us -> none  [body(): jnp.stack([upper_coef * tangent, lower_coef * tangent])[:, :, None, :]]
    ppermute x12 -> x29, starting transfers between devices: 26.3 us -> 57.1 us  [moved(): return lax.ppermute(value, AXES, route)]
  transfers between devices with their start and end apart: 12 -> 29, of which waited for: 2 -> 12; matrix products, arithmetic and copies ran while one was open for 16% -> 2% of each run, Pallas kernels for 0% -> 5%
where the time goes in v1:
time: 220 us; the launch traced here: 219 us
  Pallas kernels  116 us (53%)
  starting transfers between devices  57.1 us (26%)
  waiting for transfers between devices  30.4 us (14%)
  local copies, waits for them, and re-layouts  11.2 us (5%)
  other arithmetic  3.04 us (1%)
    ppermute x29, starting transfers between devices, moved(): return lax.ppermute(value, AXES, route)  57.1 us
    pallas_call x1, Pallas kernels, adjoint_of(): pl.pallas_call(adjoint_kernel, out_shape=[field(), field(LANES)], in_spec...  41 us
    ppermute x29, waiting for transfers between devices, moved(): return lax.ppermute(value, AXES, route)  30.4 us
    pallas_call x1, Pallas kernels, send(): pl.pallas_call(send_kernel, out_shape=[MESSAGE] * PARTNERS, in_specs=[VME...  27.4 us
    pallas_call x1, Pallas kernels, couple(): pl.pallas_call(couple_kernel, out_shape=[field()] + [MESSAGE] * PARTNERS...  26 us
    pallas_call x1, Pallas kernels, pack(): pl.pallas_call(pack_kernel, out_shape=[field()] * 5, in_specs=[VMEM] * 6,...  11.3 us
    pallas_call x1, Pallas kernels, basis_of(): pl.pallas_call(basis_kernel, out_shape=[jax.ShapeDtypeStruct((PROBES, GRO...  10.5 us
    unnamed x53, local copies, waits for them, and re-layouts  10.3 us
  transfers between devices with their start and end apart: 29, of which 12 were waited for; matrix products, arithmetic and copies ran while one was open for 2% of the time, Pallas kernels for 5%

profile of v1, /device:TPU:0, one launch (start us, length us, event | category | flops | bytes accessed | tf_op | source)
XLA Modules:
  0.0 219.0 jit_solution(1168300054442630572)
XLA Ops:
  0.6 0.8 slice_bitcast_fusion
  1.4 3.4 %collective-permute-start.2 = (f32[4,1024]{1,0:T(4,128)S(1)}, f32[4,1024]{1,0:T(4,128)S(1)}, u32[]{:S(2)}, u32[]{:S(2)}) collective-permute-start(f32[4,1024]{1,0:T(4,128)S(1)} %get-tuple-element.58), channel_id=1, source_target_pairs={{0,113},{1,114},{2,115},{3,116},{4,117},{5,118},{6,119},{7,120},{8... | collective-permute-start | bytes 49160 | tf_op jit(solution)/shard_map/ppermute | solution.py:403
  4.8 2.8 %copy.13 = f32[16,1,32768]{2,0,1:T(8,128)S(1)} copy(f32[16,1,32768]{2,1,0:T(1,128)} %param.7) | data formatting | bytes 4194304
  7.7 3.5 %collective-permute-start = (f32[16,1]{1,0:T(8,128)S(1)}, f32[16,1]{1,0:T(8,128)S(1)}, u32[]{:S(2)}, u32[]{:S(2)}) collective-permute-start(f32[16,1]{1,0:T(8,128)S(1)} %get-tuple-element.53), channel_id=1, source_target_pairs={{0,1},{1,2},{2,3},{3,4},{4,5},{5,6},{6,7},{7,8},{8,9},{9,10},{10,1... | collective-permute-start | bytes 200 | tf_op jit(solution)/shard_map/ppermute | solution.py:403
  11.2 1.3 collective-permute-start.1
  12.5 0.6 collective-permute-start.3
  13.1 6.1 %collective-permute-start.4 = (f32[4,1024]{1,0:T(4,128)S(1)}, f32[4,1024]{1,0:T(4,128)S(1)}, u32[]{:S(2)}, u32[]{:S(2)}) collective-permute-start(f32[4,1024]{1,0:T(4,128)S(1)} %get-tuple-element.56), channel_id=1, source_target_pairs={{0,127},{1,112},{2,113},{3,114},{4,115},{5,116},{6,117},{7,118},{8... | collective-permute-start | bytes 49160 | tf_op jit(solution)/shard_map/ppermute | solution.py:403
  19.2 0.9 collective-permute-start.6
  20.1 6.8 %collective-permute-start.7 = (f32[4,1024]{1,0:T(4,128)S(1)}, f32[4,1024]{1,0:T(4,128)S(1)}, u32[]{:S(2)}, u32[]{:S(2)}) collective-permute-start(f32[4,1024]{1,0:T(4,128)S(1)} %get-tuple-element.54), channel_id=1, source_target_pairs={{0,111},{1,96},{2,97},{3,98},{4,99},{5,100},{6,101},{7,102},{8,103... | collective-permute-start | bytes 49160 | tf_op jit(solution)/shard_map/ppermute | solution.py:403
  27.0 0.6 copy.11
  27.6 11.3 %pack.1 = (f32[4096,128]{1,0:T(8,128)}, f32[4096,128]{1,0:T(8,128)}, f32[4096,128]{1,0:T(8,128)}, f32[4096,128]{1,0:T(8,128)}, f32[4096,128]{1,0:T(8,128)}) custom-call(f32[16,32768]{1,0:T(8,128)} %bitcast.22, f32[1,32768]{1,0:T(1,128)} %centre.1, f32[1,32768]{1,0:T(1,128)} %lower.1, f32[1,32768]{1,0:T(1,128)} %upper.1, f32[16,1]{1,0:T(8,128)} %copy-done.21, ...), custom_call_target="tpu_custom_call" | custom-call | tf_op jit(solution)/shard_map/pack/pallas_call | solution.py:196
  39.1 0.5 copy-done.16
  39.6 27.4 %send.1 = (f32[16,1024]{1,0:T(8,128)}, f32[16,1024]{1,0:T(8,128)}, f32[16,1024]{1,0:T(8,128)}, f32[16,1024]{1,0:T(8,128)}, f32[16,1024]{1,0:T(8,128)}, /*index=5*/f32[16,1024]{1,0:T(8,128)}) custom-call(f32[4096,128]{1,0:T(8,128)} %get-tuple-element.29.refs_0_, s32[4,6144]{1,0:T(4,128)} %bitcast.24, s32[24576]{0:T(1024)} %bitcast.26, f32[4,1024]{1,0:T(4,128)} %copy-done.15, ...), custom_call_target="tpu_custom_call" | custom-call | tf_op jit(solution)/shard_map/send/pallas_call | solution.py:229
  67.1 0.1 collective-permute-start.10
  67.1 3.5 %collective-permute-start.11 = (f32[16,1024]{1,0:T(8,128)}, f32[16,1024]{1,0:T(8,128)S(1)}, u32[]{:S(2)}, u32[]{:S(2)}) collective-permute-start(f32[16,1024]{1,0:T(8,128)} %get-tuple-element.33), channel_id=1, source_target_pairs={{0,47},{1,32},{2,33},{3,34},{4,35},{5,36},{6,37},{7,38},{8,39},{9,... | collective-permute-start | bytes 196616 | tf_op jit(solution)/shard_map/ppermute | solution.py:403
  70.6 1.4 collective-permute-start.12
  72.0 7.6 %collective-permute-start.8 = (f32[16,1024]{1,0:T(8,128)}, f32[16,1024]{1,0:T(8,128)S(1)}, u32[]{:S(2)}, u32[]{:S(2)}) collective-permute-start(f32[16,1024]{1,0:T(8,128)} %get-tuple-element.30), channel_id=1, source_target_pairs={{0,31},{1,16},{2,17},{3,18},{4,19},{5,20},{6,21},{7,22},{8,23},{9,... | collective-permute-start | bytes 196616 | tf_op jit(solution)/shard_map/ppermute | solution.py:403
  79.7 0.6 broadcast_and_fusion
  80.3 1.9 collective-permute-done.13.refs_10_
  82.3 0.1 collective-permute-done.8.refs_5_
  82.4 2.4 %collective-permute-done.9.refs_6_ = f32[16,1024]{1,0:T(8,128)S(1)} collective-permute-done((f32[16,1024]{1,0:T(8,128)}, f32[16,1024]{1,0:T(8,128)S(1)}, u32[]{:S(2)}, u32[]{:S(2)}) %collective-permute-start.9) | collective-permute-done | bytes 65568 | tf_op jit(solution)/shard_map/ppermute | solution.py:403
  84.8 0.6 copy-done.8
  85.4 26.0 %couple.1 = (f32[4096,128]{1,0:T(8,128)}, f32[16,1024]{1,0:T(8,128)}, f32[16,1024]{1,0:T(8,128)}, f32[16,1024]{1,0:T(8,128)}, f32[16,1024]{1,0:T(8,128)}, /*inde...) custom-call(f32[4096,128]{1,0:T(8,128)} %get-tuple-element.26.refs_0_, ...), custom_call_target="tpu_custom_call" | custom-call | tf_op jit(solution)/shard_map/couple/pallas_call | solution.py:273
  111.5 1.3 collective-permute-start.14
  112.8 1.3 collective-permute-start.15
  114.1 7.2 %collective-permute-start.18 = (f32[16,1024]{1,0:T(8,128)}, f32[16,1024]{1,0:T(8,128)S(1)}, u32[]{:S(2)}, u32[]{:S(2)}) collective-permute-start(f32[16,1024]{1,0:T(8,128)} %get-tuple-element.42), channel_id=1, source_target_pairs={{0,127},{1,112},{2,113},{3,114},{4,115},{5,116},{6,117},{7,118},{8... | collective-permute-start | bytes 196616 | tf_op jit(solution)/shard_map/ppermute | solution.py:403
  121.3 1.1 collective-permute-start.20
  122.4 7.9 %collective-permute-start.21 = (f32[16,1024]{1,0:T(8,128)}, f32[16,1024]{1,0:T(8,128)S(1)}, u32[]{:S(2)}, u32[]{:S(2)}) collective-permute-start(f32[16,1024]{1,0:T(8,128)} %get-tuple-element.45), channel_id=1, source_target_pairs={{0,111},{1,96},{2,97},{3,98},{4,99},{5,100},{6,101},{7,102},{8,103... | collective-permute-start | bytes 196616 | tf_op jit(solution)/shard_map/ppermute | solution.py:403
  130.2 0.3 collective-permute-done.19.refs_17_
  130.6 1.9 collective-permute-done.21.refs_19_
  132.5 0.6 copy-done.14
  133.1 41.0 %adjoint.1 = (f32[4096,128]{1,0:T(8,128)}, f32[128,128]{1,0:T(8,128)}) custom-call(f32[4096,128]{1,0:T(8,128)} %get-tuple-element.36.refs_0_, f32[4096,128]{1,0:T(8,128)} %get-tuple-element.37.refs_1_, f32[4096,128]{1,0:T(8,128)} %get-tuple-element.27.refs_1_.refs_2_, f32[4096,128]{1,0:T(8,128)} %get-tuple-element.28.refs_2_.refs_3_, f32[8,128]{1,0:T(8,128)} %copy-done.23, ...), custom_call_target="tpu_custom_call" | custom-call | tf_op jit(solution)/shard_map/adjoint/pallas_call | solution.py:335
  174.1 0.9 slice_add_fusion
  175.0 0.1 collective-permute-start.22
  175.1 1.2 collective-permute-done.22
  176.3 0.9 fusion.1
  177.2 0.3 collective-permute-start.23
  177.5 3.4 %collective-permute-done.23 = f32[16,16]{1,0:T(8,128)S(1)} collective-permute-done((f32[16,16]{1,0:T(8,128)S(1)}, f32[16,16]{1,0:T(8,128)S(1)}, u32[]{:S(2)}, u32[]{:S(2)}) %collective-permute-start.23) | collective-permute-done | bytes 1056 | tf_op jit(solution)/shard_map/ppermute | solution.py:403
  180.9 0.4 collective-permute-start.24
  181.3 4.5 %collective-permute-done.24 = f32[16,16]{1,0:T(8,128)S(1)} collective-permute-done((f32[16,16]{1,0:T(8,128)S(1)}, f32[16,16]{1,0:T(8,128)S(1)}, u32[]{:S(2)}, u32[]{:S(2)}) %collective-permute-start.24) | collective-permute-done | bytes 1056 | tf_op jit(solution)/shard_map/ppermute | solution.py:403
  185.8 3.6 %collective-permute-done.25 = f32[16,16]{1,0:T(8,128)S(1)} collective-permute-done((f32[16,16]{1,0:T(8,128)S(1)}, f32[16,16]{1,0:T(8,128)S(1)}, u32[]{:S(2)}, u32[]{:S(2)}) %collective-permute-start.25) | collective-permute-done | bytes 1056 | tf_op jit(solution)/shard_map/ppermute | solution.py:403
  189.4 4.9 %collective-permute-done.26 = f32[16,16]{1,0:T(8,128)S(1)} collective-permute-done((f32[16,16]{1,0:T(8,128)S(1)}, f32[16,16]{1,0:T(8,128)S(1)}, u32[]{:S(2)}, u32[]{:S(2)}) %collective-permute-start.26) | collective-permute-done | bytes 1056 | tf_op jit(solution)/shard_map/ppermute | solution.py:403
  194.3 3.6 %collective-permute-done.27 = f32[16,16]{1,0:T(8,128)S(1)} collective-permute-done((f32[16,16]{1,0:T(8,128)S(1)}, f32[16,16]{1,0:T(8,128)S(1)}, u32[]{:S(2)}, u32[]{:S(2)}) %collective-permute-start.27) | collective-permute-done | bytes 1056 | tf_op jit(solution)/shard_map/ppermute | solution.py:403
  197.9 2.3 %collective-permute-start.28 = (f32[16,16]{1,0:T(8,128)S(1)}, f32[16,16]{1,0:T(8,128)S(1)}, u32[]{:S(2)}, u32[]{:S(2)}) collective-permute-start(f32[16,16]{1,0:T(8,128)S(1)} %add.54), channel_id=1, source_target_pairs={{0,12},{1,13},{2,14},{3,15},{4,8},{5,9},{6,10},{7,11},{8,4},{9,5},... | collective-permute-start | bytes 3080 | tf_op jit(solution)/shard_map/ppermute | solution.py:403
  200.3 2.5 %collective-permute-done.28 = f32[16,16]{1,0:T(8,128)S(1)} collective-permute-done((f32[16,16]{1,0:T(8,128)S(1)}, f32[16,16]{1,0:T(8,128)S(1)}, u32[]{:S(2)}, u32[]{:S(2)}) %collective-permute-start.28) | collective-permute-done | bytes 1056 | tf_op jit(solution)/shard_map/ppermute | solution.py:403
  202.8 0.6 add_multiply_fusion.gram
  203.4 10.5 %basis.1 = (f32[16,32768]{1,0:T(8,128)}, f32[16,16]{1,0:T(8,128)}) custom-call(f32[16,16]{1,0:T(8,128)} %add_multiply_fusion.gram, f32[4096,128]{1,0:T(8,128)} %get-tuple-element.47.adjoint), custom_call_target="tpu_custom_call" | custom-call | tf_op jit(solution)/shard_map/basis/pallas_call | solution.py:382
  213.9 5.1 %copy.9 = f32[16,1,32768]{2,1,0:T(1,128)} copy(f32[16,1,32768]{2,0,1:T(8,128)} %bitcast.23) | data formatting | bytes 4194304
  (80 shorter events, 0.4 us)
Async XLA Ops:
  1.4 25.5 %copy-start.1 = (s32[1,4,6144]{2,1,0:T(4,128)S(1)}, s32[1,4,6144]{2,1,0:T(4,128)}, u32[]{:S(2)}) copy-start(s32[1,4,6144]{2,1,0:T(4,128)} %param.11) | copy-start | bytes 294916
  1.4 18.6 %collective-permute-start.2 = (f32[4,1024]{1,0:T(4,128)S(1)}, f32[4,1024]{1,0:T(4,128)S(1)}, u32[]{:S(2)}, u32[]{:S(2)}) collective-permute-start(f32[4,1024]{1,0:T(4,128)S(1)} %get-tuple-element.58), channel_id=1, source_target_pairs={{0,113},{1,114},{2,115},{3,116},{4,117},{5,118},{6,119},{7,120},{8... | collective-permute-start | bytes 49160 | tf_op jit(solution)/shard_map/ppermute | solution.py:403
  7.6 20.0 %copy-start = (f32[16,1,32768]{2,0,1:T(8,128)}, f32[16,1,32768]{2,0,1:T(8,128)S(1)}, u32[]{:S(2)}) copy-start(f32[16,1,32768]{2,0,1:T(8,128)S(1)} %copy.13) | copy-start | bytes 6291460
  7.7 11.5 %collective-permute-start = (f32[16,1]{1,0:T(8,128)S(1)}, f32[16,1]{1,0:T(8,128)S(1)}, u32[]{:S(2)}, u32[]{:S(2)}) collective-permute-start(f32[16,1]{1,0:T(8,128)S(1)} %get-tuple-element.53), channel_id=1, source_target_pairs={{0,1},{1,2},{2,3},{3,4},{4,5},{5,6},{6,7},{7,8},{8,9},{9,10},{10,1... | collective-permute-start | bytes 200 | tf_op jit(solution)/shard_map/ppermute | solution.py:403
  11.2 8.0 %collective-permute-start.1 = (f32[16,1]{1,0:T(8,128)S(1)}, f32[16,1]{1,0:T(8,128)S(1)}, u32[]{:S(2)}, u32[]{:S(2)}) collective-permute-start(f32[16,1]{1,0:T(8,128)S(1)} %get-tuple-element.52), channel_id=1, source_target_pairs={{1,0},{2,1},{3,2},{4,3},{5,4},{6,5},{7,6},{8,7},{9,8},{10,9},{11,1... | collective-permute-start | bytes 200 | tf_op jit(solution)/shard_map/ppermute | solution.py:403
  12.5 26.5 %collective-permute-start.3 = (f32[4,1024]{1,0:T(4,128)S(1)}, f32[4,1024]{1,0:T(4,128)S(1)}, u32[]{:S(2)}, u32[]{:S(2)}) collective-permute-start(f32[4,1024]{1,0:T(4,128)S(1)} %get-tuple-element.57), channel_id=1, source_target_pairs={{0,112},{1,113},{2,114},{3,115},{4,116},{5,117},{6,118},{7,119},{8... | collective-permute-start | bytes 49160 | tf_op jit(solution)/shard_map/ppermute | solution.py:403
  13.1 25.9 %collective-permute-start.4 = (f32[4,1024]{1,0:T(4,128)S(1)}, f32[4,1024]{1,0:T(4,128)S(1)}, u32[]{:S(2)}, u32[]{:S(2)}) collective-permute-start(f32[4,1024]{1,0:T(4,128)S(1)} %get-tuple-element.56), channel_id=1, source_target_pairs={{0,127},{1,112},{2,113},{3,114},{4,115},{5,116},{6,117},{7,118},{8... | collective-permute-start | bytes 49160 | tf_op jit(solution)/shard_map/ppermute | solution.py:403
  19.2 8.4 %copy-start.21 = (f32[16,1]{1,0:T(8,128)}, f32[16,1]{1,0:T(8,128)S(1)}, u32[]{:S(2)}) copy-start(f32[16,1]{1,0:T(8,128)S(1)} %collective-permute-done.low) | copy-start | bytes 196
  19.2 19.8 %collective-permute-start.5 = (f32[4,1024]{1,0:T(4,128)S(1)}, f32[4,1024]{1,0:T(4,128)S(1)}, u32[]{:S(2)}, u32[]{:S(2)}) collective-permute-start(f32[4,1024]{1,0:T(4,128)S(1)} %get-tuple-element.55), channel_id=1, source_target_pairs={{0,97},{1,98},{2,99},{3,100},{4,101},{5,102},{6,103},{7,104},{8,10... | collective-permute-start | bytes 49160 | tf_op jit(solution)/shard_map/ppermute | solution.py:403
  19.2 8.4 %copy-start.22 = (f32[16,1]{1,0:T(8,128)}, f32[16,1]{1,0:T(8,128)S(1)}, u32[]{:S(2)}) copy-start(f32[16,1]{1,0:T(8,128)S(1)} %collective-permute-done.1.high) | copy-start | bytes 196
  19.2 19.8 %collective-permute-start.6 = (f32[4,1024]{1,0:T(4,128)S(1)}, f32[4,1024]{1,0:T(4,128)S(1)}, u32[]{:S(2)}, u32[]{:S(2)}) collective-permute-start(f32[4,1024]{1,0:T(4,128)S(1)} %get-tuple-element.59), channel_id=1, source_target_pairs={{0,96},{1,97},{2,98},{3,99},{4,100},{5,101},{6,102},{7,103},{8,104... | collective-permute-start | bytes 49160 | tf_op jit(solution)/shard_map/ppermute | solution.py:403
  20.1 19.0 %copy-start.15 = (f32[4,1024]{1,0:T(4,128)}, f32[4,1024]{1,0:T(4,128)S(1)}, u32[]{:S(2)}) copy-start(f32[4,1024]{1,0:T(4,128)S(1)} %collective-permute-done.2.refs_3_.refs_8_) | copy-start | bytes 49156
  20.1 18.9 %collective-permute-start.7 = (f32[4,1024]{1,0:T(4,128)S(1)}, f32[4,1024]{1,0:T(4,128)S(1)}, u32[]{:S(2)}, u32[]{:S(2)}) collective-permute-start(f32[4,1024]{1,0:T(4,128)S(1)} %get-tuple-element.54), channel_id=1, source_target_pairs={{0,111},{1,96},{2,97},{3,98},{4,99},{5,100},{6,101},{7,102},{8,103... | collective-permute-start | bytes 49160 | tf_op jit(solution)/shard_map/ppermute | solution.py:403
  27.6 52.1 %copy-start.2 = (s32[1,6144]{1,0:T(1,128)S(1)}, s32[1,6144]{1,0:T(1,128)}, u32[]{:S(2)}) copy-start(s32[1,6144]{1,0:T(1,128)} %refs_3_.1) | copy-start | bytes 73732
  67.1 12.6 %collective-permute-start.10 = (f32[16,1024]{1,0:T(8,128)}, f32[16,1024]{1,0:T(8,128)S(1)}, u32[]{:S(2)}, u32[]{:S(2)}) collective-permute-start(f32[16,1024]{1,0:T(8,128)} %get-tuple-element.32), channel_id=1, source_target_pairs={{0,17},{1,18},{2,19},{3,20},{4,21},{5,22},{6,23},{7,24},{8,25},{9,... | collective-permute-start | bytes 196616 | tf_op jit(solution)/shard_map/ppermute | solution.py:403
  67.1 13.2 %collective-permute-start.11 = (f32[16,1024]{1,0:T(8,128)}, f32[16,1024]{1,0:T(8,128)S(1)}, u32[]{:S(2)}, u32[]{:S(2)}) collective-permute-start(f32[16,1024]{1,0:T(8,128)} %get-tuple-element.33), channel_id=1, source_target_pairs={{0,47},{1,32},{2,33},{3,34},{4,35},{5,36},{6,37},{7,38},{8,39},{9,... | collective-permute-start | bytes 196616 | tf_op jit(solution)/shard_map/ppermute | solution.py:403
  70.6 9.7 %collective-permute-start.12 = (f32[16,1024]{1,0:T(8,128)}, f32[16,1024]{1,0:T(8,128)S(1)}, u32[]{:S(2)}, u32[]{:S(2)}) collective-permute-start(f32[16,1024]{1,0:T(8,128)} %get-tuple-element.34), channel_id=1, source_target_pairs={{0,32},{1,33},{2,34},{3,35},{4,36},{5,37},{6,38},{7,39},{8,40},{9,... | collective-permute-start | bytes 196616 | tf_op jit(solution)/shard_map/ppermute | solution.py:403
  72.0 10.2 %collective-permute-start.13 = (f32[16,1024]{1,0:T(8,128)}, f32[16,1024]{1,0:T(8,128)S(1)}, u32[]{:S(2)}, u32[]{:S(2)}) collective-permute-start(f32[16,1024]{1,0:T(8,128)} %get-tuple-element.35), channel_id=1, source_target_pairs={{0,33},{1,34},{2,35},{3,36},{4,37},{5,38},{6,39},{7,40},{8,41},{9,... | collective-permute-start | bytes 196616 | tf_op jit(solution)/shard_map/ppermute | solution.py:403
  72.0 10.3 %collective-permute-start.8 = (f32[16,1024]{1,0:T(8,128)}, f32[16,1024]{1,0:T(8,128)S(1)}, u32[]{:S(2)}, u32[]{:S(2)}) collective-permute-start(f32[16,1024]{1,0:T(8,128)} %get-tuple-element.30), channel_id=1, source_target_pairs={{0,31},{1,16},{2,17},{3,18},{4,19},{5,20},{6,21},{7,22},{8,23},{9,... | collective-permute-start | bytes 196616 | tf_op jit(solution)/shard_map/ppermute | solution.py:403
  79.7 5.1 %copy-start.3 = (f32[16,1024]{1,0:T(8,128)}, f32[16,1024]{1,0:T(8,128)S(1)}, u32[]{:S(2)}) copy-start(f32[16,1024]{1,0:T(8,128)S(1)} %collective-permute-done.10.refs_7_) | copy-start | bytes 196612
  79.7 5.1 %collective-permute-start.9 = (f32[16,1024]{1,0:T(8,128)}, f32[16,1024]{1,0:T(8,128)S(1)}, u32[]{:S(2)}, u32[]{:S(2)}) collective-permute-start(f32[16,1024]{1,0:T(8,128)} %get-tuple-element.31), channel_id=1, source_target_pairs={{0,16},{1,17},{2,18},{3,19},{4,20},{5,21},{6,22},{7,23},{8,24},{9,... | collective-permute-start | bytes 196616 | tf_op jit(solution)/shard_map/ppermute | solution.py:403
  80.3 4.5 %copy-start.4 = (f32[16,1024]{1,0:T(8,128)}, f32[16,1024]{1,0:T(8,128)S(1)}, u32[]{:S(2)}) copy-start(f32[16,1024]{1,0:T(8,128)S(1)} %collective-permute-done.11.refs_8_) | copy-start | bytes 196612
  80.3 4.5 %copy-start.5 = (f32[16,1024]{1,0:T(8,128)}, f32[16,1024]{1,0:T(8,128)S(1)}, u32[]{:S(2)}) copy-start(f32[16,1024]{1,0:T(8,128)S(1)} %collective-permute-done.12.refs_9_) | copy-start | bytes 196612
  82.3 2.5 %copy-start.6 = (f32[16,1024]{1,0:T(8,128)}, f32[16,1024]{1,0:T(8,128)S(1)}, u32[]{:S(2)}) copy-start(f32[16,1024]{1,0:T(8,128)S(1)} %collective-permute-done.13.refs_10_) | copy-start | bytes 196612
  82.4 2.4 %copy-start.7 = (f32[16,1024]{1,0:T(8,128)}, f32[16,1024]{1,0:T(8,128)S(1)}, u32[]{:S(2)}) copy-start(f32[16,1024]{1,0:T(8,128)S(1)} %collective-permute-done.8.refs_5_) | copy-start | bytes 196612
  84.8 0.6 copy-start.8
  111.4 11.0 %collective-permute-start.16 = (f32[16,1024]{1,0:T(8,128)}, f32[16,1024]{1,0:T(8,128)S(1)}, u32[]{:S(2)}, u32[]{:S(2)}) collective-permute-start(f32[16,1024]{1,0:T(8,128)} %get-tuple-element.40), channel_id=1, source_target_pairs={{0,113},{1,114},{2,115},{3,116},{4,117},{5,118},{6,119},{7,120},{8... | collective-permute-start | bytes 196616 | tf_op jit(solution)/shard_map/ppermute | solution.py:403
  111.5 9.8 %collective-permute-start.14 = (f32[8,128]{1,0:T(8,128)}, f32[8,128]{1,0:T(8,128)S(1)}, u32[]{:S(2)}, u32[]{:S(2)}) collective-permute-start(f32[8,128]{1,0:T(8,128)} %get-tuple-element.38), channel_id=1, source_target_pairs={{0,1},{1,2},{2,3},{3,4},{4,5},{5,6},{6,7},{7,8},{8,9},{9,10},{10,1... | collective-permute-start | bytes 12296 | tf_op jit(solution)/shard_map/ppermute | solution.py:403
  112.8 8.5 %collective-permute-start.15 = (f32[8,128]{1,0:T(8,128)}, f32[8,128]{1,0:T(8,128)S(1)}, u32[]{:S(2)}, u32[]{:S(2)}) collective-permute-start(f32[8,128]{1,0:T(8,128)} %get-tuple-element.39), channel_id=1, source_target_pairs={{1,0},{2,1},{3,2},{4,3},{5,4},{6,5},{7,6},{8,7},{9,8},{10,9},{11,1... | collective-permute-start | bytes 12296 | tf_op jit(solution)/shard_map/ppermute | solution.py:403
  114.1 16.2 %collective-permute-start.17 = (f32[16,1024]{1,0:T(8,128)}, f32[16,1024]{1,0:T(8,128)S(1)}, u32[]{:S(2)}, u32[]{:S(2)}) collective-permute-start(f32[16,1024]{1,0:T(8,128)} %get-tuple-element.41), channel_id=1, source_target_pairs={{0,112},{1,113},{2,114},{3,115},{4,116},{5,117},{6,118},{7,119},{8... | collective-permute-start | bytes 196616 | tf_op jit(solution)/shard_map/ppermute | solution.py:403
  114.1 16.1 %collective-permute-start.18 = (f32[16,1024]{1,0:T(8,128)}, f32[16,1024]{1,0:T(8,128)S(1)}, u32[]{:S(2)}, u32[]{:S(2)}) collective-permute-start(f32[16,1024]{1,0:T(8,128)} %get-tuple-element.42), channel_id=1, source_target_pairs={{0,127},{1,112},{2,113},{3,114},{4,115},{5,116},{6,117},{7,118},{8... | collective-permute-start | bytes 196616 | tf_op jit(solution)/shard_map/ppermute | solution.py:403
  121.3 11.2 %copy-start.23 = (f32[8,128]{1,0:T(8,128)}, f32[8,128]{1,0:T(8,128)S(1)}, u32[]{:S(2)}) copy-start(f32[8,128]{1,0:T(8,128)S(1)} %collective-permute-done.14.refs_4_) | copy-start | bytes 12292
  121.3 9.3 %collective-permute-start.19 = (f32[16,1024]{1,0:T(8,128)}, f32[16,1024]{1,0:T(8,128)S(1)}, u32[]{:S(2)}, u32[]{:S(2)}) collective-permute-start(f32[16,1024]{1,0:T(8,128)} %get-tuple-element.43), channel_id=1, source_target_pairs={{0,97},{1,98},{2,99},{3,100},{4,101},{5,102},{6,103},{7,104},{8,10... | collective-permute-start | bytes 196616 | tf_op jit(solution)/shard_map/ppermute | solution.py:403
  121.3 11.2 %copy-start.24 = (f32[8,128]{1,0:T(8,128)}, f32[8,128]{1,0:T(8,128)S(1)}, u32[]{:S(2)}) copy-start(f32[8,128]{1,0:T(8,128)S(1)} %collective-permute-done.15.refs_5_) | copy-start | bytes 12292
  121.3 9.3 %collective-permute-start.20 = (f32[16,1024]{1,0:T(8,128)}, f32[16,1024]{1,0:T(8,128)S(1)}, u32[]{:S(2)}, u32[]{:S(2)}) collective-permute-start(f32[16,1024]{1,0:T(8,128)} %get-tuple-element.44), channel_id=1, source_target_pairs={{0,96},{1,97},{2,98},{3,99},{4,100},{5,101},{6,102},{7,103},{8,104... | collective-permute-start | bytes 196616 | tf_op jit(solution)/shard_map/ppermute | solution.py:403
  122.4 10.1 %copy-start.9 = (f32[16,1024]{1,0:T(8,128)}, f32[16,1024]{1,0:T(8,128)S(1)}, u32[]{:S(2)}) copy-start(f32[16,1024]{1,0:T(8,128)S(1)} %collective-permute-done.16.refs_14_) | copy-start | bytes 196612
  122.4 10.1 %collective-permute-start.21 = (f32[16,1024]{1,0:T(8,128)}, f32[16,1024]{1,0:T(8,128)S(1)}, u32[]{:S(2)}, u32[]{:S(2)}) collective-permute-start(f32[16,1024]{1,0:T(8,128)} %get-tuple-element.45), channel_id=1, source_target_pairs={{0,111},{1,96},{2,97},{3,98},{4,99},{5,100},{6,101},{7,102},{8,103... | collective-permute-start | bytes 196616 | tf_op jit(solution)/shard_map/ppermute | solution.py:403
  130.2 2.2 %copy-start.10 = (f32[16,1024]{1,0:T(8,128)}, f32[16,1024]{1,0:T(8,128)S(1)}, u32[]{:S(2)}) copy-start(f32[16,1024]{1,0:T(8,128)S(1)} %collective-permute-done.17.refs_15_) | copy-start | bytes 196612
  130.2 2.2 %copy-start.11 = (f32[16,1024]{1,0:T(8,128)}, f32[16,1024]{1,0:T(8,128)S(1)}, u32[]{:S(2)}) copy-start(f32[16,1024]{1,0:T(8,128)S(1)} %collective-permute-done.18.refs_16_) | copy-start | bytes 196612
  130.6 1.9 copy-start.12
  130.6 1.9 copy-start.13
  175.0 1.3 collective-permute-start.22
  177.2 3.7 %collective-permute-start.23 = (f32[16,16]{1,0:T(8,128)S(1)}, f32[16,16]{1,0:T(8,128)S(1)}, u32[]{:S(2)}, u32[]{:S(2)}) collective-permute-start(f32[16,16]{1,0:T(8,128)S(1)} %fusion.1), channel_id=1, source_target_pairs={{0,32},{1,33},{2,34},{3,35},{4,36},{5,37},{6,38},{7,39},{8,40},{9,... | collective-permute-start | bytes 3080 | tf_op jit(solution)/shard_map/ppermute | solution.py:403
  180.9 4.9 %collective-permute-start.24 = (f32[16,16]{1,0:T(8,128)S(1)}, f32[16,16]{1,0:T(8,128)S(1)}, u32[]{:S(2)}, u32[]{:S(2)}) collective-permute-start(f32[16,16]{1,0:T(8,128)S(1)} %add.50), channel_id=1, source_target_pairs={{0,96},{1,97},{2,98},{3,99},{4,100},{5,101},{6,102},{7,103},{8,104... | collective-permute-start | bytes 3080 | tf_op jit(solution)/shard_map/ppermute | solution.py:403
  185.8 3.7 %collective-permute-start.25 = (f32[16,16]{1,0:T(8,128)S(1)}, f32[16,16]{1,0:T(8,128)S(1)}, u32[]{:S(2)}, u32[]{:S(2)}) collective-permute-start(f32[16,16]{1,0:T(8,128)S(1)} %add.51), channel_id=1, source_target_pairs={{0,1},{1,0},{2,3},{3,2},{4,5},{5,4},{6,7},{7,6},{8,9},{9,8},{10,11... | collective-permute-start | bytes 3080 | tf_op jit(solution)/shard_map/ppermute | solution.py:403
  189.4 4.9 %collective-permute-start.26 = (f32[16,16]{1,0:T(8,128)S(1)}, f32[16,16]{1,0:T(8,128)S(1)}, u32[]{:S(2)}, u32[]{:S(2)}) collective-permute-start(f32[16,16]{1,0:T(8,128)S(1)} %add.52), channel_id=1, source_target_pairs={{0,3},{1,2},{2,1},{3,0},{4,7},{5,6},{6,5},{7,4},{8,11},{9,10},{10,... | collective-permute-start | bytes 3080 | tf_op jit(solution)/shard_map/ppermute | solution.py:403
  194.3 3.7 %collective-permute-start.27 = (f32[16,16]{1,0:T(8,128)S(1)}, f32[16,16]{1,0:T(8,128)S(1)}, u32[]{:S(2)}, u32[]{:S(2)}) collective-permute-start(f32[16,16]{1,0:T(8,128)S(1)} %add.53), channel_id=1, source_target_pairs={{0,4},{1,5},{2,6},{3,7},{4,0},{5,1},{6,2},{7,3},{8,12},{9,13},{10,... | collective-permute-start | bytes 3080 | tf_op jit(solution)/shard_map/ppermute | solution.py:403
  197.9 4.9 %collective-permute-start.28 = (f32[16,16]{1,0:T(8,128)S(1)}, f32[16,16]{1,0:T(8,128)S(1)}, u32[]{:S(2)}, u32[]{:S(2)}) collective-permute-start(f32[16,16]{1,0:T(8,128)S(1)} %add.54), channel_id=1, source_target_pairs={{0,12},{1,13},{2,14},{3,15},{4,8},{5,9},{6,10},{7,11},{8,4},{9,5},... | collective-permute-start | bytes 3080 | tf_op jit(solution)/shard_map/ppermute | solution.py:403
  (6 other events, 3.6 us)

commit v2 on v1

v2 whole, which is shorter than its diff:
```python
import functools

import jax
import jax.numpy as jnp
from jax import lax
from jax.experimental import pallas as pl
from jax.experimental.pallas import tpu as pltpu
from jax.sharding import PartitionSpec as P

f32 = jnp.float32
i32 = jnp.int32
bf16 = jnp.bfloat16

PROBES = 16
GROUPS = 8
ROWS = 4096
LANES = 128
PARTNERS = 6
FRINGE = 1024
HALF = 3 * FRINGE
SLOTS = PARTNERS * FRINGE
TILES = ROWS // LANES
WAYS = 8
UNROLL = 8

AXES = ("grid", "cell")

VMEM = pl.BlockSpec(memory_space=pltpu.VMEM)
HBM = pl.BlockSpec(memory_space=pl.ANY)


def aligned(start, size):
    return pl.ds(pl.multiple_of(start, size), size)


def rows_of(start, size):
    return pl.ds(pl.multiple_of(start, 8), size)


def split(x):
    high = x.astype(bf16)
    return high, (x - high.astype(f32)).astype(bf16)


def params(limit_mib):
    return pltpu.CompilerParams(vmem_limit_bytes=limit_mib << 20)


def cost(microseconds):
    return pl.CostEstimate(flops=0, transcendentals=0, bytes_accessed=microseconds * 3_000_000)


def resident(*shape):
    return pltpu.VMEM(shape, f32)


def index_scratch(count):
    return [pltpu.SMEM((count // WAYS,), i32)] * WAYS + [pltpu.SemaphoreType.DMA((WAYS,))]


def index_copies(rows_hbm, many, half, parts, sem):
    size = parts[0].shape[0]
    each = WAYS // many
    copies = []
    for w in range(WAYS):
        start = (w // each) * SLOTS + half * HALF + (w % each) * size
        copies.append(pltpu.make_async_copy(rows_hbm.at[pl.ds(start, size)], parts[w], sem.at[w]))
    for copy in copies:
        copy.start()
    return copies


def finish(copies):
    for copy in copies:
        copy.wait()


def gather_rows(table, parts, staged):
    count = parts[0].shape[0]

    def step(j, carry):
        for u in range(UNROLL):
            q = j * UNROLL + u
            for w in range(WAYS):
                row = parts[w][q]
                staged[pl.ds(w * count + q, 1), :] = table[pl.ds(row, 1), :]
        return carry

    lax.fori_loop(0, count // UNROLL, step, 0)


def clear(sums):
    def step(j, carry):
        for total in sums:
            for u in range(4):
                total[rows_of(j * 32 + u * 8, 8), :] = jnp.zeros((8, LANES), f32)
        return carry

    lax.fori_loop(0, ROWS // 32, step, 0)


def add_rows(sums, parts, staged):
    count = parts[0].shape[0]

    def step(j, carry):
        for u in range(UNROLL):
            q = j * UNROLL + u
            for w in range(WAYS):
                row = parts[w][q]
                term = staged[pl.ds(w * count + q, 1), :]
                sums[w][pl.ds(row, 1), :] = sums[w][pl.ds(row, 1), :] + term
        return carry

    lax.fori_loop(0, count // UNROLL, step, 0)


def groups_of(cells, m, offset):
    return jnp.broadcast_to(cells[m : m + 1, aligned(offset, LANES)], (8, LANES)) >> 12


def select_fields(staged, cells, half, weights, out):
    many = cells.shape[0]
    for k in range(3):

        def step(b, carry):
            local = aligned(b * LANES, LANES)
            offset = k * FRINGE + b * LANES
            total = [jnp.zeros((8, LANES), f32)] * 2
            for m in range(many):
                field = staged[aligned(m * HALF + offset, LANES), :].T
                group = groups_of(cells, m, half * HALF + offset)
                scale = 1.0 if weights is None else jnp.broadcast_to(weights[k][m : m + 1, local], (8, LANES))
                for g in range(GROUPS):
                    factor = jnp.where(group == g, scale, 0.0)
                    for h in range(2):
                        at = g * PROBES + h * 8
                        total[h] = total[h] + field[at : at + 8, :] * factor
            for h in range(2):
                out[k][h * 8 : h * 8 + 8, local] = total[h]
            return carry

        lax.fori_loop(0, FRINGE // LANES, step, 0)


def spread_fields(messages, cells, half, weights, staged):
    many = cells.shape[0]
    for k in range(3):

        def step(b, carry):
            local = aligned(b * LANES, LANES)
            offset = k * FRINGE + b * LANES
            field = [messages[k][h * 8 : h * 8 + 8, local] for h in range(2)]
            for m in range(many):
                group = groups_of(cells, m, half * HALF + offset)
                scaled = field
                if weights is not None:
                    scale = jnp.broadcast_to(weights[k][m : m + 1, local], (8, LANES))
                    scaled = [part * scale for part in field]
                terms = [jnp.where(group == g, scaled[h], 0.0) for g in range(GROUPS) for h in range(2)]
                staged[aligned(m * HALF + offset, LANES), :] = jnp.concatenate(terms, axis=0).T
            return carry

        lax.fori_loop(0, FRINGE // LANES, step, 0)


def lanes(shape):
    return lax.broadcasted_iota(i32, shape, len(shape) - 1)


def fill_ends(padded, low, high):
    lane = lanes((1, LANES))
    before = pltpu.roll(padded[ROWS : ROWS + 8, :], PROBES, 1)[7:8, :]
    after = pltpu.roll(padded[8:16, :], LANES - PROBES, 1)[0:1, :]
    padded[7:8, :] = jnp.where(lane < PROBES, low, before)
    padded[ROWS + 8 : ROWS + 9, :] = jnp.where(lane >= LANES - PROBES, high, after)


def each_row_block(step):
    def outer(j, carry):
        for u in range(4):
            step(j * 32 + u * 8)
        return carry

    lax.fori_loop(0, ROWS // 32, outer, 0)


def table_kernel(probes, table, natural, sem):
    copies = [
        pltpu.make_async_copy(probes.at[p], natural.at[pl.ds(p, 1), :], sem.at[p]) for p in range(PROBES)
    ]
    for copy in copies:
        copy.start()
    finish(copies)

    def step(tile, carry):
        parts = [natural[:, aligned(g * ROWS + tile * LANES, LANES)] for g in range(GROUPS)]
        table[aligned(tile * LANES, LANES), :] = jnp.concatenate(parts, axis=0).T
        return carry

    lax.fori_loop(0, TILES, step, 0)


def table_of(probes):
    return pl.pallas_call(
        table_kernel,
        out_shape=resident(ROWS, LANES),
        in_specs=[HBM],
        out_specs=VMEM,
        scratch_shapes=[pltpu.VMEM((PROBES, GROUPS * ROWS), f32), pltpu.SemaphoreType.DMA((PROBES,))],
        compiler_params=params(8),
        cost_estimate=cost(3),
        name="table",
    )(probes)


def rows_kernel(half, table, rows_hbm, staged, *rest):
    parts, sem = rest[:WAYS], rest[WAYS]
    finish(index_copies(rows_hbm, 4, half, parts, sem))
    gather_rows(table, parts, staged)


def rows_at_donors(half, table, rows):
    count = 4 * HALF
    return pl.pallas_call(
        functools.partial(rows_kernel, half),
        out_shape=resident(count, LANES),
        in_specs=[VMEM, HBM],
        out_specs=VMEM,
        scratch_shapes=index_scratch(count),
        compiler_params=params(8),
        cost_estimate=cost(9),
        name="donor_rows",
    )(table, rows)


MESSAGE = jax.ShapeDtypeStruct((PROBES, FRINGE), f32)


def select_kernel(half, staged, cells, *rest):
    select_fields(staged, cells, half, rest[:3], rest[3:6])


def weighted_sums(half, staged, cells, weights):
    return pl.pallas_call(
        functools.partial(select_kernel, half),
        out_shape=[MESSAGE] * 3,
        in_specs=[VMEM] * 5,
        out_specs=[VMEM] * 3,
        compiler_params=params(8),
        cost_estimate=cost(3),
        name="weighted_sums",
    )(staged, cells, *weights)


def forward_kernel(table, centre, lower, upper, low, high, c_out, l_out, u_out, *rest):
    sums, padded = rest[:WAYS], rest[WAYS]

    def step(tile, carry):
        at = aligned(tile * LANES, LANES)
        padded[rows_of(tile * LANES + 8, LANES), :] = table[at, :]
        for ref, out in ((centre, c_out), (lower, l_out), (upper, u_out)):
            parts = [
                jnp.broadcast_to(ref[:, aligned(g * ROWS + tile * LANES, LANES)], (PROBES, LANES))
                for g in range(GROUPS)
            ]
            out[at, :] = jnp.concatenate(parts, axis=0).T
        return carry

    lax.fori_loop(0, TILES, step, 0)
    ends = [jnp.broadcast_to(low[...], (PROBES, LANES)), jnp.zeros((96, LANES), f32)]
    ends.append(jnp.broadcast_to(high[...], (PROBES, LANES)))
    ends = jnp.concatenate(ends, axis=0).T[0:1, :]
    fill_ends(padded, ends, ends)

    def stencil(start):
        at = rows_of(start, 8)
        sums[0][at, :] = (
            c_out[at, :] * padded[rows_of(start + 8, 8), :]
            - l_out[at, :] * padded[pl.ds(start + 7, 8), :]
            - u_out[at, :] * padded[pl.ds(start + 9, 8), :]
        )

    each_row_block(stencil)
    clear(sums[1:])


def forward(table, centre, lower, upper, low, high):
    return pl.pallas_call(
        forward_kernel,
        out_shape=[resident(ROWS, LANES)] * (3 + WAYS),
        in_specs=[VMEM] * 6,
        out_specs=[VMEM] * (3 + WAYS),
        scratch_shapes=[pltpu.VMEM((ROWS + 16, LANES), f32)],
        compiler_params=params(8),
        cost_estimate=cost(7),
        name="forward",
    )(table, centre, lower, upper, low, high)


def couple_kernel(*refs):
    lower, upper, cells, rows_hbm = refs[:4]
    messages = refs[4:10]
    tangent = refs[10 + WAYS]
    out = refs[11 + WAYS : 14 + WAYS]
    first, last = refs[14 + WAYS : 16 + WAYS]
    sums = refs[16 + WAYS : 16 + 2 * WAYS]
    staged = refs[16 + 2 * WAYS : 18 + 2 * WAYS]
    parts = refs[18 + 2 * WAYS :]
    parts, sems = (parts[:WAYS], parts[WAYS + 1 : 2 * WAYS + 1]), (parts[WAYS], parts[2 * WAYS + 1])
    copies = [index_copies(rows_hbm, 1, half, parts[half], sems[half]) for half in range(2)]
    for half in range(2):
        spread_fields(messages[half * 3 : half * 3 + 3], cells, half, None, staged[half])
    for half in range(2):
        finish(copies[half])
        add_rows(sums, parts[half], staged[half])

    def total(start):
        at = rows_of(start, 8)
        value = sums[0][at, :]
        for part in sums[1:]:
            value = value + part[at, :]
        tangent[at, :] = value

    each_row_block(total)
    first[...] = lower[0:8, :] * tangent[0:8, :]
    last[...] = upper[ROWS - 8 : ROWS, :] * tangent[ROWS - 8 : ROWS, :]
    gather_rows(tangent, parts[1], staged[1])
    select_fields(staged[1], cells, 1, None, out)


def couple(lower, upper, cells, rows, messages, sums):
    edge = jax.ShapeDtypeStruct((8, LANES), f32)
    outs = pl.pallas_call(
        couple_kernel,
        out_shape=[resident(ROWS, LANES)] + [MESSAGE] * 3 + [edge] * 2 + [resident(ROWS, LANES)] * WAYS,
        in_specs=[VMEM] * 3 + [HBM] + [VMEM] * (PARTNERS + WAYS),
        out_specs=[VMEM] * (6 + WAYS),
        scratch_shapes=[pltpu.VMEM((HALF, LANES), f32)] * 2 + index_scratch(HALF) * 2,
        input_output_aliases={10 + w: 6 + w for w in range(WAYS)},
        compiler_params=params(8),
        cost_estimate=cost(11),
        name="couple",
    )(lower, upper, cells, rows, *messages, *sums)
    return outs[0], outs[1:4], outs[4], outs[5]


def receptor_kernel(tangent, cells, rows_hbm, *rest):
    out, staged, parts, sem = rest[:3], rest[3], rest[4 : 4 + WAYS], rest[4 + WAYS]
    finish(index_copies(rows_hbm, 1, 0, parts, sem))
    gather_rows(tangent, parts, staged)
    select_fields(staged, cells, 0, None, out)


def at_receptors(tangent, cells, rows):
    return pl.pallas_call(
        receptor_kernel,
        out_shape=[MESSAGE] * 3,
        in_specs=[VMEM, VMEM, HBM],
        out_specs=[VMEM] * 3,
        scratch_shapes=[pltpu.VMEM((HALF, LANES), f32)] + index_scratch(HALF),
        compiler_params=params(8),
        cost_estimate=cost(3),
        name="at_receptors",
    )(tangent, cells, rows)


def transposed_kernel(tangent, centre, lower, upper, *rest):
    sums, raised, lowered = rest[:WAYS], rest[WAYS], rest[WAYS + 1]

    def products(start):
        at = rows_of(start, 8)
        value = tangent[at, :]
        raised[rows_of(start + 8, 8), :] = upper[at, :] * value
        lowered[rows_of(start + 8, 8), :] = lower[at, :] * value

    each_row_block(products)
    nothing = jnp.zeros((1, LANES), f32)
    fill_ends(raised, nothing, nothing)
    fill_ends(lowered, nothing, nothing)

    def stencil(start):
        at = rows_of(start, 8)
        sums[0][at, :] = (
            centre[at, :] * tangent[at, :] - raised[pl.ds(start + 7, 8), :] - lowered[pl.ds(start + 9, 8), :]
        )

    each_row_block(stencil)
    clear(sums[1:])


def transposed(tangent, centre, lower, upper):
    return pl.pallas_call(
        transposed_kernel,
        out_shape=[resident(ROWS, LANES)] * WAYS,
        in_specs=[VMEM] * 4,
        out_specs=[VMEM] * WAYS,
        scratch_shapes=[pltpu.VMEM((ROWS + 16, LANES), f32)] * 2,
        compiler_params=params(8),
        cost_estimate=cost(4),
        name="transposed",
    )(tangent, centre, lower, upper)


def donor_kernel(half, last, *refs):
    cells, rows_hbm = refs[:2]
    weights, messages = refs[2:5], refs[5:8]
    refs = refs[8:]
    if last:
        low, high = refs[:2]
        refs = refs[2:]
    refs = refs[WAYS:]
    if last:
        adjoint, gram = refs[:2]
        refs = refs[2:]
    sums, staged, parts, sem = refs[:WAYS], refs[WAYS], refs[WAYS + 1 : 1 + 2 * WAYS], refs[1 + 2 * WAYS]
    copies = index_copies(rows_hbm, 4, half, parts, sem)
    spread_fields(messages, cells, half, weights, staged)
    finish(copies)
    add_rows(sums, parts, staged)
    if not last:
        return
    lane = lanes((1, LANES))
    low_row = pltpu.roll(low[...], PROBES, 1)[7:8, :]
    high_row = pltpu.roll(high[...], LANES - PROBES, 1)[0:1, :]
    sums[0][0:1, :] = sums[0][0:1, :] - jnp.where(lane < PROBES, low_row, 0.0)
    end = sums[0][ROWS - 1 : ROWS, :]
    sums[0][ROWS - 1 : ROWS, :] = end - jnp.where(lane >= LANES - PROBES, high_row, 0.0)

    def total(tile, product):
        for u in range(LANES // 8):
            at = rows_of(tile * LANES + u * 8, 8)
            value = sums[0][at, :]
            for part in sums[1:]:
                value = value + part[at, :]
            adjoint[at, :] = value
        block = adjoint[aligned(tile * LANES, LANES), :]
        high, low = split(block)
        high_t, low_t = split(block.T)
        left_side = jnp.concatenate([high_t, high_t, low_t], axis=1)
        right_side = jnp.concatenate([high, low, high], axis=0)
        return product + jnp.dot(left_side, right_side, preferred_element_type=f32)

    product = lax.fori_loop(0, TILES, total, jnp.zeros((LANES, LANES), f32))
    group = lanes((PROBES, LANES)) // PROBES
    folded = jnp.zeros((PROBES, LANES), f32)
    for g in range(GROUPS):
        folded = folded + jnp.where(group == g, product[g * PROBES : (g + 1) * PROBES, :], 0.0)
    for shift in (64, 32, 16):
        folded = folded + pltpu.roll(folded, shift, 1)
    gram[...] = folded[:, :PROBES]


def add_at_donors(half, cells, rows, weights, messages, sums, ends=None):
    last = ends is not None
    count = 4 * HALF
    ends = list(ends) if last else []
    out_shape = [resident(ROWS, LANES)] * WAYS
    first_sum = 8 + len(ends)
    if last:
        out_shape = [resident(ROWS, LANES), jax.ShapeDtypeStruct((PROBES, PROBES), f32)] + out_shape
    skip = len(out_shape) - WAYS
    outs = pl.pallas_call(
        functools.partial(donor_kernel, half, last),
        out_shape=out_shape,
        in_specs=[VMEM, HBM] + [VMEM] * (6 + len(ends) + WAYS),
        out_specs=[VMEM] * len(out_shape),
        scratch_shapes=[pltpu.VMEM((count, LANES), f32)] + index_scratch(count),
        input_output_aliases={first_sum + w: skip + w for w in range(WAYS)},
        compiler_params=params(12),
        cost_estimate=cost(12),
        name="add_at_donors",
    )(cells, rows, *weights, *messages, *ends, *sums)
    return outs[:2] if last else outs


def basis_kernel(total_cells, gram, adjoint, basis, factor, natural, sem):
    row = lax.broadcasted_iota(i32, (PROBES, 1), 0)
    left = gram[...] / f32(total_cells)
    right = jnp.where(lax.broadcasted_iota(i32, (PROBES, LANES), 0) == lanes((PROBES, LANES)) % PROBES, 1.0, 0.0)
    for j in range(PROBES):
        pivot = left[j : j + 1, j : j + 1]
        ratio = jnp.where(row > j, left[:, j : j + 1] / pivot, 0.0)
        root = jnp.sqrt(pivot)
        left_row, right_row = left[j : j + 1, :], right[j : j + 1, :]
        left = jnp.where(row == j, left_row / root, left - ratio * left_row)
        right = jnp.where(row == j, right_row / root, right - ratio * right_row)
    down = lax.broadcasted_iota(i32, (PROBES, PROBES), 0)
    factor[...] = jnp.where(lanes((PROBES, PROBES)) >= down, left, 0.0).T
    inverse = jnp.concatenate([right] * GROUPS, axis=0)
    same = lax.broadcasted_iota(i32, (LANES, LANES), 0) // PROBES == lanes((LANES, LANES)) // PROBES
    high, low = split(jnp.where(same, inverse, 0.0))
    left_side = jnp.concatenate([high, high, low], axis=1)

    def step(j, carry):
        for u in range(2):
            tile = j * 2 + u
            high, low = split(adjoint[aligned(tile * LANES, LANES), :])
            right_side = jnp.concatenate([high, low, high], axis=1)
            block = lax.dot_general(left_side, right_side, (((1,), (1,)), ((), ())), preferred_element_type=f32)
            for g in range(GROUPS):
                natural[:, aligned(g * ROWS + tile * LANES, LANES)] = block[g * PROBES : (g + 1) * PROBES, :]
        return carry

    lax.fori_loop(0, TILES // 2, step, 0)
    copies = [
        pltpu.make_async_copy(natural.at[pl.ds(p, 1), :], basis.at[p], sem.at[p]) for p in range(PROBES)
    ]
    for copy in copies:
        copy.start()
    finish(copies)


def basis_of(total_cells, gram, adjoint):
    return pl.pallas_call(
        functools.partial(basis_kernel, total_cells),
        out_shape=[
            jax.ShapeDtypeStruct((PROBES, 1, GROUPS * ROWS), f32),
            jax.ShapeDtypeStruct((PROBES, PROBES), f32),
        ],
        in_specs=[VMEM] * 2,
        out_specs=[HBM, VMEM],
        scratch_shapes=[pltpu.VMEM((PROBES, GROUPS * ROWS), f32), pltpu.SemaphoreType.DMA((PROBES,))],
        compiler_params=params(8),
        cost_estimate=cost(6),
        name="basis",
    )(gram, adjoint)


def moved(value, place):
    grids, columns = (lax.axis_size(axis) for axis in AXES)
    route = []
    for g in range(grids):
        for c in range(columns):
            to_g, to_c = place(g, c)
            if 0 <= to_c < columns:
                route.append((g * columns + c, (to_g % grids) * columns + to_c))
    return lax.ppermute(value, AXES, route)


def to_receptors(half, messages):
    columns = lax.axis_size("cell")
    d = half + 1
    return [
        moved(message, lambda g, c, e=e: (g + d, (c + e) % columns)) for message, e in zip(messages, (-1, 0, 1))
    ]


def to_donors(half, messages):
    columns = lax.axis_size("cell")
    d = half + 1
    return [
        moved(message, lambda g, c, e=e: (g - d, (c - e) % columns)) for message, e in zip(messages, (-1, 0, 1))
    ]


def to_next(value):
    return moved(value, lambda g, c: (g, c + 1))


def to_previous(value):
    return moved(value, lambda g, c: (g, c - 1))


def summed(value):
    value = value + moved(value, lambda g, c: (g ^ 1, c))
    value = value + moved(value, lambda g, c: (g ^ 2, c))
    value = value + moved(value, lambda g, c: ((6 - (g & 6)) | (g & 1), c))
    value = value + moved(value, lambda g, c: (g, c ^ 1))
    value = value + moved(value, lambda g, c: (g, (c & 12) | (3 - (c & 3))))
    value = value + moved(value, lambda g, c: (g, c ^ 4))
    value = value + moved(value, lambda g, c: (g, (12 - (c & 12)) | (c & 3)))
    return value


def body(probes, centre, lower_coef, upper_coef, donor_cells, receptor_cells, weights):
    width = probes.shape[2]
    donors = donor_cells[0]
    donor_rows = (donors & (ROWS - 1)).reshape(-1)
    receptor_rows = (receptor_cells & (ROWS - 1)).reshape(-1)
    donor_weights = [None, None]
    for half in (1, 0):
        pieces = [weights[0, :, (half * 3 + k) * FRINGE : (half * 3 + k + 1) * FRINGE] for k in range(3)]
        donor_weights[half] = to_donors(half, pieces)
    low = to_next(probes[:, 0, width - 1 :])
    high = to_previous(probes[:, 0, :1])
    table = table_of(probes)
    messages = [None, None]
    for half in (1, 0):
        staged = rows_at_donors(half, table, donor_rows)
        messages[half] = to_receptors(half, weighted_sums(half, staged, donors, donor_weights[half]))
    c, l, u, *sums = forward(table, centre, lower_coef, upper_coef, low, high)
    tangent, returned, first, last = couple(l, u, receptor_cells, receptor_rows, messages[0] + messages[1], sums)
    far = to_donors(1, returned)
    near = to_donors(0, at_receptors(tangent, receptor_cells, receptor_rows))
    high = to_previous(first)
    low = to_next(last)
    sums = transposed(tangent, c, l, u)
    sums = add_at_donors(1, donors, donor_rows, donor_weights[1], far, sums)
    adjoint, gram = add_at_donors(0, donors, donor_rows, donor_weights[0], near, sums, (low, high))
    total_cells = lax.axis_size("grid") * lax.axis_size("cell") * width
    basis, factor = basis_of(total_cells, summed(gram), adjoint)
    return (basis, factor)


def solution(mesh):
    in_specs = (
        P(None, "grid", "cell"),
        P("grid", "cell"),
        P("grid", "cell"),
        P("grid", "cell"),
        P("grid", None, "cell"),
        P("grid", "cell"),
        P("grid", None, "cell"),
    )
    out_specs = (P(None, "grid", "cell"), P())
    return jax.shard_map(body, mesh=mesh, in_specs=in_specs, out_specs=out_specs, check_vma=False)
```

time: 220 us -> 188 us (0.85)
  Pallas kernels: 116 us -> 105 us
  local copies, waits for them, and re-layouts: 11.2 us -> 2.51 us
  waiting for transfers between devices: 30.4 us -> 21.9 us
    pallas_call x5 -> x12, Pallas kernels: 116 us -> 105 us  [the longest x2 36.5 us: add_at_donors(): pl.pallas_call(functools.partial(donor_kernel, half, last), out_shape=out...]
    unnamed x53 -> x13, local copies, waits for them, and re-layouts: 10.3 us -> 1.62 us
    ppermute x29, waiting for transfers between devices: 30.4 us -> 21.9 us  [moved(): return lax.ppermute(value, AXES, route)]
  transfers between devices with their start and end apart: 29 -> 29, of which waited for: 12 -> 8; matrix products, arithmetic and copies ran while one was open for 2% -> 1% of each run, Pallas kernels for 5% -> 32%
where the time goes in v2:
time: 188 us
  Pallas kernels  105 us (56%)
  starting transfers between devices  56 us (30%)
  waiting for transfers between devices  21.9 us (12%)
  local copies, waits for them, and re-layouts  2.51 us (1%)
    ppermute x29, starting transfers between devices, moved(): return lax.ppermute(value, AXES, route)  56 us
    pallas_call x2, Pallas kernels, add_at_donors(): pl.pallas_call(functools.partial(donor_kernel, half, last), out_shape=out...  36.5 us
    ppermute x29, waiting for transfers between devices, moved(): return lax.ppermute(value, AXES, route)  21.9 us
    pallas_call x2, Pallas kernels, rows_at_donors(): pl.pallas_call(functools.partial(rows_kernel, half), out_shape=resident(c...  18.6 us
    pallas_call x1, Pallas kernels, couple(): pl.pallas_call(couple_kernel, out_shape=[resident(ROWS, LANES)] + [MESSAG...  15.8 us
    pallas_call x1, Pallas kernels, forward(): pl.pallas_call(forward_kernel, out_shape=[resident(ROWS, LANES)] * (3 + W...  7.21 us
    pallas_call x1, Pallas kernels, basis_of(): pl.pallas_call(functools.partial(basis_kernel, total_cells), out_shape=[j...  7.17 us
    pallas_call x2, Pallas kernels, weighted_sums(): pl.pallas_call(functools.partial(select_kernel, half), out_shape=[MESSAGE...  6.98 us
  transfers between devices with their start and end apart: 29, of which 8 were waited for; matrix products, arithmetic and copies ran while one was open for 1% of the time, Pallas kernels for 32%

profile of v2, /device:TPU:0, one launch (start us, length us, event | category | flops | bytes accessed | tf_op | source)
XLA Modules:
  0.0 187.8 jit_solution(18066530752031258736)
XLA Ops:
  0.6 0.8 slice_bitcast_fusion
  1.4 8.8 %collective-permute-start.10 = (f32[4,1024]{1,0:T(4,128)S(1)}, f32[4,1024]{1,0:T(4,128)S(1)}, u32[]{:S(2)}, u32[]{:S(2)}) collective-permute-start(f32[4,1024]{1,0:T(4,128)S(1)} %get-tuple-element.92), channel_id=1, source_target_pairs={{0,111},{1,96},{2,97},{3,98},{4,99},{5,100},{6,101},{7,102},{8,103... | collective-permute-start | bytes 49160 | tf_op jit(solution)/shard_map/ppermute | solution.py:537
  10.3 4.5 %collective-permute-start.2 = (f32[4,1024]{1,0:T(4,128)S(1)}, f32[4,1024]{1,0:T(4,128)S(1)}, u32[]{:S(2)}, u32[]{:S(2)}) collective-permute-start(f32[4,1024]{1,0:T(4,128)S(1)} %get-tuple-element.94), channel_id=1, source_target_pairs={{0,127},{1,112},{2,113},{3,114},{4,115},{5,116},{6,117},{7,118},{8... | collective-permute-start | bytes 49160 | tf_op jit(solution)/shard_map/ppermute | solution.py:537
  14.7 1.4 collective-permute-start.1
  16.1 0.5 collective-permute-start.9
  16.7 0.9 and_bitcast_fusion
  17.6 1.6 copy-done.1
  19.2 4.8 %table.1 = f32[4096,128]{1,0:T(8,128)S(1)} custom-call(f32[16,1,32768]{2,1,0:T(1,128)S(1)} %copy-done.1), custom_call_target="tpu_custom_call" | custom-call | bytes 9000000 | tf_op jit(solution)/shard_map/table/pallas_call | solution.py:204
  24.0 9.3 %donor_rows.3.staged = f32[12288,128]{1,0:T(8,128)S(1)} custom-call(f32[4096,128]{1,0:T(8,128)S(1)} %table.1, s32[24576]{0:T(1024)S(1)} %bitcast.19), custom_call_target="tpu_custom_call" | custom-call | bytes 27000000 | tf_op jit(solution)/shard_map/donor_rows/pallas_call | solution.py:224
  33.3 0.1 collective-permute-start
  33.5 3.5 %weighted_sums.3 = (f32[16,1024]{1,0:T(8,128)S(1)}, f32[16,1024]{1,0:T(8,128)S(1)}, f32[16,1024]{1,0:T(8,128)S(1)}) custom-call(f32[12288,128]{1,0:T(8,128)S(1)} %donor_rows.3.staged, s32[4,6144]{1,0:T(4,128)S(1)} %bitcast.23, f32[4,1024]{1,0:T(4,128)S(1)} %collective-permute-done.8.rest_0_.refs_2_, f32[4,1024]{1,0:T(4,128)S(1)} %collective-permute-done.9.rest_1_.refs_3_, ...), custom_call_target="tpu_custom_call" | custom-call | bytes 9000000 | tf_op jit(solution)/shard_map/weighted_sums/pallas_call | solution.py:244
  37.0 5.5 %collective-permute-start.11 = (f32[16,1024]{1,0:T(8,128)S(1)}, f32[16,1024]{1,0:T(8,128)S(1)}, u32[]{:S(2)}, u32[]{:S(2)}) collective-permute-start(f32[16,1024]{1,0:T(8,128)S(1)} %get-tuple-element.51), channel_id=1, source_target_pairs={{0,47},{1,32},{2,33},{3,34},{4,35},{5,36},{6,37},{7,38},{8,39},{9,... | collective-permute-start | bytes 196616 | tf_op jit(solution)/shard_map/ppermute | solution.py:537
  42.5 0.1 fusion
  42.5 1.3 collective-permute-start.3
  43.8 9.3 %donor_rows.2.staged = f32[12288,128]{1,0:T(8,128)S(1)} custom-call(f32[4096,128]{1,0:T(8,128)S(1)} %table.1, s32[24576]{0:T(1024)S(1)} %bitcast.20), custom_call_target="tpu_custom_call" | custom-call | bytes 27000000 | tf_op jit(solution)/shard_map/donor_rows/pallas_call | solution.py:224
  53.1 1.3 collective-permute-start.4
  54.4 1.6 collective-permute-start.12
  56.0 3.4 %collective-permute-start.13 = (f32[16,1024]{1,0:T(8,128)S(1)}, f32[16,1024]{1,0:T(8,128)S(1)}, u32[]{:S(2)}, u32[]{:S(2)}) collective-permute-start(f32[16,1024]{1,0:T(8,128)S(1)} %get-tuple-element.53), channel_id=1, source_target_pairs={{0,33},{1,34},{2,35},{3,36},{4,37},{5,38},{6,39},{7,40},{8,41},{9,... | collective-permute-start | bytes 196616 | tf_op jit(solution)/shard_map/ppermute | solution.py:537
  59.4 3.5 %weighted_sums.2 = (f32[16,1024]{1,0:T(8,128)S(1)}, f32[16,1024]{1,0:T(8,128)S(1)}, f32[16,1024]{1,0:T(8,128)S(1)}) custom-call(f32[12288,128]{1,0:T(8,128)S(1)} %donor_rows.2.staged, s32[4,6144]{1,0:T(4,128)S(1)} %bitcast.24, f32[4,1024]{1,0:T(4,128)S(1)} %collective-permute-done.rest_0_.refs_2_, f32[4,1024]{1,0:T(4,128)S(1)} %collective-permute-done.1.rest_1_.refs_3_, ...), custom_call_target="tpu_custom_call" | custom-call | bytes 9000000 | tf_op jit(solution)/shard_map/weighted_sums/pallas_call | solution.py:244
  62.9 2.4 %collective-permute-start.5 = (f32[16,1024]{1,0:T(8,128)S(1)}, f32[16,1024]{1,0:T(8,128)S(1)}, u32[]{:S(2)}, u32[]{:S(2)}) collective-permute-start(f32[16,1024]{1,0:T(8,128)S(1)} %get-tuple-element.48), channel_id=1, source_target_pairs={{0,31},{1,16},{2,17},{3,18},{4,19},{5,20},{6,21},{7,22},{8,23},{9,... | collective-permute-start | bytes 196616 | tf_op jit(solution)/shard_map/ppermute | solution.py:537
  65.3 1.8 collective-permute-start.6
  67.2 7.2 %forward.1 = (f32[4096,128]{1,0:T(8,128)S(1)}, f32[4096,128]{1,0:T(8,128)S(1)}, f32[4096,128]{1,0:T(8,128)S(1)}, f32[4096,128]{1,0:T(8,128)S(1)}, f32[4096,128]{...) custom-call(f32[4096,128]{1,0:T(8,128)S(1)} %table.1, ...), custom_call_target="tpu_custom_call" | custom-call | bytes 21000000 | tf_op jit(solution)/shard_map/forward/pallas_call | solution.py:288
  74.5 1.8 collective-permute-done.7.refs_6_
  76.2 15.8 %couple.1 = (f32[4096,128]{1,0:T(8,128)S(1)}, f32[16,1024]{1,0:T(8,128)S(1)}, f32[16,1024]{1,0:T(8,128)S(1)}, f32[16,1024]{1,0:T(8,128)S(1)}, f32[8,128]{1,0:T(8...) custom-call(f32[4096,128]{1,0:T(8,128)S(1)} %get-tuple-element.46.re, ...), custom_call_target="tpu_custom_call", output_to_operand_aliasing={{6}: (10, {}), {7}: (11, {}), {8}: (12, {}), {9}: (13, {}),... | custom-call | bytes 33000000 | tf_op jit(solution)/shard_map/couple/pallas_call | solution.py:333
  92.1 0.1 collective-permute-start.19
  92.2 0.3 collective-permute-start.20
  92.5 5.5 %collective-permute-start.21 = (f32[16,1024]{1,0:T(8,128)S(1)}, f32[16,1024]{1,0:T(8,128)S(1)}, u32[]{:S(2)}, u32[]{:S(2)}) collective-permute-start(f32[16,1024]{1,0:T(8,128)S(1)} %get-tuple-element.70), channel_id=1, source_target_pairs={{0,111},{1,96},{2,97},{3,98},{4,99},{5,100},{6,101},{7,102},{8,103... | collective-permute-start | bytes 196616 | tf_op jit(solution)/shard_map/ppermute | solution.py:537
  98.0 5.2 %at_receptors.1 = (f32[16,1024]{1,0:T(8,128)S(1)}, f32[16,1024]{1,0:T(8,128)S(1)}, f32[16,1024]{1,0:T(8,128)S(1)}) custom-call(f32[4096,128]{1,0:T(8,128)S(1)} %get-tuple-element.62.tangent, s32[1,6144]{1,0:T(1,128)S(1)} %copy-done.2, s32[6144]{0:T(1024)S(1)} %bitcast.28), custom_call_target="tpu_custom_call" | custom-call | bytes 9000000 | tf_op jit(solution)/shard_map/at_receptors/pallas_call | solution.py:355
  103.3 0.2 collective-permute-start.15
  103.5 7.4 %collective-permute-start.16 = (f32[16,1024]{1,0:T(8,128)S(1)}, f32[16,1024]{1,0:T(8,128)S(1)}, u32[]{:S(2)}, u32[]{:S(2)}) collective-permute-start(f32[16,1024]{1,0:T(8,128)S(1)} %get-tuple-element.65), channel_id=1, source_target_pairs={{0,127},{1,112},{2,113},{3,114},{4,115},{5,116},{6,117},{7,118},{8... | collective-permute-start | bytes 196616 | tf_op jit(solution)/shard_map/ppermute | solution.py:537
  110.8 1.3 collective-permute-start.17
  112.1 1.3 collective-permute-start.18
  113.4 3.1 %transposed.1 = (f32[4096,128]{1,0:T(8,128)S(1)}, f32[4096,128]{1,0:T(8,128)S(1)}, f32[4096,128]{1,0:T(8,128)S(1)}, f32[4096,128]{1,0:T(8,128)S(1)}, f32[4096,12...) custom-call(f32[4096,128]{1,0:T(8,128)S(1)} %get-tuple-element.62.tangent, ...), custom_call_target="tpu_custom_call" | custom-call | bytes 12000000 | tf_op jit(solution)/shard_map/transposed/pallas_call | solution.py:392
  116.6 14.2 %add_at_donors.2 = (f32[4096,128]{1,0:T(8,128)S(1)}, f32[4096,128]{1,0:T(8,128)S(1)}, f32[4096,128]{1,0:T(8,128)S(1)}, f32[4096,128]{1,0:T(8,128)S(1)}, f32[4096...) custom-call(s32[4,6144]{1,0:T(4,128)S(1)} %bitcast.25, ...), custom_call_target="tpu_custom_call", output_to_operand_aliasing={{0}: (8, {}), {1}: (9, {}), {2}: (10, {}), {3}: (11, {}), {... | custom-call | bytes 36000000 | tf_op jit(solution)/shard_map/add_at_donors/pallas_call | solution.py:462
  130.8 22.3 %add_at_donors.3 = (f32[4096,128]{1,0:T(8,128)S(1)}, f32[16,16]{1,0:T(8,128)S(1)}, f32[4096,128]{1,0:T(8,128)S(1)}, f32[4096,128]{1,0:T(8,128)S(1)}, f32[4096,12...) custom-call(s32[4,6144]{1,0:T(4,128)S(1)} %bitcast.26, ...), custom_call_target="tpu_custom_call", output_to_operand_aliasing={{2}: (10, {}), {3}: (11, {}), {4}: (12, {}), {5}: (13, {}),... | custom-call | bytes 36000000 | tf_op jit(solution)/shard_map/add_at_donors/pallas_call | solution.py:462
  153.1 0.8 collective-permute-start.22
  153.9 0.8 collective-permute-done.22
  154.7 3.6 %collective-permute-done.23 = f32[16,16]{1,0:T(8,128)S(1)} collective-permute-done((f32[16,16]{1,0:T(8,128)S(1)}, f32[16,16]{1,0:T(8,128)S(1)}, u32[]{:S(2)}, u32[]{:S(2)}) %collective-permute-start.23) | collective-permute-done | bytes 1056 | tf_op jit(solution)/shard_map/ppermute | solution.py:537
  158.4 0.2 collective-permute-start.24
  158.6 4.6 %collective-permute-done.24 = f32[16,16]{1,0:T(8,128)S(1)} collective-permute-done((f32[16,16]{1,0:T(8,128)S(1)}, f32[16,16]{1,0:T(8,128)S(1)}, u32[]{:S(2)}, u32[]{:S(2)}) %collective-permute-start.24) | collective-permute-done | bytes 1056 | tf_op jit(solution)/shard_map/ppermute | solution.py:537
  163.2 2.4 %collective-permute-start.25 = (f32[16,16]{1,0:T(8,128)S(1)}, f32[16,16]{1,0:T(8,128)S(1)}, u32[]{:S(2)}, u32[]{:S(2)}) collective-permute-start(f32[16,16]{1,0:T(8,128)S(1)} %add.23), channel_id=1, source_target_pairs={{0,1},{1,0},{2,3},{3,2},{4,5},{5,4},{6,7},{7,6},{8,9},{9,8},{10,11... | collective-permute-start | bytes 3080 | tf_op jit(solution)/shard_map/ppermute | solution.py:537
  165.6 1.6 collective-permute-done.25
  167.2 4.9 %collective-permute-done.26 = f32[16,16]{1,0:T(8,128)S(1)} collective-permute-done((f32[16,16]{1,0:T(8,128)S(1)}, f32[16,16]{1,0:T(8,128)S(1)}, u32[]{:S(2)}, u32[]{:S(2)}) %collective-permute-start.26) | collective-permute-done | bytes 1056 | tf_op jit(solution)/shard_map/ppermute | solution.py:537
  172.1 0.8 collective-permute-start.27
  172.9 2.9 %collective-permute-done.27 = f32[16,16]{1,0:T(8,128)S(1)} collective-permute-done((f32[16,16]{1,0:T(8,128)S(1)}, f32[16,16]{1,0:T(8,128)S(1)}, u32[]{:S(2)}, u32[]{:S(2)}) %collective-permute-start.27) | collective-permute-done | bytes 1056 | tf_op jit(solution)/shard_map/ppermute | solution.py:537
  175.7 3.2 %collective-permute-start.28 = (f32[16,16]{1,0:T(8,128)S(1)}, f32[16,16]{1,0:T(8,128)S(1)}, u32[]{:S(2)}, u32[]{:S(2)}) collective-permute-start(f32[16,16]{1,0:T(8,128)S(1)} %add.26), channel_id=1, source_target_pairs={{0,12},{1,13},{2,14},{3,15},{4,8},{5,9},{6,10},{7,11},{8,4},{9,5},... | collective-permute-start | bytes 3080 | tf_op jit(solution)/shard_map/ppermute | solution.py:537
  178.9 1.7 collective-permute-done.28
  180.6 7.2 %basis.1 = (f32[16,1,32768]{2,1,0:T(1,128)}, f32[16,16]{1,0:T(8,128)}) custom-call(f32[16,16]{1,0:T(8,128)S(1)} %add.27.gram, f32[4096,128]{1,0:T(8,128)S(1)} %get-tuple-element.89.adjoint), custom_call_target="tpu_custom_call" | custom-call | bytes 18000000 | tf_op jit(solution)/shard_map/basis/pallas_call | solution.py:514
  (46 shorter events, 0.2 us)
Async XLA Ops:
  1.4 31.9 %collective-permute-start.10 = (f32[4,1024]{1,0:T(4,128)S(1)}, f32[4,1024]{1,0:T(4,128)S(1)}, u32[]{:S(2)}, u32[]{:S(2)}) collective-permute-start(f32[4,1024]{1,0:T(4,128)S(1)} %get-tuple-element.92), channel_id=1, source_target_pairs={{0,111},{1,96},{2,97},{3,98},{4,99},{5,100},{6,101},{7,102},{8,103... | collective-permute-start | bytes 49160 | tf_op jit(solution)/shard_map/ppermute | solution.py:537
  10.3 23.2 %collective-permute-start.8 = (f32[4,1024]{1,0:T(4,128)S(1)}, f32[4,1024]{1,0:T(4,128)S(1)}, u32[]{:S(2)}, u32[]{:S(2)}) collective-permute-start(f32[4,1024]{1,0:T(4,128)S(1)} %get-tuple-element.93), channel_id=1, source_target_pairs={{0,97},{1,98},{2,99},{3,100},{4,101},{5,102},{6,103},{7,104},{8,10... | collective-permute-start | bytes 49160 | tf_op jit(solution)/shard_map/ppermute | solution.py:537
  10.3 42.9 %collective-permute-start.2 = (f32[4,1024]{1,0:T(4,128)S(1)}, f32[4,1024]{1,0:T(4,128)S(1)}, u32[]{:S(2)}, u32[]{:S(2)}) collective-permute-start(f32[4,1024]{1,0:T(4,128)S(1)} %get-tuple-element.94), channel_id=1, source_target_pairs={{0,127},{1,112},{2,113},{3,114},{4,115},{5,116},{6,117},{7,118},{8... | collective-permute-start | bytes 49160 | tf_op jit(solution)/shard_map/ppermute | solution.py:537
  14.7 39.7 %collective-permute-start.1 = (f32[4,1024]{1,0:T(4,128)S(1)}, f32[4,1024]{1,0:T(4,128)S(1)}, u32[]{:S(2)}, u32[]{:S(2)}) collective-permute-start(f32[4,1024]{1,0:T(4,128)S(1)} %get-tuple-element.95), channel_id=1, source_target_pairs={{0,112},{1,113},{2,114},{3,115},{4,116},{5,117},{6,118},{7,119},{8... | collective-permute-start | bytes 49160 | tf_op jit(solution)/shard_map/ppermute | solution.py:537
  16.1 17.3 %collective-permute-start.9 = (f32[4,1024]{1,0:T(4,128)S(1)}, f32[4,1024]{1,0:T(4,128)S(1)}, u32[]{:S(2)}, u32[]{:S(2)}) collective-permute-start(f32[4,1024]{1,0:T(4,128)S(1)} %get-tuple-element.97), channel_id=1, source_target_pairs={{0,96},{1,97},{2,98},{3,99},{4,100},{5,101},{6,102},{7,103},{8,104... | collective-permute-start | bytes 49160 | tf_op jit(solution)/shard_map/ppermute | solution.py:537
  17.6 1.6 copy-start.1
  24.0 9.4 %copy-start = (s32[1,4,6144]{2,1,0:T(4,128)S(1)}, s32[1,4,6144]{2,1,0:T(4,128)}, u32[]{:S(2)}) copy-start(s32[1,4,6144]{2,1,0:T(4,128)} %param.11) | copy-start | bytes 294916
  33.3 22.7 %collective-permute-start = (f32[4,1024]{1,0:T(4,128)S(1)}, f32[4,1024]{1,0:T(4,128)S(1)}, u32[]{:S(2)}, u32[]{:S(2)}) collective-permute-start(f32[4,1024]{1,0:T(4,128)S(1)} %get-tuple-element.96), channel_id=1, source_target_pairs={{0,113},{1,114},{2,115},{3,116},{4,117},{5,118},{6,119},{7,120},{8... | collective-permute-start | bytes 49160 | tf_op jit(solution)/shard_map/ppermute | solution.py:537
  37.0 30.2 %collective-permute-start.11 = (f32[16,1024]{1,0:T(8,128)S(1)}, f32[16,1024]{1,0:T(8,128)S(1)}, u32[]{:S(2)}, u32[]{:S(2)}) collective-permute-start(f32[16,1024]{1,0:T(8,128)S(1)} %get-tuple-element.51), channel_id=1, source_target_pairs={{0,47},{1,32},{2,33},{3,34},{4,35},{5,36},{6,37},{7,38},{8,39},{9,... | collective-permute-start | bytes 196616 | tf_op jit(solution)/shard_map/ppermute | solution.py:537
  42.5 20.3 %collective-permute-start.3 = (f32[16,1]{1,0:T(8,128)S(1)}, f32[16,1]{1,0:T(8,128)S(1)}, u32[]{:S(2)}, u32[]{:S(2)}) collective-permute-start(f32[16,1]{1,0:T(8,128)S(1)} %bitcast.30), channel_id=1, source_target_pairs={{0,1},{1,2},{2,3},{3,4},{4,5},{5,6},{6,7},{7,8},{8,9},{9,10},{10,1... | collective-permute-start | bytes 200 | tf_op jit(solution)/shard_map/ppermute | solution.py:537
  53.1 12.2 %collective-permute-start.4 = (f32[16,1]{1,0:T(8,128)S(1)}, f32[16,1]{1,0:T(8,128)S(1)}, u32[]{:S(2)}, u32[]{:S(2)}) collective-permute-start(f32[16,1]{1,0:T(8,128)S(1)} %bitcast.29), channel_id=1, source_target_pairs={{1,0},{2,1},{3,2},{4,3},{5,4},{6,5},{7,6},{8,7},{9,8},{10,9},{11,1... | collective-permute-start | bytes 200 | tf_op jit(solution)/shard_map/ppermute | solution.py:537
  54.4 20.0 %collective-permute-start.12 = (f32[16,1024]{1,0:T(8,128)S(1)}, f32[16,1024]{1,0:T(8,128)S(1)}, u32[]{:S(2)}, u32[]{:S(2)}) collective-permute-start(f32[16,1024]{1,0:T(8,128)S(1)} %get-tuple-element.52), channel_id=1, source_target_pairs={{0,32},{1,33},{2,34},{3,35},{4,36},{5,37},{6,38},{7,39},{8,40},{9,... | collective-permute-start | bytes 196616 | tf_op jit(solution)/shard_map/ppermute | solution.py:537
  56.0 11.1 %copy-start.2 = (s32[1,6144]{1,0:T(1,128)S(1)}, s32[1,6144]{1,0:T(1,128)}, u32[]{:S(2)}) copy-start(s32[1,6144]{1,0:T(1,128)} %cells.1) | copy-start | bytes 73732
  56.0 11.2 %copy-start.3 = (f32[1,32768]{1,0:T(1,128)S(1)}, f32[1,32768]{1,0:T(1,128)}, u32[]{:S(2)}) copy-start(f32[1,32768]{1,0:T(1,128)} %centre.1) | copy-start | bytes 393220
  56.0 11.2 %copy-start.4 = (f32[1,32768]{1,0:T(1,128)S(1)}, f32[1,32768]{1,0:T(1,128)}, u32[]{:S(2)}) copy-start(f32[1,32768]{1,0:T(1,128)} %lower.1) | copy-start | bytes 393220
  56.0 11.2 %copy-start.5 = (f32[1,32768]{1,0:T(1,128)S(1)}, f32[1,32768]{1,0:T(1,128)}, u32[]{:S(2)}) copy-start(f32[1,32768]{1,0:T(1,128)} %upper.1) | copy-start | bytes 393220
  56.0 18.4 %collective-permute-start.13 = (f32[16,1024]{1,0:T(8,128)S(1)}, f32[16,1024]{1,0:T(8,128)S(1)}, u32[]{:S(2)}, u32[]{:S(2)}) collective-permute-start(f32[16,1024]{1,0:T(8,128)S(1)} %get-tuple-element.53), channel_id=1, source_target_pairs={{0,33},{1,34},{2,35},{3,36},{4,37},{5,38},{6,39},{7,40},{8,41},{9,... | collective-permute-start | bytes 196616 | tf_op jit(solution)/shard_map/ppermute | solution.py:537
  62.9 11.5 %collective-permute-start.5 = (f32[16,1024]{1,0:T(8,128)S(1)}, f32[16,1024]{1,0:T(8,128)S(1)}, u32[]{:S(2)}, u32[]{:S(2)}) collective-permute-start(f32[16,1024]{1,0:T(8,128)S(1)} %get-tuple-element.48), channel_id=1, source_target_pairs={{0,31},{1,16},{2,17},{3,18},{4,19},{5,20},{6,21},{7,22},{8,23},{9,... | collective-permute-start | bytes 196616 | tf_op jit(solution)/shard_map/ppermute | solution.py:537
  65.3 9.1 %collective-permute-start.6 = (f32[16,1024]{1,0:T(8,128)S(1)}, f32[16,1024]{1,0:T(8,128)S(1)}, u32[]{:S(2)}, u32[]{:S(2)}) collective-permute-start(f32[16,1024]{1,0:T(8,128)S(1)} %get-tuple-element.49), channel_id=1, source_target_pairs={{0,16},{1,17},{2,18},{3,19},{4,20},{5,21},{6,22},{7,23},{8,24},{9,... | collective-permute-start | bytes 196616 | tf_op jit(solution)/shard_map/ppermute | solution.py:537
  67.1 9.1 %collective-permute-start.7 = (f32[16,1024]{1,0:T(8,128)S(1)}, f32[16,1024]{1,0:T(8,128)S(1)}, u32[]{:S(2)}, u32[]{:S(2)}) collective-permute-start(f32[16,1024]{1,0:T(8,128)S(1)} %get-tuple-element.50), channel_id=1, source_target_pairs={{0,17},{1,18},{2,19},{3,20},{4,21},{5,22},{6,23},{7,24},{8,25},{9,... | collective-permute-start | bytes 196616 | tf_op jit(solution)/shard_map/ppermute | solution.py:537
  92.1 11.4 %collective-permute-start.19 = (f32[16,1024]{1,0:T(8,128)S(1)}, f32[16,1024]{1,0:T(8,128)S(1)}, u32[]{:S(2)}, u32[]{:S(2)}) collective-permute-start(f32[16,1024]{1,0:T(8,128)S(1)} %get-tuple-element.68), channel_id=1, source_target_pairs={{0,97},{1,98},{2,99},{3,100},{4,101},{5,102},{6,103},{7,104},{8,10... | collective-permute-start | bytes 196616 | tf_op jit(solution)/shard_map/ppermute | solution.py:537
  92.2 18.7 %collective-permute-start.20 = (f32[16,1024]{1,0:T(8,128)S(1)}, f32[16,1024]{1,0:T(8,128)S(1)}, u32[]{:S(2)}, u32[]{:S(2)}) collective-permute-start(f32[16,1024]{1,0:T(8,128)S(1)} %get-tuple-element.69), channel_id=1, source_target_pairs={{0,96},{1,97},{2,98},{3,99},{4,100},{5,101},{6,102},{7,103},{8,104... | collective-permute-start | bytes 196616 | tf_op jit(solution)/shard_map/ppermute | solution.py:537
  92.5 19.7 %collective-permute-start.21 = (f32[16,1024]{1,0:T(8,128)S(1)}, f32[16,1024]{1,0:T(8,128)S(1)}, u32[]{:S(2)}, u32[]{:S(2)}) collective-permute-start(f32[16,1024]{1,0:T(8,128)S(1)} %get-tuple-element.70), channel_id=1, source_target_pairs={{0,111},{1,96},{2,97},{3,98},{4,99},{5,100},{6,101},{7,102},{8,103... | collective-permute-start | bytes 196616 | tf_op jit(solution)/shard_map/ppermute | solution.py:537
  103.2 27.6 %collective-permute-start.14 = (f32[16,1024]{1,0:T(8,128)S(1)}, f32[16,1024]{1,0:T(8,128)S(1)}, u32[]{:S(2)}, u32[]{:S(2)}) collective-permute-start(f32[16,1024]{1,0:T(8,128)S(1)} %get-tuple-element.63), channel_id=1, source_target_pairs={{0,113},{1,114},{2,115},{3,116},{4,117},{5,118},{6,119},{7,120},{8... | collective-permute-start | bytes 196616 | tf_op jit(solution)/shard_map/ppermute | solution.py:537
  103.3 27.5 %collective-permute-start.15 = (f32[16,1024]{1,0:T(8,128)S(1)}, f32[16,1024]{1,0:T(8,128)S(1)}, u32[]{:S(2)}, u32[]{:S(2)}) collective-permute-start(f32[16,1024]{1,0:T(8,128)S(1)} %get-tuple-element.64), channel_id=1, source_target_pairs={{0,112},{1,113},{2,114},{3,115},{4,116},{5,117},{6,118},{7,119},{8... | collective-permute-start | bytes 196616 | tf_op jit(solution)/shard_map/ppermute | solution.py:537
  103.5 27.3 %collective-permute-start.16 = (f32[16,1024]{1,0:T(8,128)S(1)}, f32[16,1024]{1,0:T(8,128)S(1)}, u32[]{:S(2)}, u32[]{:S(2)}) collective-permute-start(f32[16,1024]{1,0:T(8,128)S(1)} %get-tuple-element.65), channel_id=1, source_target_pairs={{0,127},{1,112},{2,113},{3,114},{4,115},{5,116},{6,117},{7,118},{8... | collective-permute-start | bytes 196616 | tf_op jit(solution)/shard_map/ppermute | solution.py:537
  110.8 19.9 %collective-permute-start.17 = (f32[8,128]{1,0:T(8,128)S(1)}, f32[8,128]{1,0:T(8,128)S(1)}, u32[]{:S(2)}, u32[]{:S(2)}) collective-permute-start(f32[8,128]{1,0:T(8,128)S(1)} %get-tuple-element.66), channel_id=1, source_target_pairs={{0,1},{1,2},{2,3},{3,4},{4,5},{5,6},{6,7},{7,8},{8,9},{9,10},{10,1... | collective-permute-start | bytes 12296 | tf_op jit(solution)/shard_map/ppermute | solution.py:537
  112.1 18.6 %collective-permute-start.18 = (f32[8,128]{1,0:T(8,128)S(1)}, f32[8,128]{1,0:T(8,128)S(1)}, u32[]{:S(2)}, u32[]{:S(2)}) collective-permute-start(f32[8,128]{1,0:T(8,128)S(1)} %get-tuple-element.67), channel_id=1, source_target_pairs={{1,0},{2,1},{3,2},{4,3},{5,4},{6,5},{7,6},{8,7},{9,8},{10,9},{11,1... | collective-permute-start | bytes 12296 | tf_op jit(solution)/shard_map/ppermute | solution.py:537
  153.1 1.6 collective-permute-start.22
  154.7 3.7 %collective-permute-start.23 = (f32[16,16]{1,0:T(8,128)S(1)}, f32[16,16]{1,0:T(8,128)S(1)}, u32[]{:S(2)}, u32[]{:S(2)}) collective-permute-start(f32[16,16]{1,0:T(8,128)S(1)} %add.21), channel_id=1, source_target_pairs={{0,32},{1,33},{2,34},{3,35},{4,36},{5,37},{6,38},{7,39},{8,40},{9,... | collective-permute-start | bytes 3080 | tf_op jit(solution)/shard_map/ppermute | solution.py:537
  158.4 4.9 %collective-permute-start.24 = (f32[16,16]{1,0:T(8,128)S(1)}, f32[16,16]{1,0:T(8,128)S(1)}, u32[]{:S(2)}, u32[]{:S(2)}) collective-permute-start(f32[16,16]{1,0:T(8,128)S(1)} %add.22), channel_id=1, source_target_pairs={{0,96},{1,97},{2,98},{3,99},{4,100},{5,101},{6,102},{7,103},{8,104... | collective-permute-start | bytes 3080 | tf_op jit(solution)/shard_map/ppermute | solution.py:537
  163.2 4.0 %collective-permute-start.25 = (f32[16,16]{1,0:T(8,128)S(1)}, f32[16,16]{1,0:T(8,128)S(1)}, u32[]{:S(2)}, u32[]{:S(2)}) collective-permute-start(f32[16,16]{1,0:T(8,128)S(1)} %add.23), channel_id=1, source_target_pairs={{0,1},{1,0},{2,3},{3,2},{4,5},{5,4},{6,7},{7,6},{8,9},{9,8},{10,11... | collective-permute-start | bytes 3080 | tf_op jit(solution)/shard_map/ppermute | solution.py:537
  167.2 4.9 %collective-permute-start.26 = (f32[16,16]{1,0:T(8,128)S(1)}, f32[16,16]{1,0:T(8,128)S(1)}, u32[]{:S(2)}, u32[]{:S(2)}) collective-permute-start(f32[16,16]{1,0:T(8,128)S(1)} %add.24), channel_id=1, source_target_pairs={{0,3},{1,2},{2,1},{3,0},{4,7},{5,6},{6,5},{7,4},{8,11},{9,10},{10,... | collective-permute-start | bytes 3080 | tf_op jit(solution)/shard_map/ppermute | solution.py:537
  172.1 3.7 %collective-permute-start.27 = (f32[16,16]{1,0:T(8,128)S(1)}, f32[16,16]{1,0:T(8,128)S(1)}, u32[]{:S(2)}, u32[]{:S(2)}) collective-permute-start(f32[16,16]{1,0:T(8,128)S(1)} %add.25), channel_id=1, source_target_pairs={{0,4},{1,5},{2,6},{3,7},{4,0},{5,1},{6,2},{7,3},{8,12},{9,13},{10,... | collective-permute-start | bytes 3080 | tf_op jit(solution)/shard_map/ppermute | solution.py:537
  175.7 4.9 %collective-permute-start.28 = (f32[16,16]{1,0:T(8,128)S(1)}, f32[16,16]{1,0:T(8,128)S(1)}, u32[]{:S(2)}, u32[]{:S(2)}) collective-permute-start(f32[16,16]{1,0:T(8,128)S(1)} %add.26), channel_id=1, source_target_pairs={{0,12},{1,13},{2,14},{3,15},{4,8},{5,9},{6,10},{7,11},{8,4},{9,5},... | collective-permute-start | bytes 3080 | tf_op jit(solution)/shard_map/ppermute | solution.py:537

commit v3 on v2

v3 whole, which is shorter than its diff:
```python
import functools

import jax
import jax.numpy as jnp
from jax import lax
from jax.experimental import pallas as pl
from jax.experimental.pallas import tpu as pltpu
from jax.sharding import PartitionSpec as P

f32 = jnp.float32
i32 = jnp.int32
bf16 = jnp.bfloat16

PROBES = 16
GROUPS = 8
ROWS = 4096
LANES = 128
PARTNERS = 6
FRINGE = 1024
HALF = 3 * FRINGE
SLOTS = PARTNERS * FRINGE
TILES = ROWS // LANES
WAYS = 8
UNROLL = 8

AXES = ("grid", "cell")

VMEM = pl.BlockSpec(memory_space=pltpu.VMEM)
HBM = pl.BlockSpec(memory_space=pl.ANY)
FIXED = pl.BlockSpec(memory_space=pltpu.HBM)


def aligned(start, size):
    return pl.ds(pl.multiple_of(start, size), size)


def rows_of(start, size):
    return pl.ds(pl.multiple_of(start, 8), size)


def split(x):
    high = x.astype(bf16)
    return high, (x - high.astype(f32)).astype(bf16)


def params(limit_mib):
    return pltpu.CompilerParams(vmem_limit_bytes=limit_mib << 20)


def cost(microseconds):
    return pl.CostEstimate(flops=0, transcendentals=0, bytes_accessed=microseconds * 3_000_000)


def resident(*shape):
    return pltpu.VMEM(shape, f32)


HEAD = 128


def segments(many, partners):
    return [(m, k) for m in range(many) for k in partners]


def index_scratch(segs):
    size = len(segs) * FRINGE // WAYS
    return [pltpu.SMEM((size,), i32)] * WAYS + [pltpu.SemaphoreType.DMA((3 * WAYS,))]


def index_copies(rows_hbm, segs, parts, sem):
    size = parts[0].shape[0]
    cuts = sorted({0, HEAD, size} | set(range(0, size, FRINGE)))
    phases = [[], []]
    for c in range(len(cuts) - 1):
        low, high = cuts[c], cuts[c + 1]
        for w in range(WAYS):
            seg, offset = divmod(w * size + low, FRINGE)
            start = segs[seg][0] * SLOTS + segs[seg][1] * FRINGE + offset
            copy = pltpu.make_async_copy(
                rows_hbm.at[pl.ds(start, high - low)], parts[w].at[pl.ds(low, high - low)], sem.at[c * WAYS + w]
            )
            copy.start()
            phases[min(c, 1)].append(copy)
    return phases


def finish(copies):
    for copy in copies:
        copy.wait()


def row_steps(parts, low, high, step):
    def outer(j, carry):
        for n in range(UNROLL):
            q = low + j * UNROLL + n
            for w in range(WAYS):
                step(w, q, parts[w][q])
        return carry

    lax.fori_loop(0, (high - low) // UNROLL, outer, 0)


def gather_rows(table, parts, staged, phases):
    count = parts[0].shape[0]

    def step(w, q, row):
        staged[pl.ds(w * count + q, 1), :] = table[pl.ds(row, 1), :]

    finish(phases[0])
    row_steps(parts, 0, HEAD, step)
    finish(phases[1])
    row_steps(parts, HEAD, count, step)


def clear(sums):
    def step(j, carry):
        for total in sums:
            for n in range(4):
                total[rows_of(j * 32 + n * 8, 8), :] = jnp.zeros((8, LANES), f32)
        return carry

    lax.fori_loop(0, ROWS // 32, step, 0)


def add_rows(sums, parts, staged):
    count = parts[0].shape[0]

    def step(w, q, row):
        term = staged[pl.ds(w * count + q, 1), :]
        sums[w][pl.ds(row, 1), :] = sums[w][pl.ds(row, 1), :] + term

    row_steps(parts, 0, count, step)


def groups_of(cells, m, offset):
    return jnp.broadcast_to(cells[m : m + 1, aligned(offset, LANES)], (8, LANES)) >> 12


def each_block(many, step):
    unroll = 8 // many

    def outer(j, carry):
        for n in range(unroll):
            step(j * unroll + n)
        return carry

    lax.fori_loop(0, FRINGE // LANES // unroll, outer, 0)


def select_fields(staged, cells, partners, weights, out):
    many = cells.shape[0]
    for n, k in enumerate(partners):

        def step(b):
            total = [jnp.zeros((8, LANES), f32)] * 2
            for m in range(many):
                field = staged[aligned((m * len(partners) + n) * FRINGE + b * LANES, LANES), :].T
                group = groups_of(cells, m, k * FRINGE + b * LANES)
                scale = 1.0
                if weights is not None:
                    ref, row, column = weights[k]
                    scale = ref[row + m : row + m + 1, aligned(column + b * LANES, LANES)]
                    scale = jnp.broadcast_to(scale, (8, LANES))
                for g in range(GROUPS):
                    factor = jnp.where(group == g, scale, 0.0)
                    for h in range(2):
                        at = g * PROBES + h * 8
                        total[h] = total[h] + field[at : at + 8, :] * factor
            ref, row, column = out[k]
            for h in range(2):
                ref[row + h * 8 : row + h * 8 + 8, aligned(column + b * LANES, LANES)] = total[h]

        each_block(many, step)


def spread_fields(messages, cells, partners, weights, staged):
    many = cells.shape[0]
    for n, k in enumerate(partners):

        def step(b):
            ref, row, column = messages[k]
            field = [ref[row + h * 8 : row + h * 8 + 8, aligned(column + b * LANES, LANES)] for h in range(2)]
            for m in range(many):
                group = groups_of(cells, m, k * FRINGE + b * LANES)
                scaled = field
                if weights is not None:
                    ref, row, column = weights[k]
                    scale = ref[row + m : row + m + 1, aligned(column + b * LANES, LANES)]
                    scaled = [part * jnp.broadcast_to(scale, (8, LANES)) for part in field]
                terms = [jnp.where(group == g, scaled[h], 0.0) for g in range(GROUPS) for h in range(2)]
                at = aligned((m * len(partners) + n) * FRINGE + b * LANES, LANES)
                staged[at, :] = jnp.concatenate(terms, axis=0).T

        each_block(many, step)


def lanes(shape):
    return lax.broadcasted_iota(i32, shape, len(shape) - 1)


def fill_ends(padded, low, high):
    lane = lanes((1, LANES))
    before = pltpu.roll(padded[ROWS : ROWS + 8, :], PROBES, 1)[7:8, :]
    after = pltpu.roll(padded[8:16, :], LANES - PROBES, 1)[0:1, :]
    padded[7:8, :] = jnp.where(lane < PROBES, low, before)
    padded[ROWS + 8 : ROWS + 9, :] = jnp.where(lane >= LANES - PROBES, high, after)


def each_row_block(step):
    def outer(j, carry):
        for u in range(4):
            step(j * 32 + u * 8)
        return carry

    lax.fori_loop(0, ROWS // 32, outer, 0)


def table_kernel(probes, table, natural, sem):
    copies = [
        pltpu.make_async_copy(probes.at[p], natural.at[pl.ds(p, 1), :], sem.at[p]) for p in range(PROBES)
    ]
    for copy in copies:
        copy.start()
    finish(copies)

    def step(j, carry):
        for n in range(4):
            tile = j * 4 + n
            parts = [natural[:, aligned(g * ROWS + tile * LANES, LANES)] for g in range(GROUPS)]
            table[aligned(tile * LANES, LANES), :] = jnp.concatenate(parts, axis=0).T
        return carry

    lax.fori_loop(0, TILES // 4, step, 0)


def table_of(probes):
    return pl.pallas_call(
        table_kernel,
        out_shape=resident(ROWS, LANES),
        in_specs=[FIXED],
        out_specs=VMEM,
        scratch_shapes=[pltpu.VMEM((PROBES, GROUPS * ROWS), f32), pltpu.SemaphoreType.DMA((PROBES,))],
        compiler_params=params(8),
        cost_estimate=cost(3),
        name="table",
    )(probes)


BEFORE, SAME, AFTER = (0, 3), (1, 4), (2, 5)
SIDES = BEFORE + AFTER
NEAR, FAR = (0, 1, 2), (3, 4, 5)
EDGE = slice(FRINGE, FRINGE + LANES)


def weight_places(before, same, after):
    return {
        0: (before, 0, 0),
        3: (before, 4, 0),
        1: (same[0], 0, FRINGE),
        4: (same[1], 0, 4 * FRINGE),
        2: (after, 0, 0),
        5: (after, 4, 0),
    }


def pair_places(pair, ref):
    return {pair[0]: (ref, 0, 0), pair[1]: (ref, PROBES, 0)}


def grid_places(near, far):
    places = {k: (near, n * PROBES, 0) for n, k in enumerate(NEAR)}
    places.update({k: (far, n * PROBES, 0) for n, k in enumerate(FAR)})
    return places


def simple_call(kernel, out_shape, operands, name):
    return pl.pallas_call(
        kernel,
        out_shape=out_shape,
        in_specs=[VMEM] * len(operands),
        out_specs=[VMEM] * len(out_shape),
        compiler_params=params(8),
        cost_estimate=cost(1),
        name=name,
    )(*operands)


def weight_relay_kernel(near, far, table, up, down):
    for pair, out, rows in ((BEFORE, up, slice(ROWS - 8, ROWS)), (AFTER, down, slice(0, 8))):
        for n, ref in enumerate((near, far)):
            start = pair[n] * FRINGE
            out[n * 4 : n * 4 + 4, 0:FRINGE] = ref[:, start : start + FRINGE]
        out[:, EDGE] = table[rows, :]


def weight_relay(near, far, table):
    shape = jax.ShapeDtypeStruct((8, FRINGE + LANES), f32)
    return simple_call(weight_relay_kernel, [shape] * 2, (near, far, table), "weight_relay")


def rows_kernel(table, rows_hbm, staged, *rest):
    parts, sem = rest[:WAYS], rest[WAYS]
    gather_rows(table, parts, staged, index_copies(rows_hbm, segments(4, SIDES), parts, sem))


def rows_at_sides(table, rows):
    segs = segments(4, SIDES)
    return pl.pallas_call(
        rows_kernel,
        out_shape=resident(len(segs) * FRINGE, LANES),
        in_specs=[VMEM, HBM],
        out_specs=VMEM,
        scratch_shapes=index_scratch(segs),
        compiler_params=params(8),
        cost_estimate=cost(11),
        name="rows_at_sides",
    )(table, rows)


PAIR = jax.ShapeDtypeStruct((2 * PROBES, FRINGE), f32)
TRIPLE = jax.ShapeDtypeStruct((3 * PROBES, FRINGE), f32)


def side_sums_kernel(staged, cells, before, after, up, down):
    places = {**pair_places(AFTER, up), **pair_places(BEFORE, down)}
    select_fields(staged, cells, SIDES, weight_places(before, (None, None), after), places)


def side_sums(staged, cells, before, after):
    return simple_call(side_sums_kernel, [PAIR] * 2, (staged, cells, before, after), "side_sums")


def same_sums_kernel(table, cells, rows_hbm, near, far, out, staged, *rest):
    parts, sem = rest[:WAYS], rest[WAYS]
    gather_rows(table, parts, staged, index_copies(rows_hbm, segments(4, SAME), parts, sem))
    select_fields(staged, cells, SAME, weight_places(None, (near, far), None), pair_places(SAME, out))


def same_sums(table, cells, rows, near, far):
    segs = segments(4, SAME)
    return pl.pallas_call(
        same_sums_kernel,
        out_shape=PAIR,
        in_specs=[VMEM, VMEM, HBM, VMEM, VMEM],
        out_specs=VMEM,
        scratch_shapes=[pltpu.VMEM((len(segs) * FRINGE, LANES), f32)] + index_scratch(segs),
        compiler_params=params(8),
        cost_estimate=cost(8),
        name="same_sums",
    )(table, cells, rows, near, far)


def message_relay_kernel(before, same, after, near, far):
    for n, out in enumerate((near, far)):
        for i, ref in enumerate((before, same, after)):
            out[i * PROBES : (i + 1) * PROBES, :] = ref[n * PROBES : (n + 1) * PROBES, :]


def message_relay(before, same, after):
    return simple_call(message_relay_kernel, [TRIPLE] * 2, (before, same, after), "message_relay")


def end_flags():
    column = lax.axis_index("cell")
    return (column > 0).astype(f32), (column < lax.axis_size("cell") - 1).astype(f32)


def outer_rows(before, after):
    has_low, has_high = end_flags()
    low = pltpu.roll(before[0:8, EDGE], PROBES, 1)[7:8, :] * has_low
    high = pltpu.roll(after[0:8, EDGE], LANES - PROBES, 1)[0:1, :] * has_high
    return low, high


def forward_kernel(table, centre, lower, upper, before, after, c_out, l_out, u_out, *rest):
    sums, padded = rest[:WAYS], rest[WAYS]

    def step(j, carry):
        for n in range(2):
            tile = j * 2 + n
            at = aligned(tile * LANES, LANES)
            padded[rows_of(tile * LANES + 8, LANES), :] = table[at, :]
            for ref, out in ((centre, c_out), (lower, l_out), (upper, u_out)):
                parts = [
                    jnp.broadcast_to(ref[:, aligned(g * ROWS + tile * LANES, LANES)], (PROBES, LANES))
                    for g in range(GROUPS)
                ]
                out[at, :] = jnp.concatenate(parts, axis=0).T
        return carry

    lax.fori_loop(0, TILES // 2, step, 0)
    fill_ends(padded, *outer_rows(before, after))

    def stencil(start):
        at = rows_of(start, 8)
        sums[0][at, :] = (
            c_out[at, :] * padded[rows_of(start + 8, 8), :]
            - l_out[at, :] * padded[pl.ds(start + 7, 8), :]
            - u_out[at, :] * padded[pl.ds(start + 9, 8), :]
        )

    each_row_block(stencil)
    clear(sums[1:])


def forward(table, centre, lower, upper, before, after):
    return pl.pallas_call(
        forward_kernel,
        out_shape=[resident(ROWS, LANES)] * (3 + WAYS),
        in_specs=[VMEM] * 6,
        out_specs=[VMEM] * (3 + WAYS),
        scratch_shapes=[pltpu.VMEM((ROWS + 16, LANES), f32)],
        compiler_params=params(8),
        cost_estimate=cost(7),
        name="forward",
    )(table, centre, lower, upper, before, after)


def couple_kernel(cells, rows_hbm, near, far, *refs):
    refs = refs[WAYS:]
    tangent, out, sums = refs[0], refs[1], refs[2 : 2 + WAYS]
    staged, staged_far = refs[2 + WAYS : 4 + WAYS]
    refs = refs[4 + WAYS :]
    parts, sem, parts_far, sem_far = refs[:WAYS], refs[WAYS], refs[WAYS + 1 : 2 * WAYS + 1], refs[2 * WAYS + 1]
    every = NEAR + FAR
    phases = index_copies(rows_hbm, segments(1, every), parts, sem)
    phases_far = index_copies(rows_hbm, segments(1, FAR), parts_far, sem_far)
    spread_fields(grid_places(near, far), cells, every, None, staged)
    finish(phases[0] + phases[1])
    add_rows(sums, parts, staged)

    def total(start):
        at = rows_of(start, 8)
        value = sums[0][at, :]
        for part in sums[1:]:
            value = value + part[at, :]
        tangent[at, :] = value

    each_row_block(total)
    gather_rows(tangent, parts_far, staged_far, phases_far)
    select_fields(staged_far, cells, FAR, None, grid_places(None, out))


def couple(cells, rows, near, far, sums):
    every, some = segments(1, NEAR + FAR), segments(1, FAR)
    outs = pl.pallas_call(
        couple_kernel,
        out_shape=[resident(ROWS, LANES), TRIPLE] + [resident(ROWS, LANES)] * WAYS,
        in_specs=[VMEM, HBM] + [VMEM] * (2 + WAYS),
        out_specs=[VMEM] * (2 + WAYS),
        scratch_shapes=[pltpu.VMEM((SLOTS, LANES), f32), pltpu.VMEM((SLOTS // 2, LANES), f32)]
        + index_scratch(every)
        + index_scratch(some),
        input_output_aliases={4 + w: 2 + w for w in range(WAYS)},
        compiler_params=params(8),
        cost_estimate=cost(11),
        name="couple",
    )(cells, rows, near, far, *sums)
    return outs[0], outs[1]


def receptor_kernel(tangent, cells, rows_hbm, out, staged, *rest):
    parts, sem = rest[:WAYS], rest[WAYS]
    gather_rows(tangent, parts, staged, index_copies(rows_hbm, segments(1, NEAR), parts, sem))
    select_fields(staged, cells, NEAR, None, grid_places(out, None))


def at_receptors(tangent, cells, rows):
    segs = segments(1, NEAR)
    return pl.pallas_call(
        receptor_kernel,
        out_shape=TRIPLE,
        in_specs=[VMEM, VMEM, HBM],
        out_specs=VMEM,
        scratch_shapes=[pltpu.VMEM((len(segs) * FRINGE, LANES), f32)] + index_scratch(segs),
        compiler_params=params(8),
        cost_estimate=cost(3),
        name="at_receptors",
    )(tangent, cells, rows)


def return_relay_kernel(near, far, tangent, lower, upper, up, down):
    for n, ref in enumerate((near, far)):
        at = slice(n * PROBES, (n + 1) * PROBES)
        up[at, 0:FRINGE] = ref[0:PROBES, :]
        down[at, 0:FRINGE] = ref[2 * PROBES : 3 * PROBES, :]
    end = slice(ROWS - 8, ROWS)
    up[0:8, EDGE] = upper[end, :] * tangent[end, :]
    down[0:8, EDGE] = lower[0:8, :] * tangent[0:8, :]


def return_relay(near, far, tangent, lower, upper):
    shape = jax.ShapeDtypeStruct((2 * PROBES, FRINGE + LANES), f32)
    return simple_call(return_relay_kernel, [shape] * 2, (near, far, tangent, lower, upper), "return_relay")


def transposed_kernel(tangent, centre, lower, upper, *rest):
    sums, raised, lowered = rest[:WAYS], rest[WAYS], rest[WAYS + 1]

    def products(start):
        at = rows_of(start, 8)
        value = tangent[at, :]
        raised[rows_of(start + 8, 8), :] = upper[at, :] * value
        lowered[rows_of(start + 8, 8), :] = lower[at, :] * value

    each_row_block(products)
    nothing = jnp.zeros((1, LANES), f32)
    fill_ends(raised, nothing, nothing)
    fill_ends(lowered, nothing, nothing)

    def stencil(start):
        at = rows_of(start, 8)
        sums[0][at, :] = (
            centre[at, :] * tangent[at, :] - raised[pl.ds(start + 7, 8), :] - lowered[pl.ds(start + 9, 8), :]
        )

    each_row_block(stencil)
    clear(sums[1:])


def transposed(tangent, centre, lower, upper):
    return pl.pallas_call(
        transposed_kernel,
        out_shape=[resident(ROWS, LANES)] * WAYS,
        in_specs=[VMEM] * 4,
        out_specs=[VMEM] * WAYS,
        scratch_shapes=[pltpu.VMEM((ROWS + 16, LANES), f32)] * 2,
        compiler_params=params(8),
        cost_estimate=cost(4),
        name="transposed",
    )(tangent, centre, lower, upper)


def donor_same_kernel(cells, rows_hbm, near_weights, far_weights, near, far, *refs):
    refs = refs[WAYS:]
    sums, staged, parts, sem = refs[:WAYS], refs[WAYS], refs[WAYS + 1 : 2 * WAYS + 1], refs[2 * WAYS + 1]
    phases = index_copies(rows_hbm, segments(4, SAME), parts, sem)
    weights = weight_places(None, (near_weights, far_weights), None)
    spread_fields(grid_places(near, far), cells, SAME, weights, staged)
    finish(phases[0] + phases[1])
    add_rows(sums, parts, staged)


def add_same(cells, rows, near_weights, far_weights, near, far, sums):
    segs = segments(4, SAME)
    return pl.pallas_call(
        donor_same_kernel,
        out_shape=[resident(ROWS, LANES)] * WAYS,
        in_specs=[VMEM, HBM] + [VMEM] * (4 + WAYS),
        out_specs=[VMEM] * WAYS,
        scratch_shapes=[pltpu.VMEM((len(segs) * FRINGE, LANES), f32)] + index_scratch(segs),
        input_output_aliases={6 + w: w for w in range(WAYS)},
        compiler_params=params(8),
        cost_estimate=cost(9),
        name="add_same",
    )(cells, rows, near_weights, far_weights, near, far, *sums)


def donor_sides_kernel(cells, rows_hbm, before_weights, after_weights, before, after, *refs):
    refs = refs[WAYS:]
    adjoint, gram, sums, staged = refs[0], refs[1], refs[2 : 2 + WAYS], refs[2 + WAYS]
    parts, sem = refs[3 + WAYS : 3 + 2 * WAYS], refs[3 + 2 * WAYS]
    phases = index_copies(rows_hbm, segments(4, SIDES), parts, sem)
    weights = weight_places(before_weights, (None, None), after_weights)
    spread_fields({**pair_places(BEFORE, before), **pair_places(AFTER, after)}, cells, SIDES, weights, staged)
    finish(phases[0] + phases[1])
    add_rows(sums, parts, staged)
    lane = lanes((1, LANES))
    low, high = outer_rows(before, after)
    sums[0][0:1, :] = sums[0][0:1, :] - jnp.where(lane < PROBES, low, 0.0)
    end = sums[0][ROWS - 1 : ROWS, :]
    sums[0][ROWS - 1 : ROWS, :] = end - jnp.where(lane >= LANES - PROBES, high, 0.0)

    def total(start):
        at = rows_of(start, 8)
        value = sums[0][at, :]
        for part in sums[1:]:
            value = value + part[at, :]
        adjoint[at, :] = value

    each_row_block(total)

    def multiply(j, product):
        left_side, right_side = [], []
        for n in range(4):
            block = adjoint[aligned((j * 4 + n) * LANES, LANES), :]
            high, low = split(block)
            high_t, low_t = split(block.T)
            left_side += [high_t, high_t, low_t]
            right_side += [high, low, high]
        left_side = jnp.concatenate(left_side, axis=1)
        right_side = jnp.concatenate(right_side, axis=0)
        return product + jnp.dot(left_side, right_side, preferred_element_type=f32)

    product = lax.fori_loop(0, TILES // 4, multiply, jnp.zeros((LANES, LANES), f32))
    group = lanes((PROBES, LANES)) // PROBES
    folded = jnp.zeros((PROBES, LANES), f32)
    for g in range(GROUPS):
        folded = folded + jnp.where(group == g, product[g * PROBES : (g + 1) * PROBES, :], 0.0)
    for shift in (64, 32, 16):
        folded = folded + pltpu.roll(folded, shift, 1)
    gram[...] = folded[:, :PROBES]


def add_sides(cells, rows, before_weights, after_weights, before, after, sums):
    segs = segments(4, SIDES)
    outs = pl.pallas_call(
        donor_sides_kernel,
        out_shape=[resident(ROWS, LANES), jax.ShapeDtypeStruct((PROBES, PROBES), f32)]
        + [resident(ROWS, LANES)] * WAYS,
        in_specs=[VMEM, HBM] + [VMEM] * (4 + WAYS),
        out_specs=[VMEM] * (2 + WAYS),
        scratch_shapes=[pltpu.VMEM((len(segs) * FRINGE, LANES), f32)] + index_scratch(segs),
        input_output_aliases={6 + w: 2 + w for w in range(WAYS)},
        compiler_params=params(12),
        cost_estimate=cost(18),
        name="add_sides",
    )(cells, rows, before_weights, after_weights, before, after, *sums)
    return outs[0], outs[1]


def basis_kernel(total_cells, gram, adjoint, basis, factor, natural, sem):
    row = lax.broadcasted_iota(i32, (PROBES, 1), 0)
    left = gram[...] / f32(total_cells)
    right = jnp.where(lax.broadcasted_iota(i32, (PROBES, LANES), 0) == lanes((PROBES, LANES)) % PROBES, 1.0, 0.0)
    for j in range(PROBES):
        pivot = left[j : j + 1, j : j + 1]
        ratio = jnp.where(row > j, left[:, j : j + 1] / pivot, 0.0)
        root = jnp.sqrt(pivot)
        left_row, right_row = left[j : j + 1, :], right[j : j + 1, :]
        left = jnp.where(row == j, left_row / root, left - ratio * left_row)
        right = jnp.where(row == j, right_row / root, right - ratio * right_row)
    down = lax.broadcasted_iota(i32, (PROBES, PROBES), 0)
    factor[...] = jnp.where(lanes((PROBES, PROBES)) >= down, left, 0.0).T
    inverse = jnp.concatenate([right] * GROUPS, axis=0)
    same = lax.broadcasted_iota(i32, (LANES, LANES), 0) // PROBES == lanes((LANES, LANES)) // PROBES
    high, low = split(jnp.where(same, inverse, 0.0))
    left_side = jnp.concatenate([high, high, low], axis=1)

    def step(j, carry):
        for n in range(4):
            tile = j * 4 + n
            high, low = split(adjoint[aligned(tile * LANES, LANES), :])
            right_side = jnp.concatenate([high, low, high], axis=1)
            block = lax.dot_general(left_side, right_side, (((1,), (1,)), ((), ())), preferred_element_type=f32)
            for g in range(GROUPS):
                natural[:, aligned(g * ROWS + tile * LANES, LANES)] = block[g * PROBES : (g + 1) * PROBES, :]
        return carry

    lax.fori_loop(0, TILES // 4, step, 0)
    copies = [
        pltpu.make_async_copy(natural.at[pl.ds(p, 1), :], basis.at[p], sem.at[p]) for p in range(PROBES)
    ]
    for copy in copies:
        copy.start()
    finish(copies)


def basis_of(total_cells, gram, adjoint):
    return pl.pallas_call(
        functools.partial(basis_kernel, total_cells),
        out_shape=[
            jax.ShapeDtypeStruct((PROBES, 1, GROUPS * ROWS), f32),
            jax.ShapeDtypeStruct((PROBES, PROBES), f32),
        ],
        in_specs=[VMEM] * 2,
        out_specs=[FIXED, VMEM],
        scratch_shapes=[pltpu.VMEM((PROBES, GROUPS * ROWS), f32), pltpu.SemaphoreType.DMA((PROBES,))],
        compiler_params=params(8),
        cost_estimate=cost(6),
        name="basis",
    )(gram, adjoint)


def moved(value, place):
    grids, columns = (lax.axis_size(axis) for axis in AXES)
    route = []
    for g in range(grids):
        for c in range(columns):
            to_g, to_c = place(g, c)
            route.append((g * columns + c, (to_g % grids) * columns + to_c % columns))
    return lax.ppermute(value, AXES, route)


def along_grid(value, distance):
    return moved(value, lambda g, c: (g + distance, c))


def along_cell(value, distance):
    return moved(value, lambda g, c: (g, c + distance))


def summed(value):
    value = value + moved(value, lambda g, c: (g ^ 1, c))
    value = value + moved(value, lambda g, c: (g ^ 2, c))
    value = value + moved(value, lambda g, c: ((6 - (g & 6)) | (g & 1), c))
    value = value + moved(value, lambda g, c: (g, c ^ 1))
    value = value + moved(value, lambda g, c: (g, (c & 12) | (3 - (c & 3))))
    value = value + moved(value, lambda g, c: (g, c ^ 4))
    value = value + moved(value, lambda g, c: (g, (12 - (c & 12)) | (c & 3)))
    return value


def body(probes, centre, lower_coef, upper_coef, donor_cells, receptor_cells, weights):
    donors = donor_cells[0]
    donor_rows = (donors & (ROWS - 1)).reshape(-1)
    receptor_rows = (receptor_cells & (ROWS - 1)).reshape(-1)
    near_weights, far_weights = along_grid(weights, -1)[0], along_grid(weights, -2)[0]
    table = table_of(probes)
    up, down = weight_relay(near_weights, far_weights, table)
    before_weights, after_weights = along_cell(up, 1), along_cell(down, -1)
    staged = rows_at_sides(table, donor_rows)
    up, down = side_sums(staged, donors, before_weights, after_weights)
    after, before = along_cell(up, 1), along_cell(down, -1)
    same = same_sums(table, donors, donor_rows, near_weights, far_weights)
    near, far = message_relay(before, same, after)
    near, far = along_grid(near, 1), along_grid(far, 2)
    c, l, u, *sums = forward(table, centre, lower_coef, upper_coef, before_weights, after_weights)
    tangent, far = couple(receptor_cells, receptor_rows, near, far, sums)
    far = along_grid(far, -2)
    near = along_grid(at_receptors(tangent, receptor_cells, receptor_rows), -1)
    sums = transposed(tangent, c, l, u)
    up, down = return_relay(near, far, tangent, l, u)
    before, after = along_cell(up, 1), along_cell(down, -1)
    sums = add_same(donors, donor_rows, near_weights, far_weights, near, far, sums)
    adjoint, gram = add_sides(donors, donor_rows, before_weights, after_weights, before, after, sums)
    total_cells = lax.axis_size("grid") * lax.axis_size("cell") * probes.shape[2]
    basis, factor = basis_of(total_cells, summed(gram), adjoint)
    return (basis, factor)


def solution(mesh):
    in_specs = (
        P(None, "grid", "cell"),
        P("grid", "cell"),
        P("grid", "cell"),
        P("grid", "cell"),
        P("grid", None, "cell"),
        P("grid", "cell"),
        P("grid", None, "cell"),
    )
    out_specs = (P(None, "grid", "cell"), P())
    return jax.shard_map(body, mesh=mesh, in_specs=in_specs, out_specs=out_specs, check_vma=False)
```

time: 188 us -> 149 us (0.79)
  starting transfers between devices: 56 us -> 22.2 us
  Pallas kernels: 105 us -> 88.1 us
  waiting for transfers between devices: 21.9 us -> 35.6 us
    ppermute x29 -> x19, starting transfers between devices: 56 us -> 22.2 us  [moved(): return lax.ppermute(value, AXES, route)]
    pallas_call x9 -> x11, Pallas kernels: 87.9 us -> 73.4 us  [the longest x1 22.9 us: add_sides(): pl.pallas_call(donor_sides_kernel, out_shape=[resident(ROWS, LANES), jax....]
    ppermute x29 -> x19, waiting for transfers between devices: 21.9 us -> 35.6 us  [moved(): return lax.ppermute(value, AXES, route)]
  transfers between devices with their start and end apart: 29 -> 19, of which waited for: 8 -> 12; matrix products, arithmetic and copies ran while one was open for 1% -> 0% of each run, Pallas kernels for 32% -> 27%
where the time goes in v3:
time: 149 us
  Pallas kernels  88.1 us (59%)
  waiting for transfers between devices  35.6 us (24%)
  starting transfers between devices  22.2 us (15%)
  local copies, waits for them, and re-layouts  1.63 us (1%)
    ppermute x19, waiting for transfers between devices, moved(): return lax.ppermute(value, AXES, route)  35.6 us
    pallas_call x1, Pallas kernels, add_sides(): pl.pallas_call(donor_sides_kernel, out_shape=[resident(ROWS, LANES), jax....  22.9 us
    ppermute x19, starting transfers between devices, moved(): return lax.ppermute(value, AXES, route)  22.2 us
    pallas_call x1, Pallas kernels, couple(): pl.pallas_call(couple_kernel, out_shape=[resident(ROWS, LANES), TRIPLE] +...  12.1 us
    pallas_call x1, Pallas kernels, rows_at_sides(): pl.pallas_call(rows_kernel, out_shape=resident(len(segs) * FRINGE, LANES)...  11.8 us
    pallas_call x1, Pallas kernels, add_same(): pl.pallas_call(donor_same_kernel, out_shape=[resident(ROWS, LANES)] * WAY...  9.16 us
    pallas_call x1, Pallas kernels, same_sums(): pl.pallas_call(same_sums_kernel, out_shape=PAIR, in_specs=[VMEM, VMEM, HB...  7.9 us
    pallas_call x1, Pallas kernels, basis_of(): pl.pallas_call(functools.partial(basis_kernel, total_cells), out_shape=[j...  5.93 us
  transfers between devices with their start and end apart: 19, of which 12 were waited for; matrix products, arithmetic and copies ran while one was open for 0% of the time, Pallas kernels for 27%

profile of v3, /device:TPU:0, one launch (start us, length us, event | category | flops | bytes accessed | tf_op | source)
XLA Modules:
  0.0 148.5 jit_solution(16347819962289923866)
XLA Ops:
  0.6 2.9 %collective-permute-start.1 = (f32[1,4,6144]{2,1,0:T(4,128)}, f32[1,4,6144]{2,1,0:T(4,128)S(1)}, u32[]{:S(2)}, u32[]{:S(2)}) collective-permute-start(f32[1,4,6144]{2,1,0:T(4,128)} %param.13), channel_id=1, source_target_pairs={{0,96},{1,97},{2,98},{3,99},{4,100},{5,101},{6,102},{7,103},{8,104... | collective-permute-start | bytes 294920 | tf_op jit(solution)/shard_map/ppermute | solution.py:682
  3.6 0.0 collective-permute-start
  3.6 1.6 %copy-done.1 = f32[16,1,32768]{2,1,0:T(1,128)S(1)} copy-done((f32[16,1,32768]{2,1,0:T(1,128)S(1)}, f32[16,1,32768]{2,1,0:T(1,128)}, u32[]{:S(2)}) %copy-start.1) | copy-done | bytes 2097176
  5.2 2.7 %table.1 = f32[4096,128]{1,0:T(8,128)S(1)} custom-call(f32[16,1,32768]{2,1,0:T(1,128)S(1)} %copy-done.1), custom_call_target="tpu_custom_call" | custom-call | bytes 9000000 | tf_op jit(solution)/shard_map/table/pallas_call | solution.py:237
  7.9 0.0 copy-start
  7.9 1.6 %collective-permute-start.2 = (f32[8,1152]{1,0:T(8,128)S(1)}, f32[8,1152]{1,0:T(8,128)S(1)}, u32[]{:S(2)}, u32[]{:S(2)}) collective-permute-start(f32[8,1152]{1,0:T(8,128)S(1)} %get-tuple-element.41), channel_id=1, source_target_pairs={{0,1},{1,2},{2,3},{3,4},{4,5},{5,6},{6,7},{7,8},{8,9},{9,10},{10,1... | collective-permute-start | bytes 110600 | tf_op jit(solution)/shard_map/ppermute | solution.py:682
  9.6 5.0 %collective-permute-start.3 = (f32[8,1152]{1,0:T(8,128)S(1)}, f32[8,1152]{1,0:T(8,128)S(1)}, u32[]{:S(2)}, u32[]{:S(2)}) collective-permute-start(f32[8,1152]{1,0:T(8,128)S(1)} %get-tuple-element.42), channel_id=1, source_target_pairs={{0,15},{1,0},{2,1},{3,2},{4,3},{5,4},{6,5},{7,6},{8,7},{9,8},{10,9... | collective-permute-start | bytes 110600 | tf_op jit(solution)/shard_map/ppermute | solution.py:682
  14.6 11.8 %rows_at_sides.1.staged = f32[16384,128]{1,0:T(8,128)S(1)} custom-call(f32[4096,128]{1,0:T(8,128)S(1)} %table.1, s32[24576]{0:T(1024)S(1)} %bitcast.11), custom_call_target="tpu_custom_call" | custom-call | bytes 33000000 | tf_op jit(solution)/shard_map/rows_at_sides/pallas_call | solution.py:308
  26.4 0.0 collective-permute-done.2.before.before_weights
  26.5 3.4 %side_sums.1 = (f32[32,1024]{1,0:T(8,128)S(1)}, f32[32,1024]{1,0:T(8,128)S(1)}) custom-call(f32[16384,128]{1,0:T(8,128)S(1)} %rows_at_sides.1.staged, s32[4,6144]{1,0:T(4,128)S(1)} %bitcast.7, f32[8,1152]{1,0:T(8,128)S(1)} %collective-permute-done.2.before.before_weights, f32[8,1152]{1,0:T(8,128)S(1)} %collective-permute-done.3.after.after_weights), custom_call_target="tpu_custom_call" | custom-call | bytes 3000000 | tf_op jit(solution)/shard_map/side_sums/pallas_call | solution.py:277
  29.9 0.0 copy-start.2
  29.9 0.0 copy-start.3
  29.9 0.0 copy-start.4
  29.9 0.0 copy-start.5
  29.9 2.0 %collective-permute-start.4 = (f32[32,1024]{1,0:T(8,128)S(1)}, f32[32,1024]{1,0:T(8,128)S(1)}, u32[]{:S(2)}, u32[]{:S(2)}) collective-permute-start(f32[32,1024]{1,0:T(8,128)S(1)} %get-tuple-element.43), channel_id=1, source_target_pairs={{0,15},{1,0},{2,1},{3,2},{4,3},{5,4},{6,5},{7,6},{8,7},{9,8},{10,9... | collective-permute-start | bytes 393224 | tf_op jit(solution)/shard_map/ppermute | solution.py:682
  31.9 0.1 collective-permute-start.5
  32.0 7.9 %same_sums.1.same = f32[32,1024]{1,0:T(8,128)S(1)} custom-call(f32[4096,128]{1,0:T(8,128)S(1)} %table.1, s32[4,6144]{1,0:T(4,128)S(1)} %bitcast.8, s32[24576]{0:T(1024)S(1)} %bitcast.12, f32[4,6144]{1,0:T(4,128)S(1)} %bitcast.19, f32[4,6144]{1,0:T(4,128)S(1)} %bitcast.16), custom_call_target="tpu_custom_call" | custom-call | bytes 24000000 | tf_op jit(solution)/shard_map/same_sums/pallas_call | solution.py:341
  39.9 0.0 collective-permute-done.4.before
  39.9 0.4 collective-permute-done.5.after
  40.4 0.0 collective-permute-start.6
  40.4 1.1 collective-permute-start.7
  41.6 5.7 %forward.1 = (f32[4096,128]{1,0:T(8,128)S(1)}, f32[4096,128]{1,0:T(8,128)S(1)}, f32[4096,128]{1,0:T(8,128)S(1)}, f32[4096,128]{1,0:T(8,128)S(1)}, f32[4096,128]{...) custom-call(f32[4096,128]{1,0:T(8,128)S(1)} %table.1, ...), custom_call_target="tpu_custom_call" | custom-call | bytes 21000000 | tf_op jit(solution)/shard_map/forward/pallas_call | solution.py:407
  47.3 0.9 collective-permute-done.6.near
  48.2 1.2 collective-permute-done.7.far
  49.4 12.1 %couple.1 = (f32[4096,128]{1,0:T(8,128)S(1)}, f32[48,1024]{1,0:T(8,128)S(1)}, f32[4096,128]{1,0:T(8,128)S(1)}, f32[4096,128]{1,0:T(8,128)S(1)}, f32[4096,128]{1,...) custom-call(s32[1,6144]{1,0:T(1,128)S(1)} %copy-done.2, ...), custom_call_target="tpu_custom_call", output_to_operand_aliasing={{2}: (4, {}), {3}: (5, {}), {4}: (6, {}), {5}: (7, {}), {6}... | custom-call | bytes 33000000 | tf_op jit(solution)/shard_map/couple/pallas_call | solution.py:446
  61.5 3.3 %at_receptors.1 = f32[48,1024]{1,0:T(8,128)S(1)} custom-call(f32[4096,128]{1,0:T(8,128)S(1)} %get-tuple-element.55.tangent, s32[1,6144]{1,0:T(1,128)S(1)} %copy-done.2, s32[6144]{0:T(1024)S(1)} %bitcast.22), custom_call_target="tpu_custom_call" | custom-call | bytes 9000000 | tf_op jit(solution)/shard_map/at_receptors/pallas_call | solution.py:470
  64.8 1.8 %collective-permute-start.8 = (f32[48,1024]{1,0:T(8,128)S(1)}, f32[48,1024]{1,0:T(8,128)S(1)}, u32[]{:S(2)}, u32[]{:S(2)}) collective-permute-start(f32[48,1024]{1,0:T(8,128)S(1)} %at_receptors.1), channel_id=1, source_target_pairs={{0,112},{1,113},{2,114},{3,115},{4,116},{5,117},{6,118},{7,119},{8... | collective-permute-start | bytes 589832 | tf_op jit(solution)/shard_map/ppermute | solution.py:682
  66.6 0.0 collective-permute-start.9
  66.6 4.8 %collective-permute-done.8.near = f32[48,1024]{1,0:T(8,128)S(1)} collective-permute-done((f32[48,1024]{1,0:T(8,128)S(1)}, f32[48,1024]{1,0:T(8,128)S(1)}, u32[]{:S(2)}, u32[]{:S(2)}) %collective-permute-start.8) | collective-permute-done | bytes 196640 | tf_op jit(solution)/shard_map/ppermute | solution.py:682
  71.4 3.7 %collective-permute-done.9.far = f32[48,1024]{1,0:T(8,128)S(1)} collective-permute-done((f32[48,1024]{1,0:T(8,128)S(1)}, f32[48,1024]{1,0:T(8,128)S(1)}, u32[]{:S(2)}, u32[]{:S(2)}) %collective-permute-start.9) | collective-permute-done | bytes 196640 | tf_op jit(solution)/shard_map/ppermute | solution.py:682
  75.2 0.1 collective-permute-start.10
  75.3 5.3 %collective-permute-start.11 = (f32[32,1152]{1,0:T(8,128)S(1)}, f32[32,1152]{1,0:T(8,128)S(1)}, u32[]{:S(2)}, u32[]{:S(2)}) collective-permute-start(f32[32,1152]{1,0:T(8,128)S(1)} %get-tuple-element.60), channel_id=1, source_target_pairs={{0,15},{1,0},{2,1},{3,2},{4,3},{5,4},{6,5},{7,6},{8,7},{9,8},{10,9... | collective-permute-start | bytes 442376 | tf_op jit(solution)/shard_map/ppermute | solution.py:682
  80.6 3.1 %transposed.1 = (f32[4096,128]{1,0:T(8,128)S(1)}, f32[4096,128]{1,0:T(8,128)S(1)}, f32[4096,128]{1,0:T(8,128)S(1)}, f32[4096,128]{1,0:T(8,128)S(1)}, f32[4096,12...) custom-call(f32[4096,128]{1,0:T(8,128)S(1)} %get-tuple-element.55.tangent, ...), custom_call_target="tpu_custom_call" | custom-call | bytes 12000000 | tf_op jit(solution)/shard_map/transposed/pallas_call | solution.py:522
  83.7 9.2 %add_same.1 = (f32[4096,128]{1,0:T(8,128)S(1)}, f32[4096,128]{1,0:T(8,128)S(1)}, f32[4096,128]{1,0:T(8,128)S(1)}, f32[4096,128]{1,0:T(8,128)S(1)}, f32[4096,128]...) custom-call(s32[4,6144]{1,0:T(4,128)S(1)} %bitcast.9, ...), custom_call_target="tpu_custom_call", output_to_operand_aliasing={{0}: (6, {}), {1}: (7, {}), {2}: (8, {}), {3}: (9, {}), {4}... | custom-call | bytes 27000000 | tf_op jit(solution)/shard_map/add_same/pallas_call | solution.py:546
  92.9 22.9 %add_sides.1 = (f32[4096,128]{1,0:T(8,128)S(1)}, f32[16,16]{1,0:T(8,128)S(1)}, f32[4096,128]{1,0:T(8,128)S(1)}, f32[4096,128]{1,0:T(8,128)S(1)}, f32[4096,128]{1...) custom-call(s32[4,6144]{1,0:T(4,128)S(1)} %bitcast.10, ...), custom_call_target="tpu_custom_call", output_to_operand_aliasing={{2}: (6, {}), {3}: (7, {}), {4}: (8, {}), {5}: (9, {}), {6}... | custom-call | bytes 54000000 | tf_op jit(solution)/shard_map/add_sides/pallas_call | solution.py:607
  115.8 0.1 collective-permute-start.12
  115.9 1.2 collective-permute-done.12
  117.0 0.0 collective-permute-start.13
  117.0 3.6 %collective-permute-done.13 = f32[16,16]{1,0:T(8,128)S(1)} collective-permute-done((f32[16,16]{1,0:T(8,128)S(1)}, f32[16,16]{1,0:T(8,128)S(1)}, u32[]{:S(2)}, u32[]{:S(2)}) %collective-permute-start.13) | collective-permute-done | bytes 1056 | tf_op jit(solution)/shard_map/ppermute | solution.py:682
  120.7 2.1 %collective-permute-start.14 = (f32[16,16]{1,0:T(8,128)S(1)}, f32[16,16]{1,0:T(8,128)S(1)}, u32[]{:S(2)}, u32[]{:S(2)}) collective-permute-start(f32[16,16]{1,0:T(8,128)S(1)} %add.22), channel_id=1, source_target_pairs={{0,96},{1,97},{2,98},{3,99},{4,100},{5,101},{6,102},{7,103},{8,104... | collective-permute-start | bytes 3080 | tf_op jit(solution)/shard_map/ppermute | solution.py:682
  122.8 2.8 %collective-permute-done.14 = f32[16,16]{1,0:T(8,128)S(1)} collective-permute-done((f32[16,16]{1,0:T(8,128)S(1)}, f32[16,16]{1,0:T(8,128)S(1)}, u32[]{:S(2)}, u32[]{:S(2)}) %collective-permute-start.14) | collective-permute-done | bytes 1056 | tf_op jit(solution)/shard_map/ppermute | solution.py:682
  125.6 0.0 collective-permute-start.15
  125.6 3.6 %collective-permute-done.15 = f32[16,16]{1,0:T(8,128)S(1)} collective-permute-done((f32[16,16]{1,0:T(8,128)S(1)}, f32[16,16]{1,0:T(8,128)S(1)}, u32[]{:S(2)}, u32[]{:S(2)}) %collective-permute-start.15) | collective-permute-done | bytes 1056 | tf_op jit(solution)/shard_map/ppermute | solution.py:682
  129.2 4.9 %collective-permute-done.16 = f32[16,16]{1,0:T(8,128)S(1)} collective-permute-done((f32[16,16]{1,0:T(8,128)S(1)}, f32[16,16]{1,0:T(8,128)S(1)}, u32[]{:S(2)}, u32[]{:S(2)}) %collective-permute-start.16) | collective-permute-done | bytes 1056 | tf_op jit(solution)/shard_map/ppermute | solution.py:682
  134.1 3.6 %collective-permute-done.17 = f32[16,16]{1,0:T(8,128)S(1)} collective-permute-done((f32[16,16]{1,0:T(8,128)S(1)}, f32[16,16]{1,0:T(8,128)S(1)}, u32[]{:S(2)}, u32[]{:S(2)}) %collective-permute-start.17) | collective-permute-done | bytes 1056 | tf_op jit(solution)/shard_map/ppermute | solution.py:682
  137.7 0.0 collective-permute-start.18
  137.8 4.8 %collective-permute-done.18 = f32[16,16]{1,0:T(8,128)S(1)} collective-permute-done((f32[16,16]{1,0:T(8,128)S(1)}, f32[16,16]{1,0:T(8,128)S(1)}, u32[]{:S(2)}, u32[]{:S(2)}) %collective-permute-start.18) | collective-permute-done | bytes 1056 | tf_op jit(solution)/shard_map/ppermute | solution.py:682
  142.6 5.9 %basis.1 = (f32[16,1,32768]{2,1,0:T(1,128)}, f32[16,16]{1,0:T(8,128)}) custom-call(f32[16,16]{1,0:T(8,128)S(1)} %add.27.gram, f32[4096,128]{1,0:T(8,128)S(1)} %get-tuple-element.79.adjoint), custom_call_target="tpu_custom_call" | custom-call | bytes 18000000 | tf_op jit(solution)/shard_map/basis/pallas_call | solution.py:660
  (26 shorter events, 0.2 us)
Async XLA Ops:
  0.6 7.2 %collective-permute-start.1 = (f32[1,4,6144]{2,1,0:T(4,128)}, f32[1,4,6144]{2,1,0:T(4,128)S(1)}, u32[]{:S(2)}, u32[]{:S(2)}) collective-permute-start(f32[1,4,6144]{2,1,0:T(4,128)} %param.13), channel_id=1, source_target_pairs={{0,96},{1,97},{2,98},{3,99},{4,100},{5,101},{6,102},{7,103},{8,104... | collective-permute-start | bytes 294920 | tf_op jit(solution)/shard_map/ppermute | solution.py:682
  3.6 4.3 %collective-permute-start = (f32[1,4,6144]{2,1,0:T(4,128)}, f32[1,4,6144]{2,1,0:T(4,128)S(1)}, u32[]{:S(2)}, u32[]{:S(2)}) collective-permute-start(f32[1,4,6144]{2,1,0:T(4,128)} %param.13), channel_id=1, source_target_pairs={{0,112},{1,113},{2,114},{3,115},{4,116},{5,117},{6,118},{7,119},{8... | collective-permute-start | bytes 294920 | tf_op jit(solution)/shard_map/ppermute | solution.py:682
  3.6 1.6 %copy-start.1 = (f32[16,1,32768]{2,1,0:T(1,128)S(1)}, f32[16,1,32768]{2,1,0:T(1,128)}, u32[]{:S(2)}) copy-start(f32[16,1,32768]{2,1,0:T(1,128)} %probes.1) | copy-start | bytes 6291460
  7.9 6.7 %copy-start = (s32[1,4,6144]{2,1,0:T(4,128)S(1)}, s32[1,4,6144]{2,1,0:T(4,128)}, u32[]{:S(2)}) copy-start(s32[1,4,6144]{2,1,0:T(4,128)} %param.11) | copy-start | bytes 294916
  7.9 18.5 %collective-permute-start.2 = (f32[8,1152]{1,0:T(8,128)S(1)}, f32[8,1152]{1,0:T(8,128)S(1)}, u32[]{:S(2)}, u32[]{:S(2)}) collective-permute-start(f32[8,1152]{1,0:T(8,128)S(1)} %get-tuple-element.41), channel_id=1, source_target_pairs={{0,1},{1,2},{2,3},{3,4},{4,5},{5,6},{6,7},{7,8},{8,9},{9,10},{10,1... | collective-permute-start | bytes 110600 | tf_op jit(solution)/shard_map/ppermute | solution.py:682
  9.6 16.9 %collective-permute-start.3 = (f32[8,1152]{1,0:T(8,128)S(1)}, f32[8,1152]{1,0:T(8,128)S(1)}, u32[]{:S(2)}, u32[]{:S(2)}) collective-permute-start(f32[8,1152]{1,0:T(8,128)S(1)} %get-tuple-element.42), channel_id=1, source_target_pairs={{0,15},{1,0},{2,1},{3,2},{4,3},{5,4},{6,5},{7,6},{8,7},{9,8},{10,9... | collective-permute-start | bytes 110600 | tf_op jit(solution)/shard_map/ppermute | solution.py:682
  29.9 11.6 %copy-start.2 = (s32[1,6144]{1,0:T(1,128)S(1)}, s32[1,6144]{1,0:T(1,128)}, u32[]{:S(2)}) copy-start(s32[1,6144]{1,0:T(1,128)} %cells.3) | copy-start | bytes 73732
  29.9 11.7 %copy-start.3 = (f32[1,32768]{1,0:T(1,128)S(1)}, f32[1,32768]{1,0:T(1,128)}, u32[]{:S(2)}) copy-start(f32[1,32768]{1,0:T(1,128)} %centre.1) | copy-start | bytes 393220
  29.9 11.7 %copy-start.4 = (f32[1,32768]{1,0:T(1,128)S(1)}, f32[1,32768]{1,0:T(1,128)}, u32[]{:S(2)}) copy-start(f32[1,32768]{1,0:T(1,128)} %lower.1) | copy-start | bytes 393220
  29.9 11.6 %copy-start.5 = (f32[1,32768]{1,0:T(1,128)S(1)}, f32[1,32768]{1,0:T(1,128)}, u32[]{:S(2)}) copy-start(f32[1,32768]{1,0:T(1,128)} %upper.1) | copy-start | bytes 393220
  29.9 10.0 %collective-permute-start.4 = (f32[32,1024]{1,0:T(8,128)S(1)}, f32[32,1024]{1,0:T(8,128)S(1)}, u32[]{:S(2)}, u32[]{:S(2)}) collective-permute-start(f32[32,1024]{1,0:T(8,128)S(1)} %get-tuple-element.43), channel_id=1, source_target_pairs={{0,15},{1,0},{2,1},{3,2},{4,3},{5,4},{6,5},{7,6},{8,7},{9,8},{10,9... | collective-permute-start | bytes 393224 | tf_op jit(solution)/shard_map/ppermute | solution.py:682
  31.9 8.4 %collective-permute-start.5 = (f32[32,1024]{1,0:T(8,128)S(1)}, f32[32,1024]{1,0:T(8,128)S(1)}, u32[]{:S(2)}, u32[]{:S(2)}) collective-permute-start(f32[32,1024]{1,0:T(8,128)S(1)} %get-tuple-element.44), channel_id=1, source_target_pairs={{0,1},{1,2},{2,3},{3,4},{4,5},{5,6},{6,7},{7,8},{8,9},{9,10},{10,1... | collective-permute-start | bytes 393224 | tf_op jit(solution)/shard_map/ppermute | solution.py:682
  40.4 7.8 %collective-permute-start.6 = (f32[48,1024]{1,0:T(8,128)S(1)}, f32[48,1024]{1,0:T(8,128)S(1)}, u32[]{:S(2)}, u32[]{:S(2)}) collective-permute-start(f32[48,1024]{1,0:T(8,128)S(1)} %get-tuple-element.45), channel_id=1, source_target_pairs={{0,16},{1,17},{2,18},{3,19},{4,20},{5,21},{6,22},{7,23},{8,24},{9,... | collective-permute-start | bytes 589832 | tf_op jit(solution)/shard_map/ppermute | solution.py:682
  40.4 9.0 %collective-permute-start.7 = (f32[48,1024]{1,0:T(8,128)S(1)}, f32[48,1024]{1,0:T(8,128)S(1)}, u32[]{:S(2)}, u32[]{:S(2)}) collective-permute-start(f32[48,1024]{1,0:T(8,128)S(1)} %get-tuple-element.46), channel_id=1, source_target_pairs={{0,32},{1,33},{2,34},{3,35},{4,36},{5,37},{6,38},{7,39},{8,40},{9,... | collective-permute-start | bytes 589832 | tf_op jit(solution)/shard_map/ppermute | solution.py:682
  64.8 6.6 %collective-permute-start.8 = (f32[48,1024]{1,0:T(8,128)S(1)}, f32[48,1024]{1,0:T(8,128)S(1)}, u32[]{:S(2)}, u32[]{:S(2)}) collective-permute-start(f32[48,1024]{1,0:T(8,128)S(1)} %at_receptors.1), channel_id=1, source_target_pairs={{0,112},{1,113},{2,114},{3,115},{4,116},{5,117},{6,118},{7,119},{8... | collective-permute-start | bytes 589832 | tf_op jit(solution)/shard_map/ppermute | solution.py:682
  66.6 8.5 %collective-permute-start.9 = (f32[48,1024]{1,0:T(8,128)S(1)}, f32[48,1024]{1,0:T(8,128)S(1)}, u32[]{:S(2)}, u32[]{:S(2)}) collective-permute-start(f32[48,1024]{1,0:T(8,128)S(1)} %get-tuple-element.56), channel_id=1, source_target_pairs={{0,96},{1,97},{2,98},{3,99},{4,100},{5,101},{6,102},{7,103},{8,104... | collective-permute-start | bytes 589832 | tf_op jit(solution)/shard_map/ppermute | solution.py:682
  75.2 17.7 %collective-permute-start.10 = (f32[32,1152]{1,0:T(8,128)S(1)}, f32[32,1152]{1,0:T(8,128)S(1)}, u32[]{:S(2)}, u32[]{:S(2)}) collective-permute-start(f32[32,1152]{1,0:T(8,128)S(1)} %get-tuple-element.59), channel_id=1, source_target_pairs={{0,1},{1,2},{2,3},{3,4},{4,5},{5,6},{6,7},{7,8},{8,9},{9,10},{10,1... | collective-permute-start | bytes 442376 | tf_op jit(solution)/shard_map/ppermute | solution.py:682
  75.3 17.6 %collective-permute-start.11 = (f32[32,1152]{1,0:T(8,128)S(1)}, f32[32,1152]{1,0:T(8,128)S(1)}, u32[]{:S(2)}, u32[]{:S(2)}) collective-permute-start(f32[32,1152]{1,0:T(8,128)S(1)} %get-tuple-element.60), channel_id=1, source_target_pairs={{0,15},{1,0},{2,1},{3,2},{4,3},{5,4},{6,5},{7,6},{8,7},{9,8},{10,9... | collective-permute-start | bytes 442376 | tf_op jit(solution)/shard_map/ppermute | solution.py:682
  115.8 1.3 collective-permute-start.12
  117.0 3.7 %collective-permute-start.13 = (f32[16,16]{1,0:T(8,128)S(1)}, f32[16,16]{1,0:T(8,128)S(1)}, u32[]{:S(2)}, u32[]{:S(2)}) collective-permute-start(f32[16,16]{1,0:T(8,128)S(1)} %add.21), channel_id=1, source_target_pairs={{0,32},{1,33},{2,34},{3,35},{4,36},{5,37},{6,38},{7,39},{8,40},{9,... | collective-permute-start | bytes 3080 | tf_op jit(solution)/shard_map/ppermute | solution.py:682
  120.7 4.9 %collective-permute-start.14 = (f32[16,16]{1,0:T(8,128)S(1)}, f32[16,16]{1,0:T(8,128)S(1)}, u32[]{:S(2)}, u32[]{:S(2)}) collective-permute-start(f32[16,16]{1,0:T(8,128)S(1)} %add.22), channel_id=1, source_target_pairs={{0,96},{1,97},{2,98},{3,99},{4,100},{5,101},{6,102},{7,103},{8,104... | collective-permute-start | bytes 3080 | tf_op jit(solution)/shard_map/ppermute | solution.py:682
  125.6 3.7 %collective-permute-start.15 = (f32[16,16]{1,0:T(8,128)S(1)}, f32[16,16]{1,0:T(8,128)S(1)}, u32[]{:S(2)}, u32[]{:S(2)}) collective-permute-start(f32[16,16]{1,0:T(8,128)S(1)} %add.23), channel_id=1, source_target_pairs={{0,1},{1,0},{2,3},{3,2},{4,5},{5,4},{6,7},{7,6},{8,9},{9,8},{10,11... | collective-permute-start | bytes 3080 | tf_op jit(solution)/shard_map/ppermute | solution.py:682
  129.2 4.9 %collective-permute-start.16 = (f32[16,16]{1,0:T(8,128)S(1)}, f32[16,16]{1,0:T(8,128)S(1)}, u32[]{:S(2)}, u32[]{:S(2)}) collective-permute-start(f32[16,16]{1,0:T(8,128)S(1)} %add.24), channel_id=1, source_target_pairs={{0,3},{1,2},{2,1},{3,0},{4,7},{5,6},{6,5},{7,4},{8,11},{9,10},{10,... | collective-permute-start | bytes 3080 | tf_op jit(solution)/shard_map/ppermute | solution.py:682
  134.1 3.7 %collective-permute-start.17 = (f32[16,16]{1,0:T(8,128)S(1)}, f32[16,16]{1,0:T(8,128)S(1)}, u32[]{:S(2)}, u32[]{:S(2)}) collective-permute-start(f32[16,16]{1,0:T(8,128)S(1)} %add.25), channel_id=1, source_target_pairs={{0,4},{1,5},{2,6},{3,7},{4,0},{5,1},{6,2},{7,3},{8,12},{9,13},{10,... | collective-permute-start | bytes 3080 | tf_op jit(solution)/shard_map/ppermute | solution.py:682
  137.7 4.9 %collective-permute-start.18 = (f32[16,16]{1,0:T(8,128)S(1)}, f32[16,16]{1,0:T(8,128)S(1)}, u32[]{:S(2)}, u32[]{:S(2)}) collective-permute-start(f32[16,16]{1,0:T(8,128)S(1)} %add.26), channel_id=1, source_target_pairs={{0,12},{1,13},{2,14},{3,15},{4,8},{5,9},{6,10},{7,11},{8,4},{9,5},... | collective-permute-start | bytes 3080 | tf_op jit(solution)/shard_map/ppermute | solution.py:682

commit v4 on v3

--- a/solution.py
+++ b/solution.py
@@ -21,6 +21,7 @@
 SLOTS = PARTNERS * FRINGE
 TILES = ROWS // LANES
 WAYS = 8
+SUMS = 16
 UNROLL = 8
 
 AXES = ("grid", "cell")
@@ -94,7 +95,7 @@
         for n in range(UNROLL):
             q = low + j * UNROLL + n
             for w in range(WAYS):
-                step(w, q, parts[w][q])
+                step(w, n, q, parts[w][q])
         return carry
 
     lax.fori_loop(0, (high - low) // UNROLL, outer, 0)
@@ -103,7 +104,7 @@
 def gather_rows(table, parts, staged, phases):
     count = parts[0].shape[0]
 
-    def step(w, q, row):
+    def step(w, n, q, row):
         staged[pl.ds(w * count + q, 1), :] = table[pl.ds(row, 1), :]
 
     finish(phases[0])
@@ -125,9 +126,10 @@
 def add_rows(sums, parts, staged):
     count = parts[0].shape[0]
 
-    def step(w, q, row):
+    def step(w, n, q, row):
         term = staged[pl.ds(w * count + q, 1), :]
-        sums[w][pl.ds(row, 1), :] = sums[w][pl.ds(row, 1), :] + term
+        total = sums[w + n % (SUMS // WAYS) * WAYS]
+        total[pl.ds(row, 1), :] = total[pl.ds(row, 1), :] + term
 
     row_steps(parts, 0, count, step)
 
@@ -373,7 +375,7 @@
 
 
 def forward_kernel(table, centre, lower, upper, before, after, c_out, l_out, u_out, *rest):
-    sums, padded = rest[:WAYS], rest[WAYS]
+    sums, padded = rest[:SUMS], rest[SUMS]
 
     def step(j, carry):
         for n in range(2):
@@ -406,9 +408,9 @@
 def forward(table, centre, lower, upper, before, after):
     return pl.pallas_call(
         forward_kernel,
-        out_shape=[resident(ROWS, LANES)] * (3 + WAYS),
+        out_shape=[resident(ROWS, LANES)] * (3 + SUMS),
         in_specs=[VMEM] * 6,
-        out_specs=[VMEM] * (3 + WAYS),
+        out_specs=[VMEM] * (3 + SUMS),
         scratch_shapes=[pltpu.VMEM((ROWS + 16, LANES), f32)],
         compiler_params=params(8),
         cost_estimate=cost(7),
@@ -417,10 +419,10 @@
 
 
 def couple_kernel(cells, rows_hbm, near, far, *refs):
-    refs = refs[WAYS:]
-    tangent, out, sums = refs[0], refs[1], refs[2 : 2 + WAYS]
-    staged, staged_far = refs[2 + WAYS : 4 + WAYS]
-    refs = refs[4 + WAYS :]
+    refs = refs[SUMS:]
+    tangent, out, sums = refs[0], refs[1], refs[2 : 2 + SUMS]
+    staged, staged_far = refs[2 + SUMS : 4 + SUMS]
+    refs = refs[4 + SUMS :]
     parts, sem, parts_far, sem_far = refs[:WAYS], refs[WAYS], refs[WAYS + 1 : 2 * WAYS + 1], refs[2 * WAYS + 1]
     every = NEAR + FAR
     phases = index_copies(rows_hbm, segments(1, every), parts, sem)
@@ -445,13 +447,13 @@
     every, some = segments(1, NEAR + FAR), segments(1, FAR)
     outs = pl.pallas_call(
         couple_kernel,
-        out_shape=[resident(ROWS, LANES), TRIPLE] + [resident(ROWS, LANES)] * WAYS,
-        in_specs=[VMEM, HBM] + [VMEM] * (2 + WAYS),
-        out_specs=[VMEM] * (2 + WAYS),
+        out_shape=[resident(ROWS, LANES), TRIPLE] + [resident(ROWS, LANES)] * SUMS,
+        in_specs=[VMEM, HBM] + [VMEM] * (2 + SUMS),
+        out_specs=[VMEM] * (2 + SUMS),
         scratch_shapes=[pltpu.VMEM((SLOTS, LANES), f32), pltpu.VMEM((SLOTS // 2, LANES), f32)]
         + index_scratch(every)
         + index_scratch(some),
-        input_output_aliases={4 + w: 2 + w for w in range(WAYS)},
+        input_output_aliases={4 + w: 2 + w for w in range(SUMS)},
         compiler_params=params(8),
         cost_estimate=cost(11),
         name="couple",
@@ -479,7 +481,7 @@
     )(tangent, cells, rows)
 
 
-def return_relay_kernel(near, far, tangent, lower, upper, up, down):
+def return_relay_kernel(near, far, tangent, lower, upper, ready, up, down):
     for n, ref in enumerate((near, far)):
         at = slice(n * PROBES, (n + 1) * PROBES)
         up[at, 0:FRINGE] = ref[0:PROBES, :]
@@ -489,13 +491,13 @@
     down[0:8, EDGE] = lower[0:8, :] * tangent[0:8, :]
 
 
-def return_relay(near, far, tangent, lower, upper):
+def return_relay(near, far, tangent, lower, upper, ready):
     shape = jax.ShapeDtypeStruct((2 * PROBES, FRINGE + LANES), f32)
-    return simple_call(return_relay_kernel, [shape] * 2, (near, far, tangent, lower, upper), "return_relay")
+    return simple_call(return_relay_kernel, [shape] * 2, (near, far, tangent, lower, upper, ready), "return_relay")
 
 
 def transposed_kernel(tangent, centre, lower, upper, *rest):
-    sums, raised, lowered = rest[:WAYS], rest[WAYS], rest[WAYS + 1]
+    sums, raised, lowered = rest[:SUMS], rest[SUMS], rest[SUMS + 1]
 
     def products(start):
         at = rows_of(start, 8)
@@ -521,9 +523,9 @@
 def transposed(tangent, centre, lower, upper):
     return pl.pallas_call(
         transposed_kernel,
-        out_shape=[resident(ROWS, LANES)] * WAYS,
+        out_shape=[resident(ROWS, LANES)] * SUMS,
         in_specs=[VMEM] * 4,
-        out_specs=[VMEM] * WAYS,
+        out_specs=[VMEM] * SUMS,
         scratch_shapes=[pltpu.VMEM((ROWS + 16, LANES), f32)] * 2,
         compiler_params=params(8),
         cost_estimate=cost(4),
@@ -532,8 +534,8 @@
 
 
 def donor_same_kernel(cells, rows_hbm, near_weights, far_weights, near, far, *refs):
-    refs = refs[WAYS:]
-    sums, staged, parts, sem = refs[:WAYS], refs[WAYS], refs[WAYS + 1 : 2 * WAYS + 1], refs[2 * WAYS + 1]
+    refs = refs[SUMS:]
+    sums, staged, parts, sem = refs[:SUMS], refs[SUMS], refs[SUMS + 1 : SUMS + WAYS + 1], refs[SUMS + WAYS + 1]
     phases = index_copies(rows_hbm, segments(4, SAME), parts, sem)
     weights = weight_places(None, (near_weights, far_weights), None)
     spread_fields(grid_places(near, far), cells, SAME, weights, staged)
@@ -545,11 +547,11 @@
     segs = segments(4, SAME)
     return pl.pallas_call(
         donor_same_kernel,
-        out_shape=[resident(ROWS, LANES)] * WAYS,
-        in_specs=[VMEM, HBM] + [VMEM] * (4 + WAYS),
-        out_specs=[VMEM] * WAYS,
+        out_shape=[resident(ROWS, LANES)] * SUMS,
+        in_specs=[VMEM, HBM] + [VMEM] * (4 + SUMS),
+        out_specs=[VMEM] * SUMS,
         scratch_shapes=[pltpu.VMEM((len(segs) * FRINGE, LANES), f32)] + index_scratch(segs),
-        input_output_aliases={6 + w: w for w in range(WAYS)},
+        input_output_aliases={6 + w: w for w in range(SUMS)},
         compiler_params=params(8),
         cost_estimate=cost(9),
         name="add_same",
@@ -557,9 +559,9 @@
 
 
 def donor_sides_kernel(cells, rows_hbm, before_weights, after_weights, before, after, *refs):
-    refs = refs[WAYS:]
-    adjoint, gram, sums, staged = refs[0], refs[1], refs[2 : 2 + WAYS], refs[2 + WAYS]
-    parts, sem = refs[3 + WAYS : 3 + 2 * WAYS], refs[3 + 2 * WAYS]
+    refs = refs[SUMS:]
+    adjoint, gram, sums, staged = refs[0], refs[1], refs[2 : 2 + SUMS], refs[2 + SUMS]
+    parts, sem = refs[3 + SUMS : 3 + SUMS + WAYS], refs[3 + SUMS + WAYS]
     phases = index_copies(rows_hbm, segments(4, SIDES), parts, sem)
     weights = weight_places(before_weights, (None, None), after_weights)
     spread_fields({**pair_places(BEFORE, before), **pair_places(AFTER, after)}, cells, SIDES, weights, staged)
@@ -607,11 +609,11 @@
     outs = pl.pallas_call(
         donor_sides_kernel,
         out_shape=[resident(ROWS, LANES), jax.ShapeDtypeStruct((PROBES, PROBES), f32)]
-        + [resident(ROWS, LANES)] * WAYS,
-        in_specs=[VMEM, HBM] + [VMEM] * (4 + WAYS),
-        out_specs=[VMEM] * (2 + WAYS),
+        + [resident(ROWS, LANES)] * SUMS,
+        in_specs=[VMEM, HBM] + [VMEM] * (4 + SUMS),
+        out_specs=[VMEM] * (2 + SUMS),
         scratch_shapes=[pltpu.VMEM((len(segs) * FRINGE, LANES), f32)] + index_scratch(segs),
-        input_output_aliases={6 + w: 2 + w for w in range(WAYS)},
+        input_output_aliases={6 + w: 2 + w for w in range(SUMS)},
         compiler_params=params(12),
         cost_estimate=cost(18),
         name="add_sides",
@@ -690,15 +692,16 @@
     return moved(value, lambda g, c: (g, c + distance))
 
 
+def ring_sum(value, step):
+    after, across, before = (moved(value, lambda g, c, n=n: step(g, c, n)) for n in (1, 2, 3))
+    return (value + across) + (before + after)
+
+
 def summed(value):
     value = value + moved(value, lambda g, c: (g ^ 1, c))
-    value = value + moved(value, lambda g, c: (g ^ 2, c))
-    value = value + moved(value, lambda g, c: ((6 - (g & 6)) | (g & 1), c))
-    value = value + moved(value, lambda g, c: (g, c ^ 1))
-    value = value + moved(value, lambda g, c: (g, (c & 12) | (3 - (c & 3))))
-    value = value + moved(value, lambda g, c: (g, c ^ 4))
-    value = value + moved(value, lambda g, c: (g, (12 - (c & 12)) | (c & 3)))
-    return value
+    value = ring_sum(value, lambda g, c, n: (g + 2 * n, c))
+    value = ring_sum(value, lambda g, c, n: (g, (c & 12) | ((c + n) & 3)))
+    return ring_sum(value, lambda g, c, n: (g, c + 4 * n))
 
 
 def body(probes, centre, lower_coef, upper_coef, donor_cells, receptor_cells, weights):
@@ -720,7 +723,7 @@
     far = along_grid(far, -2)
     near = along_grid(at_receptors(tangent, receptor_cells, receptor_rows), -1)
     sums = transposed(tangent, c, l, u)
-    up, down = return_relay(near, far, tangent, l, u)
+    up, down = return_relay(near, far, tangent, l, u, sums[-1])
     before, after = along_cell(up, 1), along_cell(down, -1)
     sums = add_same(donors, donor_rows, near_weights, far_weights, near, far, sums)
     adjoint, gram = add_sides(donors, donor_rows, before_weights, after_weights, before, after, sums)

time: 149 us -> 147 us (0.987)
  waiting for transfers between devices: 35.6 us -> 20.8 us
  starting transfers between devices: 22.2 us -> 31 us
  Pallas kernels: 88.1 us -> 92.6 us
    ppermute x19 -> x22, waiting for transfers between devices: 35.6 us -> 20.8 us  [moved(): return lax.ppermute(value, AXES, route)]
    ppermute x19 -> x22, starting transfers between devices: 22.2 us -> 31 us  [moved(): return lax.ppermute(value, AXES, route)]
    pallas_call x3, Pallas kernels: 18 us -> 20.6 us  [the longest x1 9.2 us: add_same(): pl.pallas_call(donor_same_kernel, out_shape=[resident(ROWS, LANES)] * SUM...]
  transfers between devices with their start and end apart: 19 -> 22, of which waited for: 12 -> 10; matrix products, arithmetic and copies ran while one was open for 0% -> 0% of each run, Pallas kernels for 27% -> 29%
where the time goes in v4:
time: 147 us
  Pallas kernels  92.6 us (63%)
  starting transfers between devices  31 us (21%)
  waiting for transfers between devices  20.8 us (14%)
  local copies, waits for them, and re-layouts  1.63 us (1%)
    ppermute x22, starting transfers between devices, moved(): return lax.ppermute(value, AXES, route)  31 us
    pallas_call x1, Pallas kernels, add_sides(): pl.pallas_call(donor_sides_kernel, out_shape=[resident(ROWS, LANES), jax....  23.4 us
    ppermute x22, waiting for transfers between devices, moved(): return lax.ppermute(value, AXES, route)  20.8 us
    pallas_call x1, Pallas kernels, couple(): pl.pallas_call(couple_kernel, out_shape=[resident(ROWS, LANES), TRIPLE] +...  13.4 us
    pallas_call x1, Pallas kernels, rows_at_sides(): pl.pallas_call(rows_kernel, out_shape=resident(len(segs) * FRINGE, LANES)...  11.8 us
    pallas_call x1, Pallas kernels, add_same(): pl.pallas_call(donor_same_kernel, out_shape=[resident(ROWS, LANES)] * SUM...  9.2 us
    pallas_call x1, Pallas kernels, same_sums(): pl.pallas_call(same_sums_kernel, out_shape=PAIR, in_specs=[VMEM, VMEM, HB...  7.9 us
    pallas_call x1, Pallas kernels, forward(): pl.pallas_call(forward_kernel, out_shape=[resident(ROWS, LANES)] * (3 + S...  6.82 us
  transfers between devices with their start and end apart: 22, of which 10 were waited for; matrix products, arithmetic and copies ran while one was open for 0% of the time, Pallas kernels for 29%

profile of v4, /device:TPU:0, one launch (start us, length us, event | category | flops | bytes accessed | tf_op | source)
XLA Modules:
  0.0 147.2 jit_solution(10652181887017289420)
XLA Ops:
  0.6 2.9 %collective-permute-start.1 = (f32[1,4,6144]{2,1,0:T(4,128)}, f32[1,4,6144]{2,1,0:T(4,128)S(1)}, u32[]{:S(2)}, u32[]{:S(2)}) collective-permute-start(f32[1,4,6144]{2,1,0:T(4,128)} %param.13), channel_id=1, source_target_pairs={{0,96},{1,97},{2,98},{3,99},{4,100},{5,101},{6,102},{7,103},{8,104... | collective-permute-start | bytes 294920 | tf_op jit(solution)/shard_map/ppermute | solution.py:684
  3.6 1.6 %copy-done.1 = f32[16,1,32768]{2,1,0:T(1,128)S(1)} copy-done((f32[16,1,32768]{2,1,0:T(1,128)S(1)}, f32[16,1,32768]{2,1,0:T(1,128)}, u32[]{:S(2)}) %copy-start.1) | copy-done | bytes 2097176
  5.2 2.7 %table.1 = f32[4096,128]{1,0:T(8,128)S(1)} custom-call(f32[16,1,32768]{2,1,0:T(1,128)S(1)} %copy-done.1), custom_call_target="tpu_custom_call" | custom-call | bytes 9000000 | tf_op jit(solution)/shard_map/table/pallas_call | solution.py:239
  7.9 0.0 copy-start
  7.9 0.0 collective-permute-done.1
  7.9 0.0 collective-permute-done
  7.9 1.6 %collective-permute-start.2 = (f32[8,1152]{1,0:T(8,128)S(1)}, f32[8,1152]{1,0:T(8,128)S(1)}, u32[]{:S(2)}, u32[]{:S(2)}) collective-permute-start(f32[8,1152]{1,0:T(8,128)S(1)} %get-tuple-element.65), channel_id=1, source_target_pairs={{0,1},{1,2},{2,3},{3,4},{4,5},{5,6},{6,7},{7,8},{8,9},{9,10},{10,1... | collective-permute-start | bytes 110600 | tf_op jit(solution)/shard_map/ppermute | solution.py:684
  9.6 5.0 %collective-permute-start.3 = (f32[8,1152]{1,0:T(8,128)S(1)}, f32[8,1152]{1,0:T(8,128)S(1)}, u32[]{:S(2)}, u32[]{:S(2)}) collective-permute-start(f32[8,1152]{1,0:T(8,128)S(1)} %get-tuple-element.66), channel_id=1, source_target_pairs={{0,15},{1,0},{2,1},{3,2},{4,3},{5,4},{6,5},{7,6},{8,7},{9,8},{10,9... | collective-permute-start | bytes 110600 | tf_op jit(solution)/shard_map/ppermute | solution.py:684
  14.6 11.8 %rows_at_sides.1.staged = f32[16384,128]{1,0:T(8,128)S(1)} custom-call(f32[4096,128]{1,0:T(8,128)S(1)} %table.1, s32[24576]{0:T(1024)S(1)} %bitcast.11), custom_call_target="tpu_custom_call" | custom-call | bytes 33000000 | tf_op jit(solution)/shard_map/rows_at_sides/pallas_call | solution.py:310
  26.4 0.0 collective-permute-done.3.after.after_weights
  26.5 3.4 %side_sums.1 = (f32[32,1024]{1,0:T(8,128)S(1)}, f32[32,1024]{1,0:T(8,128)S(1)}) custom-call(f32[16384,128]{1,0:T(8,128)S(1)} %rows_at_sides.1.staged, s32[4,6144]{1,0:T(4,128)S(1)} %bitcast.7, f32[8,1152]{1,0:T(8,128)S(1)} %collective-permute-done.2.before.before_weights, f32[8,1152]{1,0:T(8,128)S(1)} %collective-permute-done.3.after.after_weights), custom_call_target="tpu_custom_call" | custom-call | bytes 3000000 | tf_op jit(solution)/shard_map/side_sums/pallas_call | solution.py:279
  29.9 0.0 copy-start.2
  29.9 0.0 copy-start.3
  29.9 0.0 copy-start.4
  29.9 0.0 copy-start.5
  29.9 2.0 %collective-permute-start.4 = (f32[32,1024]{1,0:T(8,128)S(1)}, f32[32,1024]{1,0:T(8,128)S(1)}, u32[]{:S(2)}, u32[]{:S(2)}) collective-permute-start(f32[32,1024]{1,0:T(8,128)S(1)} %get-tuple-element.67), channel_id=1, source_target_pairs={{0,15},{1,0},{2,1},{3,2},{4,3},{5,4},{6,5},{7,6},{8,7},{9,8},{10,9... | collective-permute-start | bytes 393224 | tf_op jit(solution)/shard_map/ppermute | solution.py:684
  31.9 0.1 collective-permute-start.5
  32.0 7.9 %same_sums.1.same = f32[32,1024]{1,0:T(8,128)S(1)} custom-call(f32[4096,128]{1,0:T(8,128)S(1)} %table.1, s32[4,6144]{1,0:T(4,128)S(1)} %bitcast.8, s32[24576]{0:T(1024)S(1)} %bitcast.12, f32[4,6144]{1,0:T(4,128)S(1)} %bitcast.19, f32[4,6144]{1,0:T(4,128)S(1)} %bitcast.16), custom_call_target="tpu_custom_call" | custom-call | bytes 24000000 | tf_op jit(solution)/shard_map/same_sums/pallas_call | solution.py:343
  39.9 0.0 collective-permute-done.4.before
  39.9 0.4 collective-permute-done.5.after
  40.4 0.0 collective-permute-start.6
  40.4 1.1 collective-permute-start.7
  41.6 6.8 %forward.1 = (f32[4096,128]{1,0:T(8,128)S(1)}, f32[4096,128]{1,0:T(8,128)S(1)}, f32[4096,128]{1,0:T(8,128)S(1)}, f32[4096,128]{1,0:T(8,128)S(1)}, f32[4096,128]{...) custom-call(f32[4096,128]{1,0:T(8,128)S(1)} %table.1, ...), custom_call_target="tpu_custom_call" | custom-call | bytes 21000000 | tf_op jit(solution)/shard_map/forward/pallas_call | solution.py:409
  48.4 1.0 collective-permute-done.7.far
  49.4 13.4 %couple.1 = (f32[4096,128]{1,0:T(8,128)S(1)}, f32[48,1024]{1,0:T(8,128)S(1)}, f32[4096,128]{1,0:T(8,128)S(1)}, f32[4096,128]{1,0:T(8,128)S(1)}, f32[4096,128]{1,...) custom-call(s32[1,6144]{1,0:T(1,128)S(1)} %copy-done.2, ...), custom_call_target="tpu_custom_call", output_to_operand_aliasing={{2}: (4, {}), {3}: (5, {}), {4}: (6, {}), {5}: (7, {}), {6}... | custom-call | bytes 33000000 | tf_op jit(solution)/shard_map/couple/pallas_call | solution.py:448
  62.8 3.3 %at_receptors.1 = f32[48,1024]{1,0:T(8,128)S(1)} custom-call(f32[4096,128]{1,0:T(8,128)S(1)} %get-tuple-element.87.tangent, s32[1,6144]{1,0:T(1,128)S(1)} %copy-done.2, s32[6144]{0:T(1024)S(1)} %bitcast.22), custom_call_target="tpu_custom_call" | custom-call | bytes 9000000 | tf_op jit(solution)/shard_map/at_receptors/pallas_call | solution.py:472
  66.2 1.8 %collective-permute-start.8 = (f32[48,1024]{1,0:T(8,128)S(1)}, f32[48,1024]{1,0:T(8,128)S(1)}, u32[]{:S(2)}, u32[]{:S(2)}) collective-permute-start(f32[48,1024]{1,0:T(8,128)S(1)} %at_receptors.1), channel_id=1, source_target_pairs={{0,112},{1,113},{2,114},{3,115},{4,116},{5,117},{6,118},{7,119},{8... | collective-permute-start | bytes 589832 | tf_op jit(solution)/shard_map/ppermute | solution.py:684
  68.0 0.8 collective-permute-start.9
  68.8 4.6 %transposed.1 = (f32[4096,128]{1,0:T(8,128)S(1)}, f32[4096,128]{1,0:T(8,128)S(1)}, f32[4096,128]{1,0:T(8,128)S(1)}, f32[4096,128]{1,0:T(8,128)S(1)}, f32[4096,12...) custom-call(f32[4096,128]{1,0:T(8,128)S(1)} %get-tuple-element.87.ta, ...), custom_call_target="tpu_custom_call" | custom-call | bytes 12000000 | tf_op jit(solution)/shard_map/transposed/pallas_call | solution.py:524
  73.4 3.1 %collective-permute-done.9.far = f32[48,1024]{1,0:T(8,128)S(1)} collective-permute-done((f32[48,1024]{1,0:T(8,128)S(1)}, f32[48,1024]{1,0:T(8,128)S(1)}, u32[]{:S(2)}, u32[]{:S(2)}) %collective-permute-start.9) | collective-permute-done | bytes 196640 | tf_op jit(solution)/shard_map/ppermute | solution.py:684
  76.5 0.1 collective-permute-start.10
  76.6 5.3 %collective-permute-start.11 = (f32[32,1152]{1,0:T(8,128)S(1)}, f32[32,1152]{1,0:T(8,128)S(1)}, u32[]{:S(2)}, u32[]{:S(2)}) collective-permute-start(f32[32,1152]{1,0:T(8,128)S(1)} %get-tuple-element.94), channel_id=1, source_target_pairs={{0,15},{1,0},{2,1},{3,2},{4,3},{5,4},{6,5},{7,6},{8,7},{9,8},{10,9... | collective-permute-start | bytes 442376 | tf_op jit(solution)/shard_map/ppermute | solution.py:684
  81.9 9.2 %add_same.1 = (f32[4096,128]{1,0:T(8,128)S(1)}, f32[4096,128]{1,0:T(8,128)S(1)}, f32[4096,128]{1,0:T(8,128)S(1)}, f32[4096,128]{1,0:T(8,128)S(1)}, f32[4096,128]...) custom-call(s32[4,6144]{1,0:T(4,128)S(1)} %bitcast.9, ...), custom_call_target="tpu_custom_call", output_to_operand_aliasing={{0}: (6, {}), {1}: (7, {}), {2}: (8, {}), {3}: (9, {}), {4}... | custom-call | bytes 27000000 | tf_op jit(solution)/shard_map/add_same/pallas_call | solution.py:548
  91.2 23.4 %add_sides.1 = (f32[4096,128]{1,0:T(8,128)S(1)}, f32[16,16]{1,0:T(8,128)S(1)}, f32[4096,128]{1,0:T(8,128)S(1)}, f32[4096,128]{1,0:T(8,128)S(1)}, f32[4096,128]{1...) custom-call(s32[4,6144]{1,0:T(4,128)S(1)} %bitcast.10, ...), custom_call_target="tpu_custom_call", output_to_operand_aliasing={{2}: (6, {}), {3}: (7, {}), {4}: (8, {}), {5}: (9, {}), {6}... | custom-call | bytes 54000000 | tf_op jit(solution)/shard_map/add_sides/pallas_call | solution.py:609
  114.6 0.1 collective-permute-start.12
  114.7 1.2 collective-permute-done.12
  115.9 3.2 %collective-permute-start.14 = (f32[16,16]{1,0:T(8,128)S(1)}, f32[16,16]{1,0:T(8,128)S(1)}, u32[]{:S(2)}, u32[]{:S(2)}) collective-permute-start(f32[16,16]{1,0:T(8,128)S(1)} %add.30), channel_id=1, source_target_pairs={{0,96},{1,97},{2,98},{3,99},{4,100},{5,101},{6,102},{7,103},{8,104... | collective-permute-start | bytes 3080 | tf_op jit(solution)/shard_map/ppermute | solution.py:684
  119.1 0.3 collective-permute-start.13
  119.4 1.3 collective-permute-done.15
  120.7 3.5 %collective-permute-done.13 = f32[16,16]{1,0:T(8,128)S(1)} collective-permute-done((f32[16,16]{1,0:T(8,128)S(1)}, f32[16,16]{1,0:T(8,128)S(1)}, u32[]{:S(2)}, u32[]{:S(2)}) %collective-permute-start.13) | collective-permute-done | bytes 1056 | tf_op jit(solution)/shard_map/ppermute | solution.py:684
  124.3 0.0 collective-permute-start.18
  124.3 3.2 %collective-permute-start.17 = (f32[16,16]{1,0:T(8,128)S(1)}, f32[16,16]{1,0:T(8,128)S(1)}, u32[]{:S(2)}, u32[]{:S(2)}) collective-permute-start(f32[16,16]{1,0:T(8,128)S(1)} %add_add_fusion.2), channel_id=1, source_target_pairs={{0,3},{1,0},{2,1},{3,2},{4,7},{5,4},{6,5},{7,6},{8,11},{9,8},{10,9... | collective-permute-start | bytes 3080 | tf_op jit(solution)/shard_map/ppermute | solution.py:684
  127.5 1.6 %collective-permute-done.18 = f32[16,16]{1,0:T(8,128)S(1)} collective-permute-done((f32[16,16]{1,0:T(8,128)S(1)}, f32[16,16]{1,0:T(8,128)S(1)}, u32[]{:S(2)}, u32[]{:S(2)}) %collective-permute-start.18) | collective-permute-done | bytes 1056 | tf_op jit(solution)/shard_map/ppermute | solution.py:684
  129.1 3.5 %collective-permute-done.16 = f32[16,16]{1,0:T(8,128)S(1)} collective-permute-done((f32[16,16]{1,0:T(8,128)S(1)}, f32[16,16]{1,0:T(8,128)S(1)}, u32[]{:S(2)}, u32[]{:S(2)}) %collective-permute-start.16) | collective-permute-done | bytes 1056 | tf_op jit(solution)/shard_map/ppermute | solution.py:684
  132.7 3.2 %collective-permute-start.20 = (f32[16,16]{1,0:T(8,128)S(1)}, f32[16,16]{1,0:T(8,128)S(1)}, u32[]{:S(2)}, u32[]{:S(2)}) collective-permute-start(f32[16,16]{1,0:T(8,128)S(1)} %add_add_fusion.1), channel_id=1, source_target_pairs={{0,12},{1,13},{2,14},{3,15},{4,0},{5,1},{6,2},{7,3},{8,4},{9,5},{1... | collective-permute-start | bytes 3080 | tf_op jit(solution)/shard_map/ppermute | solution.py:684
  135.9 1.6 %collective-permute-done.21 = f32[16,16]{1,0:T(8,128)S(1)} collective-permute-done((f32[16,16]{1,0:T(8,128)S(1)}, f32[16,16]{1,0:T(8,128)S(1)}, u32[]{:S(2)}, u32[]{:S(2)}) %collective-permute-start.21) | collective-permute-done | bytes 1056 | tf_op jit(solution)/shard_map/ppermute | solution.py:684
  137.5 3.5 %collective-permute-done.19 = f32[16,16]{1,0:T(8,128)S(1)} collective-permute-done((f32[16,16]{1,0:T(8,128)S(1)}, f32[16,16]{1,0:T(8,128)S(1)}, u32[]{:S(2)}, u32[]{:S(2)}) %collective-permute-start.19) | collective-permute-done | bytes 1056 | tf_op jit(solution)/shard_map/ppermute | solution.py:684
  141.1 5.9 %basis.1 = (f32[16,1,32768]{2,1,0:T(1,128)}, f32[16,16]{1,0:T(8,128)}) custom-call(f32[16,16]{1,0:T(8,128)S(1)} %add_add_fusion.gram, f32[4096,128]{1,0:T(8,128)S(1)} %get-tuple-element.127.adjoint), custom_call_target="tpu_custom_call" | custom-call | bytes 18000000 | tf_op jit(solution)/shard_map/basis/pallas_call | solution.py:662
  (29 shorter events, 0.2 us)
Async XLA Ops:
  0.6 7.2 %collective-permute-start.1 = (f32[1,4,6144]{2,1,0:T(4,128)}, f32[1,4,6144]{2,1,0:T(4,128)S(1)}, u32[]{:S(2)}, u32[]{:S(2)}) collective-permute-start(f32[1,4,6144]{2,1,0:T(4,128)} %param.13), channel_id=1, source_target_pairs={{0,96},{1,97},{2,98},{3,99},{4,100},{5,101},{6,102},{7,103},{8,104... | collective-permute-start | bytes 294920 | tf_op jit(solution)/shard_map/ppermute | solution.py:684
  3.6 4.3 %collective-permute-start = (f32[1,4,6144]{2,1,0:T(4,128)}, f32[1,4,6144]{2,1,0:T(4,128)S(1)}, u32[]{:S(2)}, u32[]{:S(2)}) collective-permute-start(f32[1,4,6144]{2,1,0:T(4,128)} %param.13), channel_id=1, source_target_pairs={{0,112},{1,113},{2,114},{3,115},{4,116},{5,117},{6,118},{7,119},{8... | collective-permute-start | bytes 294920 | tf_op jit(solution)/shard_map/ppermute | solution.py:684
  3.6 1.6 %copy-start.1 = (f32[16,1,32768]{2,1,0:T(1,128)S(1)}, f32[16,1,32768]{2,1,0:T(1,128)}, u32[]{:S(2)}) copy-start(f32[16,1,32768]{2,1,0:T(1,128)} %probes.1) | copy-start | bytes 6291460
  7.9 6.7 %copy-start = (s32[1,4,6144]{2,1,0:T(4,128)S(1)}, s32[1,4,6144]{2,1,0:T(4,128)}, u32[]{:S(2)}) copy-start(s32[1,4,6144]{2,1,0:T(4,128)} %param.11) | copy-start | bytes 294916
  7.9 18.5 %collective-permute-start.2 = (f32[8,1152]{1,0:T(8,128)S(1)}, f32[8,1152]{1,0:T(8,128)S(1)}, u32[]{:S(2)}, u32[]{:S(2)}) collective-permute-start(f32[8,1152]{1,0:T(8,128)S(1)} %get-tuple-element.65), channel_id=1, source_target_pairs={{0,1},{1,2},{2,3},{3,4},{4,5},{5,6},{6,7},{7,8},{8,9},{9,10},{10,1... | collective-permute-start | bytes 110600 | tf_op jit(solution)/shard_map/ppermute | solution.py:684
  9.6 16.9 %collective-permute-start.3 = (f32[8,1152]{1,0:T(8,128)S(1)}, f32[8,1152]{1,0:T(8,128)S(1)}, u32[]{:S(2)}, u32[]{:S(2)}) collective-permute-start(f32[8,1152]{1,0:T(8,128)S(1)} %get-tuple-element.66), channel_id=1, source_target_pairs={{0,15},{1,0},{2,1},{3,2},{4,3},{5,4},{6,5},{7,6},{8,7},{9,8},{10,9... | collective-permute-start | bytes 110600 | tf_op jit(solution)/shard_map/ppermute | solution.py:684
  29.9 11.6 %copy-start.2 = (s32[1,6144]{1,0:T(1,128)S(1)}, s32[1,6144]{1,0:T(1,128)}, u32[]{:S(2)}) copy-start(s32[1,6144]{1,0:T(1,128)} %cells.3) | copy-start | bytes 73732
  29.9 11.7 %copy-start.3 = (f32[1,32768]{1,0:T(1,128)S(1)}, f32[1,32768]{1,0:T(1,128)}, u32[]{:S(2)}) copy-start(f32[1,32768]{1,0:T(1,128)} %centre.1) | copy-start | bytes 393220
  29.9 11.7 %copy-start.4 = (f32[1,32768]{1,0:T(1,128)S(1)}, f32[1,32768]{1,0:T(1,128)}, u32[]{:S(2)}) copy-start(f32[1,32768]{1,0:T(1,128)} %lower.1) | copy-start | bytes 393220
  29.9 11.6 %copy-start.5 = (f32[1,32768]{1,0:T(1,128)S(1)}, f32[1,32768]{1,0:T(1,128)}, u32[]{:S(2)}) copy-start(f32[1,32768]{1,0:T(1,128)} %upper.1) | copy-start | bytes 393220
  29.9 10.0 %collective-permute-start.4 = (f32[32,1024]{1,0:T(8,128)S(1)}, f32[32,1024]{1,0:T(8,128)S(1)}, u32[]{:S(2)}, u32[]{:S(2)}) collective-permute-start(f32[32,1024]{1,0:T(8,128)S(1)} %get-tuple-element.67), channel_id=1, source_target_pairs={{0,15},{1,0},{2,1},{3,2},{4,3},{5,4},{6,5},{7,6},{8,7},{9,8},{10,9... | collective-permute-start | bytes 393224 | tf_op jit(solution)/shard_map/ppermute | solution.py:684
  31.9 8.4 %collective-permute-start.5 = (f32[32,1024]{1,0:T(8,128)S(1)}, f32[32,1024]{1,0:T(8,128)S(1)}, u32[]{:S(2)}, u32[]{:S(2)}) collective-permute-start(f32[32,1024]{1,0:T(8,128)S(1)} %get-tuple-element.68), channel_id=1, source_target_pairs={{0,1},{1,2},{2,3},{3,4},{4,5},{5,6},{6,7},{7,8},{8,9},{9,10},{10,1... | collective-permute-start | bytes 393224 | tf_op jit(solution)/shard_map/ppermute | solution.py:684
  40.4 8.0 %collective-permute-start.6 = (f32[48,1024]{1,0:T(8,128)S(1)}, f32[48,1024]{1,0:T(8,128)S(1)}, u32[]{:S(2)}, u32[]{:S(2)}) collective-permute-start(f32[48,1024]{1,0:T(8,128)S(1)} %get-tuple-element.69), channel_id=1, source_target_pairs={{0,16},{1,17},{2,18},{3,19},{4,20},{5,21},{6,22},{7,23},{8,24},{9,... | collective-permute-start | bytes 589832 | tf_op jit(solution)/shard_map/ppermute | solution.py:684
  40.4 9.0 %collective-permute-start.7 = (f32[48,1024]{1,0:T(8,128)S(1)}, f32[48,1024]{1,0:T(8,128)S(1)}, u32[]{:S(2)}, u32[]{:S(2)}) collective-permute-start(f32[48,1024]{1,0:T(8,128)S(1)} %get-tuple-element.70), channel_id=1, source_target_pairs={{0,32},{1,33},{2,34},{3,35},{4,36},{5,37},{6,38},{7,39},{8,40},{9,... | collective-permute-start | bytes 589832 | tf_op jit(solution)/shard_map/ppermute | solution.py:684
  66.2 7.2 %collective-permute-start.8 = (f32[48,1024]{1,0:T(8,128)S(1)}, f32[48,1024]{1,0:T(8,128)S(1)}, u32[]{:S(2)}, u32[]{:S(2)}) collective-permute-start(f32[48,1024]{1,0:T(8,128)S(1)} %at_receptors.1), channel_id=1, source_target_pairs={{0,112},{1,113},{2,114},{3,115},{4,116},{5,117},{6,118},{7,119},{8... | collective-permute-start | bytes 589832 | tf_op jit(solution)/shard_map/ppermute | solution.py:684
  68.0 8.5 %collective-permute-start.9 = (f32[48,1024]{1,0:T(8,128)S(1)}, f32[48,1024]{1,0:T(8,128)S(1)}, u32[]{:S(2)}, u32[]{:S(2)}) collective-permute-start(f32[48,1024]{1,0:T(8,128)S(1)} %get-tuple-element.88), channel_id=1, source_target_pairs={{0,96},{1,97},{2,98},{3,99},{4,100},{5,101},{6,102},{7,103},{8,104... | collective-permute-start | bytes 589832 | tf_op jit(solution)/shard_map/ppermute | solution.py:684
  76.5 14.6 %collective-permute-start.10 = (f32[32,1152]{1,0:T(8,128)S(1)}, f32[32,1152]{1,0:T(8,128)S(1)}, u32[]{:S(2)}, u32[]{:S(2)}) collective-permute-start(f32[32,1152]{1,0:T(8,128)S(1)} %get-tuple-element.93), channel_id=1, source_target_pairs={{0,1},{1,2},{2,3},{3,4},{4,5},{5,6},{6,7},{7,8},{8,9},{9,10},{10,1... | collective-permute-start | bytes 442376 | tf_op jit(solution)/shard_map/ppermute | solution.py:684
  76.6 14.6 %collective-permute-start.11 = (f32[32,1152]{1,0:T(8,128)S(1)}, f32[32,1152]{1,0:T(8,128)S(1)}, u32[]{:S(2)}, u32[]{:S(2)}) collective-permute-start(f32[32,1152]{1,0:T(8,128)S(1)} %get-tuple-element.94), channel_id=1, source_target_pairs={{0,15},{1,0},{2,1},{3,2},{4,3},{5,4},{6,5},{7,6},{8,7},{9,8},{10,9... | collective-permute-start | bytes 442376 | tf_op jit(solution)/shard_map/ppermute | solution.py:684
  114.6 1.3 collective-permute-start.12
  115.9 4.9 %collective-permute-start.15 = (f32[16,16]{1,0:T(8,128)S(1)}, f32[16,16]{1,0:T(8,128)S(1)}, u32[]{:S(2)}, u32[]{:S(2)}) collective-permute-start(f32[16,16]{1,0:T(8,128)S(1)} %add.30), channel_id=1, source_target_pairs={{0,32},{1,33},{2,34},{3,35},{4,36},{5,37},{6,38},{7,39},{8,40},{9,... | collective-permute-start | bytes 3080 | tf_op jit(solution)/shard_map/ppermute | solution.py:684
  115.9 4.9 %collective-permute-start.14 = (f32[16,16]{1,0:T(8,128)S(1)}, f32[16,16]{1,0:T(8,128)S(1)}, u32[]{:S(2)}, u32[]{:S(2)}) collective-permute-start(f32[16,16]{1,0:T(8,128)S(1)} %add.30), channel_id=1, source_target_pairs={{0,96},{1,97},{2,98},{3,99},{4,100},{5,101},{6,102},{7,103},{8,104... | collective-permute-start | bytes 3080 | tf_op jit(solution)/shard_map/ppermute | solution.py:684
  119.1 5.2 %collective-permute-start.13 = (f32[16,16]{1,0:T(8,128)S(1)}, f32[16,16]{1,0:T(8,128)S(1)}, u32[]{:S(2)}, u32[]{:S(2)}) collective-permute-start(f32[16,16]{1,0:T(8,128)S(1)} %add.30), channel_id=1, source_target_pairs={{0,64},{1,65},{2,66},{3,67},{4,68},{5,69},{6,70},{7,71},{8,72},{9,... | collective-permute-start | bytes 3080 | tf_op jit(solution)/shard_map/ppermute | solution.py:684
  124.3 4.9 %collective-permute-start.18 = (f32[16,16]{1,0:T(8,128)S(1)}, f32[16,16]{1,0:T(8,128)S(1)}, u32[]{:S(2)}, u32[]{:S(2)}) collective-permute-start(f32[16,16]{1,0:T(8,128)S(1)} %add_add_fusion.2), channel_id=1, source_target_pairs={{0,1},{1,2},{2,3},{3,0},{4,5},{5,6},{6,7},{7,4},{8,9},{9,10},{10,1... | collective-permute-start | bytes 3080 | tf_op jit(solution)/shard_map/ppermute | solution.py:684
  124.3 4.9 %collective-permute-start.17 = (f32[16,16]{1,0:T(8,128)S(1)}, f32[16,16]{1,0:T(8,128)S(1)}, u32[]{:S(2)}, u32[]{:S(2)}) collective-permute-start(f32[16,16]{1,0:T(8,128)S(1)} %add_add_fusion.2), channel_id=1, source_target_pairs={{0,3},{1,0},{2,1},{3,2},{4,7},{5,4},{6,5},{7,6},{8,11},{9,8},{10,9... | collective-permute-start | bytes 3080 | tf_op jit(solution)/shard_map/ppermute | solution.py:684
  127.5 5.2 %collective-permute-start.16 = (f32[16,16]{1,0:T(8,128)S(1)}, f32[16,16]{1,0:T(8,128)S(1)}, u32[]{:S(2)}, u32[]{:S(2)}) collective-permute-start(f32[16,16]{1,0:T(8,128)S(1)} %add_add_fusion.2), channel_id=1, source_target_pairs={{0,2},{1,3},{2,0},{3,1},{4,6},{5,7},{6,4},{7,5},{8,10},{9,11},{10,... | collective-permute-start | bytes 3080 | tf_op jit(solution)/shard_map/ppermute | solution.py:684
  132.7 4.9 %collective-permute-start.21 = (f32[16,16]{1,0:T(8,128)S(1)}, f32[16,16]{1,0:T(8,128)S(1)}, u32[]{:S(2)}, u32[]{:S(2)}) collective-permute-start(f32[16,16]{1,0:T(8,128)S(1)} %add_add_fusion.1), channel_id=1, source_target_pairs={{0,4},{1,5},{2,6},{3,7},{4,8},{5,9},{6,10},{7,11},{8,12},{9,13},{1... | collective-permute-start | bytes 3080 | tf_op jit(solution)/shard_map/ppermute | solution.py:684
  132.7 4.9 %collective-permute-start.20 = (f32[16,16]{1,0:T(8,128)S(1)}, f32[16,16]{1,0:T(8,128)S(1)}, u32[]{:S(2)}, u32[]{:S(2)}) collective-permute-start(f32[16,16]{1,0:T(8,128)S(1)} %add_add_fusion.1), channel_id=1, source_target_pairs={{0,12},{1,13},{2,14},{3,15},{4,0},{5,1},{6,2},{7,3},{8,4},{9,5},{1... | collective-permute-start | bytes 3080 | tf_op jit(solution)/shard_map/ppermute | solution.py:684
  135.9 5.2 %collective-permute-start.19 = (f32[16,16]{1,0:T(8,128)S(1)}, f32[16,16]{1,0:T(8,128)S(1)}, u32[]{:S(2)}, u32[]{:S(2)}) collective-permute-start(f32[16,16]{1,0:T(8,128)S(1)} %add_add_fusion.1), channel_id=1, source_target_pairs={{0,8},{1,9},{2,10},{3,11},{4,12},{5,13},{6,14},{7,15},{8,0},{9,1},... | collective-permute-start | bytes 3080 | tf_op jit(solution)/shard_map/ppermute | solution.py:684

commit v5 on v4

--- a/solution.py
+++ b/solution.py
@@ -21,7 +21,8 @@
 SLOTS = PARTNERS * FRINGE
 TILES = ROWS // LANES
 WAYS = 8
-SUMS = 16
+SUMS = 4
+QUARTER = SLOTS // 4
 UNROLL = 8
 
 AXES = ("grid", "cell")
@@ -95,7 +96,7 @@
         for n in range(UNROLL):
             q = low + j * UNROLL + n
             for w in range(WAYS):
-                step(w, n, q, parts[w][q])
+                step(w, q, parts[w][q])
         return carry
 
     lax.fori_loop(0, (high - low) // UNROLL, outer, 0)
@@ -104,7 +105,7 @@
 def gather_rows(table, parts, staged, phases):
     count = parts[0].shape[0]
 
-    def step(w, n, q, row):
+    def step(w, q, row):
         staged[pl.ds(w * count + q, 1), :] = table[pl.ds(row, 1), :]
 
     finish(phases[0])
@@ -126,12 +127,20 @@
 def add_rows(sums, parts, staged):
     count = parts[0].shape[0]
 
-    def step(w, n, q, row):
-        term = staged[pl.ds(w * count + q, 1), :]
-        total = sums[w + n % (SUMS // WAYS) * WAYS]
-        total[pl.ds(row, 1), :] = total[pl.ds(row, 1), :] + term
-
-    row_steps(parts, 0, count, step)
+    def outer(j, carry):
+        for n in range(UNROLL):
+            q = j * UNROLL + n
+            for half in range(2):
+                total = sums[half + n % 2 * 2]
+                lists = [2 * m + half for m in range(4)]
+                rows = [parts[w][q] for w in lists]
+                old = [total[pl.ds(row, 1), :] for row in rows]
+                new = [value + staged[pl.ds(w * count + q, 1), :] for value, w in zip(old, lists)]
+                for row, value in zip(rows, new):
+                    total[pl.ds(row, 1), :] = value
+        return carry
+
+    lax.fori_loop(0, count // UNROLL, outer, 0)
 
 
 def groups_of(cells, m, offset):
@@ -175,25 +184,60 @@
         each_block(many, step)
 
 
-def spread_fields(messages, cells, partners, weights, staged):
-    many = cells.shape[0]
+def spread_group(fields, cells, outs):
+    group = [value >> 12 for value in cells]
+    row = [value & (ROWS - 1) for value in cells]
+    terms = [[jnp.where(group[m] == g, fields[m][h], 0.0) for g in range(GROUPS) for h in range(2)] for m in range(4)]
+    for m in range(4):
+        same = [row[m] == row[i] for i in range(m)]
+        block = []
+        for v in range(2 * GROUPS):
+            value = terms[m][v]
+            for i in range(m):
+                value = value + jnp.where(same[i], terms[i][v], 0.0)
+            block.append(value)
+        ref, at = outs[m]
+        ref[aligned(at, LANES), :] = jnp.concatenate(block, axis=0).T
+
+
+def block_of(ref, row, column):
+    return jnp.broadcast_to(ref[row : row + 1, aligned(column, LANES)], (8, LANES))
+
+
+def field_of(place, b):
+    ref, row, column = place
+    return [ref[row + h * 8 : row + h * 8 + 8, aligned(column + b * LANES, LANES)] for h in range(2)]
+
+
+def spread_at_donors(messages, cells, partners, weights, staged):
     for n, k in enumerate(partners):
 
         def step(b):
-            ref, row, column = messages[k]
-            field = [ref[row + h * 8 : row + h * 8 + 8, aligned(column + b * LANES, LANES)] for h in range(2)]
-            for m in range(many):
-                group = groups_of(cells, m, k * FRINGE + b * LANES)
-                scaled = field
-                if weights is not None:
-                    ref, row, column = weights[k]
-                    scale = ref[row + m : row + m + 1, aligned(column + b * LANES, LANES)]
-                    scaled = [part * jnp.broadcast_to(scale, (8, LANES)) for part in field]
-                terms = [jnp.where(group == g, scaled[h], 0.0) for g in range(GROUPS) for h in range(2)]
-                at = aligned((m * len(partners) + n) * FRINGE + b * LANES, LANES)
-                staged[at, :] = jnp.concatenate(terms, axis=0).T
-
-        each_block(many, step)
+            field = field_of(messages[k], b)
+            ref, row, column = weights[k]
+            scale = [block_of(ref, row + m, column + b * LANES) for m in range(4)]
+            fields = [[part * scale[m] for part in field] for m in range(4)]
+            blocks = [block_of(cells, m, k * FRINGE + b * LANES) for m in range(4)]
+            spread_group(fields, blocks, [(staged, (m * len(partners) + n) * FRINGE + b * LANES) for m in range(4)])
+
+        each_block(4, step)
+
+
+def spread_at_receptors(messages, cells, staged):
+    for part in range(3):
+
+        def step(j, carry):
+            fields, blocks, outs = [], [], []
+            for m in range(4):
+                k, shift = divmod(m * QUARTER + part * 4 * LANES, FRINGE)
+                fields.append(field_of(messages[k], j + shift // LANES))
+                at = m * QUARTER + (part * 4 + j) * LANES
+                blocks.append(block_of(cells, 0, at))
+                outs.append((staged, at))
+            spread_group(fields, blocks, outs)
+            return carry
+
+        lax.fori_loop(0, 4, step, 0, unroll=2)
 
 
 def lanes(shape):
@@ -427,7 +471,7 @@
     every = NEAR + FAR
     phases = index_copies(rows_hbm, segments(1, every), parts, sem)
     phases_far = index_copies(rows_hbm, segments(1, FAR), parts_far, sem_far)
-    spread_fields(grid_places(near, far), cells, every, None, staged)
+    spread_at_receptors(grid_places(near, far), cells, staged)
     finish(phases[0] + phases[1])
     add_rows(sums, parts, staged)
 
@@ -538,7 +582,7 @@
     sums, staged, parts, sem = refs[:SUMS], refs[SUMS], refs[SUMS + 1 : SUMS + WAYS + 1], refs[SUMS + WAYS + 1]
     phases = index_copies(rows_hbm, segments(4, SAME), parts, sem)
     weights = weight_places(None, (near_weights, far_weights), None)
-    spread_fields(grid_places(near, far), cells, SAME, weights, staged)
+    spread_at_donors(grid_places(near, far), cells, SAME, weights, staged)
     finish(phases[0] + phases[1])
     add_rows(sums, parts, staged)
 
@@ -564,7 +608,7 @@
     parts, sem = refs[3 + SUMS : 3 + SUMS + WAYS], refs[3 + SUMS + WAYS]
     phases = index_copies(rows_hbm, segments(4, SIDES), parts, sem)
     weights = weight_places(before_weights, (None, None), after_weights)
-    spread_fields({**pair_places(BEFORE, before), **pair_places(AFTER, after)}, cells, SIDES, weights, staged)
+    spread_at_donors({**pair_places(BEFORE, before), **pair_places(AFTER, after)}, cells, SIDES, weights, staged)
     finish(phases[0] + phases[1])
     add_rows(sums, parts, staged)
     lane = lanes((1, LANES))

time: 147 us -> 137 us (0.932)
  Pallas kernels: 92.6 us -> 78.8 us
  waiting for transfers between devices: 20.8 us -> 25.1 us
    pallas_call x1, Pallas kernels: 23.4 us -> 18.7 us  [add_sides(): pl.pallas_call(donor_sides_kernel, out_shape=[resident(ROWS, LANES), jax....]
    ppermute x22, waiting for transfers between devices: 20.8 us -> 25.1 us  [moved(): return lax.ppermute(value, AXES, route)]
    pallas_call x1, Pallas kernels: 13.4 us -> 9.53 us  [couple(): pl.pallas_call(couple_kernel, out_shape=[resident(ROWS, LANES), TRIPLE] +...]
    pallas_call x1, Pallas kernels: 4.57 us -> 2.76 us  [transposed(): pl.pallas_call(transposed_kernel, out_shape=[resident(ROWS, LANES)] * SUM...]
    pallas_call x1, Pallas kernels: 9.2 us -> 7.5 us  [add_same(): pl.pallas_call(donor_same_kernel, out_shape=[resident(ROWS, LANES)] * SUM...]
    pallas_call x1, Pallas kernels: 6.82 us -> 5.19 us  [forward(): pl.pallas_call(forward_kernel, out_shape=[resident(ROWS, LANES)] * (3 + S...]
  transfers between devices with their start and end apart: 22 -> 22, of which waited for: 10 -> 12; matrix products, arithmetic and copies ran while one was open for 0% -> 0% of each run, Pallas kernels for 29% -> 28%
where the time goes in v5:
time: 137 us
  Pallas kernels  78.8 us (58%)
  starting transfers between devices  30.1 us (22%)
  waiting for transfers between devices  25.1 us (18%)
  local copies, waits for them, and re-layouts  1.63 us (1%)
    ppermute x22, starting transfers between devices, moved(): return lax.ppermute(value, AXES, route)  30.1 us
    ppermute x22, waiting for transfers between devices, moved(): return lax.ppermute(value, AXES, route)  25.1 us
    pallas_call x1, Pallas kernels, add_sides(): pl.pallas_call(donor_sides_kernel, out_shape=[resident(ROWS, LANES), jax....  18.7 us
    pallas_call x1, Pallas kernels, rows_at_sides(): pl.pallas_call(rows_kernel, out_shape=resident(len(segs) * FRINGE, LANES)...  11.8 us
    pallas_call x1, Pallas kernels, couple(): pl.pallas_call(couple_kernel, out_shape=[resident(ROWS, LANES), TRIPLE] +...  9.53 us
    pallas_call x1, Pallas kernels, same_sums(): pl.pallas_call(same_sums_kernel, out_shape=PAIR, in_specs=[VMEM, VMEM, HB...  7.9 us
    pallas_call x1, Pallas kernels, add_same(): pl.pallas_call(donor_same_kernel, out_shape=[resident(ROWS, LANES)] * SUM...  7.5 us
    pallas_call x1, Pallas kernels, basis_of(): pl.pallas_call(functools.partial(basis_kernel, total_cells), out_shape=[j...  5.93 us
  transfers between devices with their start and end apart: 22, of which 12 were waited for; matrix products, arithmetic and copies ran while one was open for 0% of the time, Pallas kernels for 28%

profile of v5, /device:TPU:0, one launch (start us, length us, event | category | flops | bytes accessed | tf_op | source)
XLA Modules:
  0.0 136.8 jit_solution(12740659424903460030)
XLA Ops:
  0.6 2.9 %collective-permute-start.1 = (f32[1,4,6144]{2,1,0:T(4,128)}, f32[1,4,6144]{2,1,0:T(4,128)S(1)}, u32[]{:S(2)}, u32[]{:S(2)}) collective-permute-start(f32[1,4,6144]{2,1,0:T(4,128)} %param.13), channel_id=1, source_target_pairs={{0,96},{1,97},{2,98},{3,99},{4,100},{5,101},{6,102},{7,103},{8,104... | collective-permute-start | bytes 294920 | tf_op jit(solution)/shard_map/ppermute | solution.py:728
  3.6 1.6 %copy-done.1 = f32[16,1,32768]{2,1,0:T(1,128)S(1)} copy-done((f32[16,1,32768]{2,1,0:T(1,128)S(1)}, f32[16,1,32768]{2,1,0:T(1,128)}, u32[]{:S(2)}) %copy-start.1) | copy-done | bytes 2097176
  5.2 2.7 %table.1 = f32[4096,128]{1,0:T(8,128)S(1)} custom-call(f32[16,1,32768]{2,1,0:T(1,128)S(1)} %copy-done.1), custom_call_target="tpu_custom_call" | custom-call | bytes 9000000 | tf_op jit(solution)/shard_map/table/pallas_call | solution.py:283
  7.9 0.0 copy-start
  7.9 0.0 collective-permute-done.1
  7.9 0.0 collective-permute-done
  7.9 1.6 %collective-permute-start.2 = (f32[8,1152]{1,0:T(8,128)S(1)}, f32[8,1152]{1,0:T(8,128)S(1)}, u32[]{:S(2)}, u32[]{:S(2)}) collective-permute-start(f32[8,1152]{1,0:T(8,128)S(1)} %get-tuple-element.29), channel_id=1, source_target_pairs={{0,1},{1,2},{2,3},{3,4},{4,5},{5,6},{6,7},{7,8},{8,9},{9,10},{10,1... | collective-permute-start | bytes 110600 | tf_op jit(solution)/shard_map/ppermute | solution.py:728
  9.6 5.0 %collective-permute-start.3 = (f32[8,1152]{1,0:T(8,128)S(1)}, f32[8,1152]{1,0:T(8,128)S(1)}, u32[]{:S(2)}, u32[]{:S(2)}) collective-permute-start(f32[8,1152]{1,0:T(8,128)S(1)} %get-tuple-element.30), channel_id=1, source_target_pairs={{0,15},{1,0},{2,1},{3,2},{4,3},{5,4},{6,5},{7,6},{8,7},{9,8},{10,9... | collective-permute-start | bytes 110600 | tf_op jit(solution)/shard_map/ppermute | solution.py:728
  14.6 11.8 %rows_at_sides.1.staged = f32[16384,128]{1,0:T(8,128)S(1)} custom-call(f32[4096,128]{1,0:T(8,128)S(1)} %table.1, s32[24576]{0:T(1024)S(1)} %bitcast.11), custom_call_target="tpu_custom_call" | custom-call | bytes 33000000 | tf_op jit(solution)/shard_map/rows_at_sides/pallas_call | solution.py:354
  26.4 0.0 collective-permute-done.3.after.after_weights
  26.5 3.4 %side_sums.1 = (f32[32,1024]{1,0:T(8,128)S(1)}, f32[32,1024]{1,0:T(8,128)S(1)}) custom-call(f32[16384,128]{1,0:T(8,128)S(1)} %rows_at_sides.1.staged, s32[4,6144]{1,0:T(4,128)S(1)} %bitcast.7, f32[8,1152]{1,0:T(8,128)S(1)} %collective-permute-done.2.before.before_weights, f32[8,1152]{1,0:T(8,128)S(1)} %collective-permute-done.3.after.after_weights), custom_call_target="tpu_custom_call" | custom-call | bytes 3000000 | tf_op jit(solution)/shard_map/side_sums/pallas_call | solution.py:323
  29.9 0.0 copy-start.2
  29.9 0.0 copy-start.3
  29.9 0.0 copy-start.4
  29.9 0.0 copy-start.5
  29.9 2.0 %collective-permute-start.4 = (f32[32,1024]{1,0:T(8,128)S(1)}, f32[32,1024]{1,0:T(8,128)S(1)}, u32[]{:S(2)}, u32[]{:S(2)}) collective-permute-start(f32[32,1024]{1,0:T(8,128)S(1)} %get-tuple-element.31), channel_id=1, source_target_pairs={{0,15},{1,0},{2,1},{3,2},{4,3},{5,4},{6,5},{7,6},{8,7},{9,8},{10,9... | collective-permute-start | bytes 393224 | tf_op jit(solution)/shard_map/ppermute | solution.py:728
  31.9 0.1 collective-permute-start.5
  32.0 7.9 %same_sums.1.same = f32[32,1024]{1,0:T(8,128)S(1)} custom-call(f32[4096,128]{1,0:T(8,128)S(1)} %table.1, s32[4,6144]{1,0:T(4,128)S(1)} %bitcast.8, s32[24576]{0:T(1024)S(1)} %bitcast.12, f32[4,6144]{1,0:T(4,128)S(1)} %bitcast.19, f32[4,6144]{1,0:T(4,128)S(1)} %bitcast.16), custom_call_target="tpu_custom_call" | custom-call | bytes 24000000 | tf_op jit(solution)/shard_map/same_sums/pallas_call | solution.py:387
  39.9 0.0 collective-permute-done.4.before
  39.9 0.4 collective-permute-done.5.after
  40.4 0.0 collective-permute-start.6
  40.4 1.1 collective-permute-start.7
  41.6 5.2 %forward.1 = (f32[4096,128]{1,0:T(8,128)S(1)}, f32[4096,128]{1,0:T(8,128)S(1)}, f32[4096,128]{1,0:T(8,128)S(1)}, f32[4096,128]{1,0:T(8,128)S(1)}, f32[4096,128]{...) custom-call(f32[4096,128]{1,0:T(8,128)S(1)} %table.1, f32[1,32768]{1,0:T(1,128)S(1)} %copy-done.3, ...), custom_call_target="tpu_custom_call" | custom-call | bytes 21000000 | tf_op jit(solution)/shard_map/forward/pallas_call | solution.py:453
  46.8 1.4 %collective-permute-done.6.near = f32[48,1024]{1,0:T(8,128)S(1)} collective-permute-done((f32[48,1024]{1,0:T(8,128)S(1)}, f32[48,1024]{1,0:T(8,128)S(1)}, u32[]{:S(2)}, u32[]{:S(2)}) %collective-permute-start.6) | collective-permute-done | bytes 196640 | tf_op jit(solution)/shard_map/ppermute | solution.py:728
  48.2 1.2 collective-permute-done.7.far
  49.4 9.5 %couple.1 = (f32[4096,128]{1,0:T(8,128)S(1)}, f32[48,1024]{1,0:T(8,128)S(1)}, f32[4096,128]{1,0:T(8,128)S(1)}, f32[4096,128]{1,0:T(8,128)S(1)}, f32[4096,128]{1,0:T(8,128)S(1)}, /*index=5*/f32[4096,128]{1,0:T(8,128)S(1)}) custom-call(s32[1,6144]{1,0:T(1,128)S(1)} %copy-done.2, ...), custom_call_target="tpu_custom_call", output_to_operand_aliasing={{2}: (4, {}), {3}: (5, {}), {4}: (6, {}), {5}: (7, {})} | custom-call | bytes 33000000 | tf_op jit(solution)/shard_map/couple/pallas_call | solution.py:492
  58.9 3.3 %at_receptors.1 = f32[48,1024]{1,0:T(8,128)S(1)} custom-call(f32[4096,128]{1,0:T(8,128)S(1)} %get-tuple-element.39.tangent, s32[1,6144]{1,0:T(1,128)S(1)} %copy-done.2, s32[6144]{0:T(1024)S(1)} %bitcast.22), custom_call_target="tpu_custom_call" | custom-call | bytes 9000000 | tf_op jit(solution)/shard_map/at_receptors/pallas_call | solution.py:516
  62.3 1.8 %collective-permute-start.8 = (f32[48,1024]{1,0:T(8,128)S(1)}, f32[48,1024]{1,0:T(8,128)S(1)}, u32[]{:S(2)}, u32[]{:S(2)}) collective-permute-start(f32[48,1024]{1,0:T(8,128)S(1)} %at_receptors.1), channel_id=1, source_target_pairs={{0,112},{1,113},{2,114},{3,115},{4,116},{5,117},{6,118},{7,119},{8... | collective-permute-start | bytes 589832 | tf_op jit(solution)/shard_map/ppermute | solution.py:728
  64.1 2.8 %transposed.1 = (f32[4096,128]{1,0:T(8,128)S(1)}, f32[4096,128]{1,0:T(8,128)S(1)}, f32[4096,128]{1,0:T(8,128)S(1)}, f32[4096,128]{1,0:T(8,128)S(1)}) custom-call(f32[4096,128]{1,0:T(8,128)S(1)} %get-tuple-element.39.tangent, f32[4096,128]{1,0:T(8,128)S(1)} %get-tuple-element.43.centre, f32[4096,128]{1,0:T(8,128)S(1)} %get-tuple-element.41.lower, ...), custom_call_target="tpu_custom_call" | custom-call | bytes 12000000 | tf_op jit(solution)/shard_map/transposed/pallas_call | solution.py:568
  66.8 2.0 %collective-permute-done.8.near = f32[48,1024]{1,0:T(8,128)S(1)} collective-permute-done((f32[48,1024]{1,0:T(8,128)S(1)}, f32[48,1024]{1,0:T(8,128)S(1)}, u32[]{:S(2)}, u32[]{:S(2)}) %collective-permute-start.8) | collective-permute-done | bytes 196640 | tf_op jit(solution)/shard_map/ppermute | solution.py:728
  68.9 3.7 %collective-permute-done.9.far = f32[48,1024]{1,0:T(8,128)S(1)} collective-permute-done((f32[48,1024]{1,0:T(8,128)S(1)}, f32[48,1024]{1,0:T(8,128)S(1)}, u32[]{:S(2)}, u32[]{:S(2)}) %collective-permute-start.9) | collective-permute-done | bytes 196640 | tf_op jit(solution)/shard_map/ppermute | solution.py:728
  72.6 0.1 collective-permute-start.10
  72.7 5.3 %collective-permute-start.11 = (f32[32,1152]{1,0:T(8,128)S(1)}, f32[32,1152]{1,0:T(8,128)S(1)}, u32[]{:S(2)}, u32[]{:S(2)}) collective-permute-start(f32[32,1152]{1,0:T(8,128)S(1)} %get-tuple-element.46), channel_id=1, source_target_pairs={{0,15},{1,0},{2,1},{3,2},{4,3},{5,4},{6,5},{7,6},{8,7},{9,8},{10,9... | collective-permute-start | bytes 442376 | tf_op jit(solution)/shard_map/ppermute | solution.py:728
  78.0 7.5 %add_same.1 = (f32[4096,128]{1,0:T(8,128)S(1)}, f32[4096,128]{1,0:T(8,128)S(1)}, f32[4096,128]{1,0:T(8,128)S(1)}, f32[4096,128]{1,0:T(8,128)S(1)}) custom-call(s32[4,6144]{1,0:T(4,128)S(1)} %bitcast.9, s32[24576]{0:T(1024)S(1)} %bitcast.13, f32[4,6144]{1,0:T(4,128)S(1)} %bitcast.20, ...), custom_call_target="tpu_custom_call", output_to_operand_aliasing={{0}: (6, {}), {1}: (7, {}), {2}: (8, {}), {3}: (9, {})} | custom-call | bytes 27000000 | tf_op jit(solution)/shard_map/add_same/pallas_call | solution.py:592
  85.6 18.7 %add_sides.1 = (f32[4096,128]{1,0:T(8,128)S(1)}, f32[16,16]{1,0:T(8,128)S(1)}, f32[4096,128]{1,0:T(8,128)S(1)}, f32[4096,128]{1,0:T(8,128)S(1)}, f32[4096,128]{1,0:T(8,128)S(1)}, /*index=5*/f32[4096,128]{1,0:T(8,128)S(1)}) custom-call(s32[4,6144]{1,0:T(4,128)S(1)} %bitcast.10, ...), custom_call_target="tpu_custom_call", output_to_operand_aliasing={{2}: (6, {}), {3}: (7, {}), {4}: (8, {}), {5}: (9, {})} | custom-call | bytes 54000000 | tf_op jit(solution)/shard_map/add_sides/pallas_call | solution.py:653
  104.3 0.1 collective-permute-start.12
  104.4 1.2 collective-permute-done.12
  105.5 3.2 %collective-permute-start.14 = (f32[16,16]{1,0:T(8,128)S(1)}, f32[16,16]{1,0:T(8,128)S(1)}, u32[]{:S(2)}, u32[]{:S(2)}) collective-permute-start(f32[16,16]{1,0:T(8,128)S(1)} %add.30), channel_id=1, source_target_pairs={{0,96},{1,97},{2,98},{3,99},{4,100},{5,101},{6,102},{7,103},{8,104... | collective-permute-start | bytes 3080 | tf_op jit(solution)/shard_map/ppermute | solution.py:728
  108.8 0.3 collective-permute-start.13
  109.1 1.3 collective-permute-done.15
  110.4 3.5 %collective-permute-done.13 = f32[16,16]{1,0:T(8,128)S(1)} collective-permute-done((f32[16,16]{1,0:T(8,128)S(1)}, f32[16,16]{1,0:T(8,128)S(1)}, u32[]{:S(2)}, u32[]{:S(2)}) %collective-permute-start.13) | collective-permute-done | bytes 1056 | tf_op jit(solution)/shard_map/ppermute | solution.py:728
  113.9 3.2 %collective-permute-start.17 = (f32[16,16]{1,0:T(8,128)S(1)}, f32[16,16]{1,0:T(8,128)S(1)}, u32[]{:S(2)}, u32[]{:S(2)}) collective-permute-start(f32[16,16]{1,0:T(8,128)S(1)} %add_add_fusion.2), channel_id=1, source_target_pairs={{0,3},{1,0},{2,1},{3,2},{4,7},{5,4},{6,5},{7,6},{8,11},{9,8},{10,9... | collective-permute-start | bytes 3080 | tf_op jit(solution)/shard_map/ppermute | solution.py:728
  117.2 1.6 %collective-permute-done.18 = f32[16,16]{1,0:T(8,128)S(1)} collective-permute-done((f32[16,16]{1,0:T(8,128)S(1)}, f32[16,16]{1,0:T(8,128)S(1)}, u32[]{:S(2)}, u32[]{:S(2)}) %collective-permute-start.18) | collective-permute-done | bytes 1056 | tf_op jit(solution)/shard_map/ppermute | solution.py:728
  118.8 3.5 %collective-permute-done.16 = f32[16,16]{1,0:T(8,128)S(1)} collective-permute-done((f32[16,16]{1,0:T(8,128)S(1)}, f32[16,16]{1,0:T(8,128)S(1)}, u32[]{:S(2)}, u32[]{:S(2)}) %collective-permute-start.16) | collective-permute-done | bytes 1056 | tf_op jit(solution)/shard_map/ppermute | solution.py:728
  122.3 3.2 %collective-permute-start.20 = (f32[16,16]{1,0:T(8,128)S(1)}, f32[16,16]{1,0:T(8,128)S(1)}, u32[]{:S(2)}, u32[]{:S(2)}) collective-permute-start(f32[16,16]{1,0:T(8,128)S(1)} %add_add_fusion.1), channel_id=1, source_target_pairs={{0,12},{1,13},{2,14},{3,15},{4,0},{5,1},{6,2},{7,3},{8,4},{9,5},{1... | collective-permute-start | bytes 3080 | tf_op jit(solution)/shard_map/ppermute | solution.py:728
  125.6 1.6 %collective-permute-done.21 = f32[16,16]{1,0:T(8,128)S(1)} collective-permute-done((f32[16,16]{1,0:T(8,128)S(1)}, f32[16,16]{1,0:T(8,128)S(1)}, u32[]{:S(2)}, u32[]{:S(2)}) %collective-permute-start.21) | collective-permute-done | bytes 1056 | tf_op jit(solution)/shard_map/ppermute | solution.py:728
  127.2 3.5 %collective-permute-done.19 = f32[16,16]{1,0:T(8,128)S(1)} collective-permute-done((f32[16,16]{1,0:T(8,128)S(1)}, f32[16,16]{1,0:T(8,128)S(1)}, u32[]{:S(2)}, u32[]{:S(2)}) %collective-permute-start.19) | collective-permute-done | bytes 1056 | tf_op jit(solution)/shard_map/ppermute | solution.py:728
  130.7 5.9 %basis.1 = (f32[16,1,32768]{2,1,0:T(1,128)}, f32[16,16]{1,0:T(8,128)}) custom-call(f32[16,16]{1,0:T(8,128)S(1)} %add_add_fusion.gram, f32[4096,128]{1,0:T(8,128)S(1)} %get-tuple-element.55.adjoint), custom_call_target="tpu_custom_call" | custom-call | bytes 18000000 | tf_op jit(solution)/shard_map/basis/pallas_call | solution.py:706
  (29 shorter events, 0.2 us)
Async XLA Ops:
  0.6 7.2 %collective-permute-start.1 = (f32[1,4,6144]{2,1,0:T(4,128)}, f32[1,4,6144]{2,1,0:T(4,128)S(1)}, u32[]{:S(2)}, u32[]{:S(2)}) collective-permute-start(f32[1,4,6144]{2,1,0:T(4,128)} %param.13), channel_id=1, source_target_pairs={{0,96},{1,97},{2,98},{3,99},{4,100},{5,101},{6,102},{7,103},{8,104... | collective-permute-start | bytes 294920 | tf_op jit(solution)/shard_map/ppermute | solution.py:728
  3.6 4.3 %collective-permute-start = (f32[1,4,6144]{2,1,0:T(4,128)}, f32[1,4,6144]{2,1,0:T(4,128)S(1)}, u32[]{:S(2)}, u32[]{:S(2)}) collective-permute-start(f32[1,4,6144]{2,1,0:T(4,128)} %param.13), channel_id=1, source_target_pairs={{0,112},{1,113},{2,114},{3,115},{4,116},{5,117},{6,118},{7,119},{8... | collective-permute-start | bytes 294920 | tf_op jit(solution)/shard_map/ppermute | solution.py:728
  3.6 1.6 %copy-start.1 = (f32[16,1,32768]{2,1,0:T(1,128)S(1)}, f32[16,1,32768]{2,1,0:T(1,128)}, u32[]{:S(2)}) copy-start(f32[16,1,32768]{2,1,0:T(1,128)} %probes.1) | copy-start | bytes 6291460
  7.9 6.7 %copy-start = (s32[1,4,6144]{2,1,0:T(4,128)S(1)}, s32[1,4,6144]{2,1,0:T(4,128)}, u32[]{:S(2)}) copy-start(s32[1,4,6144]{2,1,0:T(4,128)} %param.11) | copy-start | bytes 294916
  7.9 18.5 %collective-permute-start.2 = (f32[8,1152]{1,0:T(8,128)S(1)}, f32[8,1152]{1,0:T(8,128)S(1)}, u32[]{:S(2)}, u32[]{:S(2)}) collective-permute-start(f32[8,1152]{1,0:T(8,128)S(1)} %get-tuple-element.29), channel_id=1, source_target_pairs={{0,1},{1,2},{2,3},{3,4},{4,5},{5,6},{6,7},{7,8},{8,9},{9,10},{10,1... | collective-permute-start | bytes 110600 | tf_op jit(solution)/shard_map/ppermute | solution.py:728
  9.6 16.9 %collective-permute-start.3 = (f32[8,1152]{1,0:T(8,128)S(1)}, f32[8,1152]{1,0:T(8,128)S(1)}, u32[]{:S(2)}, u32[]{:S(2)}) collective-permute-start(f32[8,1152]{1,0:T(8,128)S(1)} %get-tuple-element.30), channel_id=1, source_target_pairs={{0,15},{1,0},{2,1},{3,2},{4,3},{5,4},{6,5},{7,6},{8,7},{9,8},{10,9... | collective-permute-start | bytes 110600 | tf_op jit(solution)/shard_map/ppermute | solution.py:728
  29.9 11.6 %copy-start.2 = (s32[1,6144]{1,0:T(1,128)S(1)}, s32[1,6144]{1,0:T(1,128)}, u32[]{:S(2)}) copy-start(s32[1,6144]{1,0:T(1,128)} %cells.3) | copy-start | bytes 73732
  29.9 11.7 %copy-start.3 = (f32[1,32768]{1,0:T(1,128)S(1)}, f32[1,32768]{1,0:T(1,128)}, u32[]{:S(2)}) copy-start(f32[1,32768]{1,0:T(1,128)} %centre.1) | copy-start | bytes 393220
  29.9 11.7 %copy-start.4 = (f32[1,32768]{1,0:T(1,128)S(1)}, f32[1,32768]{1,0:T(1,128)}, u32[]{:S(2)}) copy-start(f32[1,32768]{1,0:T(1,128)} %lower.1) | copy-start | bytes 393220
  29.9 11.6 %copy-start.5 = (f32[1,32768]{1,0:T(1,128)S(1)}, f32[1,32768]{1,0:T(1,128)}, u32[]{:S(2)}) copy-start(f32[1,32768]{1,0:T(1,128)} %upper.1) | copy-start | bytes 393220
  29.9 10.0 %collective-permute-start.4 = (f32[32,1024]{1,0:T(8,128)S(1)}, f32[32,1024]{1,0:T(8,128)S(1)}, u32[]{:S(2)}, u32[]{:S(2)}) collective-permute-start(f32[32,1024]{1,0:T(8,128)S(1)} %get-tuple-element.31), channel_id=1, source_target_pairs={{0,15},{1,0},{2,1},{3,2},{4,3},{5,4},{6,5},{7,6},{8,7},{9,8},{10,9... | collective-permute-start | bytes 393224 | tf_op jit(solution)/shard_map/ppermute | solution.py:728
  31.9 8.4 %collective-permute-start.5 = (f32[32,1024]{1,0:T(8,128)S(1)}, f32[32,1024]{1,0:T(8,128)S(1)}, u32[]{:S(2)}, u32[]{:S(2)}) collective-permute-start(f32[32,1024]{1,0:T(8,128)S(1)} %get-tuple-element.32), channel_id=1, source_target_pairs={{0,1},{1,2},{2,3},{3,4},{4,5},{5,6},{6,7},{7,8},{8,9},{9,10},{10,1... | collective-permute-start | bytes 393224 | tf_op jit(solution)/shard_map/ppermute | solution.py:728
  40.4 7.8 %collective-permute-start.6 = (f32[48,1024]{1,0:T(8,128)S(1)}, f32[48,1024]{1,0:T(8,128)S(1)}, u32[]{:S(2)}, u32[]{:S(2)}) collective-permute-start(f32[48,1024]{1,0:T(8,128)S(1)} %get-tuple-element.33), channel_id=1, source_target_pairs={{0,16},{1,17},{2,18},{3,19},{4,20},{5,21},{6,22},{7,23},{8,24},{9,... | collective-permute-start | bytes 589832 | tf_op jit(solution)/shard_map/ppermute | solution.py:728
  40.4 9.0 %collective-permute-start.7 = (f32[48,1024]{1,0:T(8,128)S(1)}, f32[48,1024]{1,0:T(8,128)S(1)}, u32[]{:S(2)}, u32[]{:S(2)}) collective-permute-start(f32[48,1024]{1,0:T(8,128)S(1)} %get-tuple-element.34), channel_id=1, source_target_pairs={{0,32},{1,33},{2,34},{3,35},{4,36},{5,37},{6,38},{7,39},{8,40},{9,... | collective-permute-start | bytes 589832 | tf_op jit(solution)/shard_map/ppermute | solution.py:728
  62.3 6.6 %collective-permute-start.8 = (f32[48,1024]{1,0:T(8,128)S(1)}, f32[48,1024]{1,0:T(8,128)S(1)}, u32[]{:S(2)}, u32[]{:S(2)}) collective-permute-start(f32[48,1024]{1,0:T(8,128)S(1)} %at_receptors.1), channel_id=1, source_target_pairs={{0,112},{1,113},{2,114},{3,115},{4,116},{5,117},{6,118},{7,119},{8... | collective-permute-start | bytes 589832 | tf_op jit(solution)/shard_map/ppermute | solution.py:728
  64.1 8.5 %collective-permute-start.9 = (f32[48,1024]{1,0:T(8,128)S(1)}, f32[48,1024]{1,0:T(8,128)S(1)}, u32[]{:S(2)}, u32[]{:S(2)}) collective-permute-start(f32[48,1024]{1,0:T(8,128)S(1)} %get-tuple-element.40), channel_id=1, source_target_pairs={{0,96},{1,97},{2,98},{3,99},{4,100},{5,101},{6,102},{7,103},{8,104... | collective-permute-start | bytes 589832 | tf_op jit(solution)/shard_map/ppermute | solution.py:728
  72.6 12.9 %collective-permute-start.10 = (f32[32,1152]{1,0:T(8,128)S(1)}, f32[32,1152]{1,0:T(8,128)S(1)}, u32[]{:S(2)}, u32[]{:S(2)}) collective-permute-start(f32[32,1152]{1,0:T(8,128)S(1)} %get-tuple-element.45), channel_id=1, source_target_pairs={{0,1},{1,2},{2,3},{3,4},{4,5},{5,6},{6,7},{7,8},{8,9},{9,10},{10,1... | collective-permute-start | bytes 442376 | tf_op jit(solution)/shard_map/ppermute | solution.py:728
  72.7 12.9 %collective-permute-start.11 = (f32[32,1152]{1,0:T(8,128)S(1)}, f32[32,1152]{1,0:T(8,128)S(1)}, u32[]{:S(2)}, u32[]{:S(2)}) collective-permute-start(f32[32,1152]{1,0:T(8,128)S(1)} %get-tuple-element.46), channel_id=1, source_target_pairs={{0,15},{1,0},{2,1},{3,2},{4,3},{5,4},{6,5},{7,6},{8,7},{9,8},{10,9... | collective-permute-start | bytes 442376 | tf_op jit(solution)/shard_map/ppermute | solution.py:728
  104.3 1.3 collective-permute-start.12
  105.5 4.9 %collective-permute-start.15 = (f32[16,16]{1,0:T(8,128)S(1)}, f32[16,16]{1,0:T(8,128)S(1)}, u32[]{:S(2)}, u32[]{:S(2)}) collective-permute-start(f32[16,16]{1,0:T(8,128)S(1)} %add.30), channel_id=1, source_target_pairs={{0,32},{1,33},{2,34},{3,35},{4,36},{5,37},{6,38},{7,39},{8,40},{9,... | collective-permute-start | bytes 3080 | tf_op jit(solution)/shard_map/ppermute | solution.py:728
  105.5 4.9 %collective-permute-start.14 = (f32[16,16]{1,0:T(8,128)S(1)}, f32[16,16]{1,0:T(8,128)S(1)}, u32[]{:S(2)}, u32[]{:S(2)}) collective-permute-start(f32[16,16]{1,0:T(8,128)S(1)} %add.30), channel_id=1, source_target_pairs={{0,96},{1,97},{2,98},{3,99},{4,100},{5,101},{6,102},{7,103},{8,104... | collective-permute-start | bytes 3080 | tf_op jit(solution)/shard_map/ppermute | solution.py:728
  108.8 5.2 %collective-permute-start.13 = (f32[16,16]{1,0:T(8,128)S(1)}, f32[16,16]{1,0:T(8,128)S(1)}, u32[]{:S(2)}, u32[]{:S(2)}) collective-permute-start(f32[16,16]{1,0:T(8,128)S(1)} %add.30), channel_id=1, source_target_pairs={{0,64},{1,65},{2,66},{3,67},{4,68},{5,69},{6,70},{7,71},{8,72},{9,... | collective-permute-start | bytes 3080 | tf_op jit(solution)/shard_map/ppermute | solution.py:728
  113.9 4.9 %collective-permute-start.18 = (f32[16,16]{1,0:T(8,128)S(1)}, f32[16,16]{1,0:T(8,128)S(1)}, u32[]{:S(2)}, u32[]{:S(2)}) collective-permute-start(f32[16,16]{1,0:T(8,128)S(1)} %add_add_fusion.2), channel_id=1, source_target_pairs={{0,1},{1,2},{2,3},{3,0},{4,5},{5,6},{6,7},{7,4},{8,9},{9,10},{10,1... | collective-permute-start | bytes 3080 | tf_op jit(solution)/shard_map/ppermute | solution.py:728
  113.9 4.9 %collective-permute-start.17 = (f32[16,16]{1,0:T(8,128)S(1)}, f32[16,16]{1,0:T(8,128)S(1)}, u32[]{:S(2)}, u32[]{:S(2)}) collective-permute-start(f32[16,16]{1,0:T(8,128)S(1)} %add_add_fusion.2), channel_id=1, source_target_pairs={{0,3},{1,0},{2,1},{3,2},{4,7},{5,4},{6,5},{7,6},{8,11},{9,8},{10,9... | collective-permute-start | bytes 3080 | tf_op jit(solution)/shard_map/ppermute | solution.py:728
  117.2 5.2 %collective-permute-start.16 = (f32[16,16]{1,0:T(8,128)S(1)}, f32[16,16]{1,0:T(8,128)S(1)}, u32[]{:S(2)}, u32[]{:S(2)}) collective-permute-start(f32[16,16]{1,0:T(8,128)S(1)} %add_add_fusion.2), channel_id=1, source_target_pairs={{0,2},{1,3},{2,0},{3,1},{4,6},{5,7},{6,4},{7,5},{8,10},{9,11},{10,... | collective-permute-start | bytes 3080 | tf_op jit(solution)/shard_map/ppermute | solution.py:728
  122.3 4.9 %collective-permute-start.21 = (f32[16,16]{1,0:T(8,128)S(1)}, f32[16,16]{1,0:T(8,128)S(1)}, u32[]{:S(2)}, u32[]{:S(2)}) collective-permute-start(f32[16,16]{1,0:T(8,128)S(1)} %add_add_fusion.1), channel_id=1, source_target_pairs={{0,4},{1,5},{2,6},{3,7},{4,8},{5,9},{6,10},{7,11},{8,12},{9,13},{1... | collective-permute-start | bytes 3080 | tf_op jit(solution)/shard_map/ppermute | solution.py:728
  122.3 4.9 %collective-permute-start.20 = (f32[16,16]{1,0:T(8,128)S(1)}, f32[16,16]{1,0:T(8,128)S(1)}, u32[]{:S(2)}, u32[]{:S(2)}) collective-permute-start(f32[16,16]{1,0:T(8,128)S(1)} %add_add_fusion.1), channel_id=1, source_target_pairs={{0,12},{1,13},{2,14},{3,15},{4,0},{5,1},{6,2},{7,3},{8,4},{9,5},{1... | collective-permute-start | bytes 3080 | tf_op jit(solution)/shard_map/ppermute | solution.py:728
  125.6 5.2 %collective-permute-start.19 = (f32[16,16]{1,0:T(8,128)S(1)}, f32[16,16]{1,0:T(8,128)S(1)}, u32[]{:S(2)}, u32[]{:S(2)}) collective-permute-start(f32[16,16]{1,0:T(8,128)S(1)} %add_add_fusion.1), channel_id=1, source_target_pairs={{0,8},{1,9},{2,10},{3,11},{4,12},{5,13},{6,14},{7,15},{8,0},{9,1},... | collective-permute-start | bytes 3080 | tf_op jit(solution)/shard_map/ppermute | solution.py:728

commit v6 on v5

--- a/solution.py
+++ b/solution.py
@@ -286,7 +286,7 @@
         in_specs=[FIXED],
         out_specs=VMEM,
         scratch_shapes=[pltpu.VMEM((PROBES, GROUPS * ROWS), f32), pltpu.SemaphoreType.DMA((PROBES,))],
-        compiler_params=params(8),
+        compiler_params=params(60),
         cost_estimate=cost(3),
         name="table",
     )(probes)
@@ -540,7 +540,7 @@
     return simple_call(return_relay_kernel, [shape] * 2, (near, far, tangent, lower, upper, ready), "return_relay")
 
 
-def transposed_kernel(tangent, centre, lower, upper, *rest):
+def transposed_kernel(tangent, centre, lower, upper, ready, *rest):
     sums, raised, lowered = rest[:SUMS], rest[SUMS], rest[SUMS + 1]
 
     def products(start):
@@ -564,17 +564,17 @@
     clear(sums[1:])
 
 
-def transposed(tangent, centre, lower, upper):
+def transposed(tangent, centre, lower, upper, ready):
     return pl.pallas_call(
         transposed_kernel,
         out_shape=[resident(ROWS, LANES)] * SUMS,
-        in_specs=[VMEM] * 4,
+        in_specs=[VMEM] * 5,
         out_specs=[VMEM] * SUMS,
         scratch_shapes=[pltpu.VMEM((ROWS + 16, LANES), f32)] * 2,
         compiler_params=params(8),
-        cost_estimate=cost(4),
+        cost_estimate=cost(1),
         name="transposed",
-    )(tangent, centre, lower, upper)
+    )(tangent, centre, lower, upper, ready)
 
 
 def donor_same_kernel(cells, rows_hbm, near_weights, far_weights, near, far, *refs):
@@ -600,6 +600,16 @@
         cost_estimate=cost(9),
         name="add_same",
     )(cells, rows, near_weights, far_weights, near, far, *sums)
+
+
+def sum_of_groups(value):
+    for shift in (64, 32, 16):
+        value = value + pltpu.roll(value, shift, 1)
+    return value
+
+
+def own_group():
+    return lanes((8, LANES)) // PROBES == lax.broadcasted_iota(i32, (8, LANES), 0)
 
 
 def donor_sides_kernel(cells, rows_hbm, before_weights, after_weights, before, after, *refs):
@@ -643,16 +653,16 @@
     folded = jnp.zeros((PROBES, LANES), f32)
     for g in range(GROUPS):
         folded = folded + jnp.where(group == g, product[g * PROBES : (g + 1) * PROBES, :], 0.0)
-    for shift in (64, 32, 16):
-        folded = folded + pltpu.roll(folded, shift, 1)
-    gram[...] = folded[:, :PROBES]
+    folded = sum_of_groups(folded)
+    for n in range(2):
+        gram[n : n + 1, :] = jnp.sum(jnp.where(own_group(), folded[n * 8 : n * 8 + 8, :], 0.0), axis=0, keepdims=True)
 
 
 def add_sides(cells, rows, before_weights, after_weights, before, after, sums):
     segs = segments(4, SIDES)
     outs = pl.pallas_call(
         donor_sides_kernel,
-        out_shape=[resident(ROWS, LANES), jax.ShapeDtypeStruct((PROBES, PROBES), f32)]
+        out_shape=[resident(ROWS, LANES), jax.ShapeDtypeStruct((2, LANES), f32)]
         + [resident(ROWS, LANES)] * SUMS,
         in_specs=[VMEM, HBM] + [VMEM] * (4 + SUMS),
         out_specs=[VMEM] * (2 + SUMS),
@@ -666,18 +676,25 @@
 
 
 def basis_kernel(total_cells, gram, adjoint, basis, factor, natural, sem):
-    row = lax.broadcasted_iota(i32, (PROBES, 1), 0)
-    left = gram[...] / f32(total_cells)
-    right = jnp.where(lax.broadcasted_iota(i32, (PROBES, LANES), 0) == lanes((PROBES, LANES)) % PROBES, 1.0, 0.0)
+    row = lax.broadcasted_iota(i32, (PROBES, LANES), 0)
+    lane = lanes((PROBES, LANES))
+    whole = jnp.concatenate(
+        [sum_of_groups(jnp.where(own_group(), jnp.broadcast_to(gram[n : n + 1, :], (8, LANES)), 0.0)) for n in range(2)],
+        axis=0,
+    ) / f32(total_cells)
+    columns = [jnp.broadcast_to(whole[:, j : j + 1], (PROBES, LANES)) for j in range(PROBES)]
+    right = jnp.where(row == lane % PROBES, 1.0, 0.0)
+    result = jnp.zeros((PROBES, LANES), f32)
     for j in range(PROBES):
-        pivot = left[j : j + 1, j : j + 1]
-        ratio = jnp.where(row > j, left[:, j : j + 1] / pivot, 0.0)
+        pivot = columns[j][j : j + 1, :]
         root = jnp.sqrt(pivot)
-        left_row, right_row = left[j : j + 1, :], right[j : j + 1, :]
-        left = jnp.where(row == j, left_row / root, left - ratio * left_row)
+        ratio = jnp.where(row > j, columns[j] / pivot, 0.0)
+        result = jnp.where((lane == j) & (row >= j), columns[j] / root, result)
+        right_row = right[j : j + 1, :]
         right = jnp.where(row == j, right_row / root, right - ratio * right_row)
-    down = lax.broadcasted_iota(i32, (PROBES, PROBES), 0)
-    factor[...] = jnp.where(lanes((PROBES, PROBES)) >= down, left, 0.0).T
+        for n in range(j + 1, PROBES):
+            columns[n] = columns[n] - ratio * columns[n][j : j + 1, :]
+    factor[...] = result[:, :PROBES]
     inverse = jnp.concatenate([right] * GROUPS, axis=0)
     same = lax.broadcasted_iota(i32, (LANES, LANES), 0) // PROBES == lanes((LANES, LANES)) // PROBES
     high, low = split(jnp.where(same, inverse, 0.0))
@@ -693,12 +710,13 @@
                 natural[:, aligned(g * ROWS + tile * LANES, LANES)] = block[g * PROBES : (g + 1) * PROBES, :]
         return carry
 
-    lax.fori_loop(0, TILES // 4, step, 0)
-    copies = [
-        pltpu.make_async_copy(natural.at[pl.ds(p, 1), :], basis.at[p], sem.at[p]) for p in range(PROBES)
-    ]
-    for copy in copies:
-        copy.start()
+    copies = []
+    for quarter in range(4):
+        lax.fori_loop(quarter * TILES // 16, (quarter + 1) * TILES // 16, step, 0)
+        for g in range(GROUPS):
+            at = pl.ds(g * ROWS + quarter * ROWS // 4, ROWS // 4)
+            copies.append(pltpu.make_async_copy(natural.at[:, at], basis.at[:, 0, at], sem.at[len(copies)]))
+            copies[-1].start()
     finish(copies)
 
 
@@ -711,7 +729,7 @@
         ],
         in_specs=[VMEM] * 2,
         out_specs=[FIXED, VMEM],
-        scratch_shapes=[pltpu.VMEM((PROBES, GROUPS * ROWS), f32), pltpu.SemaphoreType.DMA((PROBES,))],
+        scratch_shapes=[pltpu.VMEM((PROBES, GROUPS * ROWS), f32), pltpu.SemaphoreType.DMA((4 * GROUPS,))],
         compiler_params=params(8),
         cost_estimate=cost(6),
         name="basis",
@@ -736,16 +754,9 @@
     return moved(value, lambda g, c: (g, c + distance))
 
 
-def ring_sum(value, step):
-    after, across, before = (moved(value, lambda g, c, n=n: step(g, c, n)) for n in (1, 2, 3))
-    return (value + across) + (before + after)
-
-
-def summed(value):
-    value = value + moved(value, lambda g, c: (g ^ 1, c))
-    value = ring_sum(value, lambda g, c, n: (g + 2 * n, c))
-    value = ring_sum(value, lambda g, c, n: (g, (c & 12) | ((c + n) & 3)))
-    return ring_sum(value, lambda g, c, n: (g, c + 4 * n))
+def axis_sum(value, axis):
+    copies = jnp.broadcast_to(value, (lax.axis_size(axis),) + value.shape)
+    return jnp.sum(lax.all_to_all(copies, axis, 0, 0), axis=0)
 
 
 def body(probes, centre, lower_coef, upper_coef, donor_cells, receptor_cells, weights):
@@ -766,13 +777,13 @@
     tangent, far = couple(receptor_cells, receptor_rows, near, far, sums)
     far = along_grid(far, -2)
     near = along_grid(at_receptors(tangent, receptor_cells, receptor_rows), -1)
-    sums = transposed(tangent, c, l, u)
+    sums = transposed(tangent, c, l, u, far)
     up, down = return_relay(near, far, tangent, l, u, sums[-1])
     before, after = along_cell(up, 1), along_cell(down, -1)
     sums = add_same(donors, donor_rows, near_weights, far_weights, near, far, sums)
     adjoint, gram = add_sides(donors, donor_rows, before_weights, after_weights, before, after, sums)
     total_cells = lax.axis_size("grid") * lax.axis_size("cell") * probes.shape[2]
-    basis, factor = basis_of(total_cells, summed(gram), adjoint)
+    basis, factor = basis_of(total_cells, axis_sum(axis_sum(gram, "grid"), "cell"), adjoint)
     return (basis, factor)
 
 

time: 137 us -> 125 us (0.912)
  waiting for transfers between devices: 25.1 us -> 5.52 us
  blocking collectives: 0 us -> 19.5 us
  starting transfers between devices: 30.1 us -> 20.5 us
  local copies, waits for them, and re-layouts: 1.63 us -> 0.05 us
    ppermute x22 -> x12, waiting for transfers between devices: 25.1 us -> 5.52 us  [moved(): return lax.ppermute(value, AXES, route)]
    all_to_all x0 -> x2, blocking collectives: none -> 19.5 us  [axis_sum(): return jnp.sum(lax.all_to_all(copies, axis, 0, 0), axis=0)]
    ppermute x22 -> x12, starting transfers between devices: 30.1 us -> 20.5 us  [moved(): return lax.ppermute(value, AXES, route)]
    unnamed x13 -> x11, local copies, waits for them, and re-layouts: 1.63 us -> 0.04 us
  transfers between devices with their start and end apart: 22 -> 12, of which waited for: 12 -> 5; matrix products, arithmetic and copies ran while one was open for 0% -> 0% of each run, Pallas kernels for 28% -> 33%
where the time goes in v6:
time: 125 us; the launch traced here: 124 us
  Pallas kernels  77.8 us (62%)
  starting transfers between devices  20.5 us (16%)
  blocking collectives  19.5 us (16%)
  waiting for transfers between devices  5.52 us (4%)
    ppermute x12, starting transfers between devices, moved(): return lax.ppermute(value, AXES, route)  20.5 us
    all_to_all x2, blocking collectives, axis_sum(): return jnp.sum(lax.all_to_all(copies, axis, 0, 0), axis=0)  19.5 us
    pallas_call x1, Pallas kernels, add_sides(): pl.pallas_call(donor_sides_kernel, out_shape=[resident(ROWS, LANES), jax....  18.7 us
    pallas_call x1, Pallas kernels, rows_at_sides(): pl.pallas_call(rows_kernel, out_shape=resident(len(segs) * FRINGE, LANES)...  11.8 us
    pallas_call x1, Pallas kernels, couple(): pl.pallas_call(couple_kernel, out_shape=[resident(ROWS, LANES), TRIPLE] +...  9.52 us
    pallas_call x1, Pallas kernels, same_sums(): pl.pallas_call(same_sums_kernel, out_shape=PAIR, in_specs=[VMEM, VMEM, HB...  7.9 us
    pallas_call x1, Pallas kernels, add_same(): pl.pallas_call(donor_same_kernel, out_shape=[resident(ROWS, LANES)] * SUM...  7.5 us
    ppermute x12, waiting for transfers between devices, moved(): return lax.ppermute(value, AXES, route)  5.52 us
  transfers between devices with their start and end apart: 12, of which 5 were waited for; matrix products, arithmetic and copies ran while one was open for 0% of the time, Pallas kernels for 33%

profile of v6, /device:TPU:0, one launch (start us, length us, event | category | flops | bytes accessed | tf_op | source)
XLA Modules:
  0.0 124.4 jit_solution(13549723705865408242)
XLA Ops:
  0.6 2.9 %collective-permute-start.1 = (f32[1,4,6144]{2,1,0:T(4,128)}, f32[1,4,6144]{2,1,0:T(4,128)S(1)}, u32[]{:S(2)}, u32[]{:S(2)}) collective-permute-start(f32[1,4,6144]{2,1,0:T(4,128)} %param.13), channel_id=1, source_target_pairs={{0,96},{1,97},{2,98},{3,99},{4,100},{5,101},{6,102},{7,103},{8,104... | collective-permute-start | bytes 294920 | tf_op jit(solution)/shard_map/ppermute | solution.py:746
  3.6 0.0 collective-permute-start
  3.6 2.8 %table.1 = f32[4096,128]{1,0:T(8,128)S(1)} custom-call(f32[16,1,32768]{2,1,0:T(1,128)} %probes.1), custom_call_target="tpu_custom_call" | custom-call | bytes 9000000 | tf_op jit(solution)/shard_map/table/pallas_call | solution.py:283
  6.4 0.0 copy-start
  6.4 0.0 collective-permute-done.1
  6.4 0.7 collective-permute-done
  7.1 1.6 %collective-permute-start.2 = (f32[8,1152]{1,0:T(8,128)S(1)}, f32[8,1152]{1,0:T(8,128)S(1)}, u32[]{:S(2)}, u32[]{:S(2)}) collective-permute-start(f32[8,1152]{1,0:T(8,128)S(1)} %get-tuple-element.29), channel_id=1, source_target_pairs={{0,1},{1,2},{2,3},{3,4},{4,5},{5,6},{6,7},{7,8},{8,9},{9,10},{10,1... | collective-permute-start | bytes 110600 | tf_op jit(solution)/shard_map/ppermute | solution.py:746
  8.7 5.0 %collective-permute-start.3 = (f32[8,1152]{1,0:T(8,128)S(1)}, f32[8,1152]{1,0:T(8,128)S(1)}, u32[]{:S(2)}, u32[]{:S(2)}) collective-permute-start(f32[8,1152]{1,0:T(8,128)S(1)} %get-tuple-element.30), channel_id=1, source_target_pairs={{0,15},{1,0},{2,1},{3,2},{4,3},{5,4},{6,5},{7,6},{8,7},{9,8},{10,9... | collective-permute-start | bytes 110600 | tf_op jit(solution)/shard_map/ppermute | solution.py:746
  13.7 0.0 copy-done
  13.8 11.8 %rows_at_sides.1.staged = f32[16384,128]{1,0:T(8,128)S(1)} custom-call(f32[4096,128]{1,0:T(8,128)S(1)} %table.1, s32[24576]{0:T(1024)S(1)} %bitcast.11), custom_call_target="tpu_custom_call" | custom-call | bytes 33000000 | tf_op jit(solution)/shard_map/rows_at_sides/pallas_call | solution.py:354
  25.6 0.0 collective-permute-done.2.before.before_weights
  25.6 0.0 collective-permute-done.3.after.after_weights
  25.6 3.4 %side_sums.1 = (f32[32,1024]{1,0:T(8,128)S(1)}, f32[32,1024]{1,0:T(8,128)S(1)}) custom-call(f32[16384,128]{1,0:T(8,128)S(1)} %rows_at_sides.1.staged, s32[4,6144]{1,0:T(4,128)S(1)} %bitcast.7, f32[8,1152]{1,0:T(8,128)S(1)} %collective-permute-done.2.before.before_weights, f32[8,1152]{1,0:T(8,128)S(1)} %collective-permute-done.3.after.after_weights), custom_call_target="tpu_custom_call" | custom-call | bytes 3000000 | tf_op jit(solution)/shard_map/side_sums/pallas_call | solution.py:323
  29.0 0.0 copy-start.1
  29.1 0.0 copy-start.2
  29.1 0.0 copy-start.3
  29.1 0.0 copy-start.4
  29.1 2.0 %collective-permute-start.4 = (f32[32,1024]{1,0:T(8,128)S(1)}, f32[32,1024]{1,0:T(8,128)S(1)}, u32[]{:S(2)}, u32[]{:S(2)}) collective-permute-start(f32[32,1024]{1,0:T(8,128)S(1)} %get-tuple-element.31), channel_id=1, source_target_pairs={{0,15},{1,0},{2,1},{3,2},{4,3},{5,4},{6,5},{7,6},{8,7},{9,8},{10,9... | collective-permute-start | bytes 393224 | tf_op jit(solution)/shard_map/ppermute | solution.py:746
  31.1 0.1 collective-permute-start.5
  31.2 7.9 %same_sums.1.same = f32[32,1024]{1,0:T(8,128)S(1)} custom-call(f32[4096,128]{1,0:T(8,128)S(1)} %table.1, s32[4,6144]{1,0:T(4,128)S(1)} %bitcast.8, s32[24576]{0:T(1024)S(1)} %bitcast.12, f32[4,6144]{1,0:T(4,128)S(1)} %bitcast.19, f32[4,6144]{1,0:T(4,128)S(1)} %bitcast.16), custom_call_target="tpu_custom_call" | custom-call | bytes 24000000 | tf_op jit(solution)/shard_map/same_sums/pallas_call | solution.py:387
  39.1 0.0 collective-permute-done.4.before
  39.1 0.3 collective-permute-done.5.after
  39.4 0.0 collective-permute-start.6
  39.4 0.6 collective-permute-start.7
  40.1 0.0 copy-done.1
  40.1 0.0 copy-done.2
  40.1 0.0 copy-done.3
  40.1 0.0 copy-done.4
  40.1 5.2 %forward.1 = (f32[4096,128]{1,0:T(8,128)S(1)}, f32[4096,128]{1,0:T(8,128)S(1)}, f32[4096,128]{1,0:T(8,128)S(1)}, f32[4096,128]{1,0:T(8,128)S(1)}, f32[4096,128]{...) custom-call(f32[4096,128]{1,0:T(8,128)S(1)} %table.1, f32[1,32768]{1,0:T(1,128)S(1)} %copy-done.2, ...), custom_call_target="tpu_custom_call" | custom-call | bytes 21000000 | tf_op jit(solution)/shard_map/forward/pallas_call | solution.py:453
  45.3 1.9 %collective-permute-done.6.near = f32[48,1024]{1,0:T(8,128)S(1)} collective-permute-done((f32[48,1024]{1,0:T(8,128)S(1)}, f32[48,1024]{1,0:T(8,128)S(1)}, u32[]{:S(2)}, u32[]{:S(2)}) %collective-permute-start.6) | collective-permute-done | bytes 196640 | tf_op jit(solution)/shard_map/ppermute | solution.py:746
  47.2 1.2 collective-permute-done.7.far
  48.5 9.5 %couple.1 = (f32[4096,128]{1,0:T(8,128)S(1)}, f32[48,1024]{1,0:T(8,128)S(1)}, f32[4096,128]{1,0:T(8,128)S(1)}, f32[4096,128]{1,0:T(8,128)S(1)}, f32[4096,128]{1,0:T(8,128)S(1)}, /*index=5*/f32[4096,128]{1,0:T(8,128)S(1)}) custom-call(s32[1,6144]{1,0:T(1,128)S(1)} %copy-done.1, ...), custom_call_target="tpu_custom_call", output_to_operand_aliasing={{2}: (4, {}), {3}: (5, {}), {4}: (6, {}), {5}: (7, {})} | custom-call | bytes 33000000 | tf_op jit(solution)/shard_map/couple/pallas_call | solution.py:492
  58.0 1.9 %collective-permute-start.9 = (f32[48,1024]{1,0:T(8,128)S(1)}, f32[48,1024]{1,0:T(8,128)S(1)}, u32[]{:S(2)}, u32[]{:S(2)}) collective-permute-start(f32[48,1024]{1,0:T(8,128)S(1)} %get-tuple-element.40), channel_id=1, source_target_pairs={{0,96},{1,97},{2,98},{3,99},{4,100},{5,101},{6,102},{7,103},{8,104... | collective-permute-start | bytes 589832 | tf_op jit(solution)/shard_map/ppermute | solution.py:746
  59.8 3.3 %at_receptors.1 = f32[48,1024]{1,0:T(8,128)S(1)} custom-call(f32[4096,128]{1,0:T(8,128)S(1)} %get-tuple-element.39.tangent, s32[1,6144]{1,0:T(1,128)S(1)} %copy-done.1, s32[6144]{0:T(1024)S(1)} %bitcast.22), custom_call_target="tpu_custom_call" | custom-call | bytes 9000000 | tf_op jit(solution)/shard_map/at_receptors/pallas_call | solution.py:516
  63.2 1.0 collective-permute-start.8
  64.1 1.4 %collective-permute-done.9.ready.far = f32[48,1024]{1,0:T(8,128)S(1)} collective-permute-done((f32[48,1024]{1,0:T(8,128)S(1)}, f32[48,1024]{1,0:T(8,128)S(1)}, u32[]{:S(2)}, u32[]{:S(2)}) %collective-permute-start.9) | collective-permute-done | bytes 196640 | tf_op jit(solution)/shard_map/ppermute | solution.py:746
  65.6 2.8 %transposed.1 = (f32[4096,128]{1,0:T(8,128)S(1)}, f32[4096,128]{1,0:T(8,128)S(1)}, f32[4096,128]{1,0:T(8,128)S(1)}, f32[4096,128]{1,0:T(8,128)S(1)}) custom-call(f32[4096,128]{1,0:T(8,128)S(1)} %get-tuple-element.39.tangent, f32[4096,128]{1,0:T(8,128)S(1)} %get-tuple-element.43.centre, f32[4096,128]{1,0:T(8,128)S(1)} %get-tuple-element.41.lower, ...), custom_call_target="tpu_custom_call" | custom-call | bytes 3000000 | tf_op jit(solution)/shard_map/transposed/pallas_call | solution.py:568
  68.3 0.0 collective-permute-done.8.near
  68.4 0.1 collective-permute-start.10
  68.5 5.3 %collective-permute-start.11 = (f32[32,1152]{1,0:T(8,128)S(1)}, f32[32,1152]{1,0:T(8,128)S(1)}, u32[]{:S(2)}, u32[]{:S(2)}) collective-permute-start(f32[32,1152]{1,0:T(8,128)S(1)} %get-tuple-element.46), channel_id=1, source_target_pairs={{0,15},{1,0},{2,1},{3,2},{4,3},{5,4},{6,5},{7,6},{8,7},{9,8},{10,9... | collective-permute-start | bytes 442376 | tf_op jit(solution)/shard_map/ppermute | solution.py:746
  73.8 7.5 %add_same.1 = (f32[4096,128]{1,0:T(8,128)S(1)}, f32[4096,128]{1,0:T(8,128)S(1)}, f32[4096,128]{1,0:T(8,128)S(1)}, f32[4096,128]{1,0:T(8,128)S(1)}) custom-call(s32[4,6144]{1,0:T(4,128)S(1)} %bitcast.9, s32[24576]{0:T(1024)S(1)} %bitcast.13, f32[4,6144]{1,0:T(4,128)S(1)} %bitcast.20, ...), custom_call_target="tpu_custom_call", output_to_operand_aliasing={{0}: (6, {}), {1}: (7, {}), {2}: (8, {}), {3}: (9, {})} | custom-call | bytes 27000000 | tf_op jit(solution)/shard_map/add_same/pallas_call | solution.py:592
  81.3 0.0 collective-permute-done.10.before
  81.3 0.0 collective-permute-done.11.after
  81.3 18.7 %add_sides.1 = (f32[4096,128]{1,0:T(8,128)S(1)}, f32[2,128]{1,0:T(2,128)S(1)}, f32[4096,128]{1,0:T(8,128)S(1)}, f32[4096,128]{1,0:T(8,128)S(1)}, f32[4096,128]{1,0:T(8,128)S(1)}, /*index=5*/f32[4096,128]{1,0:T(8,128)S(1)}) custom-call(s32[4,6144]{1,0:T(4,128)S(1)} %bitcast.10, ...), custom_call_target="tpu_custom_call", output_to_operand_aliasing={{2}: (6, {}), {3}: (7, {}), {4}: (8, {}), {5}: (9, {})} | custom-call | bytes 54000000 | tf_op jit(solution)/shard_map/add_sides/pallas_call | solution.py:663
  100.0 9.4 %all_to_all.10 = f32[8,2,128]{2,1,0:T(2,128)S(1)} all-to-all(f32[8,2,128]{2,1,0:T(2,128)S(1)} %broadcast_in_dim.6), channel_id=1, replica_groups=mesh['grid'=8,'cell'=16] {'grid'}, dimensions={0} | all-to-all | bytes 16384 | tf_op jit(solution)/shard_map/all_to_all | solution.py:759
  109.5 10.1 %all_to_all.11 = f32[16,2,128]{2,1,0:T(2,128)S(1)} all-to-all(f32[16,2,128]{2,1,0:T(2,128)S(1)} %broadcast_in_dim.7), channel_id=1, replica_groups=mesh['grid'=8,'cell'=16] {'cell'}, dimensions={0} | all-to-all | bytes 32768 | tf_op jit(solution)/shard_map/all_to_all | solution.py:759
  119.6 4.8 %basis.1 = (f32[16,1,32768]{2,1,0:T(1,128)}, f32[16,16]{1,0:T(8,128)}) custom-call(f32[2,128]{1,0:T(2,128)S(1)} %reduce_sum.19.gram, f32[4096,128]{1,0:T(8,128)S(1)} %get-tuple-element.55.adjoint), custom_call_target="tpu_custom_call" | custom-call | bytes 18000000 | tf_op jit(solution)/shard_map/basis/pallas_call | solution.py:724
  (10 shorter events, 0.2 us)
Async XLA Ops:
  0.6 5.8 %collective-permute-start.1 = (f32[1,4,6144]{2,1,0:T(4,128)}, f32[1,4,6144]{2,1,0:T(4,128)S(1)}, u32[]{:S(2)}, u32[]{:S(2)}) collective-permute-start(f32[1,4,6144]{2,1,0:T(4,128)} %param.13), channel_id=1, source_target_pairs={{0,96},{1,97},{2,98},{3,99},{4,100},{5,101},{6,102},{7,103},{8,104... | collective-permute-start | bytes 294920 | tf_op jit(solution)/shard_map/ppermute | solution.py:746
  3.6 3.5 %collective-permute-start = (f32[1,4,6144]{2,1,0:T(4,128)}, f32[1,4,6144]{2,1,0:T(4,128)S(1)}, u32[]{:S(2)}, u32[]{:S(2)}) collective-permute-start(f32[1,4,6144]{2,1,0:T(4,128)} %param.13), channel_id=1, source_target_pairs={{0,112},{1,113},{2,114},{3,115},{4,116},{5,117},{6,118},{7,119},{8... | collective-permute-start | bytes 294920 | tf_op jit(solution)/shard_map/ppermute | solution.py:746
  6.4 7.3 %copy-start = (s32[1,4,6144]{2,1,0:T(4,128)S(1)}, s32[1,4,6144]{2,1,0:T(4,128)}, u32[]{:S(2)}) copy-start(s32[1,4,6144]{2,1,0:T(4,128)} %param.11) | copy-start | bytes 294916
  7.1 18.5 %collective-permute-start.2 = (f32[8,1152]{1,0:T(8,128)S(1)}, f32[8,1152]{1,0:T(8,128)S(1)}, u32[]{:S(2)}, u32[]{:S(2)}) collective-permute-start(f32[8,1152]{1,0:T(8,128)S(1)} %get-tuple-element.29), channel_id=1, source_target_pairs={{0,1},{1,2},{2,3},{3,4},{4,5},{5,6},{6,7},{7,8},{8,9},{9,10},{10,1... | collective-permute-start | bytes 110600 | tf_op jit(solution)/shard_map/ppermute | solution.py:746
  8.7 16.9 %collective-permute-start.3 = (f32[8,1152]{1,0:T(8,128)S(1)}, f32[8,1152]{1,0:T(8,128)S(1)}, u32[]{:S(2)}, u32[]{:S(2)}) collective-permute-start(f32[8,1152]{1,0:T(8,128)S(1)} %get-tuple-element.30), channel_id=1, source_target_pairs={{0,15},{1,0},{2,1},{3,2},{4,3},{5,4},{6,5},{7,6},{8,7},{9,8},{10,9... | collective-permute-start | bytes 110600 | tf_op jit(solution)/shard_map/ppermute | solution.py:746
  29.0 11.0 %copy-start.1 = (s32[1,6144]{1,0:T(1,128)S(1)}, s32[1,6144]{1,0:T(1,128)}, u32[]{:S(2)}) copy-start(s32[1,6144]{1,0:T(1,128)} %cells.3) | copy-start | bytes 73732
  29.1 11.0 %copy-start.2 = (f32[1,32768]{1,0:T(1,128)S(1)}, f32[1,32768]{1,0:T(1,128)}, u32[]{:S(2)}) copy-start(f32[1,32768]{1,0:T(1,128)} %centre.1) | copy-start | bytes 393220
  29.1 11.0 %copy-start.3 = (f32[1,32768]{1,0:T(1,128)S(1)}, f32[1,32768]{1,0:T(1,128)}, u32[]{:S(2)}) copy-start(f32[1,32768]{1,0:T(1,128)} %lower.1) | copy-start | bytes 393220
  29.1 11.0 %copy-start.4 = (f32[1,32768]{1,0:T(1,128)S(1)}, f32[1,32768]{1,0:T(1,128)}, u32[]{:S(2)}) copy-start(f32[1,32768]{1,0:T(1,128)} %upper.1) | copy-start | bytes 393220
  29.1 10.0 %collective-permute-start.4 = (f32[32,1024]{1,0:T(8,128)S(1)}, f32[32,1024]{1,0:T(8,128)S(1)}, u32[]{:S(2)}, u32[]{:S(2)}) collective-permute-start(f32[32,1024]{1,0:T(8,128)S(1)} %get-tuple-element.31), channel_id=1, source_target_pairs={{0,15},{1,0},{2,1},{3,2},{4,3},{5,4},{6,5},{7,6},{8,7},{9,8},{10,9... | collective-permute-start | bytes 393224 | tf_op jit(solution)/shard_map/ppermute | solution.py:746
  31.1 8.3 %collective-permute-start.5 = (f32[32,1024]{1,0:T(8,128)S(1)}, f32[32,1024]{1,0:T(8,128)S(1)}, u32[]{:S(2)}, u32[]{:S(2)}) collective-permute-start(f32[32,1024]{1,0:T(8,128)S(1)} %get-tuple-element.32), channel_id=1, source_target_pairs={{0,1},{1,2},{2,3},{3,4},{4,5},{5,6},{6,7},{7,8},{8,9},{9,10},{10,1... | collective-permute-start | bytes 393224 | tf_op jit(solution)/shard_map/ppermute | solution.py:746
  39.4 7.8 %collective-permute-start.6 = (f32[48,1024]{1,0:T(8,128)S(1)}, f32[48,1024]{1,0:T(8,128)S(1)}, u32[]{:S(2)}, u32[]{:S(2)}) collective-permute-start(f32[48,1024]{1,0:T(8,128)S(1)} %get-tuple-element.33), channel_id=1, source_target_pairs={{0,16},{1,17},{2,18},{3,19},{4,20},{5,21},{6,22},{7,23},{8,24},{9,... | collective-permute-start | bytes 589832 | tf_op jit(solution)/shard_map/ppermute | solution.py:746
  39.4 9.0 %collective-permute-start.7 = (f32[48,1024]{1,0:T(8,128)S(1)}, f32[48,1024]{1,0:T(8,128)S(1)}, u32[]{:S(2)}, u32[]{:S(2)}) collective-permute-start(f32[48,1024]{1,0:T(8,128)S(1)} %get-tuple-element.34), channel_id=1, source_target_pairs={{0,32},{1,33},{2,34},{3,35},{4,36},{5,37},{6,38},{7,39},{8,40},{9,... | collective-permute-start | bytes 589832 | tf_op jit(solution)/shard_map/ppermute | solution.py:746
  58.0 7.6 %collective-permute-start.9 = (f32[48,1024]{1,0:T(8,128)S(1)}, f32[48,1024]{1,0:T(8,128)S(1)}, u32[]{:S(2)}, u32[]{:S(2)}) collective-permute-start(f32[48,1024]{1,0:T(8,128)S(1)} %get-tuple-element.40), channel_id=1, source_target_pairs={{0,96},{1,97},{2,98},{3,99},{4,100},{5,101},{6,102},{7,103},{8,104... | collective-permute-start | bytes 589832 | tf_op jit(solution)/shard_map/ppermute | solution.py:746
  63.2 5.1 %collective-permute-start.8 = (f32[48,1024]{1,0:T(8,128)S(1)}, f32[48,1024]{1,0:T(8,128)S(1)}, u32[]{:S(2)}, u32[]{:S(2)}) collective-permute-start(f32[48,1024]{1,0:T(8,128)S(1)} %at_receptors.1), channel_id=1, source_target_pairs={{0,112},{1,113},{2,114},{3,115},{4,116},{5,117},{6,118},{7,119},{8... | collective-permute-start | bytes 589832 | tf_op jit(solution)/shard_map/ppermute | solution.py:746
  68.4 12.9 %collective-permute-start.10 = (f32[32,1152]{1,0:T(8,128)S(1)}, f32[32,1152]{1,0:T(8,128)S(1)}, u32[]{:S(2)}, u32[]{:S(2)}) collective-permute-start(f32[32,1152]{1,0:T(8,128)S(1)} %get-tuple-element.45), channel_id=1, source_target_pairs={{0,1},{1,2},{2,3},{3,4},{4,5},{5,6},{6,7},{7,8},{8,9},{9,10},{10,1... | collective-permute-start | bytes 442376 | tf_op jit(solution)/shard_map/ppermute | solution.py:746
  68.5 12.9 %collective-permute-start.11 = (f32[32,1152]{1,0:T(8,128)S(1)}, f32[32,1152]{1,0:T(8,128)S(1)}, u32[]{:S(2)}, u32[]{:S(2)}) collective-permute-start(f32[32,1152]{1,0:T(8,128)S(1)} %get-tuple-element.46), channel_id=1, source_target_pairs={{0,15},{1,0},{2,1},{3,2},{4,3},{5,4},{6,5},{7,6},{8,7},{9,8},{10,9... | collective-permute-start | bytes 442376 | tf_op jit(solution)/shard_map/ppermute | solution.py:746

commit v7 on v6

--- a/solution.py
+++ b/solution.py
@@ -147,12 +147,24 @@
     return jnp.broadcast_to(cells[m : m + 1, aligned(offset, LANES)], (8, LANES)) >> 12
 
 
+def identity_pair():
+    row = lax.broadcasted_iota(i32, (LANES, 2 * LANES), 0)
+    return jnp.where(lanes((LANES, 2 * LANES)) % LANES == row, 1.0, 0.0).astype(bf16)
+
+
+def turned(block, m, pair):
+    if m % 2 == 0:
+        return block.T
+    both = jnp.concatenate(split(block), axis=1)
+    return lax.dot_general(pair, both, (((1,), (1,)), ((), ())), preferred_element_type=f32)
+
+
 def each_block(many, step):
     unroll = 8 // many
 
     def outer(j, carry):
         for n in range(unroll):
-            step(j * unroll + n)
+            step(j * unroll + n, n)
         return carry
 
     lax.fori_loop(0, FRINGE // LANES // unroll, outer, 0)
@@ -160,12 +172,14 @@
 
 def select_fields(staged, cells, partners, weights, out):
     many = cells.shape[0]
+    pair = identity_pair()
     for n, k in enumerate(partners):
 
-        def step(b):
+        def step(b, mark=0):
             total = [jnp.zeros((8, LANES), f32)] * 2
             for m in range(many):
-                field = staged[aligned((m * len(partners) + n) * FRINGE + b * LANES, LANES), :].T
+                field = staged[aligned((m * len(partners) + n) * FRINGE + b * LANES, LANES), :]
+                field = turned(field, m if many > 1 else mark, pair)
                 group = groups_of(cells, m, k * FRINGE + b * LANES)
                 scale = 1.0
                 if weights is not None:
@@ -184,7 +198,7 @@
         each_block(many, step)
 
 
-def spread_group(fields, cells, outs):
+def spread_group(fields, cells, outs, pair):
     group = [value >> 12 for value in cells]
     row = [value & (ROWS - 1) for value in cells]
     terms = [[jnp.where(group[m] == g, fields[m][h], 0.0) for g in range(GROUPS) for h in range(2)] for m in range(4)]
@@ -197,7 +211,7 @@
                 value = value + jnp.where(same[i], terms[i][v], 0.0)
             block.append(value)
         ref, at = outs[m]
-        ref[aligned(at, LANES), :] = jnp.concatenate(block, axis=0).T
+        ref[aligned(at, LANES), :] = turned(jnp.concatenate(block, axis=0), m, pair)
 
 
 def block_of(ref, row, column):
@@ -210,20 +224,23 @@
 
 
 def spread_at_donors(messages, cells, partners, weights, staged):
+    pair = identity_pair()
     for n, k in enumerate(partners):
 
-        def step(b):
+        def step(b, mark=0):
             field = field_of(messages[k], b)
             ref, row, column = weights[k]
             scale = [block_of(ref, row + m, column + b * LANES) for m in range(4)]
             fields = [[part * scale[m] for part in field] for m in range(4)]
             blocks = [block_of(cells, m, k * FRINGE + b * LANES) for m in range(4)]
-            spread_group(fields, blocks, [(staged, (m * len(partners) + n) * FRINGE + b * LANES) for m in range(4)])
+            outs = [(staged, (m * len(partners) + n) * FRINGE + b * LANES) for m in range(4)]
+            spread_group(fields, blocks, outs, pair)
 
         each_block(4, step)
 
 
 def spread_at_receptors(messages, cells, staged):
+    pair = identity_pair()
     for part in range(3):
 
         def step(j, carry):
@@ -234,7 +251,7 @@
                 at = m * QUARTER + (part * 4 + j) * LANES
                 blocks.append(block_of(cells, 0, at))
                 outs.append((staged, at))
-            spread_group(fields, blocks, outs)
+            spread_group(fields, blocks, outs, pair)
             return carry
 
         lax.fori_loop(0, 4, step, 0, unroll=2)

time: 125 us -> 128 us (1.024)
  Pallas kernels: 77.8 us -> 80.9 us
  transfers between devices with their start and end apart: 12 -> 12, of which waited for: 5 -> 4; matrix products, arithmetic and copies ran while one was open for 0% -> 0% of each run, Pallas kernels for 33% -> 33%
where the time goes in v7:
time: 128 us; the launch traced here: 127 us
  Pallas kernels  80.9 us (63%)
  starting transfers between devices  20.4 us (16%)
  blocking collectives  19.6 us (15%)
  waiting for transfers between devices  5.44 us (4%)
    ppermute x12, starting transfers between devices, moved(): return lax.ppermute(value, AXES, route)  20.4 us
    pallas_call x1, Pallas kernels, add_sides(): pl.pallas_call(donor_sides_kernel, out_shape=[resident(ROWS, LANES), jax....  19.8 us
    all_to_all x2, blocking collectives, axis_sum(): return jnp.sum(lax.all_to_all(copies, axis, 0, 0), axis=0)  19.6 us
    pallas_call x1, Pallas kernels, rows_at_sides(): pl.pallas_call(rows_kernel, out_shape=resident(len(segs) * FRINGE, LANES)...  11.8 us
    pallas_call x1, Pallas kernels, couple(): pl.pallas_call(couple_kernel, out_shape=[resident(ROWS, LANES), TRIPLE] +...  9.84 us
    pallas_call x1, Pallas kernels, same_sums(): pl.pallas_call(same_sums_kernel, out_shape=PAIR, in_specs=[VMEM, VMEM, HB...  8.28 us
    pallas_call x1, Pallas kernels, add_same(): pl.pallas_call(donor_same_kernel, out_shape=[resident(ROWS, LANES)] * SUM...  8.06 us
    ppermute x12, waiting for transfers between devices, moved(): return lax.ppermute(value, AXES, route)  5.44 us
  transfers between devices with their start and end apart: 12, of which 4 were waited for; matrix products, arithmetic and copies ran while one was open for 0% of the time, Pallas kernels for 33%

profile of v7, /device:TPU:0, one launch (start us, length us, event | category | flops | bytes accessed | tf_op | source)
XLA Modules:
  0.0 127.5 jit_solution(267366062370596898)
XLA Ops:
  0.6 2.9 %collective-permute-start.1 = (f32[1,4,6144]{2,1,0:T(4,128)}, f32[1,4,6144]{2,1,0:T(4,128)S(1)}, u32[]{:S(2)}, u32[]{:S(2)}) collective-permute-start(f32[1,4,6144]{2,1,0:T(4,128)} %param.13), channel_id=1, source_target_pairs={{0,96},{1,97},{2,98},{3,99},{4,100},{5,101},{6,102},{7,103},{8,104... | collective-permute-start | bytes 294920 | tf_op jit(solution)/shard_map/ppermute | solution.py:763
  3.6 0.0 collective-permute-start
  3.6 2.8 %table.1 = f32[4096,128]{1,0:T(8,128)S(1)} custom-call(f32[16,1,32768]{2,1,0:T(1,128)} %probes.1), custom_call_target="tpu_custom_call" | custom-call | bytes 9000000 | tf_op jit(solution)/shard_map/table/pallas_call | solution.py:300
  6.4 0.0 copy-start
  6.4 0.0 collective-permute-done.1
  6.4 0.7 collective-permute-done
  7.1 1.6 %collective-permute-start.2 = (f32[8,1152]{1,0:T(8,128)S(1)}, f32[8,1152]{1,0:T(8,128)S(1)}, u32[]{:S(2)}, u32[]{:S(2)}) collective-permute-start(f32[8,1152]{1,0:T(8,128)S(1)} %get-tuple-element.29), channel_id=1, source_target_pairs={{0,1},{1,2},{2,3},{3,4},{4,5},{5,6},{6,7},{7,8},{8,9},{9,10},{10,1... | collective-permute-start | bytes 110600 | tf_op jit(solution)/shard_map/ppermute | solution.py:763
  8.7 5.0 %collective-permute-start.3 = (f32[8,1152]{1,0:T(8,128)S(1)}, f32[8,1152]{1,0:T(8,128)S(1)}, u32[]{:S(2)}, u32[]{:S(2)}) collective-permute-start(f32[8,1152]{1,0:T(8,128)S(1)} %get-tuple-element.30), channel_id=1, source_target_pairs={{0,15},{1,0},{2,1},{3,2},{4,3},{5,4},{6,5},{7,6},{8,7},{9,8},{10,9... | collective-permute-start | bytes 110600 | tf_op jit(solution)/shard_map/ppermute | solution.py:763
  13.7 0.0 copy-done
  13.8 11.8 %rows_at_sides.1.staged = f32[16384,128]{1,0:T(8,128)S(1)} custom-call(f32[4096,128]{1,0:T(8,128)S(1)} %table.1, s32[24576]{0:T(1024)S(1)} %bitcast.11), custom_call_target="tpu_custom_call" | custom-call | bytes 33000000 | tf_op jit(solution)/shard_map/rows_at_sides/pallas_call | solution.py:371
  25.6 0.0 collective-permute-done.2.before.before_weights
  25.6 0.0 collective-permute-done.3.after.after_weights
  25.6 4.2 %side_sums.1 = (f32[32,1024]{1,0:T(8,128)S(1)}, f32[32,1024]{1,0:T(8,128)S(1)}) custom-call(f32[16384,128]{1,0:T(8,128)S(1)} %rows_at_sides.1.staged, s32[4,6144]{1,0:T(4,128)S(1)} %bitcast.7, f32[8,1152]{1,0:T(8,128)S(1)} %collective-permute-done.2.before.before_weights, f32[8,1152]{1,0:T(8,128)S(1)} %collective-permute-done.3.after.after_weights), custom_call_target="tpu_custom_call" | custom-call | bytes 3000000 | tf_op jit(solution)/shard_map/side_sums/pallas_call | solution.py:340
  29.9 0.0 copy-start.1
  29.9 0.0 copy-start.2
  29.9 0.0 copy-start.3
  29.9 0.0 copy-start.4
  29.9 2.0 %collective-permute-start.4 = (f32[32,1024]{1,0:T(8,128)S(1)}, f32[32,1024]{1,0:T(8,128)S(1)}, u32[]{:S(2)}, u32[]{:S(2)}) collective-permute-start(f32[32,1024]{1,0:T(8,128)S(1)} %get-tuple-element.31), channel_id=1, source_target_pairs={{0,15},{1,0},{2,1},{3,2},{4,3},{5,4},{6,5},{7,6},{8,7},{9,8},{10,9... | collective-permute-start | bytes 393224 | tf_op jit(solution)/shard_map/ppermute | solution.py:763
  31.9 0.1 collective-permute-start.5
  32.0 8.3 %same_sums.1.same = f32[32,1024]{1,0:T(8,128)S(1)} custom-call(f32[4096,128]{1,0:T(8,128)S(1)} %table.1, s32[4,6144]{1,0:T(4,128)S(1)} %bitcast.8, s32[24576]{0:T(1024)S(1)} %bitcast.12, f32[4,6144]{1,0:T(4,128)S(1)} %bitcast.19, f32[4,6144]{1,0:T(4,128)S(1)} %bitcast.16), custom_call_target="tpu_custom_call" | custom-call | bytes 24000000 | tf_op jit(solution)/shard_map/same_sums/pallas_call | solution.py:404
  40.3 0.0 collective-permute-done.4.before
  40.3 0.0 collective-permute-done.5.after
  40.3 0.0 collective-permute-start.6
  40.4 0.6 collective-permute-start.7
  41.0 0.0 copy-done.1
  41.0 0.0 copy-done.2
  41.0 0.0 copy-done.3
  41.0 0.0 copy-done.4
  41.0 5.2 %forward.1 = (f32[4096,128]{1,0:T(8,128)S(1)}, f32[4096,128]{1,0:T(8,128)S(1)}, f32[4096,128]{1,0:T(8,128)S(1)}, f32[4096,128]{1,0:T(8,128)S(1)}, f32[4096,128]{...) custom-call(f32[4096,128]{1,0:T(8,128)S(1)} %table.1, f32[1,32768]{1,0:T(1,128)S(1)} %copy-done.2, ...), custom_call_target="tpu_custom_call" | custom-call | bytes 21000000 | tf_op jit(solution)/shard_map/forward/pallas_call | solution.py:470
  46.2 1.9 %collective-permute-done.6.near = f32[48,1024]{1,0:T(8,128)S(1)} collective-permute-done((f32[48,1024]{1,0:T(8,128)S(1)}, f32[48,1024]{1,0:T(8,128)S(1)}, u32[]{:S(2)}, u32[]{:S(2)}) %collective-permute-start.6) | collective-permute-done | bytes 196640 | tf_op jit(solution)/shard_map/ppermute | solution.py:763
  48.2 1.2 collective-permute-done.7.far
  49.4 9.8 %couple.1 = (f32[4096,128]{1,0:T(8,128)S(1)}, f32[48,1024]{1,0:T(8,128)S(1)}, f32[4096,128]{1,0:T(8,128)S(1)}, f32[4096,128]{1,0:T(8,128)S(1)}, f32[4096,128]{1,0:T(8,128)S(1)}, /*index=5*/f32[4096,128]{1,0:T(8,128)S(1)}) custom-call(s32[1,6144]{1,0:T(1,128)S(1)} %copy-done.1, ...), custom_call_target="tpu_custom_call", output_to_operand_aliasing={{2}: (4, {}), {3}: (5, {}), {4}: (6, {}), {5}: (7, {})} | custom-call | bytes 33000000 | tf_op jit(solution)/shard_map/couple/pallas_call | solution.py:509
  59.2 1.8 %collective-permute-start.9 = (f32[48,1024]{1,0:T(8,128)S(1)}, f32[48,1024]{1,0:T(8,128)S(1)}, u32[]{:S(2)}, u32[]{:S(2)}) collective-permute-start(f32[48,1024]{1,0:T(8,128)S(1)} %get-tuple-element.40), channel_id=1, source_target_pairs={{0,96},{1,97},{2,98},{3,99},{4,100},{5,101},{6,102},{7,103},{8,104... | collective-permute-start | bytes 589832 | tf_op jit(solution)/shard_map/ppermute | solution.py:763
  61.0 3.3 %at_receptors.1 = f32[48,1024]{1,0:T(8,128)S(1)} custom-call(f32[4096,128]{1,0:T(8,128)S(1)} %get-tuple-element.39.tangent, s32[1,6144]{1,0:T(1,128)S(1)} %copy-done.1, s32[6144]{0:T(1024)S(1)} %bitcast.22), custom_call_target="tpu_custom_call" | custom-call | bytes 9000000 | tf_op jit(solution)/shard_map/at_receptors/pallas_call | solution.py:533
  64.3 0.9 collective-permute-start.8
  65.2 1.6 %collective-permute-done.9.ready.far = f32[48,1024]{1,0:T(8,128)S(1)} collective-permute-done((f32[48,1024]{1,0:T(8,128)S(1)}, f32[48,1024]{1,0:T(8,128)S(1)}, u32[]{:S(2)}, u32[]{:S(2)}) %collective-permute-start.9) | collective-permute-done | bytes 196640 | tf_op jit(solution)/shard_map/ppermute | solution.py:763
  66.8 2.8 %transposed.1 = (f32[4096,128]{1,0:T(8,128)S(1)}, f32[4096,128]{1,0:T(8,128)S(1)}, f32[4096,128]{1,0:T(8,128)S(1)}, f32[4096,128]{1,0:T(8,128)S(1)}) custom-call(f32[4096,128]{1,0:T(8,128)S(1)} %get-tuple-element.39.tangent, f32[4096,128]{1,0:T(8,128)S(1)} %get-tuple-element.43.centre, f32[4096,128]{1,0:T(8,128)S(1)} %get-tuple-element.41.lower, ...), custom_call_target="tpu_custom_call" | custom-call | bytes 3000000 | tf_op jit(solution)/shard_map/transposed/pallas_call | solution.py:585
  69.6 0.0 collective-permute-done.8.near
  69.6 0.1 collective-permute-start.10
  69.7 5.3 %collective-permute-start.11 = (f32[32,1152]{1,0:T(8,128)S(1)}, f32[32,1152]{1,0:T(8,128)S(1)}, u32[]{:S(2)}, u32[]{:S(2)}) collective-permute-start(f32[32,1152]{1,0:T(8,128)S(1)} %get-tuple-element.46), channel_id=1, source_target_pairs={{0,15},{1,0},{2,1},{3,2},{4,3},{5,4},{6,5},{7,6},{8,7},{9,8},{10,9... | collective-permute-start | bytes 442376 | tf_op jit(solution)/shard_map/ppermute | solution.py:763
  75.0 8.1 %add_same.1 = (f32[4096,128]{1,0:T(8,128)S(1)}, f32[4096,128]{1,0:T(8,128)S(1)}, f32[4096,128]{1,0:T(8,128)S(1)}, f32[4096,128]{1,0:T(8,128)S(1)}) custom-call(s32[4,6144]{1,0:T(4,128)S(1)} %bitcast.9, s32[24576]{0:T(1024)S(1)} %bitcast.13, f32[4,6144]{1,0:T(4,128)S(1)} %bitcast.20, ...), custom_call_target="tpu_custom_call", output_to_operand_aliasing={{0}: (6, {}), {1}: (7, {}), {2}: (8, {}), {3}: (9, {})} | custom-call | bytes 27000000 | tf_op jit(solution)/shard_map/add_same/pallas_call | solution.py:609
  83.1 0.0 collective-permute-done.10.before
  83.1 0.0 collective-permute-done.11.after
  83.1 19.8 %add_sides.1 = (f32[4096,128]{1,0:T(8,128)S(1)}, f32[2,128]{1,0:T(2,128)S(1)}, f32[4096,128]{1,0:T(8,128)S(1)}, f32[4096,128]{1,0:T(8,128)S(1)}, f32[4096,128]{1,0:T(8,128)S(1)}, /*index=5*/f32[4096,128]{1,0:T(8,128)S(1)}) custom-call(s32[4,6144]{1,0:T(4,128)S(1)} %bitcast.10, ...), custom_call_target="tpu_custom_call", output_to_operand_aliasing={{2}: (6, {}), {3}: (7, {}), {4}: (8, {}), {5}: (9, {})} | custom-call | bytes 54000000 | tf_op jit(solution)/shard_map/add_sides/pallas_call | solution.py:680
  103.0 9.2 %all_to_all.10 = f32[8,2,128]{2,1,0:T(2,128)S(1)} all-to-all(f32[8,2,128]{2,1,0:T(2,128)S(1)} %broadcast_in_dim.6), channel_id=1, replica_groups=mesh['grid'=8,'cell'=16] {'grid'}, dimensions={0} | all-to-all | bytes 16384 | tf_op jit(solution)/shard_map/all_to_all | solution.py:776
  112.2 10.4 %all_to_all.11 = f32[16,2,128]{2,1,0:T(2,128)S(1)} all-to-all(f32[16,2,128]{2,1,0:T(2,128)S(1)} %broadcast_in_dim.7), channel_id=1, replica_groups=mesh['grid'=8,'cell'=16] {'cell'}, dimensions={0} | all-to-all | bytes 32768 | tf_op jit(solution)/shard_map/all_to_all | solution.py:776
  122.7 4.8 %basis.1 = (f32[16,1,32768]{2,1,0:T(1,128)}, f32[16,16]{1,0:T(8,128)}) custom-call(f32[2,128]{1,0:T(2,128)S(1)} %reduce_sum.19.gram, f32[4096,128]{1,0:T(8,128)S(1)} %get-tuple-element.55.adjoint), custom_call_target="tpu_custom_call" | custom-call | bytes 18000000 | tf_op jit(solution)/shard_map/basis/pallas_call | solution.py:741
  (10 shorter events, 0.2 us)
Async XLA Ops:
  0.6 5.8 %collective-permute-start.1 = (f32[1,4,6144]{2,1,0:T(4,128)}, f32[1,4,6144]{2,1,0:T(4,128)S(1)}, u32[]{:S(2)}, u32[]{:S(2)}) collective-permute-start(f32[1,4,6144]{2,1,0:T(4,128)} %param.13), channel_id=1, source_target_pairs={{0,96},{1,97},{2,98},{3,99},{4,100},{5,101},{6,102},{7,103},{8,104... | collective-permute-start | bytes 294920 | tf_op jit(solution)/shard_map/ppermute | solution.py:763
  3.6 3.5 %collective-permute-start = (f32[1,4,6144]{2,1,0:T(4,128)}, f32[1,4,6144]{2,1,0:T(4,128)S(1)}, u32[]{:S(2)}, u32[]{:S(2)}) collective-permute-start(f32[1,4,6144]{2,1,0:T(4,128)} %param.13), channel_id=1, source_target_pairs={{0,112},{1,113},{2,114},{3,115},{4,116},{5,117},{6,118},{7,119},{8... | collective-permute-start | bytes 294920 | tf_op jit(solution)/shard_map/ppermute | solution.py:763
  6.4 7.3 %copy-start = (s32[1,4,6144]{2,1,0:T(4,128)S(1)}, s32[1,4,6144]{2,1,0:T(4,128)}, u32[]{:S(2)}) copy-start(s32[1,4,6144]{2,1,0:T(4,128)} %param.11) | copy-start | bytes 294916
  7.1 18.5 %collective-permute-start.2 = (f32[8,1152]{1,0:T(8,128)S(1)}, f32[8,1152]{1,0:T(8,128)S(1)}, u32[]{:S(2)}, u32[]{:S(2)}) collective-permute-start(f32[8,1152]{1,0:T(8,128)S(1)} %get-tuple-element.29), channel_id=1, source_target_pairs={{0,1},{1,2},{2,3},{3,4},{4,5},{5,6},{6,7},{7,8},{8,9},{9,10},{10,1... | collective-permute-start | bytes 110600 | tf_op jit(solution)/shard_map/ppermute | solution.py:763
  8.7 16.9 %collective-permute-start.3 = (f32[8,1152]{1,0:T(8,128)S(1)}, f32[8,1152]{1,0:T(8,128)S(1)}, u32[]{:S(2)}, u32[]{:S(2)}) collective-permute-start(f32[8,1152]{1,0:T(8,128)S(1)} %get-tuple-element.30), channel_id=1, source_target_pairs={{0,15},{1,0},{2,1},{3,2},{4,3},{5,4},{6,5},{7,6},{8,7},{9,8},{10,9... | collective-permute-start | bytes 110600 | tf_op jit(solution)/shard_map/ppermute | solution.py:763
  29.9 11.1 %copy-start.1 = (s32[1,6144]{1,0:T(1,128)S(1)}, s32[1,6144]{1,0:T(1,128)}, u32[]{:S(2)}) copy-start(s32[1,6144]{1,0:T(1,128)} %cells.3) | copy-start | bytes 73732
  29.9 11.1 %copy-start.2 = (f32[1,32768]{1,0:T(1,128)S(1)}, f32[1,32768]{1,0:T(1,128)}, u32[]{:S(2)}) copy-start(f32[1,32768]{1,0:T(1,128)} %centre.1) | copy-start | bytes 393220
  29.9 11.1 %copy-start.3 = (f32[1,32768]{1,0:T(1,128)S(1)}, f32[1,32768]{1,0:T(1,128)}, u32[]{:S(2)}) copy-start(f32[1,32768]{1,0:T(1,128)} %lower.1) | copy-start | bytes 393220
  29.9 11.1 %copy-start.4 = (f32[1,32768]{1,0:T(1,128)S(1)}, f32[1,32768]{1,0:T(1,128)}, u32[]{:S(2)}) copy-start(f32[1,32768]{1,0:T(1,128)} %upper.1) | copy-start | bytes 393220
  29.9 10.4 %collective-permute-start.4 = (f32[32,1024]{1,0:T(8,128)S(1)}, f32[32,1024]{1,0:T(8,128)S(1)}, u32[]{:S(2)}, u32[]{:S(2)}) collective-permute-start(f32[32,1024]{1,0:T(8,128)S(1)} %get-tuple-element.31), channel_id=1, source_target_pairs={{0,15},{1,0},{2,1},{3,2},{4,3},{5,4},{6,5},{7,6},{8,7},{9,8},{10,9... | collective-permute-start | bytes 393224 | tf_op jit(solution)/shard_map/ppermute | solution.py:763
  31.9 8.4 %collective-permute-start.5 = (f32[32,1024]{1,0:T(8,128)S(1)}, f32[32,1024]{1,0:T(8,128)S(1)}, u32[]{:S(2)}, u32[]{:S(2)}) collective-permute-start(f32[32,1024]{1,0:T(8,128)S(1)} %get-tuple-element.32), channel_id=1, source_target_pairs={{0,1},{1,2},{2,3},{3,4},{4,5},{5,6},{6,7},{7,8},{8,9},{9,10},{10,1... | collective-permute-start | bytes 393224 | tf_op jit(solution)/shard_map/ppermute | solution.py:763
  40.3 7.8 %collective-permute-start.6 = (f32[48,1024]{1,0:T(8,128)S(1)}, f32[48,1024]{1,0:T(8,128)S(1)}, u32[]{:S(2)}, u32[]{:S(2)}) collective-permute-start(f32[48,1024]{1,0:T(8,128)S(1)} %get-tuple-element.33), channel_id=1, source_target_pairs={{0,16},{1,17},{2,18},{3,19},{4,20},{5,21},{6,22},{7,23},{8,24},{9,... | collective-permute-start | bytes 589832 | tf_op jit(solution)/shard_map/ppermute | solution.py:763
  40.4 9.0 %collective-permute-start.7 = (f32[48,1024]{1,0:T(8,128)S(1)}, f32[48,1024]{1,0:T(8,128)S(1)}, u32[]{:S(2)}, u32[]{:S(2)}) collective-permute-start(f32[48,1024]{1,0:T(8,128)S(1)} %get-tuple-element.34), channel_id=1, source_target_pairs={{0,32},{1,33},{2,34},{3,35},{4,36},{5,37},{6,38},{7,39},{8,40},{9,... | collective-permute-start | bytes 589832 | tf_op jit(solution)/shard_map/ppermute | solution.py:763
  59.2 7.6 %collective-permute-start.9 = (f32[48,1024]{1,0:T(8,128)S(1)}, f32[48,1024]{1,0:T(8,128)S(1)}, u32[]{:S(2)}, u32[]{:S(2)}) collective-permute-start(f32[48,1024]{1,0:T(8,128)S(1)} %get-tuple-element.40), channel_id=1, source_target_pairs={{0,96},{1,97},{2,98},{3,99},{4,100},{5,101},{6,102},{7,103},{8,104... | collective-permute-start | bytes 589832 | tf_op jit(solution)/shard_map/ppermute | solution.py:763
  64.3 5.3 %collective-permute-start.8 = (f32[48,1024]{1,0:T(8,128)S(1)}, f32[48,1024]{1,0:T(8,128)S(1)}, u32[]{:S(2)}, u32[]{:S(2)}) collective-permute-start(f32[48,1024]{1,0:T(8,128)S(1)} %at_receptors.1), channel_id=1, source_target_pairs={{0,112},{1,113},{2,114},{3,115},{4,116},{5,117},{6,118},{7,119},{8... | collective-permute-start | bytes 589832 | tf_op jit(solution)/shard_map/ppermute | solution.py:763
  69.6 13.5 %collective-permute-start.10 = (f32[32,1152]{1,0:T(8,128)S(1)}, f32[32,1152]{1,0:T(8,128)S(1)}, u32[]{:S(2)}, u32[]{:S(2)}) collective-permute-start(f32[32,1152]{1,0:T(8,128)S(1)} %get-tuple-element.45), channel_id=1, source_target_pairs={{0,1},{1,2},{2,3},{3,4},{4,5},{5,6},{6,7},{7,8},{8,9},{9,10},{10,1... | collective-permute-start | bytes 442376 | tf_op jit(solution)/shard_map/ppermute | solution.py:763
  69.7 13.4 %collective-permute-start.11 = (f32[32,1152]{1,0:T(8,128)S(1)}, f32[32,1152]{1,0:T(8,128)S(1)}, u32[]{:S(2)}, u32[]{:S(2)}) collective-permute-start(f32[32,1152]{1,0:T(8,128)S(1)} %get-tuple-element.46), channel_id=1, source_target_pairs={{0,15},{1,0},{2,1},{3,2},{4,3},{5,4},{6,5},{7,6},{8,7},{9,8},{10,9... | collective-permute-start | bytes 442376 | tf_op jit(solution)/shard_map/ppermute | solution.py:763

commit v8 on v6

--- a/solution.py
+++ b/solution.py
@@ -24,6 +24,7 @@
 SUMS = 4
 QUARTER = SLOTS // 4
 UNROLL = 8
+ADD_UNROLL = 32
 
 AXES = ("grid", "cell")
 
@@ -128,8 +129,8 @@
     count = parts[0].shape[0]
 
     def outer(j, carry):
-        for n in range(UNROLL):
-            q = j * UNROLL + n
+        for n in range(ADD_UNROLL):
+            q = j * ADD_UNROLL + n
             for half in range(2):
                 total = sums[half + n % 2 * 2]
                 lists = [2 * m + half for m in range(4)]
@@ -140,7 +141,7 @@
                     total[pl.ds(row, 1), :] = value
         return carry
 
-    lax.fori_loop(0, count // UNROLL, outer, 0)
+    lax.fori_loop(0, count // ADD_UNROLL, outer, 0)
 
 
 def groups_of(cells, m, offset):
@@ -638,8 +639,8 @@
 
     def multiply(j, product):
         left_side, right_side = [], []
-        for n in range(4):
-            block = adjoint[aligned((j * 4 + n) * LANES, LANES), :]
+        for n in range(8):
+            block = adjoint[aligned((j * 8 + n) * LANES, LANES), :]
             high, low = split(block)
             high_t, low_t = split(block.T)
             left_side += [high_t, high_t, low_t]
@@ -648,7 +649,7 @@
         right_side = jnp.concatenate(right_side, axis=0)
         return product + jnp.dot(left_side, right_side, preferred_element_type=f32)
 
-    product = lax.fori_loop(0, TILES // 4, multiply, jnp.zeros((LANES, LANES), f32))
+    product = lax.fori_loop(0, TILES // 8, multiply, jnp.zeros((LANES, LANES), f32))
     group = lanes((PROBES, LANES)) // PROBES
     folded = jnp.zeros((PROBES, LANES), f32)
     for g in range(GROUPS):

time: 125 us -> 123 us (0.984)
  Pallas kernels: 77.8 us -> 75.4 us
    pallas_call x1, Pallas kernels: 18.7 us -> 17 us  [add_sides(): pl.pallas_call(donor_sides_kernel, out_shape=[resident(ROWS, LANES), jax....]
where the time goes in v8:
time: 123 us; the launch traced here: 122 us
  Pallas kernels  75.4 us (61%)
  starting transfers between devices  20.5 us (17%)
  blocking collectives  19.9 us (16%)
  waiting for transfers between devices  5.53 us (4%)
    ppermute x12, starting transfers between devices, moved(): return lax.ppermute(value, AXES, route)  20.5 us
    all_to_all x2, blocking collectives, axis_sum(): return jnp.sum(lax.all_to_all(copies, axis, 0, 0), axis=0)  19.9 us
    pallas_call x1, Pallas kernels, add_sides(): pl.pallas_call(donor_sides_kernel, out_shape=[resident(ROWS, LANES), jax....  17 us
    pallas_call x1, Pallas kernels, rows_at_sides(): pl.pallas_call(rows_kernel, out_shape=resident(len(segs) * FRINGE, LANES)...  11.8 us
    pallas_call x1, Pallas kernels, couple(): pl.pallas_call(couple_kernel, out_shape=[resident(ROWS, LANES), TRIPLE] +...  9.2 us
    pallas_call x1, Pallas kernels, same_sums(): pl.pallas_call(same_sums_kernel, out_shape=PAIR, in_specs=[VMEM, VMEM, HB...  7.9 us
    pallas_call x1, Pallas kernels, add_same(): pl.pallas_call(donor_same_kernel, out_shape=[resident(ROWS, LANES)] * SUM...  7.13 us
    ppermute x12, waiting for transfers between devices, moved(): return lax.ppermute(value, AXES, route)  5.53 us
  transfers between devices with their start and end apart: 12, of which 5 were waited for; matrix products, arithmetic and copies ran while one was open for 0% of the time, Pallas kernels for 33%

profile of v8, /device:TPU:0, one launch (start us, length us, event | category | flops | bytes accessed | tf_op | source)
XLA Modules:
  0.0 122.3 jit_solution(9198053745497346172)
XLA Ops:
  0.6 2.9 %collective-permute-start.1 = (f32[1,4,6144]{2,1,0:T(4,128)}, f32[1,4,6144]{2,1,0:T(4,128)S(1)}, u32[]{:S(2)}, u32[]{:S(2)}) collective-permute-start(f32[1,4,6144]{2,1,0:T(4,128)} %param.13), channel_id=1, source_target_pairs={{0,96},{1,97},{2,98},{3,99},{4,100},{5,101},{6,102},{7,103},{8,104... | collective-permute-start | bytes 294920 | tf_op jit(solution)/shard_map/ppermute | solution.py:747
  3.6 0.0 collective-permute-start
  3.6 2.8 %table.1 = f32[4096,128]{1,0:T(8,128)S(1)} custom-call(f32[16,1,32768]{2,1,0:T(1,128)} %probes.1), custom_call_target="tpu_custom_call" | custom-call | bytes 9000000 | tf_op jit(solution)/shard_map/table/pallas_call | solution.py:284
  6.4 0.0 copy-start
  6.4 0.0 collective-permute-done.1
  6.4 0.7 collective-permute-done
  7.1 1.6 %collective-permute-start.2 = (f32[8,1152]{1,0:T(8,128)S(1)}, f32[8,1152]{1,0:T(8,128)S(1)}, u32[]{:S(2)}, u32[]{:S(2)}) collective-permute-start(f32[8,1152]{1,0:T(8,128)S(1)} %get-tuple-element.29), channel_id=1, source_target_pairs={{0,1},{1,2},{2,3},{3,4},{4,5},{5,6},{6,7},{7,8},{8,9},{9,10},{10,1... | collective-permute-start | bytes 110600 | tf_op jit(solution)/shard_map/ppermute | solution.py:747
  8.7 5.0 %collective-permute-start.3 = (f32[8,1152]{1,0:T(8,128)S(1)}, f32[8,1152]{1,0:T(8,128)S(1)}, u32[]{:S(2)}, u32[]{:S(2)}) collective-permute-start(f32[8,1152]{1,0:T(8,128)S(1)} %get-tuple-element.30), channel_id=1, source_target_pairs={{0,15},{1,0},{2,1},{3,2},{4,3},{5,4},{6,5},{7,6},{8,7},{9,8},{10,9... | collective-permute-start | bytes 110600 | tf_op jit(solution)/shard_map/ppermute | solution.py:747
  13.7 0.0 copy-done
  13.8 11.8 %rows_at_sides.1.staged = f32[16384,128]{1,0:T(8,128)S(1)} custom-call(f32[4096,128]{1,0:T(8,128)S(1)} %table.1, s32[24576]{0:T(1024)S(1)} %bitcast.11), custom_call_target="tpu_custom_call" | custom-call | bytes 33000000 | tf_op jit(solution)/shard_map/rows_at_sides/pallas_call | solution.py:355
  25.6 0.0 collective-permute-done.2.before.before_weights
  25.6 0.0 collective-permute-done.3.after.after_weights
  25.6 3.4 %side_sums.1 = (f32[32,1024]{1,0:T(8,128)S(1)}, f32[32,1024]{1,0:T(8,128)S(1)}) custom-call(f32[16384,128]{1,0:T(8,128)S(1)} %rows_at_sides.1.staged, s32[4,6144]{1,0:T(4,128)S(1)} %bitcast.7, f32[8,1152]{1,0:T(8,128)S(1)} %collective-permute-done.2.before.before_weights, f32[8,1152]{1,0:T(8,128)S(1)} %collective-permute-done.3.after.after_weights), custom_call_target="tpu_custom_call" | custom-call | bytes 3000000 | tf_op jit(solution)/shard_map/side_sums/pallas_call | solution.py:324
  29.0 0.0 copy-start.1
  29.1 0.0 copy-start.2
  29.1 0.0 copy-start.3
  29.1 0.0 copy-start.4
  29.1 2.0 %collective-permute-start.4 = (f32[32,1024]{1,0:T(8,128)S(1)}, f32[32,1024]{1,0:T(8,128)S(1)}, u32[]{:S(2)}, u32[]{:S(2)}) collective-permute-start(f32[32,1024]{1,0:T(8,128)S(1)} %get-tuple-element.31), channel_id=1, source_target_pairs={{0,15},{1,0},{2,1},{3,2},{4,3},{5,4},{6,5},{7,6},{8,7},{9,8},{10,9... | collective-permute-start | bytes 393224 | tf_op jit(solution)/shard_map/ppermute | solution.py:747
  31.1 0.1 collective-permute-start.5
  31.2 7.9 %same_sums.1.same = f32[32,1024]{1,0:T(8,128)S(1)} custom-call(f32[4096,128]{1,0:T(8,128)S(1)} %table.1, s32[4,6144]{1,0:T(4,128)S(1)} %bitcast.8, s32[24576]{0:T(1024)S(1)} %bitcast.12, f32[4,6144]{1,0:T(4,128)S(1)} %bitcast.19, f32[4,6144]{1,0:T(4,128)S(1)} %bitcast.16), custom_call_target="tpu_custom_call" | custom-call | bytes 24000000 | tf_op jit(solution)/shard_map/same_sums/pallas_call | solution.py:388
  39.1 0.0 collective-permute-done.4.before
  39.1 0.3 collective-permute-done.5.after
  39.4 0.0 collective-permute-start.6
  39.4 0.6 collective-permute-start.7
  40.1 0.0 copy-done.1
  40.1 0.0 copy-done.2
  40.1 0.0 copy-done.3
  40.1 0.0 copy-done.4
  40.1 5.2 %forward.1 = (f32[4096,128]{1,0:T(8,128)S(1)}, f32[4096,128]{1,0:T(8,128)S(1)}, f32[4096,128]{1,0:T(8,128)S(1)}, f32[4096,128]{1,0:T(8,128)S(1)}, f32[4096,128]{...) custom-call(f32[4096,128]{1,0:T(8,128)S(1)} %table.1, f32[1,32768]{1,0:T(1,128)S(1)} %copy-done.2, ...), custom_call_target="tpu_custom_call" | custom-call | bytes 21000000 | tf_op jit(solution)/shard_map/forward/pallas_call | solution.py:454
  45.3 1.9 %collective-permute-done.6.near = f32[48,1024]{1,0:T(8,128)S(1)} collective-permute-done((f32[48,1024]{1,0:T(8,128)S(1)}, f32[48,1024]{1,0:T(8,128)S(1)}, u32[]{:S(2)}, u32[]{:S(2)}) %collective-permute-start.6) | collective-permute-done | bytes 196640 | tf_op jit(solution)/shard_map/ppermute | solution.py:747
  47.2 1.2 collective-permute-done.7.far
  48.5 9.2 %couple.1 = (f32[4096,128]{1,0:T(8,128)S(1)}, f32[48,1024]{1,0:T(8,128)S(1)}, f32[4096,128]{1,0:T(8,128)S(1)}, f32[4096,128]{1,0:T(8,128)S(1)}, f32[4096,128]{1,0:T(8,128)S(1)}, /*index=5*/f32[4096,128]{1,0:T(8,128)S(1)}) custom-call(s32[1,6144]{1,0:T(1,128)S(1)} %copy-done.1, ...), custom_call_target="tpu_custom_call", output_to_operand_aliasing={{2}: (4, {}), {3}: (5, {}), {4}: (6, {}), {5}: (7, {})} | custom-call | bytes 33000000 | tf_op jit(solution)/shard_map/couple/pallas_call | solution.py:493
  57.7 1.9 %collective-permute-start.9 = (f32[48,1024]{1,0:T(8,128)S(1)}, f32[48,1024]{1,0:T(8,128)S(1)}, u32[]{:S(2)}, u32[]{:S(2)}) collective-permute-start(f32[48,1024]{1,0:T(8,128)S(1)} %get-tuple-element.40), channel_id=1, source_target_pairs={{0,96},{1,97},{2,98},{3,99},{4,100},{5,101},{6,102},{7,103},{8,104... | collective-permute-start | bytes 589832 | tf_op jit(solution)/shard_map/ppermute | solution.py:747
  59.5 3.3 %at_receptors.1 = f32[48,1024]{1,0:T(8,128)S(1)} custom-call(f32[4096,128]{1,0:T(8,128)S(1)} %get-tuple-element.39.tangent, s32[1,6144]{1,0:T(1,128)S(1)} %copy-done.1, s32[6144]{0:T(1024)S(1)} %bitcast.22), custom_call_target="tpu_custom_call" | custom-call | bytes 9000000 | tf_op jit(solution)/shard_map/at_receptors/pallas_call | solution.py:517
  62.9 1.0 collective-permute-start.8
  63.8 1.4 %collective-permute-done.9.ready.far = f32[48,1024]{1,0:T(8,128)S(1)} collective-permute-done((f32[48,1024]{1,0:T(8,128)S(1)}, f32[48,1024]{1,0:T(8,128)S(1)}, u32[]{:S(2)}, u32[]{:S(2)}) %collective-permute-start.9) | collective-permute-done | bytes 196640 | tf_op jit(solution)/shard_map/ppermute | solution.py:747
  65.3 2.8 %transposed.1 = (f32[4096,128]{1,0:T(8,128)S(1)}, f32[4096,128]{1,0:T(8,128)S(1)}, f32[4096,128]{1,0:T(8,128)S(1)}, f32[4096,128]{1,0:T(8,128)S(1)}) custom-call(f32[4096,128]{1,0:T(8,128)S(1)} %get-tuple-element.39.tangent, f32[4096,128]{1,0:T(8,128)S(1)} %get-tuple-element.43.centre, f32[4096,128]{1,0:T(8,128)S(1)} %get-tuple-element.41.lower, ...), custom_call_target="tpu_custom_call" | custom-call | bytes 3000000 | tf_op jit(solution)/shard_map/transposed/pallas_call | solution.py:569
  68.0 0.0 collective-permute-done.8.near
  68.1 0.1 collective-permute-start.10
  68.1 5.3 %collective-permute-start.11 = (f32[32,1152]{1,0:T(8,128)S(1)}, f32[32,1152]{1,0:T(8,128)S(1)}, u32[]{:S(2)}, u32[]{:S(2)}) collective-permute-start(f32[32,1152]{1,0:T(8,128)S(1)} %get-tuple-element.46), channel_id=1, source_target_pairs={{0,15},{1,0},{2,1},{3,2},{4,3},{5,4},{6,5},{7,6},{8,7},{9,8},{10,9... | collective-permute-start | bytes 442376 | tf_op jit(solution)/shard_map/ppermute | solution.py:747
  73.5 7.1 %add_same.1 = (f32[4096,128]{1,0:T(8,128)S(1)}, f32[4096,128]{1,0:T(8,128)S(1)}, f32[4096,128]{1,0:T(8,128)S(1)}, f32[4096,128]{1,0:T(8,128)S(1)}) custom-call(s32[4,6144]{1,0:T(4,128)S(1)} %bitcast.9, s32[24576]{0:T(1024)S(1)} %bitcast.13, f32[4,6144]{1,0:T(4,128)S(1)} %bitcast.20, ...), custom_call_target="tpu_custom_call", output_to_operand_aliasing={{0}: (6, {}), {1}: (7, {}), {2}: (8, {}), {3}: (9, {})} | custom-call | bytes 27000000 | tf_op jit(solution)/shard_map/add_same/pallas_call | solution.py:593
  80.6 0.0 collective-permute-done.10.before
  80.6 0.0 collective-permute-done.11.after
  80.6 17.0 %add_sides.1 = (f32[4096,128]{1,0:T(8,128)S(1)}, f32[2,128]{1,0:T(2,128)S(1)}, f32[4096,128]{1,0:T(8,128)S(1)}, f32[4096,128]{1,0:T(8,128)S(1)}, f32[4096,128]{1,0:T(8,128)S(1)}, /*index=5*/f32[4096,128]{1,0:T(8,128)S(1)}) custom-call(s32[4,6144]{1,0:T(4,128)S(1)} %bitcast.10, ...), custom_call_target="tpu_custom_call", output_to_operand_aliasing={{2}: (6, {}), {3}: (7, {}), {4}: (8, {}), {5}: (9, {})} | custom-call | bytes 54000000 | tf_op jit(solution)/shard_map/add_sides/pallas_call | solution.py:664
  97.6 9.3 %all_to_all.10 = f32[8,2,128]{2,1,0:T(2,128)S(1)} all-to-all(f32[8,2,128]{2,1,0:T(2,128)S(1)} %broadcast_in_dim.6), channel_id=1, replica_groups=mesh['grid'=8,'cell'=16] {'grid'}, dimensions={0} | all-to-all | bytes 16384 | tf_op jit(solution)/shard_map/all_to_all | solution.py:760
  107.0 10.5 %all_to_all.11 = f32[16,2,128]{2,1,0:T(2,128)S(1)} all-to-all(f32[16,2,128]{2,1,0:T(2,128)S(1)} %broadcast_in_dim.7), channel_id=1, replica_groups=mesh['grid'=8,'cell'=16] {'cell'}, dimensions={0} | all-to-all | bytes 32768 | tf_op jit(solution)/shard_map/all_to_all | solution.py:760
  117.6 4.8 %basis.1 = (f32[16,1,32768]{2,1,0:T(1,128)}, f32[16,16]{1,0:T(8,128)}) custom-call(f32[2,128]{1,0:T(2,128)S(1)} %reduce_sum.19.gram, f32[4096,128]{1,0:T(8,128)S(1)} %get-tuple-element.55.adjoint), custom_call_target="tpu_custom_call" | custom-call | bytes 18000000 | tf_op jit(solution)/shard_map/basis/pallas_call | solution.py:725
  (10 shorter events, 0.2 us)
Async XLA Ops:
  0.6 5.8 %collective-permute-start.1 = (f32[1,4,6144]{2,1,0:T(4,128)}, f32[1,4,6144]{2,1,0:T(4,128)S(1)}, u32[]{:S(2)}, u32[]{:S(2)}) collective-permute-start(f32[1,4,6144]{2,1,0:T(4,128)} %param.13), channel_id=1, source_target_pairs={{0,96},{1,97},{2,98},{3,99},{4,100},{5,101},{6,102},{7,103},{8,104... | collective-permute-start | bytes 294920 | tf_op jit(solution)/shard_map/ppermute | solution.py:747
  3.6 3.5 %collective-permute-start = (f32[1,4,6144]{2,1,0:T(4,128)}, f32[1,4,6144]{2,1,0:T(4,128)S(1)}, u32[]{:S(2)}, u32[]{:S(2)}) collective-permute-start(f32[1,4,6144]{2,1,0:T(4,128)} %param.13), channel_id=1, source_target_pairs={{0,112},{1,113},{2,114},{3,115},{4,116},{5,117},{6,118},{7,119},{8... | collective-permute-start | bytes 294920 | tf_op jit(solution)/shard_map/ppermute | solution.py:747
  6.4 7.3 %copy-start = (s32[1,4,6144]{2,1,0:T(4,128)S(1)}, s32[1,4,6144]{2,1,0:T(4,128)}, u32[]{:S(2)}) copy-start(s32[1,4,6144]{2,1,0:T(4,128)} %param.11) | copy-start | bytes 294916
  7.1 18.5 %collective-permute-start.2 = (f32[8,1152]{1,0:T(8,128)S(1)}, f32[8,1152]{1,0:T(8,128)S(1)}, u32[]{:S(2)}, u32[]{:S(2)}) collective-permute-start(f32[8,1152]{1,0:T(8,128)S(1)} %get-tuple-element.29), channel_id=1, source_target_pairs={{0,1},{1,2},{2,3},{3,4},{4,5},{5,6},{6,7},{7,8},{8,9},{9,10},{10,1... | collective-permute-start | bytes 110600 | tf_op jit(solution)/shard_map/ppermute | solution.py:747
  8.7 16.9 %collective-permute-start.3 = (f32[8,1152]{1,0:T(8,128)S(1)}, f32[8,1152]{1,0:T(8,128)S(1)}, u32[]{:S(2)}, u32[]{:S(2)}) collective-permute-start(f32[8,1152]{1,0:T(8,128)S(1)} %get-tuple-element.30), channel_id=1, source_target_pairs={{0,15},{1,0},{2,1},{3,2},{4,3},{5,4},{6,5},{7,6},{8,7},{9,8},{10,9... | collective-permute-start | bytes 110600 | tf_op jit(solution)/shard_map/ppermute | solution.py:747
  29.0 11.0 %copy-start.1 = (s32[1,6144]{1,0:T(1,128)S(1)}, s32[1,6144]{1,0:T(1,128)}, u32[]{:S(2)}) copy-start(s32[1,6144]{1,0:T(1,128)} %cells.3) | copy-start | bytes 73732
  29.1 11.0 %copy-start.2 = (f32[1,32768]{1,0:T(1,128)S(1)}, f32[1,32768]{1,0:T(1,128)}, u32[]{:S(2)}) copy-start(f32[1,32768]{1,0:T(1,128)} %centre.1) | copy-start | bytes 393220
  29.1 11.0 %copy-start.3 = (f32[1,32768]{1,0:T(1,128)S(1)}, f32[1,32768]{1,0:T(1,128)}, u32[]{:S(2)}) copy-start(f32[1,32768]{1,0:T(1,128)} %lower.1) | copy-start | bytes 393220
  29.1 11.0 %copy-start.4 = (f32[1,32768]{1,0:T(1,128)S(1)}, f32[1,32768]{1,0:T(1,128)}, u32[]{:S(2)}) copy-start(f32[1,32768]{1,0:T(1,128)} %upper.1) | copy-start | bytes 393220
  29.1 10.0 %collective-permute-start.4 = (f32[32,1024]{1,0:T(8,128)S(1)}, f32[32,1024]{1,0:T(8,128)S(1)}, u32[]{:S(2)}, u32[]{:S(2)}) collective-permute-start(f32[32,1024]{1,0:T(8,128)S(1)} %get-tuple-element.31), channel_id=1, source_target_pairs={{0,15},{1,0},{2,1},{3,2},{4,3},{5,4},{6,5},{7,6},{8,7},{9,8},{10,9... | collective-permute-start | bytes 393224 | tf_op jit(solution)/shard_map/ppermute | solution.py:747
  31.1 8.3 %collective-permute-start.5 = (f32[32,1024]{1,0:T(8,128)S(1)}, f32[32,1024]{1,0:T(8,128)S(1)}, u32[]{:S(2)}, u32[]{:S(2)}) collective-permute-start(f32[32,1024]{1,0:T(8,128)S(1)} %get-tuple-element.32), channel_id=1, source_target_pairs={{0,1},{1,2},{2,3},{3,4},{4,5},{5,6},{6,7},{7,8},{8,9},{9,10},{10,1... | collective-permute-start | bytes 393224 | tf_op jit(solution)/shard_map/ppermute | solution.py:747
  39.4 7.8 %collective-permute-start.6 = (f32[48,1024]{1,0:T(8,128)S(1)}, f32[48,1024]{1,0:T(8,128)S(1)}, u32[]{:S(2)}, u32[]{:S(2)}) collective-permute-start(f32[48,1024]{1,0:T(8,128)S(1)} %get-tuple-element.33), channel_id=1, source_target_pairs={{0,16},{1,17},{2,18},{3,19},{4,20},{5,21},{6,22},{7,23},{8,24},{9,... | collective-permute-start | bytes 589832 | tf_op jit(solution)/shard_map/ppermute | solution.py:747
  39.4 9.0 %collective-permute-start.7 = (f32[48,1024]{1,0:T(8,128)S(1)}, f32[48,1024]{1,0:T(8,128)S(1)}, u32[]{:S(2)}, u32[]{:S(2)}) collective-permute-start(f32[48,1024]{1,0:T(8,128)S(1)} %get-tuple-element.34), channel_id=1, source_target_pairs={{0,32},{1,33},{2,34},{3,35},{4,36},{5,37},{6,38},{7,39},{8,40},{9,... | collective-permute-start | bytes 589832 | tf_op jit(solution)/shard_map/ppermute | solution.py:747
  57.7 7.6 %collective-permute-start.9 = (f32[48,1024]{1,0:T(8,128)S(1)}, f32[48,1024]{1,0:T(8,128)S(1)}, u32[]{:S(2)}, u32[]{:S(2)}) collective-permute-start(f32[48,1024]{1,0:T(8,128)S(1)} %get-tuple-element.40), channel_id=1, source_target_pairs={{0,96},{1,97},{2,98},{3,99},{4,100},{5,101},{6,102},{7,103},{8,104... | collective-permute-start | bytes 589832 | tf_op jit(solution)/shard_map/ppermute | solution.py:747
  62.9 5.2 %collective-permute-start.8 = (f32[48,1024]{1,0:T(8,128)S(1)}, f32[48,1024]{1,0:T(8,128)S(1)}, u32[]{:S(2)}, u32[]{:S(2)}) collective-permute-start(f32[48,1024]{1,0:T(8,128)S(1)} %at_receptors.1), channel_id=1, source_target_pairs={{0,112},{1,113},{2,114},{3,115},{4,116},{5,117},{6,118},{7,119},{8... | collective-permute-start | bytes 589832 | tf_op jit(solution)/shard_map/ppermute | solution.py:747
  68.1 12.6 %collective-permute-start.10 = (f32[32,1152]{1,0:T(8,128)S(1)}, f32[32,1152]{1,0:T(8,128)S(1)}, u32[]{:S(2)}, u32[]{:S(2)}) collective-permute-start(f32[32,1152]{1,0:T(8,128)S(1)} %get-tuple-element.45), channel_id=1, source_target_pairs={{0,1},{1,2},{2,3},{3,4},{4,5},{5,6},{6,7},{7,8},{8,9},{9,10},{10,1... | collective-permute-start | bytes 442376 | tf_op jit(solution)/shard_map/ppermute | solution.py:747
  68.1 12.5 %collective-permute-start.11 = (f32[32,1152]{1,0:T(8,128)S(1)}, f32[32,1152]{1,0:T(8,128)S(1)}, u32[]{:S(2)}, u32[]{:S(2)}) collective-permute-start(f32[32,1152]{1,0:T(8,128)S(1)} %get-tuple-element.46), channel_id=1, source_target_pairs={{0,15},{1,0},{2,1},{3,2},{4,3},{5,4},{6,5},{7,6},{8,7},{9,8},{10,9... | collective-permute-start | bytes 442376 | tf_op jit(solution)/shard_map/ppermute | solution.py:747

commit v9 on v8

--- a/solution.py
+++ b/solution.py
@@ -23,7 +23,7 @@
 WAYS = 8
 SUMS = 4
 QUARTER = SLOTS // 4
-UNROLL = 8
+UNROLL = 16
 ADD_UNROLL = 32
 
 AXES = ("grid", "cell")

time: 123 us -> 122 us (level)
  no operation moved by 1% of the time
where the time goes in v9:
time: 122 us
  Pallas kernels  74.5 us (61%)
  starting transfers between devices  20.5 us (17%)
  blocking collectives  19.9 us (16%)
  waiting for transfers between devices  5.82 us (5%)
    ppermute x12, starting transfers between devices, moved(): return lax.ppermute(value, AXES, route)  20.5 us
    all_to_all x2, blocking collectives, axis_sum(): return jnp.sum(lax.all_to_all(copies, axis, 0, 0), axis=0)  19.9 us
    pallas_call x1, Pallas kernels, add_sides(): pl.pallas_call(donor_sides_kernel, out_shape=[resident(ROWS, LANES), jax....  17 us
    pallas_call x1, Pallas kernels, rows_at_sides(): pl.pallas_call(rows_kernel, out_shape=resident(len(segs) * FRINGE, LANES)...  11.3 us
    pallas_call x1, Pallas kernels, couple(): pl.pallas_call(couple_kernel, out_shape=[resident(ROWS, LANES), TRIPLE] +...  9.11 us
    pallas_call x1, Pallas kernels, same_sums(): pl.pallas_call(same_sums_kernel, out_shape=PAIR, in_specs=[VMEM, VMEM, HB...  7.63 us
    pallas_call x1, Pallas kernels, add_same(): pl.pallas_call(donor_same_kernel, out_shape=[resident(ROWS, LANES)] * SUM...  7.12 us
    ppermute x12, waiting for transfers between devices, moved(): return lax.ppermute(value, AXES, route)  5.82 us
  transfers between devices with their start and end apart: 12, of which 5 were waited for; matrix products, arithmetic and copies ran while one was open for 0% of the time, Pallas kernels for 33%

profile of v9, /device:TPU:0, one launch (start us, length us, event | category | flops | bytes accessed | tf_op | source)
XLA Modules:
  0.0 121.7 jit_solution(5752935411378320121)
XLA Ops:
  0.6 2.9 %collective-permute-start.1 = (f32[1,4,6144]{2,1,0:T(4,128)}, f32[1,4,6144]{2,1,0:T(4,128)S(1)}, u32[]{:S(2)}, u32[]{:S(2)}) collective-permute-start(f32[1,4,6144]{2,1,0:T(4,128)} %param.13), channel_id=1, source_target_pairs={{0,96},{1,97},{2,98},{3,99},{4,100},{5,101},{6,102},{7,103},{8,104... | collective-permute-start | bytes 294920 | tf_op jit(solution)/shard_map/ppermute | solution.py:747
  3.6 0.0 collective-permute-start
  3.6 2.8 %table.1 = f32[4096,128]{1,0:T(8,128)S(1)} custom-call(f32[16,1,32768]{2,1,0:T(1,128)} %probes.1), custom_call_target="tpu_custom_call" | custom-call | bytes 9000000 | tf_op jit(solution)/shard_map/table/pallas_call | solution.py:284
  6.4 0.0 copy-start
  6.4 0.0 collective-permute-done.1
  6.4 0.7 collective-permute-done
  7.1 1.6 %collective-permute-start.2 = (f32[8,1152]{1,0:T(8,128)S(1)}, f32[8,1152]{1,0:T(8,128)S(1)}, u32[]{:S(2)}, u32[]{:S(2)}) collective-permute-start(f32[8,1152]{1,0:T(8,128)S(1)} %get-tuple-element.29), channel_id=1, source_target_pairs={{0,1},{1,2},{2,3},{3,4},{4,5},{5,6},{6,7},{7,8},{8,9},{9,10},{10,1... | collective-permute-start | bytes 110600 | tf_op jit(solution)/shard_map/ppermute | solution.py:747
  8.7 5.0 %collective-permute-start.3 = (f32[8,1152]{1,0:T(8,128)S(1)}, f32[8,1152]{1,0:T(8,128)S(1)}, u32[]{:S(2)}, u32[]{:S(2)}) collective-permute-start(f32[8,1152]{1,0:T(8,128)S(1)} %get-tuple-element.30), channel_id=1, source_target_pairs={{0,15},{1,0},{2,1},{3,2},{4,3},{5,4},{6,5},{7,6},{8,7},{9,8},{10,9... | collective-permute-start | bytes 110600 | tf_op jit(solution)/shard_map/ppermute | solution.py:747
  13.7 0.0 copy-done
  13.8 11.3 %rows_at_sides.1.staged = f32[16384,128]{1,0:T(8,128)S(1)} custom-call(f32[4096,128]{1,0:T(8,128)S(1)} %table.1, s32[24576]{0:T(1024)S(1)} %bitcast.11), custom_call_target="tpu_custom_call" | custom-call | bytes 33000000 | tf_op jit(solution)/shard_map/rows_at_sides/pallas_call | solution.py:355
  25.1 0.0 collective-permute-done.2.before.before_weights
  25.1 0.0 collective-permute-done.3.after.after_weights
  25.1 3.4 %side_sums.1 = (f32[32,1024]{1,0:T(8,128)S(1)}, f32[32,1024]{1,0:T(8,128)S(1)}) custom-call(f32[16384,128]{1,0:T(8,128)S(1)} %rows_at_sides.1.staged, s32[4,6144]{1,0:T(4,128)S(1)} %bitcast.7, f32[8,1152]{1,0:T(8,128)S(1)} %collective-permute-done.2.before.before_weights, f32[8,1152]{1,0:T(8,128)S(1)} %collective-permute-done.3.after.after_weights), custom_call_target="tpu_custom_call" | custom-call | bytes 3000000 | tf_op jit(solution)/shard_map/side_sums/pallas_call | solution.py:324
  28.5 0.0 copy-start.1
  28.6 0.0 copy-start.2
  28.6 0.0 copy-start.3
  28.6 0.0 copy-start.4
  28.6 2.0 %collective-permute-start.4 = (f32[32,1024]{1,0:T(8,128)S(1)}, f32[32,1024]{1,0:T(8,128)S(1)}, u32[]{:S(2)}, u32[]{:S(2)}) collective-permute-start(f32[32,1024]{1,0:T(8,128)S(1)} %get-tuple-element.31), channel_id=1, source_target_pairs={{0,15},{1,0},{2,1},{3,2},{4,3},{5,4},{6,5},{7,6},{8,7},{9,8},{10,9... | collective-permute-start | bytes 393224 | tf_op jit(solution)/shard_map/ppermute | solution.py:747
  30.6 0.1 collective-permute-start.5
  30.7 7.6 %same_sums.1.same = f32[32,1024]{1,0:T(8,128)S(1)} custom-call(f32[4096,128]{1,0:T(8,128)S(1)} %table.1, s32[4,6144]{1,0:T(4,128)S(1)} %bitcast.8, s32[24576]{0:T(1024)S(1)} %bitcast.12, f32[4,6144]{1,0:T(4,128)S(1)} %bitcast.19, f32[4,6144]{1,0:T(4,128)S(1)} %bitcast.16), custom_call_target="tpu_custom_call" | custom-call | bytes 24000000 | tf_op jit(solution)/shard_map/same_sums/pallas_call | solution.py:388
  38.3 0.0 collective-permute-done.4.before
  38.3 0.6 collective-permute-done.5.after
  38.9 0.0 collective-permute-start.6
  38.9 0.6 collective-permute-start.7
  39.6 0.0 copy-done.1
  39.6 0.0 copy-done.2
  39.6 0.0 copy-done.3
  39.6 0.0 copy-done.4
  39.6 5.2 %forward.1 = (f32[4096,128]{1,0:T(8,128)S(1)}, f32[4096,128]{1,0:T(8,128)S(1)}, f32[4096,128]{1,0:T(8,128)S(1)}, f32[4096,128]{1,0:T(8,128)S(1)}, f32[4096,128]{...) custom-call(f32[4096,128]{1,0:T(8,128)S(1)} %table.1, f32[1,32768]{1,0:T(1,128)S(1)} %copy-done.2, ...), custom_call_target="tpu_custom_call" | custom-call | bytes 21000000 | tf_op jit(solution)/shard_map/forward/pallas_call | solution.py:454
  44.8 1.9 %collective-permute-done.6.near = f32[48,1024]{1,0:T(8,128)S(1)} collective-permute-done((f32[48,1024]{1,0:T(8,128)S(1)}, f32[48,1024]{1,0:T(8,128)S(1)}, u32[]{:S(2)}, u32[]{:S(2)}) %collective-permute-start.6) | collective-permute-done | bytes 196640 | tf_op jit(solution)/shard_map/ppermute | solution.py:747
  46.7 1.2 collective-permute-done.7.far
  47.9 9.1 %couple.1 = (f32[4096,128]{1,0:T(8,128)S(1)}, f32[48,1024]{1,0:T(8,128)S(1)}, f32[4096,128]{1,0:T(8,128)S(1)}, f32[4096,128]{1,0:T(8,128)S(1)}, f32[4096,128]{1,0:T(8,128)S(1)}, /*index=5*/f32[4096,128]{1,0:T(8,128)S(1)}) custom-call(s32[1,6144]{1,0:T(1,128)S(1)} %copy-done.1, ...), custom_call_target="tpu_custom_call", output_to_operand_aliasing={{2}: (4, {}), {3}: (5, {}), {4}: (6, {}), {5}: (7, {})} | custom-call | bytes 33000000 | tf_op jit(solution)/shard_map/couple/pallas_call | solution.py:493
  57.1 1.9 %collective-permute-start.9 = (f32[48,1024]{1,0:T(8,128)S(1)}, f32[48,1024]{1,0:T(8,128)S(1)}, u32[]{:S(2)}, u32[]{:S(2)}) collective-permute-start(f32[48,1024]{1,0:T(8,128)S(1)} %get-tuple-element.40), channel_id=1, source_target_pairs={{0,96},{1,97},{2,98},{3,99},{4,100},{5,101},{6,102},{7,103},{8,104... | collective-permute-start | bytes 589832 | tf_op jit(solution)/shard_map/ppermute | solution.py:747
  58.9 3.2 %at_receptors.1 = f32[48,1024]{1,0:T(8,128)S(1)} custom-call(f32[4096,128]{1,0:T(8,128)S(1)} %get-tuple-element.39.tangent, s32[1,6144]{1,0:T(1,128)S(1)} %copy-done.1, s32[6144]{0:T(1024)S(1)} %bitcast.22), custom_call_target="tpu_custom_call" | custom-call | bytes 9000000 | tf_op jit(solution)/shard_map/at_receptors/pallas_call | solution.py:517
  62.2 0.9 collective-permute-start.8
  63.1 1.5 %collective-permute-done.9.ready.far = f32[48,1024]{1,0:T(8,128)S(1)} collective-permute-done((f32[48,1024]{1,0:T(8,128)S(1)}, f32[48,1024]{1,0:T(8,128)S(1)}, u32[]{:S(2)}, u32[]{:S(2)}) %collective-permute-start.9) | collective-permute-done | bytes 196640 | tf_op jit(solution)/shard_map/ppermute | solution.py:747
  64.6 2.8 %transposed.1 = (f32[4096,128]{1,0:T(8,128)S(1)}, f32[4096,128]{1,0:T(8,128)S(1)}, f32[4096,128]{1,0:T(8,128)S(1)}, f32[4096,128]{1,0:T(8,128)S(1)}) custom-call(f32[4096,128]{1,0:T(8,128)S(1)} %get-tuple-element.39.tangent, f32[4096,128]{1,0:T(8,128)S(1)} %get-tuple-element.43.centre, f32[4096,128]{1,0:T(8,128)S(1)} %get-tuple-element.41.lower, ...), custom_call_target="tpu_custom_call" | custom-call | bytes 3000000 | tf_op jit(solution)/shard_map/transposed/pallas_call | solution.py:569
  67.3 0.0 collective-permute-done.8.near
  67.4 0.1 collective-permute-start.10
  67.5 5.3 %collective-permute-start.11 = (f32[32,1152]{1,0:T(8,128)S(1)}, f32[32,1152]{1,0:T(8,128)S(1)}, u32[]{:S(2)}, u32[]{:S(2)}) collective-permute-start(f32[32,1152]{1,0:T(8,128)S(1)} %get-tuple-element.46), channel_id=1, source_target_pairs={{0,15},{1,0},{2,1},{3,2},{4,3},{5,4},{6,5},{7,6},{8,7},{9,8},{10,9... | collective-permute-start | bytes 442376 | tf_op jit(solution)/shard_map/ppermute | solution.py:747
  72.8 7.1 %add_same.1 = (f32[4096,128]{1,0:T(8,128)S(1)}, f32[4096,128]{1,0:T(8,128)S(1)}, f32[4096,128]{1,0:T(8,128)S(1)}, f32[4096,128]{1,0:T(8,128)S(1)}) custom-call(s32[4,6144]{1,0:T(4,128)S(1)} %bitcast.9, s32[24576]{0:T(1024)S(1)} %bitcast.13, f32[4,6144]{1,0:T(4,128)S(1)} %bitcast.20, ...), custom_call_target="tpu_custom_call", output_to_operand_aliasing={{0}: (6, {}), {1}: (7, {}), {2}: (8, {}), {3}: (9, {})} | custom-call | bytes 27000000 | tf_op jit(solution)/shard_map/add_same/pallas_call | solution.py:593
  79.9 0.0 collective-permute-done.10.before
  79.9 0.0 collective-permute-done.11.after
  79.9 17.0 %add_sides.1 = (f32[4096,128]{1,0:T(8,128)S(1)}, f32[2,128]{1,0:T(2,128)S(1)}, f32[4096,128]{1,0:T(8,128)S(1)}, f32[4096,128]{1,0:T(8,128)S(1)}, f32[4096,128]{1,0:T(8,128)S(1)}, /*index=5*/f32[4096,128]{1,0:T(8,128)S(1)}) custom-call(s32[4,6144]{1,0:T(4,128)S(1)} %bitcast.10, ...), custom_call_target="tpu_custom_call", output_to_operand_aliasing={{2}: (6, {}), {3}: (7, {}), {4}: (8, {}), {5}: (9, {})} | custom-call | bytes 54000000 | tf_op jit(solution)/shard_map/add_sides/pallas_call | solution.py:664
  97.0 9.4 %all_to_all.10 = f32[8,2,128]{2,1,0:T(2,128)S(1)} all-to-all(f32[8,2,128]{2,1,0:T(2,128)S(1)} %broadcast_in_dim.6), channel_id=1, replica_groups=mesh['grid'=8,'cell'=16] {'grid'}, dimensions={0} | all-to-all | bytes 16384 | tf_op jit(solution)/shard_map/all_to_all | solution.py:760
  106.4 10.6 %all_to_all.11 = f32[16,2,128]{2,1,0:T(2,128)S(1)} all-to-all(f32[16,2,128]{2,1,0:T(2,128)S(1)} %broadcast_in_dim.7), channel_id=1, replica_groups=mesh['grid'=8,'cell'=16] {'cell'}, dimensions={0} | all-to-all | bytes 32768 | tf_op jit(solution)/shard_map/all_to_all | solution.py:760
  116.9 4.8 %basis.1 = (f32[16,1,32768]{2,1,0:T(1,128)}, f32[16,16]{1,0:T(8,128)}) custom-call(f32[2,128]{1,0:T(2,128)S(1)} %reduce_sum.19.gram, f32[4096,128]{1,0:T(8,128)S(1)} %get-tuple-element.55.adjoint), custom_call_target="tpu_custom_call" | custom-call | bytes 18000000 | tf_op jit(solution)/shard_map/basis/pallas_call | solution.py:725
  (10 shorter events, 0.2 us)
Async XLA Ops:
  0.6 5.8 %collective-permute-start.1 = (f32[1,4,6144]{2,1,0:T(4,128)}, f32[1,4,6144]{2,1,0:T(4,128)S(1)}, u32[]{:S(2)}, u32[]{:S(2)}) collective-permute-start(f32[1,4,6144]{2,1,0:T(4,128)} %param.13), channel_id=1, source_target_pairs={{0,96},{1,97},{2,98},{3,99},{4,100},{5,101},{6,102},{7,103},{8,104... | collective-permute-start | bytes 294920 | tf_op jit(solution)/shard_map/ppermute | solution.py:747
  3.6 3.5 %collective-permute-start = (f32[1,4,6144]{2,1,0:T(4,128)}, f32[1,4,6144]{2,1,0:T(4,128)S(1)}, u32[]{:S(2)}, u32[]{:S(2)}) collective-permute-start(f32[1,4,6144]{2,1,0:T(4,128)} %param.13), channel_id=1, source_target_pairs={{0,112},{1,113},{2,114},{3,115},{4,116},{5,117},{6,118},{7,119},{8... | collective-permute-start | bytes 294920 | tf_op jit(solution)/shard_map/ppermute | solution.py:747
  6.4 7.3 %copy-start = (s32[1,4,6144]{2,1,0:T(4,128)S(1)}, s32[1,4,6144]{2,1,0:T(4,128)}, u32[]{:S(2)}) copy-start(s32[1,4,6144]{2,1,0:T(4,128)} %param.11) | copy-start | bytes 294916
  7.1 18.0 %collective-permute-start.2 = (f32[8,1152]{1,0:T(8,128)S(1)}, f32[8,1152]{1,0:T(8,128)S(1)}, u32[]{:S(2)}, u32[]{:S(2)}) collective-permute-start(f32[8,1152]{1,0:T(8,128)S(1)} %get-tuple-element.29), channel_id=1, source_target_pairs={{0,1},{1,2},{2,3},{3,4},{4,5},{5,6},{6,7},{7,8},{8,9},{9,10},{10,1... | collective-permute-start | bytes 110600 | tf_op jit(solution)/shard_map/ppermute | solution.py:747
  8.7 16.4 %collective-permute-start.3 = (f32[8,1152]{1,0:T(8,128)S(1)}, f32[8,1152]{1,0:T(8,128)S(1)}, u32[]{:S(2)}, u32[]{:S(2)}) collective-permute-start(f32[8,1152]{1,0:T(8,128)S(1)} %get-tuple-element.30), channel_id=1, source_target_pairs={{0,15},{1,0},{2,1},{3,2},{4,3},{5,4},{6,5},{7,6},{8,7},{9,8},{10,9... | collective-permute-start | bytes 110600 | tf_op jit(solution)/shard_map/ppermute | solution.py:747
  28.5 11.0 %copy-start.1 = (s32[1,6144]{1,0:T(1,128)S(1)}, s32[1,6144]{1,0:T(1,128)}, u32[]{:S(2)}) copy-start(s32[1,6144]{1,0:T(1,128)} %cells.3) | copy-start | bytes 73732
  28.6 11.0 %copy-start.2 = (f32[1,32768]{1,0:T(1,128)S(1)}, f32[1,32768]{1,0:T(1,128)}, u32[]{:S(2)}) copy-start(f32[1,32768]{1,0:T(1,128)} %centre.1) | copy-start | bytes 393220
  28.6 11.0 %copy-start.3 = (f32[1,32768]{1,0:T(1,128)S(1)}, f32[1,32768]{1,0:T(1,128)}, u32[]{:S(2)}) copy-start(f32[1,32768]{1,0:T(1,128)} %lower.1) | copy-start | bytes 393220
  28.6 11.0 %copy-start.4 = (f32[1,32768]{1,0:T(1,128)S(1)}, f32[1,32768]{1,0:T(1,128)}, u32[]{:S(2)}) copy-start(f32[1,32768]{1,0:T(1,128)} %upper.1) | copy-start | bytes 393220
  28.6 9.7 %collective-permute-start.4 = (f32[32,1024]{1,0:T(8,128)S(1)}, f32[32,1024]{1,0:T(8,128)S(1)}, u32[]{:S(2)}, u32[]{:S(2)}) collective-permute-start(f32[32,1024]{1,0:T(8,128)S(1)} %get-tuple-element.31), channel_id=1, source_target_pairs={{0,15},{1,0},{2,1},{3,2},{4,3},{5,4},{6,5},{7,6},{8,7},{9,8},{10,9... | collective-permute-start | bytes 393224 | tf_op jit(solution)/shard_map/ppermute | solution.py:747
  30.6 8.3 %collective-permute-start.5 = (f32[32,1024]{1,0:T(8,128)S(1)}, f32[32,1024]{1,0:T(8,128)S(1)}, u32[]{:S(2)}, u32[]{:S(2)}) collective-permute-start(f32[32,1024]{1,0:T(8,128)S(1)} %get-tuple-element.32), channel_id=1, source_target_pairs={{0,1},{1,2},{2,3},{3,4},{4,5},{5,6},{6,7},{7,8},{8,9},{9,10},{10,1... | collective-permute-start | bytes 393224 | tf_op jit(solution)/shard_map/ppermute | solution.py:747
  38.9 7.8 %collective-permute-start.6 = (f32[48,1024]{1,0:T(8,128)S(1)}, f32[48,1024]{1,0:T(8,128)S(1)}, u32[]{:S(2)}, u32[]{:S(2)}) collective-permute-start(f32[48,1024]{1,0:T(8,128)S(1)} %get-tuple-element.33), channel_id=1, source_target_pairs={{0,16},{1,17},{2,18},{3,19},{4,20},{5,21},{6,22},{7,23},{8,24},{9,... | collective-permute-start | bytes 589832 | tf_op jit(solution)/shard_map/ppermute | solution.py:747
  38.9 9.0 %collective-permute-start.7 = (f32[48,1024]{1,0:T(8,128)S(1)}, f32[48,1024]{1,0:T(8,128)S(1)}, u32[]{:S(2)}, u32[]{:S(2)}) collective-permute-start(f32[48,1024]{1,0:T(8,128)S(1)} %get-tuple-element.34), channel_id=1, source_target_pairs={{0,32},{1,33},{2,34},{3,35},{4,36},{5,37},{6,38},{7,39},{8,40},{9,... | collective-permute-start | bytes 589832 | tf_op jit(solution)/shard_map/ppermute | solution.py:747
  57.1 7.5 %collective-permute-start.9 = (f32[48,1024]{1,0:T(8,128)S(1)}, f32[48,1024]{1,0:T(8,128)S(1)}, u32[]{:S(2)}, u32[]{:S(2)}) collective-permute-start(f32[48,1024]{1,0:T(8,128)S(1)} %get-tuple-element.40), channel_id=1, source_target_pairs={{0,96},{1,97},{2,98},{3,99},{4,100},{5,101},{6,102},{7,103},{8,104... | collective-permute-start | bytes 589832 | tf_op jit(solution)/shard_map/ppermute | solution.py:747
  62.2 5.2 %collective-permute-start.8 = (f32[48,1024]{1,0:T(8,128)S(1)}, f32[48,1024]{1,0:T(8,128)S(1)}, u32[]{:S(2)}, u32[]{:S(2)}) collective-permute-start(f32[48,1024]{1,0:T(8,128)S(1)} %at_receptors.1), channel_id=1, source_target_pairs={{0,112},{1,113},{2,114},{3,115},{4,116},{5,117},{6,118},{7,119},{8... | collective-permute-start | bytes 589832 | tf_op jit(solution)/shard_map/ppermute | solution.py:747
  67.4 12.6 %collective-permute-start.10 = (f32[32,1152]{1,0:T(8,128)S(1)}, f32[32,1152]{1,0:T(8,128)S(1)}, u32[]{:S(2)}, u32[]{:S(2)}) collective-permute-start(f32[32,1152]{1,0:T(8,128)S(1)} %get-tuple-element.45), channel_id=1, source_target_pairs={{0,1},{1,2},{2,3},{3,4},{4,5},{5,6},{6,7},{7,8},{8,9},{9,10},{10,1... | collective-permute-start | bytes 442376 | tf_op jit(solution)/shard_map/ppermute | solution.py:747
  67.5 12.5 %collective-permute-start.11 = (f32[32,1152]{1,0:T(8,128)S(1)}, f32[32,1152]{1,0:T(8,128)S(1)}, u32[]{:S(2)}, u32[]{:S(2)}) collective-permute-start(f32[32,1152]{1,0:T(8,128)S(1)} %get-tuple-element.46), channel_id=1, source_target_pairs={{0,15},{1,0},{2,1},{3,2},{4,3},{5,4},{6,5},{7,6},{8,7},{9,8},{10,9... | collective-permute-start | bytes 442376 | tf_op jit(solution)/shard_map/ppermute | solution.py:747

commit v10 on v9

--- a/solution.py
+++ b/solution.py
@@ -23,7 +23,7 @@
 WAYS = 8
 SUMS = 4
 QUARTER = SLOTS // 4
-UNROLL = 16
+UNROLL = 32
 ADD_UNROLL = 32
 
 AXES = ("grid", "cell")

time: 122 us -> 122 us (level)
  no operation moved by 1% of the time
where the time goes in v10:
time: 122 us
  Pallas kernels  74.1 us (61%)
  starting transfers between devices  20.5 us (17%)
  blocking collectives  19.9 us (16%)
  waiting for transfers between devices  6.05 us (5%)
    ppermute x12, starting transfers between devices, moved(): return lax.ppermute(value, AXES, route)  20.5 us
    all_to_all x2, blocking collectives, axis_sum(): return jnp.sum(lax.all_to_all(copies, axis, 0, 0), axis=0)  19.9 us
    pallas_call x1, Pallas kernels, add_sides(): pl.pallas_call(donor_sides_kernel, out_shape=[resident(ROWS, LANES), jax....  17 us
    pallas_call x1, Pallas kernels, rows_at_sides(): pl.pallas_call(rows_kernel, out_shape=resident(len(segs) * FRINGE, LANES)...  11.1 us
    pallas_call x1, Pallas kernels, couple(): pl.pallas_call(couple_kernel, out_shape=[resident(ROWS, LANES), TRIPLE] +...  9.07 us
    pallas_call x1, Pallas kernels, same_sums(): pl.pallas_call(same_sums_kernel, out_shape=PAIR, in_specs=[VMEM, VMEM, HB...  7.52 us
    pallas_call x1, Pallas kernels, add_same(): pl.pallas_call(donor_same_kernel, out_shape=[resident(ROWS, LANES)] * SUM...  7.13 us
    ppermute x12, waiting for transfers between devices, moved(): return lax.ppermute(value, AXES, route)  6.05 us
  transfers between devices with their start and end apart: 12, of which 5 were waited for; matrix products, arithmetic and copies ran while one was open for 0% of the time, Pallas kernels for 33%

profile of v10, /device:TPU:0, one launch (start us, length us, event | category | flops | bytes accessed | tf_op | source)
XLA Modules:
  0.0 121.5 jit_solution(13664086101530104207)
XLA Ops:
  0.6 2.9 %collective-permute-start.1 = (f32[1,4,6144]{2,1,0:T(4,128)}, f32[1,4,6144]{2,1,0:T(4,128)S(1)}, u32[]{:S(2)}, u32[]{:S(2)}) collective-permute-start(f32[1,4,6144]{2,1,0:T(4,128)} %param.13), channel_id=1, source_target_pairs={{0,96},{1,97},{2,98},{3,99},{4,100},{5,101},{6,102},{7,103},{8,104... | collective-permute-start | bytes 294920 | tf_op jit(solution)/shard_map/ppermute | solution.py:747
  3.6 0.0 collective-permute-start
  3.6 2.8 %table.1 = f32[4096,128]{1,0:T(8,128)S(1)} custom-call(f32[16,1,32768]{2,1,0:T(1,128)} %probes.1), custom_call_target="tpu_custom_call" | custom-call | bytes 9000000 | tf_op jit(solution)/shard_map/table/pallas_call | solution.py:284
  6.4 0.0 copy-start
  6.4 0.0 collective-permute-done.1
  6.4 0.7 collective-permute-done
  7.1 1.6 %collective-permute-start.2 = (f32[8,1152]{1,0:T(8,128)S(1)}, f32[8,1152]{1,0:T(8,128)S(1)}, u32[]{:S(2)}, u32[]{:S(2)}) collective-permute-start(f32[8,1152]{1,0:T(8,128)S(1)} %get-tuple-element.29), channel_id=1, source_target_pairs={{0,1},{1,2},{2,3},{3,4},{4,5},{5,6},{6,7},{7,8},{8,9},{9,10},{10,1... | collective-permute-start | bytes 110600 | tf_op jit(solution)/shard_map/ppermute | solution.py:747
  8.7 5.0 %collective-permute-start.3 = (f32[8,1152]{1,0:T(8,128)S(1)}, f32[8,1152]{1,0:T(8,128)S(1)}, u32[]{:S(2)}, u32[]{:S(2)}) collective-permute-start(f32[8,1152]{1,0:T(8,128)S(1)} %get-tuple-element.30), channel_id=1, source_target_pairs={{0,15},{1,0},{2,1},{3,2},{4,3},{5,4},{6,5},{7,6},{8,7},{9,8},{10,9... | collective-permute-start | bytes 110600 | tf_op jit(solution)/shard_map/ppermute | solution.py:747
  13.7 0.0 copy-done
  13.8 11.1 %rows_at_sides.1.staged = f32[16384,128]{1,0:T(8,128)S(1)} custom-call(f32[4096,128]{1,0:T(8,128)S(1)} %table.1, s32[24576]{0:T(1024)S(1)} %bitcast.11), custom_call_target="tpu_custom_call" | custom-call | bytes 33000000 | tf_op jit(solution)/shard_map/rows_at_sides/pallas_call | solution.py:355
  24.9 0.0 collective-permute-done.2.before.before_weights
  24.9 0.0 collective-permute-done.3.after.after_weights
  24.9 3.4 %side_sums.1 = (f32[32,1024]{1,0:T(8,128)S(1)}, f32[32,1024]{1,0:T(8,128)S(1)}) custom-call(f32[16384,128]{1,0:T(8,128)S(1)} %rows_at_sides.1.staged, s32[4,6144]{1,0:T(4,128)S(1)} %bitcast.7, f32[8,1152]{1,0:T(8,128)S(1)} %collective-permute-done.2.before.before_weights, f32[8,1152]{1,0:T(8,128)S(1)} %collective-permute-done.3.after.after_weights), custom_call_target="tpu_custom_call" | custom-call | bytes 3000000 | tf_op jit(solution)/shard_map/side_sums/pallas_call | solution.py:324
  28.3 0.0 copy-start.1
  28.4 0.0 copy-start.2
  28.4 0.0 copy-start.3
  28.4 0.0 copy-start.4
  28.4 2.0 %collective-permute-start.4 = (f32[32,1024]{1,0:T(8,128)S(1)}, f32[32,1024]{1,0:T(8,128)S(1)}, u32[]{:S(2)}, u32[]{:S(2)}) collective-permute-start(f32[32,1024]{1,0:T(8,128)S(1)} %get-tuple-element.31), channel_id=1, source_target_pairs={{0,15},{1,0},{2,1},{3,2},{4,3},{5,4},{6,5},{7,6},{8,7},{9,8},{10,9... | collective-permute-start | bytes 393224 | tf_op jit(solution)/shard_map/ppermute | solution.py:747
  30.4 0.1 collective-permute-start.5
  30.5 7.5 %same_sums.1.same = f32[32,1024]{1,0:T(8,128)S(1)} custom-call(f32[4096,128]{1,0:T(8,128)S(1)} %table.1, s32[4,6144]{1,0:T(4,128)S(1)} %bitcast.8, s32[24576]{0:T(1024)S(1)} %bitcast.12, f32[4,6144]{1,0:T(4,128)S(1)} %bitcast.19, f32[4,6144]{1,0:T(4,128)S(1)} %bitcast.16), custom_call_target="tpu_custom_call" | custom-call | bytes 24000000 | tf_op jit(solution)/shard_map/same_sums/pallas_call | solution.py:388
  38.0 0.0 collective-permute-done.4.before
  38.0 0.7 collective-permute-done.5.after
  38.7 0.0 collective-permute-start.6
  38.8 0.6 collective-permute-start.7
  39.4 0.0 copy-done.1
  39.4 0.0 copy-done.2
  39.4 0.0 copy-done.3
  39.4 0.0 copy-done.4
  39.4 5.2 %forward.1 = (f32[4096,128]{1,0:T(8,128)S(1)}, f32[4096,128]{1,0:T(8,128)S(1)}, f32[4096,128]{1,0:T(8,128)S(1)}, f32[4096,128]{1,0:T(8,128)S(1)}, f32[4096,128]{...) custom-call(f32[4096,128]{1,0:T(8,128)S(1)} %table.1, f32[1,32768]{1,0:T(1,128)S(1)} %copy-done.2, ...), custom_call_target="tpu_custom_call" | custom-call | bytes 21000000 | tf_op jit(solution)/shard_map/forward/pallas_call | solution.py:454
  44.6 1.9 %collective-permute-done.6.near = f32[48,1024]{1,0:T(8,128)S(1)} collective-permute-done((f32[48,1024]{1,0:T(8,128)S(1)}, f32[48,1024]{1,0:T(8,128)S(1)}, u32[]{:S(2)}, u32[]{:S(2)}) %collective-permute-start.6) | collective-permute-done | bytes 196640 | tf_op jit(solution)/shard_map/ppermute | solution.py:747
  46.5 1.2 collective-permute-done.7.far
  47.8 9.1 %couple.1 = (f32[4096,128]{1,0:T(8,128)S(1)}, f32[48,1024]{1,0:T(8,128)S(1)}, f32[4096,128]{1,0:T(8,128)S(1)}, f32[4096,128]{1,0:T(8,128)S(1)}, f32[4096,128]{1,0:T(8,128)S(1)}, /*index=5*/f32[4096,128]{1,0:T(8,128)S(1)}) custom-call(s32[1,6144]{1,0:T(1,128)S(1)} %copy-done.1, ...), custom_call_target="tpu_custom_call", output_to_operand_aliasing={{2}: (4, {}), {3}: (5, {}), {4}: (6, {}), {5}: (7, {})} | custom-call | bytes 33000000 | tf_op jit(solution)/shard_map/couple/pallas_call | solution.py:493
  56.8 1.8 %collective-permute-start.9 = (f32[48,1024]{1,0:T(8,128)S(1)}, f32[48,1024]{1,0:T(8,128)S(1)}, u32[]{:S(2)}, u32[]{:S(2)}) collective-permute-start(f32[48,1024]{1,0:T(8,128)S(1)} %get-tuple-element.40), channel_id=1, source_target_pairs={{0,96},{1,97},{2,98},{3,99},{4,100},{5,101},{6,102},{7,103},{8,104... | collective-permute-start | bytes 589832 | tf_op jit(solution)/shard_map/ppermute | solution.py:747
  58.7 3.2 %at_receptors.1 = f32[48,1024]{1,0:T(8,128)S(1)} custom-call(f32[4096,128]{1,0:T(8,128)S(1)} %get-tuple-element.39.tangent, s32[1,6144]{1,0:T(1,128)S(1)} %copy-done.1, s32[6144]{0:T(1024)S(1)} %bitcast.22), custom_call_target="tpu_custom_call" | custom-call | bytes 9000000 | tf_op jit(solution)/shard_map/at_receptors/pallas_call | solution.py:517
  61.9 0.9 collective-permute-start.8
  62.8 1.6 %collective-permute-done.9.ready.far = f32[48,1024]{1,0:T(8,128)S(1)} collective-permute-done((f32[48,1024]{1,0:T(8,128)S(1)}, f32[48,1024]{1,0:T(8,128)S(1)}, u32[]{:S(2)}, u32[]{:S(2)}) %collective-permute-start.9) | collective-permute-done | bytes 196640 | tf_op jit(solution)/shard_map/ppermute | solution.py:747
  64.4 2.8 %transposed.1 = (f32[4096,128]{1,0:T(8,128)S(1)}, f32[4096,128]{1,0:T(8,128)S(1)}, f32[4096,128]{1,0:T(8,128)S(1)}, f32[4096,128]{1,0:T(8,128)S(1)}) custom-call(f32[4096,128]{1,0:T(8,128)S(1)} %get-tuple-element.39.tangent, f32[4096,128]{1,0:T(8,128)S(1)} %get-tuple-element.43.centre, f32[4096,128]{1,0:T(8,128)S(1)} %get-tuple-element.41.lower, ...), custom_call_target="tpu_custom_call" | custom-call | bytes 3000000 | tf_op jit(solution)/shard_map/transposed/pallas_call | solution.py:569
  67.2 0.0 collective-permute-done.8.near
  67.2 0.1 collective-permute-start.10
  67.3 5.3 %collective-permute-start.11 = (f32[32,1152]{1,0:T(8,128)S(1)}, f32[32,1152]{1,0:T(8,128)S(1)}, u32[]{:S(2)}, u32[]{:S(2)}) collective-permute-start(f32[32,1152]{1,0:T(8,128)S(1)} %get-tuple-element.46), channel_id=1, source_target_pairs={{0,15},{1,0},{2,1},{3,2},{4,3},{5,4},{6,5},{7,6},{8,7},{9,8},{10,9... | collective-permute-start | bytes 442376 | tf_op jit(solution)/shard_map/ppermute | solution.py:747
  72.6 7.1 %add_same.1 = (f32[4096,128]{1,0:T(8,128)S(1)}, f32[4096,128]{1,0:T(8,128)S(1)}, f32[4096,128]{1,0:T(8,128)S(1)}, f32[4096,128]{1,0:T(8,128)S(1)}) custom-call(s32[4,6144]{1,0:T(4,128)S(1)} %bitcast.9, s32[24576]{0:T(1024)S(1)} %bitcast.13, f32[4,6144]{1,0:T(4,128)S(1)} %bitcast.20, ...), custom_call_target="tpu_custom_call", output_to_operand_aliasing={{0}: (6, {}), {1}: (7, {}), {2}: (8, {}), {3}: (9, {})} | custom-call | bytes 27000000 | tf_op jit(solution)/shard_map/add_same/pallas_call | solution.py:593
  79.8 0.0 collective-permute-done.10.before
  79.8 0.0 collective-permute-done.11.after
  79.8 17.0 %add_sides.1 = (f32[4096,128]{1,0:T(8,128)S(1)}, f32[2,128]{1,0:T(2,128)S(1)}, f32[4096,128]{1,0:T(8,128)S(1)}, f32[4096,128]{1,0:T(8,128)S(1)}, f32[4096,128]{1,0:T(8,128)S(1)}, /*index=5*/f32[4096,128]{1,0:T(8,128)S(1)}) custom-call(s32[4,6144]{1,0:T(4,128)S(1)} %bitcast.10, ...), custom_call_target="tpu_custom_call", output_to_operand_aliasing={{2}: (6, {}), {3}: (7, {}), {4}: (8, {}), {5}: (9, {})} | custom-call | bytes 54000000 | tf_op jit(solution)/shard_map/add_sides/pallas_call | solution.py:664
  96.8 9.4 %all_to_all.10 = f32[8,2,128]{2,1,0:T(2,128)S(1)} all-to-all(f32[8,2,128]{2,1,0:T(2,128)S(1)} %broadcast_in_dim.6), channel_id=1, replica_groups=mesh['grid'=8,'cell'=16] {'grid'}, dimensions={0} | all-to-all | bytes 16384 | tf_op jit(solution)/shard_map/all_to_all | solution.py:760
  106.2 10.5 %all_to_all.11 = f32[16,2,128]{2,1,0:T(2,128)S(1)} all-to-all(f32[16,2,128]{2,1,0:T(2,128)S(1)} %broadcast_in_dim.7), channel_id=1, replica_groups=mesh['grid'=8,'cell'=16] {'cell'}, dimensions={0} | all-to-all | bytes 32768 | tf_op jit(solution)/shard_map/all_to_all | solution.py:760
  116.7 4.8 %basis.1 = (f32[16,1,32768]{2,1,0:T(1,128)}, f32[16,16]{1,0:T(8,128)}) custom-call(f32[2,128]{1,0:T(2,128)S(1)} %reduce_sum.19.gram, f32[4096,128]{1,0:T(8,128)S(1)} %get-tuple-element.55.adjoint), custom_call_target="tpu_custom_call" | custom-call | bytes 18000000 | tf_op jit(solution)/shard_map/basis/pallas_call | solution.py:725
  (10 shorter events, 0.2 us)
Async XLA Ops:
  0.6 5.8 %collective-permute-start.1 = (f32[1,4,6144]{2,1,0:T(4,128)}, f32[1,4,6144]{2,1,0:T(4,128)S(1)}, u32[]{:S(2)}, u32[]{:S(2)}) collective-permute-start(f32[1,4,6144]{2,1,0:T(4,128)} %param.13), channel_id=1, source_target_pairs={{0,96},{1,97},{2,98},{3,99},{4,100},{5,101},{6,102},{7,103},{8,104... | collective-permute-start | bytes 294920 | tf_op jit(solution)/shard_map/ppermute | solution.py:747
  3.6 3.5 %collective-permute-start = (f32[1,4,6144]{2,1,0:T(4,128)}, f32[1,4,6144]{2,1,0:T(4,128)S(1)}, u32[]{:S(2)}, u32[]{:S(2)}) collective-permute-start(f32[1,4,6144]{2,1,0:T(4,128)} %param.13), channel_id=1, source_target_pairs={{0,112},{1,113},{2,114},{3,115},{4,116},{5,117},{6,118},{7,119},{8... | collective-permute-start | bytes 294920 | tf_op jit(solution)/shard_map/ppermute | solution.py:747
  6.4 7.3 %copy-start = (s32[1,4,6144]{2,1,0:T(4,128)S(1)}, s32[1,4,6144]{2,1,0:T(4,128)}, u32[]{:S(2)}) copy-start(s32[1,4,6144]{2,1,0:T(4,128)} %param.11) | copy-start | bytes 294916
  7.1 17.8 %collective-permute-start.2 = (f32[8,1152]{1,0:T(8,128)S(1)}, f32[8,1152]{1,0:T(8,128)S(1)}, u32[]{:S(2)}, u32[]{:S(2)}) collective-permute-start(f32[8,1152]{1,0:T(8,128)S(1)} %get-tuple-element.29), channel_id=1, source_target_pairs={{0,1},{1,2},{2,3},{3,4},{4,5},{5,6},{6,7},{7,8},{8,9},{9,10},{10,1... | collective-permute-start | bytes 110600 | tf_op jit(solution)/shard_map/ppermute | solution.py:747
  8.7 16.2 %collective-permute-start.3 = (f32[8,1152]{1,0:T(8,128)S(1)}, f32[8,1152]{1,0:T(8,128)S(1)}, u32[]{:S(2)}, u32[]{:S(2)}) collective-permute-start(f32[8,1152]{1,0:T(8,128)S(1)} %get-tuple-element.30), channel_id=1, source_target_pairs={{0,15},{1,0},{2,1},{3,2},{4,3},{5,4},{6,5},{7,6},{8,7},{9,8},{10,9... | collective-permute-start | bytes 110600 | tf_op jit(solution)/shard_map/ppermute | solution.py:747
  28.3 11.0 %copy-start.1 = (s32[1,6144]{1,0:T(1,128)S(1)}, s32[1,6144]{1,0:T(1,128)}, u32[]{:S(2)}) copy-start(s32[1,6144]{1,0:T(1,128)} %cells.3) | copy-start | bytes 73732
  28.4 11.0 %copy-start.2 = (f32[1,32768]{1,0:T(1,128)S(1)}, f32[1,32768]{1,0:T(1,128)}, u32[]{:S(2)}) copy-start(f32[1,32768]{1,0:T(1,128)} %centre.1) | copy-start | bytes 393220
  28.4 11.0 %copy-start.3 = (f32[1,32768]{1,0:T(1,128)S(1)}, f32[1,32768]{1,0:T(1,128)}, u32[]{:S(2)}) copy-start(f32[1,32768]{1,0:T(1,128)} %lower.1) | copy-start | bytes 393220
  28.4 11.0 %copy-start.4 = (f32[1,32768]{1,0:T(1,128)S(1)}, f32[1,32768]{1,0:T(1,128)}, u32[]{:S(2)}) copy-start(f32[1,32768]{1,0:T(1,128)} %upper.1) | copy-start | bytes 393220
  28.4 9.6 %collective-permute-start.4 = (f32[32,1024]{1,0:T(8,128)S(1)}, f32[32,1024]{1,0:T(8,128)S(1)}, u32[]{:S(2)}, u32[]{:S(2)}) collective-permute-start(f32[32,1024]{1,0:T(8,128)S(1)} %get-tuple-element.31), channel_id=1, source_target_pairs={{0,15},{1,0},{2,1},{3,2},{4,3},{5,4},{6,5},{7,6},{8,7},{9,8},{10,9... | collective-permute-start | bytes 393224 | tf_op jit(solution)/shard_map/ppermute | solution.py:747
  30.4 8.3 %collective-permute-start.5 = (f32[32,1024]{1,0:T(8,128)S(1)}, f32[32,1024]{1,0:T(8,128)S(1)}, u32[]{:S(2)}, u32[]{:S(2)}) collective-permute-start(f32[32,1024]{1,0:T(8,128)S(1)} %get-tuple-element.32), channel_id=1, source_target_pairs={{0,1},{1,2},{2,3},{3,4},{4,5},{5,6},{6,7},{7,8},{8,9},{9,10},{10,1... | collective-permute-start | bytes 393224 | tf_op jit(solution)/shard_map/ppermute | solution.py:747
  38.7 7.8 %collective-permute-start.6 = (f32[48,1024]{1,0:T(8,128)S(1)}, f32[48,1024]{1,0:T(8,128)S(1)}, u32[]{:S(2)}, u32[]{:S(2)}) collective-permute-start(f32[48,1024]{1,0:T(8,128)S(1)} %get-tuple-element.33), channel_id=1, source_target_pairs={{0,16},{1,17},{2,18},{3,19},{4,20},{5,21},{6,22},{7,23},{8,24},{9,... | collective-permute-start | bytes 589832 | tf_op jit(solution)/shard_map/ppermute | solution.py:747
  38.8 9.0 %collective-permute-start.7 = (f32[48,1024]{1,0:T(8,128)S(1)}, f32[48,1024]{1,0:T(8,128)S(1)}, u32[]{:S(2)}, u32[]{:S(2)}) collective-permute-start(f32[48,1024]{1,0:T(8,128)S(1)} %get-tuple-element.34), channel_id=1, source_target_pairs={{0,32},{1,33},{2,34},{3,35},{4,36},{5,37},{6,38},{7,39},{8,40},{9,... | collective-permute-start | bytes 589832 | tf_op jit(solution)/shard_map/ppermute | solution.py:747
  56.8 7.6 %collective-permute-start.9 = (f32[48,1024]{1,0:T(8,128)S(1)}, f32[48,1024]{1,0:T(8,128)S(1)}, u32[]{:S(2)}, u32[]{:S(2)}) collective-permute-start(f32[48,1024]{1,0:T(8,128)S(1)} %get-tuple-element.40), channel_id=1, source_target_pairs={{0,96},{1,97},{2,98},{3,99},{4,100},{5,101},{6,102},{7,103},{8,104... | collective-permute-start | bytes 589832 | tf_op jit(solution)/shard_map/ppermute | solution.py:747
  61.9 5.3 %collective-permute-start.8 = (f32[48,1024]{1,0:T(8,128)S(1)}, f32[48,1024]{1,0:T(8,128)S(1)}, u32[]{:S(2)}, u32[]{:S(2)}) collective-permute-start(f32[48,1024]{1,0:T(8,128)S(1)} %at_receptors.1), channel_id=1, source_target_pairs={{0,112},{1,113},{2,114},{3,115},{4,116},{5,117},{6,118},{7,119},{8... | collective-permute-start | bytes 589832 | tf_op jit(solution)/shard_map/ppermute | solution.py:747
  67.2 12.6 %collective-permute-start.10 = (f32[32,1152]{1,0:T(8,128)S(1)}, f32[32,1152]{1,0:T(8,128)S(1)}, u32[]{:S(2)}, u32[]{:S(2)}) collective-permute-start(f32[32,1152]{1,0:T(8,128)S(1)} %get-tuple-element.45), channel_id=1, source_target_pairs={{0,1},{1,2},{2,3},{3,4},{4,5},{5,6},{6,7},{7,8},{8,9},{9,10},{10,1... | collective-permute-start | bytes 442376 | tf_op jit(solution)/shard_map/ppermute | solution.py:747
  67.3 12.5 %collective-permute-start.11 = (f32[32,1152]{1,0:T(8,128)S(1)}, f32[32,1152]{1,0:T(8,128)S(1)}, u32[]{:S(2)}, u32[]{:S(2)}) collective-permute-start(f32[32,1152]{1,0:T(8,128)S(1)} %get-tuple-element.46), channel_id=1, source_target_pairs={{0,15},{1,0},{2,1},{3,2},{4,3},{5,4},{6,5},{7,6},{8,7},{9,8},{10,9... | collective-permute-start | bytes 442376 | tf_op jit(solution)/shard_map/ppermute | solution.py:747

commit v11 on v9

--- a/solution.py
+++ b/solution.py
@@ -656,14 +656,14 @@
         folded = folded + jnp.where(group == g, product[g * PROBES : (g + 1) * PROBES, :], 0.0)
     folded = sum_of_groups(folded)
     for n in range(2):
-        gram[n : n + 1, :] = jnp.sum(jnp.where(own_group(), folded[n * 8 : n * 8 + 8, :], 0.0), axis=0, keepdims=True)
+        gram[:, n * LANES : (n + 1) * LANES] = jnp.sum(jnp.where(own_group(), folded[n * 8 : n * 8 + 8, :], 0.0), axis=0, keepdims=True)
 
 
 def add_sides(cells, rows, before_weights, after_weights, before, after, sums):
     segs = segments(4, SIDES)
     outs = pl.pallas_call(
         donor_sides_kernel,
-        out_shape=[resident(ROWS, LANES), jax.ShapeDtypeStruct((2, LANES), f32)]
+        out_shape=[resident(ROWS, LANES), jax.ShapeDtypeStruct((1, 2 * LANES), f32)]
         + [resident(ROWS, LANES)] * SUMS,
         in_specs=[VMEM, HBM] + [VMEM] * (4 + SUMS),
         out_specs=[VMEM] * (2 + SUMS),
@@ -680,7 +680,7 @@
     row = lax.broadcasted_iota(i32, (PROBES, LANES), 0)
     lane = lanes((PROBES, LANES))
     whole = jnp.concatenate(
-        [sum_of_groups(jnp.where(own_group(), jnp.broadcast_to(gram[n : n + 1, :], (8, LANES)), 0.0)) for n in range(2)],
+        [sum_of_groups(jnp.where(own_group(), jnp.broadcast_to(gram[:, n * LANES : (n + 1) * LANES], (8, LANES)), 0.0)) for n in range(2)],
         axis=0,
     ) / f32(total_cells)
     columns = [jnp.broadcast_to(whole[:, j : j + 1], (PROBES, LANES)) for j in range(PROBES)]
@@ -755,9 +755,10 @@
     return moved(value, lambda g, c: (g, c + distance))
 
 
-def axis_sum(value, axis):
-    copies = jnp.broadcast_to(value, (lax.axis_size(axis),) + value.shape)
-    return jnp.sum(lax.all_to_all(copies, axis, 0, 0), axis=0)
+def summed(value):
+    devices = lax.axis_size(AXES)
+    copies = jnp.broadcast_to(value, (devices,) + value.shape)
+    return jnp.sum(lax.all_to_all(copies, AXES, 0, 0), axis=0)
 
 
 def body(probes, centre, lower_coef, upper_coef, donor_cells, receptor_cells, weights):
@@ -784,7 +785,7 @@
     sums = add_same(donors, donor_rows, near_weights, far_weights, near, far, sums)
     adjoint, gram = add_sides(donors, donor_rows, before_weights, after_weights, before, after, sums)
     total_cells = lax.axis_size("grid") * lax.axis_size("cell") * probes.shape[2]
-    basis, factor = basis_of(total_cells, axis_sum(axis_sum(gram, "grid"), "cell"), adjoint)
+    basis, factor = basis_of(total_cells, summed(gram), adjoint)
     return (basis, factor)
 
 

time: 122 us -> 119 us (0.975)
  blocking collectives: 19.9 us -> 15.7 us
    all_to_all x2 -> x1, blocking collectives: 19.9 us -> 15.7 us  [summed(): return jnp.sum(lax.all_to_all(copies, AXES, 0, 0), axis=0)]
  transfers between devices with their start and end apart: 12 -> 12, of which waited for: 5 -> 5; matrix products, arithmetic and copies ran while one was open for 0% -> 0% of each run, Pallas kernels for 33% -> 34%
where the time goes in v11:
time: 119 us; the launch traced here: 118 us
  Pallas kernels  74.5 us (63%)
  starting transfers between devices  20.5 us (17%)
  blocking collectives  15.7 us (13%)
  waiting for transfers between devices  5.89 us (5%)
    ppermute x12, starting transfers between devices, moved(): return lax.ppermute(value, AXES, route)  20.5 us
    pallas_call x1, Pallas kernels, add_sides(): pl.pallas_call(donor_sides_kernel, out_shape=[resident(ROWS, LANES), jax....  17 us
    all_to_all x1, blocking collectives, summed(): return jnp.sum(lax.all_to_all(copies, AXES, 0, 0), axis=0)  15.7 us
    pallas_call x1, Pallas kernels, rows_at_sides(): pl.pallas_call(rows_kernel, out_shape=resident(len(segs) * FRINGE, LANES)...  11.3 us
    pallas_call x1, Pallas kernels, couple(): pl.pallas_call(couple_kernel, out_shape=[resident(ROWS, LANES), TRIPLE] +...  9.1 us
    pallas_call x1, Pallas kernels, same_sums(): pl.pallas_call(same_sums_kernel, out_shape=PAIR, in_specs=[VMEM, VMEM, HB...  7.63 us
    pallas_call x1, Pallas kernels, add_same(): pl.pallas_call(donor_same_kernel, out_shape=[resident(ROWS, LANES)] * SUM...  7.12 us
    ppermute x12, waiting for transfers between devices, moved(): return lax.ppermute(value, AXES, route)  5.89 us
  transfers between devices with their start and end apart: 12, of which 5 were waited for; matrix products, arithmetic and copies ran while one was open for 0% of the time, Pallas kernels for 34%

profile of v11, /device:TPU:0, one launch (start us, length us, event | category | flops | bytes accessed | tf_op | source)
XLA Modules:
  0.0 117.8 jit_solution(2157819703904821745)
XLA Ops:
  0.6 2.9 %collective-permute-start.1 = (f32[1,4,6144]{2,1,0:T(4,128)}, f32[1,4,6144]{2,1,0:T(4,128)S(1)}, u32[]{:S(2)}, u32[]{:S(2)}) collective-permute-start(f32[1,4,6144]{2,1,0:T(4,128)} %param.13), channel_id=1, source_target_pairs={{0,96},{1,97},{2,98},{3,99},{4,100},{5,101},{6,102},{7,103},{8,104... | collective-permute-start | bytes 294920 | tf_op jit(solution)/shard_map/ppermute | solution.py:747
  3.6 0.0 collective-permute-start
  3.6 2.8 %table.1 = f32[4096,128]{1,0:T(8,128)S(1)} custom-call(f32[16,1,32768]{2,1,0:T(1,128)} %probes.1), custom_call_target="tpu_custom_call" | custom-call | bytes 9000000 | tf_op jit(solution)/shard_map/table/pallas_call | solution.py:284
  6.4 0.0 copy-start
  6.4 0.0 collective-permute-done.1
  6.4 0.7 collective-permute-done
  7.1 1.6 %collective-permute-start.2 = (f32[8,1152]{1,0:T(8,128)S(1)}, f32[8,1152]{1,0:T(8,128)S(1)}, u32[]{:S(2)}, u32[]{:S(2)}) collective-permute-start(f32[8,1152]{1,0:T(8,128)S(1)} %get-tuple-element.29), channel_id=1, source_target_pairs={{0,1},{1,2},{2,3},{3,4},{4,5},{5,6},{6,7},{7,8},{8,9},{9,10},{10,1... | collective-permute-start | bytes 110600 | tf_op jit(solution)/shard_map/ppermute | solution.py:747
  8.7 5.0 %collective-permute-start.3 = (f32[8,1152]{1,0:T(8,128)S(1)}, f32[8,1152]{1,0:T(8,128)S(1)}, u32[]{:S(2)}, u32[]{:S(2)}) collective-permute-start(f32[8,1152]{1,0:T(8,128)S(1)} %get-tuple-element.30), channel_id=1, source_target_pairs={{0,15},{1,0},{2,1},{3,2},{4,3},{5,4},{6,5},{7,6},{8,7},{9,8},{10,9... | collective-permute-start | bytes 110600 | tf_op jit(solution)/shard_map/ppermute | solution.py:747
  13.7 0.0 copy-done
  13.8 11.3 %rows_at_sides.1.staged = f32[16384,128]{1,0:T(8,128)S(1)} custom-call(f32[4096,128]{1,0:T(8,128)S(1)} %table.1, s32[24576]{0:T(1024)S(1)} %bitcast.13), custom_call_target="tpu_custom_call" | custom-call | bytes 33000000 | tf_op jit(solution)/shard_map/rows_at_sides/pallas_call | solution.py:355
  25.1 0.0 collective-permute-done.2.before.before_weights
  25.1 0.0 collective-permute-done.3.after.after_weights
  25.1 3.4 %side_sums.1 = (f32[32,1024]{1,0:T(8,128)S(1)}, f32[32,1024]{1,0:T(8,128)S(1)}) custom-call(f32[16384,128]{1,0:T(8,128)S(1)} %rows_at_sides.1.staged, s32[4,6144]{1,0:T(4,128)S(1)} %bitcast.9, f32[8,1152]{1,0:T(8,128)S(1)} %collective-permute-done.2.before.before_weights, f32[8,1152]{1,0:T(8,128)S(1)} %collective-permute-done.3.after.after_weights), custom_call_target="tpu_custom_call" | custom-call | bytes 3000000 | tf_op jit(solution)/shard_map/side_sums/pallas_call | solution.py:324
  28.5 0.0 copy-start.1
  28.6 0.0 copy-start.2
  28.6 0.0 copy-start.3
  28.6 0.0 copy-start.4
  28.6 2.0 %collective-permute-start.4 = (f32[32,1024]{1,0:T(8,128)S(1)}, f32[32,1024]{1,0:T(8,128)S(1)}, u32[]{:S(2)}, u32[]{:S(2)}) collective-permute-start(f32[32,1024]{1,0:T(8,128)S(1)} %get-tuple-element.31), channel_id=1, source_target_pairs={{0,15},{1,0},{2,1},{3,2},{4,3},{5,4},{6,5},{7,6},{8,7},{9,8},{10,9... | collective-permute-start | bytes 393224 | tf_op jit(solution)/shard_map/ppermute | solution.py:747
  30.6 0.1 collective-permute-start.5
  30.7 7.6 %same_sums.1.same = f32[32,1024]{1,0:T(8,128)S(1)} custom-call(f32[4096,128]{1,0:T(8,128)S(1)} %table.1, s32[4,6144]{1,0:T(4,128)S(1)} %bitcast.10, s32[24576]{0:T(1024)S(1)} %bitcast.14, f32[4,6144]{1,0:T(4,128)S(1)} %bitcast.21, f32[4,6144]{1,0:T(4,128)S(1)} %bitcast.18), custom_call_target="tpu_custom_call" | custom-call | bytes 24000000 | tf_op jit(solution)/shard_map/same_sums/pallas_call | solution.py:388
  38.3 0.0 collective-permute-done.4.before
  38.3 0.6 collective-permute-done.5.after
  38.9 0.0 collective-permute-start.6
  38.9 0.6 collective-permute-start.7
  39.6 0.0 copy-done.1
  39.6 0.0 copy-done.2
  39.6 0.0 copy-done.3
  39.6 0.0 copy-done.4
  39.6 5.2 %forward.1 = (f32[4096,128]{1,0:T(8,128)S(1)}, f32[4096,128]{1,0:T(8,128)S(1)}, f32[4096,128]{1,0:T(8,128)S(1)}, f32[4096,128]{1,0:T(8,128)S(1)}, f32[4096,128]{...) custom-call(f32[4096,128]{1,0:T(8,128)S(1)} %table.1, f32[1,32768]{1,0:T(1,128)S(1)} %copy-done.2, ...), custom_call_target="tpu_custom_call" | custom-call | bytes 21000000 | tf_op jit(solution)/shard_map/forward/pallas_call | solution.py:454
  44.8 1.9 %collective-permute-done.6.near = f32[48,1024]{1,0:T(8,128)S(1)} collective-permute-done((f32[48,1024]{1,0:T(8,128)S(1)}, f32[48,1024]{1,0:T(8,128)S(1)}, u32[]{:S(2)}, u32[]{:S(2)}) %collective-permute-start.6) | collective-permute-done | bytes 196640 | tf_op jit(solution)/shard_map/ppermute | solution.py:747
  46.7 1.2 %collective-permute-done.7.far = f32[48,1024]{1,0:T(8,128)S(1)} collective-permute-done((f32[48,1024]{1,0:T(8,128)S(1)}, f32[48,1024]{1,0:T(8,128)S(1)}, u32[]{:S(2)}, u32[]{:S(2)}) %collective-permute-start.7) | collective-permute-done | bytes 196640 | tf_op jit(solution)/shard_map/ppermute | solution.py:747
  47.9 9.1 %couple.1 = (f32[4096,128]{1,0:T(8,128)S(1)}, f32[48,1024]{1,0:T(8,128)S(1)}, f32[4096,128]{1,0:T(8,128)S(1)}, f32[4096,128]{1,0:T(8,128)S(1)}, f32[4096,128]{1,0:T(8,128)S(1)}, /*index=5*/f32[4096,128]{1,0:T(8,128)S(1)}) custom-call(s32[1,6144]{1,0:T(1,128)S(1)} %copy-done.1, ...), custom_call_target="tpu_custom_call", output_to_operand_aliasing={{2}: (4, {}), {3}: (5, {}), {4}: (6, {}), {5}: (7, {})} | custom-call | bytes 33000000 | tf_op jit(solution)/shard_map/couple/pallas_call | solution.py:493
  57.1 1.9 %collective-permute-start.9 = (f32[48,1024]{1,0:T(8,128)S(1)}, f32[48,1024]{1,0:T(8,128)S(1)}, u32[]{:S(2)}, u32[]{:S(2)}) collective-permute-start(f32[48,1024]{1,0:T(8,128)S(1)} %get-tuple-element.40), channel_id=1, source_target_pairs={{0,96},{1,97},{2,98},{3,99},{4,100},{5,101},{6,102},{7,103},{8,104... | collective-permute-start | bytes 589832 | tf_op jit(solution)/shard_map/ppermute | solution.py:747
  58.9 3.2 %at_receptors.1 = f32[48,1024]{1,0:T(8,128)S(1)} custom-call(f32[4096,128]{1,0:T(8,128)S(1)} %get-tuple-element.39.tangent, s32[1,6144]{1,0:T(1,128)S(1)} %copy-done.1, s32[6144]{0:T(1024)S(1)} %bitcast.24), custom_call_target="tpu_custom_call" | custom-call | bytes 9000000 | tf_op jit(solution)/shard_map/at_receptors/pallas_call | solution.py:517
  62.2 1.0 collective-permute-start.8
  63.1 1.5 %collective-permute-done.9.ready.far = f32[48,1024]{1,0:T(8,128)S(1)} collective-permute-done((f32[48,1024]{1,0:T(8,128)S(1)}, f32[48,1024]{1,0:T(8,128)S(1)}, u32[]{:S(2)}, u32[]{:S(2)}) %collective-permute-start.9) | collective-permute-done | bytes 196640 | tf_op jit(solution)/shard_map/ppermute | solution.py:747
  64.6 2.8 %transposed.1 = (f32[4096,128]{1,0:T(8,128)S(1)}, f32[4096,128]{1,0:T(8,128)S(1)}, f32[4096,128]{1,0:T(8,128)S(1)}, f32[4096,128]{1,0:T(8,128)S(1)}) custom-call(f32[4096,128]{1,0:T(8,128)S(1)} %get-tuple-element.39.tangent, f32[4096,128]{1,0:T(8,128)S(1)} %get-tuple-element.43.centre, f32[4096,128]{1,0:T(8,128)S(1)} %get-tuple-element.41.lower, ...), custom_call_target="tpu_custom_call" | custom-call | bytes 3000000 | tf_op jit(solution)/shard_map/transposed/pallas_call | solution.py:569
  67.4 0.0 collective-permute-done.8.near
  67.5 0.1 collective-permute-start.10
  67.5 5.3 %collective-permute-start.11 = (f32[32,1152]{1,0:T(8,128)S(1)}, f32[32,1152]{1,0:T(8,128)S(1)}, u32[]{:S(2)}, u32[]{:S(2)}) collective-permute-start(f32[32,1152]{1,0:T(8,128)S(1)} %get-tuple-element.46), channel_id=1, source_target_pairs={{0,15},{1,0},{2,1},{3,2},{4,3},{5,4},{6,5},{7,6},{8,7},{9,8},{10,9... | collective-permute-start | bytes 442376 | tf_op jit(solution)/shard_map/ppermute | solution.py:747
  72.9 7.1 %add_same.1 = (f32[4096,128]{1,0:T(8,128)S(1)}, f32[4096,128]{1,0:T(8,128)S(1)}, f32[4096,128]{1,0:T(8,128)S(1)}, f32[4096,128]{1,0:T(8,128)S(1)}) custom-call(s32[4,6144]{1,0:T(4,128)S(1)} %bitcast.11, s32[24576]{0:T(1024)S(1)} %bitcast.15, f32[4,6144]{1,0:T(4,128)S(1)} %bitcast.22, ...), custom_call_target="tpu_custom_call", output_to_operand_aliasing={{0}: (6, {}), {1}: (7, {}), {2}: (8, {}), {3}: (9, {})} | custom-call | bytes 27000000 | tf_op jit(solution)/shard_map/add_same/pallas_call | solution.py:593
  80.0 0.0 collective-permute-done.10.before
  80.0 0.0 collective-permute-done.11.after
  80.0 17.0 %add_sides.1 = (f32[4096,128]{1,0:T(8,128)S(1)}, f32[1,256]{1,0:T(1,128)S(1)}, f32[4096,128]{1,0:T(8,128)S(1)}, f32[4096,128]{1,0:T(8,128)S(1)}, f32[4096,128]{1,0:T(8,128)S(1)}, /*index=5*/f32[4096,128]{1,0:T(8,128)S(1)}) custom-call(s32[4,6144]{1,0:T(4,128)S(1)} %bitcast.12, ...), custom_call_target="tpu_custom_call", output_to_operand_aliasing={{2}: (6, {}), {3}: (7, {}), {4}: (8, {}), {5}: (9, {})} | custom-call | bytes 54000000 | tf_op jit(solution)/shard_map/add_sides/pallas_call | solution.py:664
  97.0 0.1 broadcast_in_dim.3
  97.1 15.7 %all_to_all.5 = f32[128,1,256]{2,1,0:T(1,128)S(1)} all-to-all(f32[128,1,256]{2,1,0:T(1,128)S(1)} %broadcast_in_dim.3), channel_id=1, replica_groups=mesh['grid'=8,'cell'=16] {'grid','cell'}, dimensions={0} | all-to-all | bytes 262144 | tf_op jit(solution)/shard_map/all_to_all | solution.py:761
  112.8 0.2 reduce_sum.11
  113.0 4.8 %basis.1 = (f32[16,1,32768]{2,1,0:T(1,128)}, f32[16,16]{1,0:T(8,128)}) custom-call(f32[1,256]{1,0:T(1,128)S(1)} %bitcast.25, f32[4096,128]{1,0:T(8,128)S(1)} %get-tuple-element.55.adjoint), custom_call_target="tpu_custom_call" | custom-call | bytes 18000000 | tf_op jit(solution)/shard_map/basis/pallas_call | solution.py:725
  (6 shorter events, 0.1 us)
Async XLA Ops:
  0.6 5.8 %collective-permute-start.1 = (f32[1,4,6144]{2,1,0:T(4,128)}, f32[1,4,6144]{2,1,0:T(4,128)S(1)}, u32[]{:S(2)}, u32[]{:S(2)}) collective-permute-start(f32[1,4,6144]{2,1,0:T(4,128)} %param.13), channel_id=1, source_target_pairs={{0,96},{1,97},{2,98},{3,99},{4,100},{5,101},{6,102},{7,103},{8,104... | collective-permute-start | bytes 294920 | tf_op jit(solution)/shard_map/ppermute | solution.py:747
  3.6 3.5 %collective-permute-start = (f32[1,4,6144]{2,1,0:T(4,128)}, f32[1,4,6144]{2,1,0:T(4,128)S(1)}, u32[]{:S(2)}, u32[]{:S(2)}) collective-permute-start(f32[1,4,6144]{2,1,0:T(4,128)} %param.13), channel_id=1, source_target_pairs={{0,112},{1,113},{2,114},{3,115},{4,116},{5,117},{6,118},{7,119},{8... | collective-permute-start | bytes 294920 | tf_op jit(solution)/shard_map/ppermute | solution.py:747
  6.4 7.3 %copy-start = (s32[1,4,6144]{2,1,0:T(4,128)S(1)}, s32[1,4,6144]{2,1,0:T(4,128)}, u32[]{:S(2)}) copy-start(s32[1,4,6144]{2,1,0:T(4,128)} %param.11) | copy-start | bytes 294916
  7.1 18.0 %collective-permute-start.2 = (f32[8,1152]{1,0:T(8,128)S(1)}, f32[8,1152]{1,0:T(8,128)S(1)}, u32[]{:S(2)}, u32[]{:S(2)}) collective-permute-start(f32[8,1152]{1,0:T(8,128)S(1)} %get-tuple-element.29), channel_id=1, source_target_pairs={{0,1},{1,2},{2,3},{3,4},{4,5},{5,6},{6,7},{7,8},{8,9},{9,10},{10,1... | collective-permute-start | bytes 110600 | tf_op jit(solution)/shard_map/ppermute | solution.py:747
  8.7 16.4 %collective-permute-start.3 = (f32[8,1152]{1,0:T(8,128)S(1)}, f32[8,1152]{1,0:T(8,128)S(1)}, u32[]{:S(2)}, u32[]{:S(2)}) collective-permute-start(f32[8,1152]{1,0:T(8,128)S(1)} %get-tuple-element.30), channel_id=1, source_target_pairs={{0,15},{1,0},{2,1},{3,2},{4,3},{5,4},{6,5},{7,6},{8,7},{9,8},{10,9... | collective-permute-start | bytes 110600 | tf_op jit(solution)/shard_map/ppermute | solution.py:747
  28.5 11.0 %copy-start.1 = (s32[1,6144]{1,0:T(1,128)S(1)}, s32[1,6144]{1,0:T(1,128)}, u32[]{:S(2)}) copy-start(s32[1,6144]{1,0:T(1,128)} %cells.3) | copy-start | bytes 73732
  28.6 11.0 %copy-start.2 = (f32[1,32768]{1,0:T(1,128)S(1)}, f32[1,32768]{1,0:T(1,128)}, u32[]{:S(2)}) copy-start(f32[1,32768]{1,0:T(1,128)} %centre.1) | copy-start | bytes 393220
  28.6 11.0 %copy-start.3 = (f32[1,32768]{1,0:T(1,128)S(1)}, f32[1,32768]{1,0:T(1,128)}, u32[]{:S(2)}) copy-start(f32[1,32768]{1,0:T(1,128)} %lower.1) | copy-start | bytes 393220
  28.6 11.0 %copy-start.4 = (f32[1,32768]{1,0:T(1,128)S(1)}, f32[1,32768]{1,0:T(1,128)}, u32[]{:S(2)}) copy-start(f32[1,32768]{1,0:T(1,128)} %upper.1) | copy-start | bytes 393220
  28.6 9.7 %collective-permute-start.4 = (f32[32,1024]{1,0:T(8,128)S(1)}, f32[32,1024]{1,0:T(8,128)S(1)}, u32[]{:S(2)}, u32[]{:S(2)}) collective-permute-start(f32[32,1024]{1,0:T(8,128)S(1)} %get-tuple-element.31), channel_id=1, source_target_pairs={{0,15},{1,0},{2,1},{3,2},{4,3},{5,4},{6,5},{7,6},{8,7},{9,8},{10,9... | collective-permute-start | bytes 393224 | tf_op jit(solution)/shard_map/ppermute | solution.py:747
  30.6 8.3 %collective-permute-start.5 = (f32[32,1024]{1,0:T(8,128)S(1)}, f32[32,1024]{1,0:T(8,128)S(1)}, u32[]{:S(2)}, u32[]{:S(2)}) collective-permute-start(f32[32,1024]{1,0:T(8,128)S(1)} %get-tuple-element.32), channel_id=1, source_target_pairs={{0,1},{1,2},{2,3},{3,4},{4,5},{5,6},{6,7},{7,8},{8,9},{9,10},{10,1... | collective-permute-start | bytes 393224 | tf_op jit(solution)/shard_map/ppermute | solution.py:747
  38.9 7.8 %collective-permute-start.6 = (f32[48,1024]{1,0:T(8,128)S(1)}, f32[48,1024]{1,0:T(8,128)S(1)}, u32[]{:S(2)}, u32[]{:S(2)}) collective-permute-start(f32[48,1024]{1,0:T(8,128)S(1)} %get-tuple-element.33), channel_id=1, source_target_pairs={{0,16},{1,17},{2,18},{3,19},{4,20},{5,21},{6,22},{7,23},{8,24},{9,... | collective-permute-start | bytes 589832 | tf_op jit(solution)/shard_map/ppermute | solution.py:747
  38.9 9.0 %collective-permute-start.7 = (f32[48,1024]{1,0:T(8,128)S(1)}, f32[48,1024]{1,0:T(8,128)S(1)}, u32[]{:S(2)}, u32[]{:S(2)}) collective-permute-start(f32[48,1024]{1,0:T(8,128)S(1)} %get-tuple-element.34), channel_id=1, source_target_pairs={{0,32},{1,33},{2,34},{3,35},{4,36},{5,37},{6,38},{7,39},{8,40},{9,... | collective-permute-start | bytes 589832 | tf_op jit(solution)/shard_map/ppermute | solution.py:747
  57.1 7.6 %collective-permute-start.9 = (f32[48,1024]{1,0:T(8,128)S(1)}, f32[48,1024]{1,0:T(8,128)S(1)}, u32[]{:S(2)}, u32[]{:S(2)}) collective-permute-start(f32[48,1024]{1,0:T(8,128)S(1)} %get-tuple-element.40), channel_id=1, source_target_pairs={{0,96},{1,97},{2,98},{3,99},{4,100},{5,101},{6,102},{7,103},{8,104... | collective-permute-start | bytes 589832 | tf_op jit(solution)/shard_map/ppermute | solution.py:747
  62.2 5.2 %collective-permute-start.8 = (f32[48,1024]{1,0:T(8,128)S(1)}, f32[48,1024]{1,0:T(8,128)S(1)}, u32[]{:S(2)}, u32[]{:S(2)}) collective-permute-start(f32[48,1024]{1,0:T(8,128)S(1)} %at_receptors.1), channel_id=1, source_target_pairs={{0,112},{1,113},{2,114},{3,115},{4,116},{5,117},{6,118},{7,119},{8... | collective-permute-start | bytes 589832 | tf_op jit(solution)/shard_map/ppermute | solution.py:747
  67.5 12.5 %collective-permute-start.10 = (f32[32,1152]{1,0:T(8,128)S(1)}, f32[32,1152]{1,0:T(8,128)S(1)}, u32[]{:S(2)}, u32[]{:S(2)}) collective-permute-start(f32[32,1152]{1,0:T(8,128)S(1)} %get-tuple-element.45), channel_id=1, source_target_pairs={{0,1},{1,2},{2,3},{3,4},{4,5},{5,6},{6,7},{7,8},{8,9},{9,10},{10,1... | collective-permute-start | bytes 442376 | tf_op jit(solution)/shard_map/ppermute | solution.py:747
  67.5 12.5 %collective-permute-start.11 = (f32[32,1152]{1,0:T(8,128)S(1)}, f32[32,1152]{1,0:T(8,128)S(1)}, u32[]{:S(2)}, u32[]{:S(2)}) collective-permute-start(f32[32,1152]{1,0:T(8,128)S(1)} %get-tuple-element.46), channel_id=1, source_target_pairs={{0,15},{1,0},{2,1},{3,2},{4,3},{5,4},{6,5},{7,6},{8,7},{9,8},{10,9... | collective-permute-start | bytes 442376 | tf_op jit(solution)/shard_map/ppermute | solution.py:747

commit v12 on v11

--- a/solution.py
+++ b/solution.py
@@ -304,7 +304,7 @@
         0: (before, 0, 0),
         3: (before, 4, 0),
         1: (same[0], 0, FRINGE),
-        4: (same[1], 0, 4 * FRINGE),
+        4: (same[1], 0, FRINGE),
         2: (after, 0, 0),
         5: (after, 4, 0),
     }
@@ -335,7 +335,7 @@
 def weight_relay_kernel(near, far, table, up, down):
     for pair, out, rows in ((BEFORE, up, slice(ROWS - 8, ROWS)), (AFTER, down, slice(0, 8))):
         for n, ref in enumerate((near, far)):
-            start = pair[n] * FRINGE
+            start = pair[0] * FRINGE
             out[n * 4 : n * 4 + 4, 0:FRINGE] = ref[:, start : start + FRINGE]
         out[:, EDGE] = table[rows, :]
 
@@ -765,7 +765,8 @@
     donors = donor_cells[0]
     donor_rows = (donors & (ROWS - 1)).reshape(-1)
     receptor_rows = (receptor_cells & (ROWS - 1)).reshape(-1)
-    near_weights, far_weights = along_grid(weights, -1)[0], along_grid(weights, -2)[0]
+    half = SLOTS // 2
+    near_weights, far_weights = along_grid(weights[0, :, :half], -1), along_grid(weights[0, :, half:], -2)
     table = table_of(probes)
     up, down = weight_relay(near_weights, far_weights, table)
     before_weights, after_weights = along_cell(up, 1), along_cell(down, -1)

time: 119 us -> 119 us (level)
  transfers between devices with their start and end apart: 12 -> 12, of which waited for: 5 -> 4; matrix products, arithmetic and copies ran while one was open for 0% -> 0% of each run, Pallas kernels for 34% -> 34%
where the time goes in v12:
time: 119 us; the launch traced here: 117 us
  Pallas kernels  74.5 us (63%)
  starting transfers between devices  20.4 us (17%)
  blocking collectives  15.2 us (13%)
  waiting for transfers between devices  5.41 us (5%)
    ppermute x12, starting transfers between devices, moved(): return lax.ppermute(value, AXES, route)  20.4 us
    pallas_call x1, Pallas kernels, add_sides(): pl.pallas_call(donor_sides_kernel, out_shape=[resident(ROWS, LANES), jax....  17 us
    all_to_all x1, blocking collectives, summed(): return jnp.sum(lax.all_to_all(copies, AXES, 0, 0), axis=0)  15.2 us
    pallas_call x1, Pallas kernels, rows_at_sides(): pl.pallas_call(rows_kernel, out_shape=resident(len(segs) * FRINGE, LANES)...  11.3 us
    pallas_call x1, Pallas kernels, couple(): pl.pallas_call(couple_kernel, out_shape=[resident(ROWS, LANES), TRIPLE] +...  9.12 us
    pallas_call x1, Pallas kernels, same_sums(): pl.pallas_call(same_sums_kernel, out_shape=PAIR, in_specs=[VMEM, VMEM, HB...  7.63 us
    pallas_call x1, Pallas kernels, add_same(): pl.pallas_call(donor_same_kernel, out_shape=[resident(ROWS, LANES)] * SUM...  7.11 us
    ppermute x12, waiting for transfers between devices, moved(): return lax.ppermute(value, AXES, route)  5.41 us
  transfers between devices with their start and end apart: 12, of which 4 were waited for; matrix products, arithmetic and copies ran while one was open for 0% of the time, Pallas kernels for 34%

profile of v12, /device:TPU:0, one launch (start us, length us, event | category | flops | bytes accessed | tf_op | source)
XLA Modules:
  0.0 117.4 jit_solution(11950728940483459819)
XLA Ops:
  0.6 0.8 slice_bitcast_fusion
  1.5 2.9 %collective-permute-start.1 = (f32[4,3072]{1,0:T(4,128)S(1)}, f32[4,3072]{1,0:T(4,128)S(1)}, u32[]{:S(2)}, u32[]{:S(2)}) collective-permute-start(f32[4,3072]{1,0:T(4,128)S(1)} %get-tuple-element.56), channel_id=1, source_target_pairs={{0,96},{1,97},{2,98},{3,99},{4,100},{5,101},{6,102},{7,103},{8,104... | collective-permute-start | bytes 147464 | tf_op jit(solution)/shard_map/ppermute | solution.py:747
  4.4 0.0 collective-permute-start
  4.4 2.8 %table.1 = f32[4096,128]{1,0:T(8,128)S(1)} custom-call(f32[16,1,32768]{2,1,0:T(1,128)} %probes.1), custom_call_target="tpu_custom_call" | custom-call | bytes 9000000 | tf_op jit(solution)/shard_map/table/pallas_call | solution.py:284
  7.2 0.0 copy-start
  7.2 0.0 collective-permute-done.1.far.far_weights
  7.2 0.0 collective-permute-done.near.near_weights
  7.3 1.6 %collective-permute-start.2 = (f32[8,1152]{1,0:T(8,128)S(1)}, f32[8,1152]{1,0:T(8,128)S(1)}, u32[]{:S(2)}, u32[]{:S(2)}) collective-permute-start(f32[8,1152]{1,0:T(8,128)S(1)} %get-tuple-element.29), channel_id=1, source_target_pairs={{0,1},{1,2},{2,3},{3,4},{4,5},{5,6},{6,7},{7,8},{8,9},{9,10},{10,1... | collective-permute-start | bytes 110600 | tf_op jit(solution)/shard_map/ppermute | solution.py:747
  8.9 5.0 %collective-permute-start.3 = (f32[8,1152]{1,0:T(8,128)S(1)}, f32[8,1152]{1,0:T(8,128)S(1)}, u32[]{:S(2)}, u32[]{:S(2)}) collective-permute-start(f32[8,1152]{1,0:T(8,128)S(1)} %get-tuple-element.30), channel_id=1, source_target_pairs={{0,15},{1,0},{2,1},{3,2},{4,3},{5,4},{6,5},{7,6},{8,7},{9,8},{10,9... | collective-permute-start | bytes 110600 | tf_op jit(solution)/shard_map/ppermute | solution.py:747
  13.9 0.0 copy-done
  13.9 11.3 %rows_at_sides.1.staged = f32[16384,128]{1,0:T(8,128)S(1)} custom-call(f32[4096,128]{1,0:T(8,128)S(1)} %table.1, s32[24576]{0:T(1024)S(1)} %bitcast.15), custom_call_target="tpu_custom_call" | custom-call | bytes 33000000 | tf_op jit(solution)/shard_map/rows_at_sides/pallas_call | solution.py:355
  25.3 0.0 collective-permute-done.2.before.before_weights
  25.3 0.0 collective-permute-done.3.after.after_weights
  25.3 3.4 %side_sums.1 = (f32[32,1024]{1,0:T(8,128)S(1)}, f32[32,1024]{1,0:T(8,128)S(1)}) custom-call(f32[16384,128]{1,0:T(8,128)S(1)} %rows_at_sides.1.staged, s32[4,6144]{1,0:T(4,128)S(1)} %bitcast.11, f32[8,1152]{1,0:T(8,128)S(1)} %collective-permute-done.2.before.before_weights, f32[8,1152]{1,0:T(8,128)S(1)} %collective-permute-done.3.after.after_weights), custom_call_target="tpu_custom_call" | custom-call | bytes 3000000 | tf_op jit(solution)/shard_map/side_sums/pallas_call | solution.py:324
  28.7 0.0 copy-start.1
  28.7 0.0 copy-start.2
  28.7 0.0 copy-start.3
  28.7 0.0 copy-start.4
  28.8 2.0 %collective-permute-start.4 = (f32[32,1024]{1,0:T(8,128)S(1)}, f32[32,1024]{1,0:T(8,128)S(1)}, u32[]{:S(2)}, u32[]{:S(2)}) collective-permute-start(f32[32,1024]{1,0:T(8,128)S(1)} %get-tuple-element.31), channel_id=1, source_target_pairs={{0,15},{1,0},{2,1},{3,2},{4,3},{5,4},{6,5},{7,6},{8,7},{9,8},{10,9... | collective-permute-start | bytes 393224 | tf_op jit(solution)/shard_map/ppermute | solution.py:747
  30.8 0.1 collective-permute-start.5
  30.9 7.6 %same_sums.1.same = f32[32,1024]{1,0:T(8,128)S(1)} custom-call(f32[4096,128]{1,0:T(8,128)S(1)} %table.1, s32[4,6144]{1,0:T(4,128)S(1)} %bitcast.12, s32[24576]{0:T(1024)S(1)} %bitcast.16, f32[4,3072]{1,0:T(4,128)S(1)} %collective-permute-done.near.near_weights, f32[4,3072]{1,0:T(4,128)S(1)} %collective-permute-done.1.far.far_weights), custom_call_target="tpu_custom_call" | custom-call | bytes 24000000 | tf_op jit(solution)/shard_map/same_sums/pallas_call | solution.py:388
  38.5 0.0 collective-permute-done.4.before
  38.5 0.7 collective-permute-done.5.after
  39.2 0.0 collective-permute-start.6
  39.2 1.1 collective-permute-start.7
  40.3 0.0 copy-done.1
  40.4 0.0 copy-done.2
  40.4 0.0 copy-done.3
  40.4 5.2 %forward.1 = (f32[4096,128]{1,0:T(8,128)S(1)}, f32[4096,128]{1,0:T(8,128)S(1)}, f32[4096,128]{1,0:T(8,128)S(1)}, f32[4096,128]{1,0:T(8,128)S(1)}, f32[4096,128]{...) custom-call(f32[4096,128]{1,0:T(8,128)S(1)} %table.1, f32[1,32768]{1,0:T(1,128)S(1)} %copy-done.2, ...), custom_call_target="tpu_custom_call" | custom-call | bytes 21000000 | tf_op jit(solution)/shard_map/forward/pallas_call | solution.py:454
  45.6 1.4 %collective-permute-done.6.near = f32[48,1024]{1,0:T(8,128)S(1)} collective-permute-done((f32[48,1024]{1,0:T(8,128)S(1)}, f32[48,1024]{1,0:T(8,128)S(1)}, u32[]{:S(2)}, u32[]{:S(2)}) %collective-permute-start.6) | collective-permute-done | bytes 196640 | tf_op jit(solution)/shard_map/ppermute | solution.py:747
  47.0 1.2 %collective-permute-done.7.far = f32[48,1024]{1,0:T(8,128)S(1)} collective-permute-done((f32[48,1024]{1,0:T(8,128)S(1)}, f32[48,1024]{1,0:T(8,128)S(1)}, u32[]{:S(2)}, u32[]{:S(2)}) %collective-permute-start.7) | collective-permute-done | bytes 196640 | tf_op jit(solution)/shard_map/ppermute | solution.py:747
  48.2 9.1 %couple.1 = (f32[4096,128]{1,0:T(8,128)S(1)}, f32[48,1024]{1,0:T(8,128)S(1)}, f32[4096,128]{1,0:T(8,128)S(1)}, f32[4096,128]{1,0:T(8,128)S(1)}, f32[4096,128]{1,0:T(8,128)S(1)}, /*index=5*/f32[4096,128]{1,0:T(8,128)S(1)}) custom-call(s32[1,6144]{1,0:T(1,128)S(1)} %copy-done.1, ...), custom_call_target="tpu_custom_call", output_to_operand_aliasing={{2}: (4, {}), {3}: (5, {}), {4}: (6, {}), {5}: (7, {})} | custom-call | bytes 33000000 | tf_op jit(solution)/shard_map/couple/pallas_call | solution.py:493
  57.3 1.2 %collective-permute-start.9 = (f32[48,1024]{1,0:T(8,128)S(1)}, f32[48,1024]{1,0:T(8,128)S(1)}, u32[]{:S(2)}, u32[]{:S(2)}) collective-permute-start(f32[48,1024]{1,0:T(8,128)S(1)} %get-tuple-element.40), channel_id=1, source_target_pairs={{0,96},{1,97},{2,98},{3,99},{4,100},{5,101},{6,102},{7,103},{8,104... | collective-permute-start | bytes 589832 | tf_op jit(solution)/shard_map/ppermute | solution.py:747
  58.5 3.2 %at_receptors.1 = f32[48,1024]{1,0:T(8,128)S(1)} custom-call(f32[4096,128]{1,0:T(8,128)S(1)} %get-tuple-element.39.tangent, s32[1,6144]{1,0:T(1,128)S(1)} %copy-done.1, s32[6144]{0:T(1024)S(1)} %bitcast.20), custom_call_target="tpu_custom_call" | custom-call | bytes 9000000 | tf_op jit(solution)/shard_map/at_receptors/pallas_call | solution.py:517
  61.8 1.0 collective-permute-start.8
  62.7 2.1 %collective-permute-done.9.ready.far = f32[48,1024]{1,0:T(8,128)S(1)} collective-permute-done((f32[48,1024]{1,0:T(8,128)S(1)}, f32[48,1024]{1,0:T(8,128)S(1)}, u32[]{:S(2)}, u32[]{:S(2)}) %collective-permute-start.9) | collective-permute-done | bytes 196640 | tf_op jit(solution)/shard_map/ppermute | solution.py:747
  64.9 2.8 %transposed.1 = (f32[4096,128]{1,0:T(8,128)S(1)}, f32[4096,128]{1,0:T(8,128)S(1)}, f32[4096,128]{1,0:T(8,128)S(1)}, f32[4096,128]{1,0:T(8,128)S(1)}) custom-call(f32[4096,128]{1,0:T(8,128)S(1)} %get-tuple-element.39.tangent, f32[4096,128]{1,0:T(8,128)S(1)} %get-tuple-element.43.centre, f32[4096,128]{1,0:T(8,128)S(1)} %get-tuple-element.41.lower, ...), custom_call_target="tpu_custom_call" | custom-call | bytes 3000000 | tf_op jit(solution)/shard_map/transposed/pallas_call | solution.py:569
  67.6 0.0 collective-permute-done.8.near
  67.7 0.1 collective-permute-start.10
  67.7 5.3 %collective-permute-start.11 = (f32[32,1152]{1,0:T(8,128)S(1)}, f32[32,1152]{1,0:T(8,128)S(1)}, u32[]{:S(2)}, u32[]{:S(2)}) collective-permute-start(f32[32,1152]{1,0:T(8,128)S(1)} %get-tuple-element.46), channel_id=1, source_target_pairs={{0,15},{1,0},{2,1},{3,2},{4,3},{5,4},{6,5},{7,6},{8,7},{9,8},{10,9... | collective-permute-start | bytes 442376 | tf_op jit(solution)/shard_map/ppermute | solution.py:747
  73.1 7.1 %add_same.1 = (f32[4096,128]{1,0:T(8,128)S(1)}, f32[4096,128]{1,0:T(8,128)S(1)}, f32[4096,128]{1,0:T(8,128)S(1)}, f32[4096,128]{1,0:T(8,128)S(1)}) custom-call(s32[4,6144]{1,0:T(4,128)S(1)} %bitcast.13, s32[24576]{0:T(1024)S(1)} %bitcast.17, ...), custom_call_target="tpu_custom_call", output_to_operand_aliasing={{0}: (6, {}), {1}: (7, {}), {2}: (8, {}), {3}: (9, {})} | custom-call | bytes 27000000 | tf_op jit(solution)/shard_map/add_same/pallas_call | solution.py:593
  80.2 0.0 collective-permute-done.10.before
  80.2 0.0 collective-permute-done.11.after
  80.2 17.0 %add_sides.1 = (f32[4096,128]{1,0:T(8,128)S(1)}, f32[1,256]{1,0:T(1,128)S(1)}, f32[4096,128]{1,0:T(8,128)S(1)}, f32[4096,128]{1,0:T(8,128)S(1)}, f32[4096,128]{1,0:T(8,128)S(1)}, /*index=5*/f32[4096,128]{1,0:T(8,128)S(1)}) custom-call(s32[4,6144]{1,0:T(4,128)S(1)} %bitcast.14, ...), custom_call_target="tpu_custom_call", output_to_operand_aliasing={{2}: (6, {}), {3}: (7, {}), {4}: (8, {}), {5}: (9, {})} | custom-call | bytes 54000000 | tf_op jit(solution)/shard_map/add_sides/pallas_call | solution.py:664
  97.2 0.1 broadcast_in_dim.3
  97.3 15.2 %all_to_all.5 = f32[128,1,256]{2,1,0:T(1,128)S(1)} all-to-all(f32[128,1,256]{2,1,0:T(1,128)S(1)} %broadcast_in_dim.3), channel_id=1, replica_groups=mesh['grid'=8,'cell'=16] {'grid','cell'}, dimensions={0} | all-to-all | bytes 262144 | tf_op jit(solution)/shard_map/all_to_all | solution.py:761
  112.5 0.2 reduce_sum.11
  112.6 4.8 %basis.1 = (f32[16,1,32768]{2,1,0:T(1,128)}, f32[16,16]{1,0:T(8,128)}) custom-call(f32[1,256]{1,0:T(1,128)S(1)} %bitcast.21, f32[4096,128]{1,0:T(8,128)S(1)} %get-tuple-element.55.adjoint), custom_call_target="tpu_custom_call" | custom-call | bytes 18000000 | tf_op jit(solution)/shard_map/basis/pallas_call | solution.py:725
  (7 shorter events, 0.1 us)
Async XLA Ops:
  1.5 5.8 %collective-permute-start.1 = (f32[4,3072]{1,0:T(4,128)S(1)}, f32[4,3072]{1,0:T(4,128)S(1)}, u32[]{:S(2)}, u32[]{:S(2)}) collective-permute-start(f32[4,3072]{1,0:T(4,128)S(1)} %get-tuple-element.56), channel_id=1, source_target_pairs={{0,96},{1,97},{2,98},{3,99},{4,100},{5,101},{6,102},{7,103},{8,104... | collective-permute-start | bytes 147464 | tf_op jit(solution)/shard_map/ppermute | solution.py:747
  4.4 2.8 %collective-permute-start = (f32[4,3072]{1,0:T(4,128)S(1)}, f32[4,3072]{1,0:T(4,128)S(1)}, u32[]{:S(2)}, u32[]{:S(2)}) collective-permute-start(f32[4,3072]{1,0:T(4,128)S(1)} %get-tuple-element.57), channel_id=1, source_target_pairs={{0,112},{1,113},{2,114},{3,115},{4,116},{5,117},{6,118},{7,119},{8... | collective-permute-start | bytes 147464 | tf_op jit(solution)/shard_map/ppermute | solution.py:747
  7.2 6.7 %copy-start = (s32[1,4,6144]{2,1,0:T(4,128)S(1)}, s32[1,4,6144]{2,1,0:T(4,128)}, u32[]{:S(2)}) copy-start(s32[1,4,6144]{2,1,0:T(4,128)} %param.11) | copy-start | bytes 294916
  7.3 18.0 %collective-permute-start.2 = (f32[8,1152]{1,0:T(8,128)S(1)}, f32[8,1152]{1,0:T(8,128)S(1)}, u32[]{:S(2)}, u32[]{:S(2)}) collective-permute-start(f32[8,1152]{1,0:T(8,128)S(1)} %get-tuple-element.29), channel_id=1, source_target_pairs={{0,1},{1,2},{2,3},{3,4},{4,5},{5,6},{6,7},{7,8},{8,9},{9,10},{10,1... | collective-permute-start | bytes 110600 | tf_op jit(solution)/shard_map/ppermute | solution.py:747
  8.9 16.4 %collective-permute-start.3 = (f32[8,1152]{1,0:T(8,128)S(1)}, f32[8,1152]{1,0:T(8,128)S(1)}, u32[]{:S(2)}, u32[]{:S(2)}) collective-permute-start(f32[8,1152]{1,0:T(8,128)S(1)} %get-tuple-element.30), channel_id=1, source_target_pairs={{0,15},{1,0},{2,1},{3,2},{4,3},{5,4},{6,5},{7,6},{8,7},{9,8},{10,9... | collective-permute-start | bytes 110600 | tf_op jit(solution)/shard_map/ppermute | solution.py:747
  28.7 11.6 %copy-start.1 = (s32[1,6144]{1,0:T(1,128)S(1)}, s32[1,6144]{1,0:T(1,128)}, u32[]{:S(2)}) copy-start(s32[1,6144]{1,0:T(1,128)} %cells.3) | copy-start | bytes 73732
  28.7 11.7 %copy-start.2 = (f32[1,32768]{1,0:T(1,128)S(1)}, f32[1,32768]{1,0:T(1,128)}, u32[]{:S(2)}) copy-start(f32[1,32768]{1,0:T(1,128)} %centre.1) | copy-start | bytes 393220
  28.7 11.7 %copy-start.3 = (f32[1,32768]{1,0:T(1,128)S(1)}, f32[1,32768]{1,0:T(1,128)}, u32[]{:S(2)}) copy-start(f32[1,32768]{1,0:T(1,128)} %lower.1) | copy-start | bytes 393220
  28.7 11.6 %copy-start.4 = (f32[1,32768]{1,0:T(1,128)S(1)}, f32[1,32768]{1,0:T(1,128)}, u32[]{:S(2)}) copy-start(f32[1,32768]{1,0:T(1,128)} %upper.1) | copy-start | bytes 393220
  28.8 9.7 %collective-permute-start.4 = (f32[32,1024]{1,0:T(8,128)S(1)}, f32[32,1024]{1,0:T(8,128)S(1)}, u32[]{:S(2)}, u32[]{:S(2)}) collective-permute-start(f32[32,1024]{1,0:T(8,128)S(1)} %get-tuple-element.31), channel_id=1, source_target_pairs={{0,15},{1,0},{2,1},{3,2},{4,3},{5,4},{6,5},{7,6},{8,7},{9,8},{10,9... | collective-permute-start | bytes 393224 | tf_op jit(solution)/shard_map/ppermute | solution.py:747
  30.8 8.4 %collective-permute-start.5 = (f32[32,1024]{1,0:T(8,128)S(1)}, f32[32,1024]{1,0:T(8,128)S(1)}, u32[]{:S(2)}, u32[]{:S(2)}) collective-permute-start(f32[32,1024]{1,0:T(8,128)S(1)} %get-tuple-element.32), channel_id=1, source_target_pairs={{0,1},{1,2},{2,3},{3,4},{4,5},{5,6},{6,7},{7,8},{8,9},{9,10},{10,1... | collective-permute-start | bytes 393224 | tf_op jit(solution)/shard_map/ppermute | solution.py:747
  39.2 7.8 %collective-permute-start.6 = (f32[48,1024]{1,0:T(8,128)S(1)}, f32[48,1024]{1,0:T(8,128)S(1)}, u32[]{:S(2)}, u32[]{:S(2)}) collective-permute-start(f32[48,1024]{1,0:T(8,128)S(1)} %get-tuple-element.33), channel_id=1, source_target_pairs={{0,16},{1,17},{2,18},{3,19},{4,20},{5,21},{6,22},{7,23},{8,24},{9,... | collective-permute-start | bytes 589832 | tf_op jit(solution)/shard_map/ppermute | solution.py:747
  39.2 9.0 %collective-permute-start.7 = (f32[48,1024]{1,0:T(8,128)S(1)}, f32[48,1024]{1,0:T(8,128)S(1)}, u32[]{:S(2)}, u32[]{:S(2)}) collective-permute-start(f32[48,1024]{1,0:T(8,128)S(1)} %get-tuple-element.34), channel_id=1, source_target_pairs={{0,32},{1,33},{2,34},{3,35},{4,36},{5,37},{6,38},{7,39},{8,40},{9,... | collective-permute-start | bytes 589832 | tf_op jit(solution)/shard_map/ppermute | solution.py:747
  57.3 7.5 %collective-permute-start.9 = (f32[48,1024]{1,0:T(8,128)S(1)}, f32[48,1024]{1,0:T(8,128)S(1)}, u32[]{:S(2)}, u32[]{:S(2)}) collective-permute-start(f32[48,1024]{1,0:T(8,128)S(1)} %get-tuple-element.40), channel_id=1, source_target_pairs={{0,96},{1,97},{2,98},{3,99},{4,100},{5,101},{6,102},{7,103},{8,104... | collective-permute-start | bytes 589832 | tf_op jit(solution)/shard_map/ppermute | solution.py:747
  61.8 5.8 %collective-permute-start.8 = (f32[48,1024]{1,0:T(8,128)S(1)}, f32[48,1024]{1,0:T(8,128)S(1)}, u32[]{:S(2)}, u32[]{:S(2)}) collective-permute-start(f32[48,1024]{1,0:T(8,128)S(1)} %at_receptors.1), channel_id=1, source_target_pairs={{0,112},{1,113},{2,114},{3,115},{4,116},{5,117},{6,118},{7,119},{8... | collective-permute-start | bytes 589832 | tf_op jit(solution)/shard_map/ppermute | solution.py:747
  67.7 12.5 %collective-permute-start.10 = (f32[32,1152]{1,0:T(8,128)S(1)}, f32[32,1152]{1,0:T(8,128)S(1)}, u32[]{:S(2)}, u32[]{:S(2)}) collective-permute-start(f32[32,1152]{1,0:T(8,128)S(1)} %get-tuple-element.45), channel_id=1, source_target_pairs={{0,1},{1,2},{2,3},{3,4},{4,5},{5,6},{6,7},{7,8},{8,9},{9,10},{10,1... | collective-permute-start | bytes 442376 | tf_op jit(solution)/shard_map/ppermute | solution.py:747
  67.7 12.5 %collective-permute-start.11 = (f32[32,1152]{1,0:T(8,128)S(1)}, f32[32,1152]{1,0:T(8,128)S(1)}, u32[]{:S(2)}, u32[]{:S(2)}) collective-permute-start(f32[32,1152]{1,0:T(8,128)S(1)} %get-tuple-element.46), channel_id=1, source_target_pairs={{0,15},{1,0},{2,1},{3,2},{4,3},{5,4},{6,5},{7,6},{8,7},{9,8},{10,9... | collective-permute-start | bytes 442376 | tf_op jit(solution)/shard_map/ppermute | solution.py:747
